TPU v7x, 32 devices: a whole 2x2x4 slice. The times are simulated.
32 devices in a mesh: groups: 2 (over x), basis: 16 (over z, y, core).
Axes of the slice: x: 2, y: 2, z: 4, core: 2. Of those that a mesh axis runs over, the one named last changes fastest.
Arguments:
- factors: bfloat16 [32, 30, 512, 128], P(('groups', 'basis')), parts along dimension 0, may hold values from -3 to 3
- coefs: bfloat16 [32, 30, 128], P(('groups', 'basis')), parts along dimension 0, may hold values from -0.0234375 to 0.0234375
- domains: int32 [32, 30], P('groups'), parts along dimension 0, may hold values from 0 to 89, as said below
- pairs: int32 [32, 4], P(('groups', 'basis')), parts along dimension 0, may hold values 0 or 1
Outputs:
- exchange_band: float32 [32, 9, 128, 128], P(('groups', 'basis')), parts along dimension 0
- coulomb_half: float32 [32, 30, 128], P(('groups', 'basis')), parts along dimension 0
There are 2 independent parts, one for each index of `groups`. A program takes and returns all parts, laid end to end along the dimension named above; each array names one. Nothing has to cross between parts.
Inputs may be any that keep to these rules, and one draw needn't show every extreme that they name: `domains`: each row holds 30 different ids, all in [2 b, 2 b + 60) for block b, among them 2 b and 2 b + 2 * 30 - 1.
All inputs are finite; a program needn't handle non-finite values. No bound on the sum of `pairs` on one device may be relied on, other than what follows from the above.
Results may differ from a plain program's by a relative error of at most 0.003.
Values may be sent and summed in bfloat16 or wider, within the bound.
No kernel may reach another device: no remote copies, remote signals or barrier semaphores. Data moves between devices by JAX's collectives and lax.ppermute only.
A program may use at most 128 MiB of HBM per device.

v0:
```python
import jax
import jax.numpy as jnp
from jax import lax
from jax.sharding import PartitionSpec as P


def passed_along(block, axis, distance):
    devices = range(lax.axis_size(axis))
    route = [(i - distance, i) for i in devices if i - distance in devices]
    return lax.ppermute(block, axis, route)


def contract(own, own_dom, remote, remote_dom):
    width = own.shape[-1]
    match = (own_dom[:, None] == remote_dom[None, :]).astype(jnp.bfloat16)
    aligned = jnp.einsum("kl,lpm->kpm", match, remote, preferred_element_type=jnp.float32).astype(
        jnp.bfloat16
    )
    return lax.dot_general(
        own.reshape(-1, width),
        aligned.reshape(-1, width),
        (((0,), (0,)), ((), ())),
        preferred_element_type=jnp.float32,
    )


def per_device(factors, coefs, domains, pairs):
    own = factors[0]
    coef = coefs[0]
    count = lax.axis_size("basis")
    me = lax.axis_index("basis")
    depth = pairs.shape[1]
    own_dom = lax.dynamic_slice_in_dim(domains, me, 1, 0)[0]
    partial_sum = jnp.einsum("kpm,km->p", own, coef, preferred_element_type=jnp.float32)
    gamma = lax.psum(partial_sum, "basis")
    gamma_low = gamma.astype(jnp.bfloat16)
    coulomb_half = jnp.einsum("kpm,p->km", own, gamma_low, preferred_element_type=jnp.float32)
    band = [None] * (2 * depth + 1)
    band[depth] = contract(own, own_dom, own, own_dom)
    carried = own
    for offset in range(1, depth + 1):
        carried = passed_along(carried, "basis", -1)
        other = jnp.minimum(me + offset, count - 1)
        remote_dom = lax.dynamic_slice_in_dim(domains, other, 1, 0)[0]
        valid = jnp.logical_and(pairs[0, offset - 1] == 1, me + offset < count)
        value = contract(own, own_dom, carried, remote_dom)
        block = jnp.where(valid, value, jnp.zeros_like(value))
        band[depth + offset] = block
        band[depth - offset] = passed_along(block.T, "basis", offset)
    return (jnp.stack(band)[None], coulomb_half[None])


def solution(mesh):
    placed = (
        P(("groups", "basis"), None, None, None),
        P(("groups", "basis"), None, None),
        P("groups", None),
        P(("groups", "basis"), None),
    )
    return jax.shard_map(
        per_device,
        mesh=mesh,
        in_specs=placed,
        out_specs=(P(("groups", "basis"), None, None, None), P(("groups", "basis"), None, None)),
        check_vma=False,
    )
```

profile of v0, /device:TPU:0, one launch (start us, length us, event | category | flops | bytes accessed | tf_op | source)
XLA Modules:
  0.0 276.0 jit_solution(13108761754584664854)
XLA Ops:
  0.6 1.3 collective-permute-start
  1.9 7.6 %collective-permute-done = bf16[30,512,128]{2,1,0:T(8,128)(2,1)S(1)} collective-permute-done((bf16[30,512,128]{2,1,0:T(8,128)(2,1)}, bf16[30,512,128]{2,1,0:T(8,128)(2,1)S(1)}, u32[]{:S(2)}, u32[]{:S(2)}) %collective-permute-start) | collective-permute-done | bytes 3932192 | tf_op jit(solution)/shard_map/ppermute | solution.py:10
  10.8 46.6 %collective-permute-done.1 = bf16[30,512,128]{2,1,0:T(8,128)(2,1)S(1)} collective-permute-done((bf16[30,512,128]{2,1,0:T(8,128)(2,1)S(1)}, bf16[30,512,128]{2,1,0:T(8,128)(2,1)S(1)}, u32[]{:S(2)}, u32[]{:S(2)}) %collective-permute-start.1) | collective-permute-done | bytes 3932192 | tf_op jit(solution)/shard_map/ppermute | solution.py:10
  57.4 1.9 copy-done.2
  60.6 45.8 %collective-permute-done.2 = bf16[30,512,128]{2,1,0:T(8,128)(2,1)} collective-permute-done((bf16[30,512,128]{2,1,0:T(8,128)(2,1)S(1)}, bf16[30,512,128]{2,1,0:T(8,128)(2,1)}, u32[]{:S(2)}, u32[]{:S(2)}) %collective-permute-start.2) | collective-permute-done | bytes 3932192 | tf_op jit(solution)/shard_map/ppermute | solution.py:10
  107.7 1.5 fusion.56
  111.7 3.2 %fusion.36 = f32[1,512,1]{1,0,2:T(1,128)S(1)} fusion(bf16[30,128,1]{1,0,2:T(8,128)(2,1)S(1)} %bitcast.86, bf16[1,30,512,128]{3,2,1,0:T(8,128)(2,1)} %param.4), kind=kOutput, calls=%fused_computation.40 | convolution fusion | flops 3932160 | bytes 3941888 | tf_op jit(solution)/shard_map/kpm,km->p/dot_general | solution.py:34
  115.0 99.9 %psum.7 = bf16[512]{0:T(512)(128)(2,1)S(1)} all-reduce(f32[512]{0:T(512)S(1)} %bitcast.104), channel_id=1, replica_groups=mesh['groups'=2,'basis'=16] {'basis'}, use_global_device_ids=true, to_apply=%region_0.0 | all-reduce | flops 512 | bytes 3072 | tf_op jit(solution)/shard_map/psum | solution.py:35
  215.8 6.9 %fusion.22 = bf16[30,512,128]{2,0,1:T(8,128)(2,1)} fusion(bf16[30,512,128]{2,1,0:T(8,128)(2,1)} %bitcast.88, s32[30]{0:T(128)S(1)} %get-tuple-element.11), kind=kOutput, calls=%fused_computation.14 | convolution fusion | flops 119931776 | bytes 7864440 | tf_op jit(solution)/shard_map/kl,lpm->kpm/dot_general | solution.py:16
  222.6 2.7 fusion.19
  225.3 1.5 copy.31
  228.6 1.5 collective-permute-start.7
  230.1 2.7 fusion.16
  232.8 1.5 copy.29
  235.6 1.9 collective-permute-start.6
  237.5 4.8 %fusion.13 = bf16[30,512,128]{2,0,1:T(8,128)(2,1)S(1)} fusion(bf16[30,512,128]{2,1,0:T(8,128)(2,1)} %collective-permute-done.2, s32[30]{0:T(128)S(1)} %get-tuple-element.9, s32[30]{0:T(128)S(1)} %get-tuple-element.11), kind=kOutput, calls=%fused_computation.11 | convolution fusion | flops 119931776 | bytes 7864560 | tf_op jit(solution)/shard_map/kl,lpm->kpm/dot_general | solution.py:16
  242.2 1.5 copy.27
  245.0 4.9 %collective-permute-start.5 = (f32[128,128]{1,0:T(8,128)S(1)}, f32[128,128]{1,0:T(8,128)S(1)}, u32[]{:S(2)}, u32[]{:S(2)}) collective-permute-start(f32[128,128]{1,0:T(8,128)S(1)} %convolution_select_fusion.2), channel_id=1, source_target_pairs={{0,3},{1,4},{2,5},{3,6},{4,7},{5,8},{6,9},{7,10},{8,11},{9,12},{10... | collective-permute-start | bytes 196616 | tf_op jit(solution)/shard_map/ppermute | solution.py:10
  249.9 4.8 %fusion.10 = bf16[30,512,128]{2,0,1:T(8,128)(2,1)S(1)} fusion(bf16[30,512,128]{2,1,0:T(8,128)(2,1)} %collective-permute-done.3, s32[30]{0:T(128)S(1)} %get-tuple-element.10, s32[30]{0:T(128)S(1)} %get-tuple-element.11), kind=kOutput, calls=%fused_computation.10 | convolution fusion | flops 119931776 | bytes 7864560 | tf_op jit(solution)/shard_map/kl,lpm->kpm/dot_general | solution.py:16
  254.7 1.5 copy.24
  257.5 3.5 %collective-permute-start.4 = (f32[128,128]{0,1:T(8,128)S(1)}, f32[128,128]{0,1:T(8,128)S(1)}, u32[]{:S(2)}, u32[]{:S(2)}) collective-permute-start(f32[128,128]{0,1:T(8,128)S(1)} %copy.25), channel_id=1, source_target_pairs={{0,4},{1,5},{2,6},{3,7},{4,8},{5,9},{6,10},{7,11},{8,12},{9,13},{1... | collective-permute-start | bytes 196616 | tf_op jit(solution)/shard_map/ppermute | solution.py:10
  261.1 2.7 fusion.53
  263.8 5.6 %copy.33 = bf16[30,512,128]{2,1,0:T(8,128)(2,1)} copy(bf16[30,512,128]{2,0,1:T(8,128)(2,1)} %fusion.22) | data formatting | bytes 7864320 | tf_op jit(solution)/shard_map/convert_element_type | solution.py:16
  270.4 4.5 %fusion.25 = f32[9,128,128]{1,2,0:T(8,128)S(1)} fusion(f32[9,128,128]{1,2,0:T(8,128)S(1)} %constant_dynamic-update-slice_fusion, bf16[15360,128]{1,0:T(8,128)(2,1)} %bitcast.94, bf16[15360,128]{1,0:T(8,128)(2,1)} %bitcast.89), kind=kOutput, calls=%fused_computation.16 | convolution fusion | flops 503316480 | bytes 7929856 | tf_op jit(solution)/shard_map/dot_general | solution.py:19
  (40 shorter events, 12.3 us)
Async XLA Ops:
  0.6 111.1 %copy-start = (bf16[1,30,128]{2,1,0:T(8,128)(2,1)S(1)}, bf16[1,30,128]{2,1,0:T(8,128)(2,1)}, u32[]{:S(2)}) copy-start(bf16[1,30,128]{2,1,0:T(8,128)(2,1)} %param.5) | copy-start | bytes 23044
  0.6 8.9 %collective-permute-start = (bf16[30,512,128]{2,1,0:T(8,128)(2,1)}, bf16[30,512,128]{2,1,0:T(8,128)(2,1)S(1)}, u32[]{:S(2)}, u32[]{:S(2)}) collective-permute-start(bf16[30,512,128]{2,1,0:T(8,128)(2,1)} %bitcast.87), channel_id=1, source_target_pairs={{1,0},{2,1},{3,2},{4,3},{5,4},{6,5},{7,6},{8,7},{9,8},{10,9},{11,1... | collective-permute-start | bytes 11796488 | tf_op jit(solution)/shard_map/ppermute | solution.py:10
  9.5 96.9 %copy-start.4 = (bf16[30,512,128]{2,1,0:T(8,128)(2,1)}, bf16[30,512,128]{2,1,0:T(8,128)(2,1)S(1)}, u32[]{:S(2)}) copy-start(bf16[30,512,128]{2,1,0:T(8,128)(2,1)S(1)} %collective-permute-done) | copy-start | bytes 11796484
  9.5 47.9 %collective-permute-start.1 = (bf16[30,512,128]{2,1,0:T(8,128)(2,1)S(1)}, bf16[30,512,128]{2,1,0:T(8,128)(2,1)S(1)}, u32[]{:S(2)}, u32[]{:S(2)}) collective-permute-start(bf16[30,512,128]{2,1,0:T(8,128)(2,1)S(1)} %collective-permute-done), channel_id=1, source_target_pairs={{1,0},{2,1},{3,2},{4,3},{5,4},{6,5},{7,6},{8,7},{9,8},{10,9},{11,1... | collective-permute-start | bytes 11796488 | tf_op jit(solution)/shard_map/ppermute | solution.py:10
  57.4 1.9 copy-start.2
  59.3 47.1 %collective-permute-start.2 = (bf16[30,512,128]{2,1,0:T(8,128)(2,1)S(1)}, bf16[30,512,128]{2,1,0:T(8,128)(2,1)}, u32[]{:S(2)}, u32[]{:S(2)}) collective-permute-start(bf16[30,512,128]{2,1,0:T(8,128)(2,1)S(1)} %collective-permute-done.1), channel_id=1, source_target_pairs={{1,0},{2,1},{3,2},{4,3},{5,4},{6,5},{7,6},{8,7},{9,8},{10,9},{11,1... | collective-permute-start | bytes 11796488 | tf_op jit(solution)/shard_map/ppermute | solution.py:10
  106.4 143.5 %collective-permute-start.3 = (bf16[30,512,128]{2,1,0:T(8,128)(2,1)}, bf16[30,512,128]{2,1,0:T(8,128)(2,1)}, u32[]{:S(2)}, u32[]{:S(2)}) collective-permute-start(bf16[30,512,128]{2,1,0:T(8,128)(2,1)} %collective-permute-done.2), channel_id=1, source_target_pairs={{1,0},{2,1},{3,2},{4,3},{5,4},{6,5},{7,6},{8,7},{9,8},{10,9},{11,1... | collective-permute-start | bytes 11796488 | tf_op jit(solution)/shard_map/ppermute | solution.py:10
  215.8 6.9 %copy-start.5 = (bf16[30,512,128]{2,1,0:T(8,128)(2,1)S(1)}, bf16[30,512,128]{2,1,0:T(8,128)(2,1)}, u32[]{:S(2)}) copy-start(bf16[30,512,128]{2,1,0:T(8,128)(2,1)} %copy-done.4) | copy-start | bytes 11796484
  225.3 2.1 copy-start.1
  227.4 2.7 copy-start.3
  228.6 41.4 %collective-permute-start.7 = (f32[128,128]{1,0:T(8,128)S(1)}, f32[128,128]{1,0:T(8,128)S(1)}, u32[]{:S(2)}, u32[]{:S(2)}) collective-permute-start(f32[128,128]{1,0:T(8,128)S(1)} %convolution_select_fusion), channel_id=1, source_target_pairs={{0,1},{1,2},{2,3},{3,4},{4,5},{5,6},{6,7},{7,8},{8,9},{9,10},{10,1... | collective-permute-start | bytes 196616 | tf_op jit(solution)/shard_map/ppermute | solution.py:10
  235.6 34.6 %collective-permute-start.6 = (f32[128,128]{1,0:T(8,128)S(1)}, f32[128,128]{1,0:T(8,128)S(1)}, u32[]{:S(2)}, u32[]{:S(2)}) collective-permute-start(f32[128,128]{1,0:T(8,128)S(1)} %convolution_select_fusion.1), channel_id=1, source_target_pairs={{0,2},{1,3},{2,4},{3,5},{4,6},{5,7},{6,8},{7,9},{8,10},{9,11},{10,... | collective-permute-start | bytes 196616 | tf_op jit(solution)/shard_map/ppermute | solution.py:10
  245.0 25.2 %collective-permute-start.5 = (f32[128,128]{1,0:T(8,128)S(1)}, f32[128,128]{1,0:T(8,128)S(1)}, u32[]{:S(2)}, u32[]{:S(2)}) collective-permute-start(f32[128,128]{1,0:T(8,128)S(1)} %convolution_select_fusion.2), channel_id=1, source_target_pairs={{0,3},{1,4},{2,5},{3,6},{4,7},{5,8},{6,9},{7,10},{8,11},{9,12},{10... | collective-permute-start | bytes 196616 | tf_op jit(solution)/shard_map/ppermute | solution.py:10
  257.5 12.8 %collective-permute-start.4 = (f32[128,128]{0,1:T(8,128)S(1)}, f32[128,128]{0,1:T(8,128)S(1)}, u32[]{:S(2)}, u32[]{:S(2)}) collective-permute-start(f32[128,128]{0,1:T(8,128)S(1)} %copy.25), channel_id=1, source_target_pairs={{0,4},{1,5},{2,6},{3,7},{4,8},{5,9},{6,10},{7,11},{8,12},{9,13},{1... | collective-permute-start | bytes 196616 | tf_op jit(solution)/shard_map/ppermute | solution.py:10
where the time goes:
time: 277 us; the launch traced here: 276 us
  waiting for transfers between devices  100 us (36%)
  blocking collectives  99.9 us (36%)
  matrix products  37.1 us (13%)
  local copies, waits for them, and re-layouts  18.6 us (7%)
  starting transfers between devices  16.9 us (6%)
  between operations  3.53 us (1%)
    ppermute x8, waiting for transfers between devices, passed_along(): return lax.ppermute(block, axis, route)  100 us
    psum x1, blocking collectives, per_device(): gamma = lax.psum(partial_sum, 'basis')  99.9 us
    dot_general x5, matrix products, contract(): jnp.einsum('kl,lpm->kpm', match, remote, preferred_element_type=jnp.float32)  21.7 us
    ppermute x8, starting transfers between devices, passed_along(): return lax.ppermute(block, axis, route)  16.9 us
    convert_element_type x5, local copies, waits for them, and re-layouts, contract(): jnp.einsum('kl,lpm->kpm', match, remote, preferred_element_type=jnp.float32)  11.7 us
    dot_general x5, matrix products, contract(): lax.dot_general(own.reshape(-1, width), aligned.reshape(-1, width), (((0,...  9.46 us
  transfers between devices with their start and end apart: 8, of which 3 were waited for; matrix products, arithmetic and copies ran while one was open for 17% of the time, Pallas kernels for 0%

commit v1 on v0

v1 whole, which is shorter than its diff:
```python
import functools

import jax
import jax.numpy as jnp
from jax import lax
from jax.experimental import pallas as pl
from jax.experimental.pallas import tpu as pltpu
from jax.sharding import PartitionSpec as P

F32 = jnp.float32
BF16 = jnp.bfloat16

XJ, XO, YJ, YO, FJ, FO, GJ, GO = range(8)
PRODUCTS = (
    (XJ, XJ, None),
    (XJ, XO, None),
    (XJ, YJ, "main"),
    (XJ, YO, "main"),
    (YJ, XO, "main"),
    (XJ, FJ, "main"),
    (None, None, "main"),
    (YJ, FJ, "main"),
    (YJ, FO, "main"),
    (FJ, YO, "main"),
    (XJ, GJ, "side"),
    (None, None, "side"),
)
FIRST_SHARED = 2
CROSS_F, CROSS_G = 6, 11
CUT = 192


def chip_route(count, target, swap=False):
    chips = count // 2
    route = []
    for chip in range(chips):
        to = target(chip)
        if 0 <= to < chips:
            for core in range(2):
                route.append((2 * chip + core, 2 * to + (1 - core if swap else core)))
    return route


def matches(left, right, valid):
    rows = left.shape[1]
    width = 32
    equal = jnp.logical_and(left[:, :, None] == right[:, None, :], valid[:, None, None])
    row = jnp.arange(rows, dtype=jnp.int32)
    partner = jnp.sum(jnp.where(equal, row[None, None, :], 0), axis=2)
    hit = jnp.sum(equal.astype(jnp.int32), axis=2)
    place = jnp.sum(jnp.where(row[None, None, :] < row[None, :, None], hit[:, None, :], 0), axis=2)
    slot = jnp.arange(width, dtype=jnp.int32)
    chosen = jnp.logical_and(place[:, None, :] == slot[None, :, None], hit[:, None, :] == 1)
    mine = jnp.sum(jnp.where(chosen, row[None, None, :], 0), axis=2)
    theirs = jnp.sum(jnp.where(chosen, partner[:, None, :], 0), axis=2)
    return jnp.sum(hit, axis=1), mine, theirs


def multiply(left, right):
    return lax.dot_general(left, right, (((0,), (0,)), ((), ())), preferred_element_type=F32)


def chunk_kernel(first, last, start, size, stack, *refs):
    refs = list(refs)
    place, number, mine, theirs = refs[:4]
    refs = refs[4:]
    before = None if first else refs.pop(0)
    blocks, outs = refs[:8], refs[8:]
    total = outs[0] if not last else outs[-1]
    if first:
        total[...] = jnp.zeros_like(total)
    else:
        total[...] = before[...]
    flag = place[2] == 1

    def rows_of(block, row, half):
        if block in (XJ, XO):
            offset = pl.multiple_of(place[0 if half == "main" else 1] + start, 16)
            return blocks[block][row, pl.ds(offset, size), :]
        return blocks[block][row]

    def operand(q, side, row):
        left_or_right = PRODUCTS[q][side]
        half = PRODUCTS[q][2]
        if left_or_right is not None:
            return rows_of(left_or_right, row, half)
        if q == CROSS_F:
            one, two = ((FJ, XJ), (XO, FO))[side]
        else:
            one, two = ((XJ, GJ), (GO, XO))[side]
        return jnp.where(flag, rows_of(one, row, half), rows_of(two, row, half))

    def add(q, group):
        lefts, rights = [], []
        for i in range(stack):
            slot = group * stack + i
            left = operand(q, 0, mine[q, slot])
            if stack > 1:
                left = jnp.where(slot < number[q], left, jnp.zeros_like(left))
            lefts.append(left)
            rights.append(operand(q, 1, theirs[q, slot]))
        if stack == 1:
            left = jnp.where(group < number[q], lefts[0], jnp.zeros_like(lefts[0]))
            total[q] += multiply(left, rights[0])
        else:
            total[q] += multiply(jnp.concatenate(lefts, axis=0), jnp.concatenate(rights, axis=0))

    shared = range(FIRST_SHARED, len(PRODUCTS))
    most = number[FIRST_SHARED]
    for q in shared:
        most = jnp.maximum(most, number[q])

    def step(group, carry):
        for q in shared:
            add(q, group)
        return carry

    lax.fori_loop(0, (most + stack - 1) // stack, step, 0)

    if first:
        def own(row, carry):
            left = blocks[XJ][row]
            total[0] += multiply(left, left)
            return carry

        lax.fori_loop(0, blocks[XJ].shape[0], own, 0)

        def inner(slot, carry):
            total[1] += multiply(blocks[XJ][mine[1, slot]], blocks[XO][theirs[1, slot]])
            return carry

        lax.fori_loop(0, number[1], inner, 0)

    if last:
        kept, to_y, to_f, to_g = outs[:4]
        for q, place_in in ((0, 0), (1, 1), (2, 2), (3, 3), (5, 4), (10, 5)):
            kept[place_in] = total[q]
        kept[6] = jnp.where(flag, total[CROSS_G], total[CROSS_F])
        to_y[0] = total[2].T
        to_y[1] = total[4]
        to_y[2] = total[7]
        to_y[3] = total[8]
        to_f[0] = total[5].T
        to_f[1] = jnp.where(flag, total[CROSS_F], 0.0)
        to_f[2] = total[7].T
        to_f[3] = total[9]
        to_g[0] = total[10].T
        to_g[1] = jnp.where(flag, 0.0, total[CROSS_G])


def chunk(first, last, start, size, stack, tables, before, blocks):
    width = blocks[0].shape[-1]
    square = lambda n: jax.ShapeDtypeStruct((n, width, width), F32)
    smem = pl.BlockSpec(memory_space=pltpu.SMEM)
    vmem = pl.BlockSpec(memory_space=pltpu.VMEM)
    inputs = list(tables) + ([] if first else [before]) + list(blocks)
    specs = [smem] * len(tables) + [vmem] * (len(inputs) - len(tables))
    products = len(PRODUCTS)
    if last:
        out_shape, out_specs = [square(7), square(4), square(4), square(2)], [vmem] * 4
        scratch = [pltpu.VMEM((products, width, width), F32)]
    else:
        out_shape, out_specs, scratch = square(products), vmem, []
    return pl.pallas_call(
        functools.partial(chunk_kernel, first, last, start, size, stack),
        out_shape=out_shape,
        in_specs=specs,
        out_specs=out_specs,
        scratch_shapes=scratch,
        compiler_params=pltpu.CompilerParams(vmem_limit_bytes=50 * 2**20),
        cost_estimate=pl.CostEstimate(
            flops=2 * width * width * size * 15 * products, bytes_accessed=8 * 30 * size * width * 2, transcendentals=0
        ),
    )(*inputs)


def band_kernel(depth, place, keep, kept, from_y, from_f, from_g, band):
    def put(slot, value):
        where = place[slot]
        band[where] = jnp.where(keep[where] == 1, value, 0.0)

    band[depth] = kept[0]
    put(0, kept[1])
    put(1, kept[2] + from_y[0])
    put(2, kept[3] + from_y[1])
    put(3, from_y[2] + from_f[2])
    put(4, from_y[3] + from_f[3])
    put(5, kept[4] + from_g[0])
    put(6, kept[5] + from_f[0])
    put(7, kept[6] + from_f[1] + from_g[1])


def finish(depth, place, keep, kept, from_y, from_f, from_g):
    width = kept.shape[-1]
    smem = pl.BlockSpec(memory_space=pltpu.SMEM)
    vmem = pl.BlockSpec(memory_space=pltpu.VMEM)
    return pl.pallas_call(
        functools.partial(band_kernel, depth),
        out_shape=jax.ShapeDtypeStruct((2 * depth + 1, width, width), F32),
        in_specs=[smem] * 2 + [vmem] * 4,
        out_specs=vmem,
        compiler_params=pltpu.CompilerParams(vmem_limit_bytes=50 * 2**20),
    )(place, keep, kept, from_y, from_f, from_g)


def summed(values, count):
    if count & (count - 1):
        return lax.psum(values, "basis")
    step = 1
    while step < count:
        values = values + lax.ppermute(values, "basis", [(i, i ^ step) for i in range(count)])
        step *= 2
    return values


def per_device(factors, coefs, domains, pairs):
    own = factors[0]
    coef = coefs[0]
    rows, aux, width = own.shape
    count = lax.axis_size("basis")
    depth = pairs.shape[1]
    me = lax.axis_index("basis")
    core, chip = me % 2, me // 2
    odd = chip % 2
    flag = core == odd
    half = aux // 2
    main, side = odd * half, (1 - odd) * half

    swap = chip_route(count, lambda c: c, swap=True)
    across = chip_route(count, lambda c: c ^ 1)
    f_route = chip_route(count, lambda c: c - 2 if c % 2 == 0 else c + 2)
    g_route = chip_route(count, lambda c: c + 2 if c % 2 == 0 else c - 2)
    f_back, g_back = [(b, a) for a, b in f_route], [(b, a) for a, b in g_route]
    send = lambda value, route: lax.ppermute(value, "basis", route)

    f_chip = jnp.where(odd == 0, chip + 2, chip - 2)
    g_chip = jnp.where(odd == 0, chip - 2, chip + 2)
    chips = count // 2
    ids, here = [], []
    for other in (chip, chip ^ 1, f_chip, g_chip):
        there = jnp.logical_and(other >= 0, other < chips)
        two = lax.dynamic_slice_in_dim(domains, 2 * jnp.clip(other, 0, chips - 1), 2, 0)
        ids += [jnp.where(core == 0, two[0], two[1]), jnp.where(core == 0, two[1], two[0])]
        here += [there, there]
    left, right, valid = [], [], []
    for q, (a, b, _) in enumerate(PRODUCTS):
        if a is None:
            (a, b), (c, d) = (((FJ, XO), (XJ, FO)) if q == CROSS_F else ((XJ, GO), (GJ, XO)))
            left.append(jnp.where(flag, ids[a], ids[c]))
            right.append(jnp.where(flag, ids[b], ids[d]))
        else:
            left.append(ids[a])
            right.append(ids[b])
        valid.append(jnp.logical_and(here[a], here[b]))
    number, mine, theirs = matches(jnp.stack(left), jnp.stack(right), jnp.stack(valid))
    place = jnp.stack([main, side, flag.astype(jnp.int32)]).astype(jnp.int32)
    tables = (place, number, mine, theirs)

    cuts = ((0, CUT), (CUT, half - CUT))
    part = lambda at, cut: lax.dynamic_slice_in_dim(own, at + cut[0], cut[1], 1)
    other = send(own, swap)
    pieces = []
    for cut in cuts:
        main_part, side_part = part(main, cut), part(side, cut)
        y = send(side_part, across)
        f = send(main_part, f_route)
        g = send(side_part, g_route)
        pieces.append((own, other, y, send(y, swap), f, send(f, swap), g, send(g, swap)))

    total = chunk(True, False, cuts[0][0], cuts[0][1], 2, tables, None, pieces[0])
    kept, to_y, to_f, to_g = chunk(False, True, cuts[1][0], cuts[1][1], 4, tables, total, pieces[1])
    from_y, from_f, from_g = send(to_y, across), send(to_f, f_back), send(to_g, g_back)

    partial_sum = jnp.einsum("kpm,km->p", own, coef, preferred_element_type=F32)
    marks = (jnp.arange(count)[:, None] == me).astype(F32) * pairs.astype(F32)
    gathered = summed(jnp.concatenate([partial_sum, marks.reshape(-1)]), count)
    gamma_low = gathered[:aux].astype(BF16)
    coulomb_half = jnp.einsum("kpm,p->km", own, gamma_low, preferred_element_type=F32)
    all_pairs = gathered[aux:].reshape(count, depth)

    keep = [jnp.int32(1)] * (2 * depth + 1)
    for r in range(1, depth + 1):
        keep[depth + r] = (pairs[0, r - 1] == 1).astype(jnp.int32)
        lower = lax.dynamic_slice_in_dim(all_pairs, jnp.maximum(me - r, 0), 1, 0)[0, r - 1]
        keep[depth - r] = (lower > 0.5).astype(jnp.int32)
    sign = 1 - 2 * odd
    cross = 1 - 2 * core
    y_at, f_at = 2 * sign, 4 * sign
    spots = [cross, y_at, y_at + cross, -y_at, -y_at + cross, f_at, -f_at, jnp.where(core == 0, -3, 3)]
    band = finish(depth, jnp.stack(spots).astype(jnp.int32) + depth, jnp.stack(keep), kept, from_y, from_f, from_g)
    return (band[None], coulomb_half[None])


def solution(mesh):
    placed = (
        P(("groups", "basis"), None, None, None),
        P(("groups", "basis"), None, None),
        P("groups", None),
        P(("groups", "basis"), None),
    )
    return jax.shard_map(
        per_device,
        mesh=mesh,
        in_specs=placed,
        out_specs=(P(("groups", "basis"), None, None, None), P(("groups", "basis"), None, None)),
        check_vma=False,
    )
```

time: 277 us -> 132 us (0.48)
  blocking collectives: 99.9 us -> 0 us
  waiting for transfers between devices: 100 us -> 55 us
  matrix products: 37.1 us -> 3.84 us
  Pallas kernels: 0 us -> 28.1 us
  starting transfers between devices: 16.9 us -> 27.2 us
  local copies, waits for them, and re-layouts: 18.6 us -> 10.1 us
    psum x1 -> x0, blocking collectives: 99.9 us -> none  [per_device(): gamma = lax.psum(partial_sum, 'basis')]
    ppermute x8 -> x20, waiting for transfers between devices: 100 us -> 55 us  [the longest x4 29.1 us: summed(): lax.ppermute(values, 'basis', [(i, i ^ step) for i in range(count)])]
    dot_general x12 -> x2, matrix products: 37.1 us -> 3.84 us  [the longest x1 3.22 us: per_device(): partial_sum = jnp.einsum('kpm,km->p', own, coef, preferred_element_type=F32)]
    pallas_call x0 -> x3, Pallas kernels: none -> 28.1 us  [the longest x2 26.7 us: chunk(): pl.pallas_call(functools.partial(chunk_kernel, first, last, start, size,...]
    convert_element_type x6 -> x0, local copies, waits for them, and re-layouts: 11.7 us -> none  [the longest x5 11.7 us: contract(): jnp.einsum('kl,lpm->kpm', match, remote, preferred_element_type=jnp.float32)]
    ppermute x8 -> x20, starting transfers between devices: 16.9 us -> 27.2 us  [the longest x16 20.7 us: per_device(): send = lambda value, route: lax.ppermute(value, 'basis', route)]
    dynamic_slice x0 -> x4, local copies, waits for them, and re-layouts: none -> 5.41 us  [the longest x2 5.38 us: per_device(): part = lambda at, cut: lax.dynamic_slice_in_dim(own, at + cut[0], cut[1], 1)]
  transfers between devices with their start and end apart: 8 -> 20, of which waited for: 3 -> 8; matrix products, arithmetic and copies ran while one was open for 17% -> 11% of each run, Pallas kernels for 0% -> 15%
where the time goes in v1:
time: 132 us
  waiting for transfers between devices  55 us (42%)
  Pallas kernels  28.1 us (21%)
  starting transfers between devices  27.2 us (21%)
  local copies, waits for them, and re-layouts  10.1 us (8%)
  between operations  5.5 us (4%)
  matrix products  3.84 us (3%)
  other arithmetic  1.81 us (1%)
    ppermute x4, waiting for transfers between devices, summed(): lax.ppermute(values, 'basis', [(i, i ^ step) for i in range(count)])  29.1 us
    pallas_call x2, Pallas kernels, chunk(): pl.pallas_call(functools.partial(chunk_kernel, first, last, start, size,...  26.7 us
    ppermute x16, waiting for transfers between devices, per_device(): send = lambda value, route: lax.ppermute(value, 'basis', route)  25.9 us
    ppermute x16, starting transfers between devices, per_device(): send = lambda value, route: lax.ppermute(value, 'basis', route)  20.7 us
    ppermute x4, starting transfers between devices, summed(): lax.ppermute(values, 'basis', [(i, i ^ step) for i in range(count)])  6.51 us
    dynamic_slice x2, local copies, waits for them, and re-layouts, per_device(): part = lambda at, cut: lax.dynamic_slice_in_dim(own, at + cut[0], cut[1], 1)  5.38 us
    dot_general x1, matrix products, per_device(): partial_sum = jnp.einsum('kpm,km->p', own, coef, preferred_element_type=F32)  3.22 us
  transfers between devices with their start and end apart: 20, of which 8 were waited for; matrix products, arithmetic and copies ran while one was open for 11% of the time, Pallas kernels for 15%

profile of v1, /device:TPU:0, one launch (start us, length us, event | category | flops | bytes accessed | tf_op | source)
XLA Modules:
  0.0 131.6 jit_solution(6408506144201387136)
XLA Ops:
  1.2 3.2 %dynamic-slice_bitcast_fusion = (bf16[30,192,128]{2,1,0:T(8,128)(2,1)}, bf16[30,192,128]{2,1,0:T(8,128)(2,1)S(1)}) fusion(bf16[1,30,512,128]{3,2,1,0:T(8,128)(2,1)} %param.4, s32[]{:T(128)S(6)} %select_n.171, s32[]{:T(128)S(6)} %select_n.170), kind=kLoop, calls=%fused_computation | loop fusion | bytes 5898248 | tf_op jit(solution)/shard_map/dynamic_slice | solution.py:260
  4.4 5.7 %collective-permute-start.9 = (bf16[30,192,128]{2,1,0:T(8,128)(2,1)S(1)}, bf16[30,192,128]{2,1,0:T(8,128)(2,1)}, u32[]{:S(2)}, u32[]{:S(2)}) collective-permute-start(bf16[30,192,128]{2,1,0:T(8,128)(2,1)S(1)} %get-tuple-element.29), channel_id=1, source_target_pairs={{0,4},{1,5},{4,8},{5,9},{6,2},{7,3},{8,12},{9,13},{10,6},{11,7},{1... | collective-permute-start | bytes 4423688 | tf_op jit(solution)/shard_map/ppermute | solution.py:234
  10.0 1.3 collective-permute-start.7
  11.5 3.2 %fusion.1 = f32[1,512,1]{1,0,2:T(1,128)S(1)} fusion(bf16[30,128,1]{1,0,2:T(8,128)(2,1)S(1)} %bitcast.49, bf16[1,30,512,128]{3,2,1,0:T(8,128)(2,1)} %param.4), kind=kOutput, calls=%fused_computation.15 | convolution fusion | flops 3932160 | bytes 3941888 | tf_op jit(solution)/shard_map/kpm,km->p/dot_general | solution.py:274
  15.0 1.0 collective-permute-done
  16.0 4.3 %collective-permute-start.1 = (f32[576]{0:T(1024)S(1)}, f32[576]{0:T(1024)S(1)}, u32[]{:S(2)}, u32[]{:S(2)}) collective-permute-start(f32[576]{0:T(1024)S(1)} %fusion.3), channel_id=1, source_target_pairs={{0,2},{1,3},{2,0},{3,1},{4,6},{5,7},{6,4},{7,5},{8,10},{9,11},{10,... | collective-permute-start | bytes 6920 | tf_op jit(solution)/shard_map/ppermute | solution.py:211
  20.3 24.2 %collective-permute-done.1 = f32[576]{0:T(1024)S(1)} collective-permute-done((f32[576]{0:T(1024)S(1)}, f32[576]{0:T(1024)S(1)}, u32[]{:S(2)}, u32[]{:S(2)}) %collective-permute-start.1) | collective-permute-done | bytes 2336 | tf_op jit(solution)/shard_map/ppermute | solution.py:211
  45.0 3.1 %collective-permute-done.2 = f32[576]{0:T(1024)S(1)} collective-permute-done((f32[576]{0:T(1024)S(1)}, f32[576]{0:T(1024)S(1)}, u32[]{:S(2)}, u32[]{:S(2)}) %collective-permute-start.2) | collective-permute-done | bytes 2336 | tf_op jit(solution)/shard_map/ppermute | solution.py:211
  48.1 1.5 %collective-permute-start.3 = (f32[576]{0:T(1024)S(1)}, f32[576]{0:T(1024)S(1)}, u32[]{:S(2)}, u32[]{:S(2)}) collective-permute-start(f32[576]{0:T(1024)S(1)} %add.83), channel_id=1, source_target_pairs={{0,8},{1,9},{2,10},{3,11},{4,12},{5,13},{6,14},{7,15},{8,0},{9,1},... | collective-permute-start | bytes 6920 | tf_op jit(solution)/shard_map/ppermute | solution.py:211
  49.6 2.2 %dynamic-slice_bitcast_fusion.2 = (bf16[30,64,128]{2,1,0:T(8,128)(2,1)}, bf16[30,64,128]{2,1,0:T(8,128)(2,1)}) fusion(bf16[1,30,512,128]{3,2,1,0:T(8,128)(2,1)} %param.4, s32[]{:T(128)S(6)} %select_n.173, s32[]{:T(128)S(6)} %select_n.172), kind=kLoop, calls=%fused_computation.2 | loop fusion | bytes 1966088 | tf_op jit(solution)/shard_map/dynamic_slice | solution.py:260
  51.8 0.8 collective-permute-done.3
  53.4 10.2 %collective-permute-done.11.refs_7_ = bf16[30,64,128]{2,1,0:T(8,128)(2,1)S(1)} collective-permute-done((bf16[30,64,128]{2,1,0:T(8,128)(2,1)}, bf16[30,64,128]{2,1,0:T(8,128)(2,1)S(1)}, u32[]{:S(2)}, u32[]{:S(2)}) %collective-permute-start.11) | collective-permute-done | bytes 491552 | tf_op jit(solution)/shard_map/ppermute | solution.py:234
  63.7 1.3 collective-permute-start.13
  65.3 0.8 select_reduce_fusion.1
  66.4 9.4 %collective-permute-done.13.refs_9_ = bf16[30,64,128]{2,1,0:T(8,128)(2,1)} collective-permute-done((bf16[30,64,128]{2,1,0:T(8,128)(2,1)}, bf16[30,64,128]{2,1,0:T(8,128)(2,1)}, u32[]{:S(2)}, u32[]{:S(2)}) %collective-permute-start.13) | collective-permute-done | bytes 491552 | tf_op jit(solution)/shard_map/ppermute | solution.py:234
  75.8 4.4 %collective-permute-start.15 = (bf16[30,64,128]{2,1,0:T(8,128)(2,1)}, bf16[30,64,128]{2,1,0:T(8,128)(2,1)}, u32[]{:S(2)}, u32[]{:S(2)}) collective-permute-start(bf16[30,64,128]{2,1,0:T(8,128)(2,1)} %get-tuple-element.27), channel_id=1, source_target_pairs={{0,4},{1,5},{4,8},{5,9},{6,2},{7,3},{8,12},{9,13},{10,6},{11,7},{1... | collective-permute-start | bytes 1474568 | tf_op jit(solution)/shard_map/ppermute | solution.py:234
  81.0 5.8 %collective-permute-done.15.refs_11_ = bf16[30,64,128]{2,1,0:T(8,128)(2,1)} collective-permute-done((bf16[30,64,128]{2,1,0:T(8,128)(2,1)}, bf16[30,64,128]{2,1,0:T(8,128)(2,1)}, u32[]{:S(2)}, u32[]{:S(2)}) %collective-permute-start.15) | collective-permute-done | bytes 491552 | tf_op jit(solution)/shard_map/ppermute | solution.py:234
  90.6 20.0 %shard_map.59.refs_4_ = f32[12,128,128]{2,1,0:T(8,128)S(1)} custom-call(s32[3]{0:T(128)S(1)} %pad_add_fusion.refs_0_, s32[12]{0:T(128)S(1)} %get-tuple-element.12.refs_1_, s32[12,32]{1,0:T(8,128)S(1)} %get-tuple-element.14.refs_2_, s32[12,32]{1,0:T(8,128)S(1)} %get-tuple-element.13.refs_3_, bf16[30,512,128]{2,1,0:T(8,128)(2,1)} %bitcast.51, ...), custom_call_target="tpu_custom_call" | custom-call | flops 1132462080 | bytes 11796480 | tf_op jit(solution)/shard_map/pallas_call | solution.py:164
  110.6 0.9 copy-done.1
  111.5 6.7 %shard_map.60 = (f32[7,128,128]{2,1,0:T(8,128)S(1)}, f32[4,128,128]{2,1,0:T(8,128)S(1)}, f32[4,128,128]{2,1,0:T(8,128)S(1)}, f32[2,128,128]{2,1,0:T(8,128)S(1)}) custom-call(s32[3]{0:T(128)S(1)} %pad_add_fusion.refs_0_, s32[12]{0:T(128)S(1)} %get-tuple-element.12.refs_1_, s32[12,32]{1,0:T(8,128)S(1)} %get-tuple-element.14.refs_2_, ...), custom_call_target="tpu_custom_call" | custom-call | flops 377487360 | bytes 3932160 | tf_op jit(solution)/shard_map/pallas_call | solution.py:164
  118.2 2.8 %collective-permute-start.17 = (f32[4,128,128]{2,1,0:T(8,128)S(1)}, f32[4,128,128]{2,1,0:T(8,128)S(1)}, u32[]{:S(2)}, u32[]{:S(2)}) collective-permute-start(f32[4,128,128]{2,1,0:T(8,128)S(1)} %get-tuple-element.7), channel_id=1, source_target_pairs={{0,2},{1,3},{2,0},{3,1},{4,6},{5,7},{6,4},{7,5},{8,10},{9,11},{10,... | collective-permute-start | bytes 786440 | tf_op jit(solution)/shard_map/ppermute | solution.py:234
  121.0 2.0 %collective-permute-start.18 = (f32[4,128,128]{2,1,0:T(8,128)S(1)}, f32[4,128,128]{2,1,0:T(8,128)S(1)}, u32[]{:S(2)}, u32[]{:S(2)}) collective-permute-start(f32[4,128,128]{2,1,0:T(8,128)S(1)} %get-tuple-element.8), channel_id=1, source_target_pairs={{6,2},{7,3},{0,4},{1,5},{10,6},{11,7},{4,8},{5,9},{14,10},{15,11},... | collective-permute-start | bytes 786440 | tf_op jit(solution)/shard_map/ppermute | solution.py:234
  123.0 1.3 collective-permute-start.19
  130.2 1.4 %shard_map.61 = f32[9,128,128]{2,1,0:T(8,128)} custom-call(s32[8]{0:T(128)S(1)} %broadcast_add_fusion.place, s32[9]{0:T(128)S(1)} %stack.152.keep, f32[7,128,128]{2,1,0:T(8,128)S(1)} %get-tuple-element.6.kept, f32[4,128,128]{2,1,0:T(8,128)S(1)} %collective-permute-done.17.from_y, f32[4,128,128]{2,1,0:T(8,128)S(1)} %collective-permute-done.18.from_f, ...), custom_call_target="tpu_custom_call" | custom-call | tf_op jit(solution)/shard_map/pallas_call | solution.py:197
  (69 shorter events, 8.6 us)
Async XLA Ops:
  0.6 10.9 %copy-start = (bf16[1,30,128]{2,1,0:T(8,128)(2,1)S(1)}, bf16[1,30,128]{2,1,0:T(8,128)(2,1)}, u32[]{:S(2)}) copy-start(bf16[1,30,128]{2,1,0:T(8,128)(2,1)} %param.5) | copy-start | bytes 23044
  0.6 10.7 %copy-start.3 = (s32[1,4]{1,0:T(1,128)S(1)}, s32[1,4]{1,0:T(1,128)}, u32[]{:S(2)}) copy-start(s32[1,4]{1,0:T(1,128)} %param.7) | copy-start | bytes 52
  0.7 89.9 %collective-permute-start.4 = (bf16[30,512,128]{2,1,0:T(8,128)(2,1)}, bf16[30,512,128]{2,1,0:T(8,128)(2,1)}, u32[]{:S(2)}, u32[]{:S(2)}) collective-permute-start(bf16[30,512,128]{2,1,0:T(8,128)(2,1)} %bitcast.50), channel_id=1, source_target_pairs={{0,1},{1,0},{2,3},{3,2},{4,5},{5,4},{6,7},{7,6},{8,9},{9,8},{10,11... | collective-permute-start | bytes 11796488 | tf_op jit(solution)/shard_map/ppermute | solution.py:234
  4.4 48.5 %collective-permute-start.9 = (bf16[30,192,128]{2,1,0:T(8,128)(2,1)S(1)}, bf16[30,192,128]{2,1,0:T(8,128)(2,1)}, u32[]{:S(2)}, u32[]{:S(2)}) collective-permute-start(bf16[30,192,128]{2,1,0:T(8,128)(2,1)S(1)} %get-tuple-element.29), channel_id=1, source_target_pairs={{0,4},{1,5},{4,8},{5,9},{6,2},{7,3},{8,12},{9,13},{10,6},{11,7},{1... | collective-permute-start | bytes 4423688 | tf_op jit(solution)/shard_map/ppermute | solution.py:234
  10.0 42.9 %collective-permute-start.5 = (bf16[30,192,128]{2,1,0:T(8,128)(2,1)S(1)}, bf16[30,192,128]{2,1,0:T(8,128)(2,1)S(1)}, u32[]{:S(2)}, u32[]{:S(2)}) collective-permute-start(bf16[30,192,128]{2,1,0:T(8,128)(2,1)S(1)} %get-tuple-element.29), channel_id=1, source_target_pairs={{0,2},{1,3},{2,0},{3,1},{4,6},{5,7},{6,4},{7,5},{8,10},{9,11},{10,... | collective-permute-start | bytes 4423688 | tf_op jit(solution)/shard_map/ppermute | solution.py:234
  10.0 54.9 %collective-permute-start.7 = (bf16[30,192,128]{2,1,0:T(8,128)(2,1)}, bf16[30,192,128]{2,1,0:T(8,128)(2,1)}, u32[]{:S(2)}, u32[]{:S(2)}) collective-permute-start(bf16[30,192,128]{2,1,0:T(8,128)(2,1)} %get-tuple-element.28), channel_id=1, source_target_pairs={{2,6},{3,7},{4,0},{5,1},{6,10},{7,11},{8,4},{9,5},{10,14},{11,15},... | collective-permute-start | bytes 4423688 | tf_op jit(solution)/shard_map/ppermute | solution.py:234
  11.5 41.9 %copy-start.4 = (s32[16,30]{1,0:T(8,128)S(1)}, s32[16,30]{1,0:T(8,128)}, u32[]{:S(2)}) copy-start(s32[16,30]{1,0:T(8,128)} %param.6) | copy-start | bytes 5764
  14.8 1.2 collective-permute-start
  16.0 28.5 %collective-permute-start.1 = (f32[576]{0:T(1024)S(1)}, f32[576]{0:T(1024)S(1)}, u32[]{:S(2)}, u32[]{:S(2)}) collective-permute-start(f32[576]{0:T(1024)S(1)} %fusion.3), channel_id=1, source_target_pairs={{0,2},{1,3},{2,0},{3,1},{4,6},{5,7},{6,4},{7,5},{8,10},{9,11},{10,... | collective-permute-start | bytes 6920 | tf_op jit(solution)/shard_map/ppermute | solution.py:211
  44.5 3.6 %collective-permute-start.2 = (f32[576]{0:T(1024)S(1)}, f32[576]{0:T(1024)S(1)}, u32[]{:S(2)}, u32[]{:S(2)}) collective-permute-start(f32[576]{0:T(1024)S(1)} %add.82), channel_id=1, source_target_pairs={{0,4},{1,5},{2,6},{3,7},{4,0},{5,1},{6,2},{7,3},{8,12},{9,13},{10,... | collective-permute-start | bytes 6920 | tf_op jit(solution)/shard_map/ppermute | solution.py:211
  48.1 4.5 %collective-permute-start.3 = (f32[576]{0:T(1024)S(1)}, f32[576]{0:T(1024)S(1)}, u32[]{:S(2)}, u32[]{:S(2)}) collective-permute-start(f32[576]{0:T(1024)S(1)} %add.83), channel_id=1, source_target_pairs={{0,8},{1,9},{2,10},{3,11},{4,12},{5,13},{6,14},{7,15},{8,0},{9,1},... | collective-permute-start | bytes 6920 | tf_op jit(solution)/shard_map/ppermute | solution.py:211
  52.6 11.1 %collective-permute-start.11 = (bf16[30,64,128]{2,1,0:T(8,128)(2,1)}, bf16[30,64,128]{2,1,0:T(8,128)(2,1)S(1)}, u32[]{:S(2)}, u32[]{:S(2)}) collective-permute-start(bf16[30,64,128]{2,1,0:T(8,128)(2,1)} %get-tuple-element.27), channel_id=1, source_target_pairs={{0,2},{1,3},{2,0},{3,1},{4,6},{5,7},{6,4},{7,5},{8,10},{9,11},{10,... | collective-permute-start | bytes 1474568 | tf_op jit(solution)/shard_map/ppermute | solution.py:234
  52.9 34.0 %collective-permute-start.10 = (bf16[30,192,128]{2,1,0:T(8,128)(2,1)}, bf16[30,192,128]{2,1,0:T(8,128)(2,1)}, u32[]{:S(2)}, u32[]{:S(2)}) collective-permute-start(bf16[30,192,128]{2,1,0:T(8,128)(2,1)} %collective-permute-done.9.refs_10_), channel_id=1, source_target_pairs={{0,1},{1,0},{2,3},{3,2},{4,5},{5,4},{6,7},{7,6},{8,9},{9,8},{10,11... | collective-permute-start | bytes 4423688 | tf_op jit(solution)/shard_map/ppermute | solution.py:234
  52.9 34.5 %collective-permute-start.6 = (bf16[30,192,128]{2,1,0:T(8,128)(2,1)S(1)}, bf16[30,192,128]{2,1,0:T(8,128)(2,1)S(1)}, u32[]{:S(2)}, u32[]{:S(2)}) collective-permute-start(bf16[30,192,128]{2,1,0:T(8,128)(2,1)S(1)} %collective-permute-done.5.refs_6_), channel_id=1, source_target_pairs={{0,1},{1,0},{2,3},{3,2},{4,5},{5,4},{6,7},{7,6},{8,9},{9,8},{10,11... | collective-permute-start | bytes 4423688 | tf_op jit(solution)/shard_map/ppermute | solution.py:234
  63.7 12.1 %collective-permute-start.13 = (bf16[30,64,128]{2,1,0:T(8,128)(2,1)}, bf16[30,64,128]{2,1,0:T(8,128)(2,1)}, u32[]{:S(2)}, u32[]{:S(2)}) collective-permute-start(bf16[30,64,128]{2,1,0:T(8,128)(2,1)} %get-tuple-element.26), channel_id=1, source_target_pairs={{2,6},{3,7},{4,0},{5,1},{6,10},{7,11},{8,4},{9,5},{10,14},{11,15},... | collective-permute-start | bytes 1474568 | tf_op jit(solution)/shard_map/ppermute | solution.py:234
  65.0 25.6 %collective-permute-start.8 = (bf16[30,192,128]{2,1,0:T(8,128)(2,1)}, bf16[30,192,128]{2,1,0:T(8,128)(2,1)}, u32[]{:S(2)}, u32[]{:S(2)}) collective-permute-start(bf16[30,192,128]{2,1,0:T(8,128)(2,1)} %collective-permute-done.7.refs_8_), channel_id=1, source_target_pairs={{0,1},{1,0},{2,3},{3,2},{4,5},{5,4},{6,7},{7,6},{8,9},{9,8},{10,11... | collective-permute-start | bytes 4423688 | tf_op jit(solution)/shard_map/ppermute | solution.py:234
  75.8 11.1 %collective-permute-start.15 = (bf16[30,64,128]{2,1,0:T(8,128)(2,1)}, bf16[30,64,128]{2,1,0:T(8,128)(2,1)}, u32[]{:S(2)}, u32[]{:S(2)}) collective-permute-start(bf16[30,64,128]{2,1,0:T(8,128)(2,1)} %get-tuple-element.27), channel_id=1, source_target_pairs={{0,4},{1,5},{4,8},{5,9},{6,2},{7,3},{8,12},{9,13},{10,6},{11,7},{1... | collective-permute-start | bytes 1474568 | tf_op jit(solution)/shard_map/ppermute | solution.py:234
  86.9 24.6 %collective-permute-start.12 = (bf16[30,64,128]{2,1,0:T(8,128)(2,1)S(1)}, bf16[30,64,128]{2,1,0:T(8,128)(2,1)}, u32[]{:S(2)}, u32[]{:S(2)}) collective-permute-start(bf16[30,64,128]{2,1,0:T(8,128)(2,1)S(1)} %collective-permute-done.11.refs_7_), channel_id=1, source_target_pairs={{0,1},{1,0},{2,3},{3,2},{4,5},{5,4},{6,7},{7,6},{8,9},{9,8},{10,11... | collective-permute-start | bytes 1474568 | tf_op jit(solution)/shard_map/ppermute | solution.py:234
  86.9 24.6 %collective-permute-start.14 = (bf16[30,64,128]{2,1,0:T(8,128)(2,1)}, bf16[30,64,128]{2,1,0:T(8,128)(2,1)}, u32[]{:S(2)}, u32[]{:S(2)}) collective-permute-start(bf16[30,64,128]{2,1,0:T(8,128)(2,1)} %collective-permute-done.13.refs_9_), channel_id=1, source_target_pairs={{0,1},{1,0},{2,3},{3,2},{4,5},{5,4},{6,7},{7,6},{8,9},{9,8},{10,11... | collective-permute-start | bytes 1474568 | tf_op jit(solution)/shard_map/ppermute | solution.py:234
  87.4 24.1 %collective-permute-start.16 = (bf16[30,64,128]{2,1,0:T(8,128)(2,1)}, bf16[30,64,128]{2,1,0:T(8,128)(2,1)}, u32[]{:S(2)}, u32[]{:S(2)}) collective-permute-start(bf16[30,64,128]{2,1,0:T(8,128)(2,1)} %collective-permute-done.15.refs_11_), channel_id=1, source_target_pairs={{0,1},{1,0},{2,3},{3,2},{4,5},{5,4},{6,7},{7,6},{8,9},{9,8},{10,11... | collective-permute-start | bytes 1474568 | tf_op jit(solution)/shard_map/ppermute | solution.py:234
  111.5 12.8 %copy-start.2 = (bf16[1,30,512,128]{3,2,1,0:T(8,128)(2,1)S(1)}, bf16[1,30,512,128]{3,2,1,0:T(8,128)(2,1)}, u32[]{:S(2)}) copy-start(bf16[1,30,512,128]{3,2,1,0:T(8,128)(2,1)} %param.4) | copy-start | bytes 11796484
  118.2 12.0 %collective-permute-start.17 = (f32[4,128,128]{2,1,0:T(8,128)S(1)}, f32[4,128,128]{2,1,0:T(8,128)S(1)}, u32[]{:S(2)}, u32[]{:S(2)}) collective-permute-start(f32[4,128,128]{2,1,0:T(8,128)S(1)} %get-tuple-element.7), channel_id=1, source_target_pairs={{0,2},{1,3},{2,0},{3,1},{4,6},{5,7},{6,4},{7,5},{8,10},{9,11},{10,... | collective-permute-start | bytes 786440 | tf_op jit(solution)/shard_map/ppermute | solution.py:234
  121.0 9.2 %collective-permute-start.18 = (f32[4,128,128]{2,1,0:T(8,128)S(1)}, f32[4,128,128]{2,1,0:T(8,128)S(1)}, u32[]{:S(2)}, u32[]{:S(2)}) collective-permute-start(f32[4,128,128]{2,1,0:T(8,128)S(1)} %get-tuple-element.8), channel_id=1, source_target_pairs={{6,2},{7,3},{0,4},{1,5},{10,6},{11,7},{4,8},{5,9},{14,10},{15,11},... | collective-permute-start | bytes 786440 | tf_op jit(solution)/shard_map/ppermute | solution.py:234
  123.0 7.2 %collective-permute-start.19 = (f32[2,128,128]{2,1,0:T(8,128)S(1)}, f32[2,128,128]{2,1,0:T(8,128)S(1)}, u32[]{:S(2)}, u32[]{:S(2)}) collective-permute-start(f32[2,128,128]{2,1,0:T(8,128)S(1)} %get-tuple-element.9), channel_id=1, source_target_pairs={{4,0},{5,1},{8,4},{9,5},{2,6},{3,7},{12,8},{13,9},{6,10},{7,11},{1... | collective-permute-start | bytes 393224 | tf_op jit(solution)/shard_map/ppermute | solution.py:234
  (1 other events, 0.9 us)

commit v2 on v0

v2 whole, which is shorter than its diff:
```python
import functools

import jax
import jax.numpy as jnp
from jax import lax
from jax.experimental import pallas as pl
from jax.experimental.pallas import tpu as pltpu
from jax.sharding import PartitionSpec as P

F32 = jnp.float32
BF16 = jnp.bfloat16

XJ, XO, YJ, YO, YO_HIGH, FJ, GJ, XS = range(8)
XY, XYO, XF, YF, YOF, XG, CROSS = range(7)
PRODUCTS = ((XJ, YJ), (XO, YJ), (XJ, FJ), (YJ, FJ), (YO, FJ), (XJ, GJ), (XO, None))
OWN = len(PRODUCTS)
STACK, OWN_STACK = 9, 4
LIMIT = 12 * 2**20


def cost(*arrays):
    return pl.CostEstimate(flops=1, bytes_accessed=sum(a.size * a.dtype.itemsize for a in arrays), transcendentals=0)


def smem(n):
    return [pl.BlockSpec(memory_space=pltpu.SMEM)] * n


def vmem(n):
    return [pl.BlockSpec(memory_space=pltpu.VMEM)] * n


def squares(n, width):
    return jax.ShapeDtypeStruct((n, width, width), F32)


def multiply(left, right):
    return lax.dot_general(left, right, (((0,), (0,)), ((), ())), preferred_element_type=F32)


def chip_route(count, target, swap=False):
    chips = count // 2
    route = []
    for chip in range(chips):
        to = target(chip)
        if 0 <= to < chips:
            for core in range(2):
                route.append((2 * chip + core, 2 * to + (1 - core if swap else core)))
    return route


def place_of(me):
    core, chip = me & 1, me >> 1
    odd = chip & 1
    return core, chip, odd, core == odd, chip + 2 - 4 * odd, chip - 2 + 4 * odd


def cut_kernel(size, me, own, side, main, sems):
    odd = place_of(me[0])[2]
    copies = []
    for i, (out, start) in enumerate(((side, (1 - odd) * size), (main, odd * size))):
        rows = pl.ds(pl.multiple_of(start, 16), size)
        copies.append(pltpu.make_async_copy(own.at[:, rows, :], out, sems.at[i]))
    for copy in copies:
        copy.start()
    for copy in copies:
        copy.wait()


def cut(me, own):
    rows, aux, width = own.shape
    part = jax.ShapeDtypeStruct((rows, aux // 2, width), own.dtype)
    return pl.pallas_call(
        functools.partial(cut_kernel, aux // 2),
        out_shape=[part] * 2,
        in_specs=smem(1) + vmem(1),
        out_specs=vmem(2),
        scratch_shapes=[pltpu.SemaphoreType.DMA((2,))],
        compiler_params=pltpu.CompilerParams(vmem_limit_bytes=LIMIT),
        cost_estimate=cost(own, own),
    )(me, own)


def find_matches(here, domains, number, mine, theirs, spot):
    count, rows = domains.shape
    width = mine.shape[1]
    core, chip, odd, flag, f_chip, g_chip = place_of(here)
    cross_chip = jnp.where(flag, f_chip, g_chip)
    block = {XJ: (chip, core), XO: (chip, 1 - core), YJ: (chip ^ 1, core), YO: (chip ^ 1, 1 - core)}
    block |= {FJ: (f_chip, core), GJ: (g_chip, core), None: (cross_chip, core)}

    for q, (left, right) in enumerate(PRODUCTS + ((XJ, XO),)):
        there, ids = [], []
        for name in (left, right):
            at, one = block[name]
            there.append(jnp.logical_and(at >= 0, 2 * at < count))
            ids.append(2 * jnp.clip(at, 0, count // 2 - 1) + one)
        both = jnp.logical_and(*there)
        base = 2 * ids[1]

        def clear(i, carry):
            spot[i] = -1
            return carry

        def fill(row, carry):
            spot[domains[ids[1], row] - base] = row
            return carry

        def clean(slot, carry):
            mine[q, slot] = 0
            theirs[q, slot] = 0
            return carry

        def scan(row, found):
            away = domains[ids[0], row] - base
            inside = jnp.logical_and(away >= 0, away < 2 * rows)
            other_row = spot[jnp.clip(away, 0, 2 * rows - 1)]
            hit = jnp.logical_and(jnp.logical_and(inside, both), other_row >= 0)
            mine[q, found] = row
            theirs[q, found] = jnp.maximum(other_row, 0)
            return found + hit.astype(jnp.int32)

        lax.fori_loop(0, 2 * rows, clear, 0, unroll=10)
        lax.fori_loop(0, rows, fill, 0, unroll=10)
        lax.fori_loop(0, width, clean, 0, unroll=9)
        number[q] = lax.fori_loop(0, rows, scan, 0, unroll=5)


def own_kernel(me, domains, pairs, own, other, coef, out, share, number, mine, theirs, spot):
    rows, aux, width = own.shape
    here = me[0]
    find_matches(here, domains, number, mine, theirs, spot)
    out[...] = jnp.zeros_like(out)
    size = max(n for n in range(1, 11) if rows % n == 0)

    def square(step, carry):
        left = own[pl.ds(size * step, size)].reshape(size * aux, width)
        out[0] += multiply(left, left)
        return carry

    lax.fori_loop(0, rows // size, square, 0)

    def beside(step, carry):
        lefts, rights = [], []
        for i in range(OWN_STACK):
            slot = OWN_STACK * step + i
            left = own[mine[OWN, slot]]
            lefts.append(jnp.where(slot < number[OWN], left, jnp.zeros_like(left)))
            rights.append(other[theirs[OWN, slot]])
        out[1] += multiply(jnp.concatenate(lefts, axis=0), jnp.concatenate(rights, axis=0))
        return carry

    lax.fori_loop(0, (number[OWN] + OWN_STACK - 1) // OWN_STACK, beside, 0)

    tile = 128
    for start in range(0, aux, tile):
        total = jnp.zeros((tile, width), F32)
        for row in range(rows):
            total += own[row, start:start + tile, :].astype(F32) * coef[row:row + 1, :].astype(F32)
        share[:, start:start + tile] = jnp.sum(total.T, axis=0, keepdims=True)
    depth = pairs.shape[1]
    lane = lax.broadcasted_iota(jnp.int32, (1, share.shape[1] - aux), 1)
    marks = jnp.zeros(lane.shape, F32)
    for r in range(depth):
        marks = jnp.where(lane == here * depth + r, pairs[0, r].astype(F32), marks)
    share[:, aux:] = marks


def own_products(me, domains, pairs, own, other, coef):
    rows, aux, width = own.shape
    count = domains.shape[0]
    marks = -(-count * pairs.shape[1] // 128) * 128
    most = max(-(-rows // n) * n for n in (STACK, OWN_STACK))
    table = jax.ShapeDtypeStruct((OWN + 1, most), jnp.int32)
    return pl.pallas_call(
        own_kernel,
        out_shape=[
            squares(2, width),
            jax.ShapeDtypeStruct((1, aux + marks), F32),
            jax.ShapeDtypeStruct((OWN + 1,), jnp.int32),
            table,
            table,
        ],
        in_specs=smem(3) + vmem(3),
        out_specs=vmem(2) + smem(3),
        scratch_shapes=[pltpu.SMEM((2 * rows,), jnp.int32)],
        compiler_params=pltpu.CompilerParams(vmem_limit_bytes=LIMIT),
        cost_estimate=cost(own, other),
    )(me, domains, pairs, own, other, coef)


def relay_kernel(value, *refs):
    shares, (low, high, total, sems) = refs[:-4], refs[-4:]
    size = low.shape[1]
    copies = [
        pltpu.make_async_copy(value.at[:, :size, :], low, sems.at[0]),
        pltpu.make_async_copy(value.at[:, size:, :], high, sems.at[1]),
    ]
    for copy in copies:
        copy.start()
    total[...] = sum(share[...] for share in shares)
    for copy in copies:
        copy.wait()


def relay(value, shares):
    rows, size, width = value.shape
    part = jax.ShapeDtypeStruct((rows, size // 2, width), value.dtype)
    return pl.pallas_call(
        relay_kernel,
        out_shape=[part, part, jax.ShapeDtypeStruct(shares[0].shape, F32)],
        in_specs=vmem(1 + len(shares)),
        out_specs=vmem(3),
        scratch_shapes=[pltpu.SemaphoreType.DMA((2,))],
        compiler_params=pltpu.CompilerParams(vmem_limit_bytes=LIMIT),
        cost_estimate=cost(value, value),
    )(value, *shares)


def shared_kernel(me, number, mine, theirs, *refs):
    blocks, shares = refs[:8], refs[8:-8]
    kept, to_y, to_f, to_g, to_mate, coulomb, summed, total = refs[-8:]
    rows, size, _ = blocks[XJ].shape
    _, _, odd, flag, _, _ = place_of(me[0])
    main_half = pl.ds(pl.multiple_of(odd * size, 16), size)
    cross_half = pl.ds(pl.multiple_of(jnp.where(flag, odd, 1 - odd) * size, 16), size)
    total[...] = jnp.zeros_like(total)

    def add(q, group):
        lefts, rights = [], []
        left_block, right_block = PRODUCTS[q]
        if q == XG:
            left_block = XS
        for i in range(STACK):
            slot = group * STACK + i
            row, other_row = mine[q, slot], theirs[q, slot]
            if left_block == XO:
                left = blocks[XO][row, cross_half if q == CROSS else main_half, :]
            elif left_block == YO:
                left = jnp.concatenate([blocks[YO][row], blocks[YO_HIGH][row]], axis=0)
            else:
                left = blocks[left_block][row]
            lefts.append(jnp.where(slot < number[q], left, jnp.zeros_like(left)))
            if q == CROSS:
                rights.append(jnp.where(flag, blocks[FJ][other_row], blocks[GJ][other_row]))
            else:
                rights.append(blocks[right_block][other_row])
        total[q] += multiply(jnp.concatenate(lefts, axis=0), jnp.concatenate(rights, axis=0))

    products = range(len(PRODUCTS))
    most = number[0]
    for q in products:
        most = jnp.maximum(most, number[q])

    def step(group, carry):
        for q in products:
            add(q, group)
        return carry

    lax.fori_loop(0, (most + STACK - 1) // STACK, step, 0)

    kept[0] = total[XY]
    kept[1] = total[XF]
    kept[2] = total[XG]
    to_y[0] = total[XY].T
    to_y[1] = total[XYO].T
    to_y[2] = total[YF]
    to_y[3] = total[YOF]
    to_f[0] = total[XF].T
    to_f[1] = jnp.where(flag, total[CROSS].T, 0.0)
    to_f[2] = total[YF].T
    to_f[3] = total[YOF].T
    to_g[0] = total[XG].T
    to_g[1] = jnp.where(flag, 0.0, total[CROSS].T)
    to_mate[0] = total[XYO]
    to_mate[1] = total[CROSS]

    gathered = sum(share[...] for share in shares)
    summed[...] = gathered
    low, high = gathered[:, :size], gathered[:, size:2 * size]
    main_gamma = jnp.where(odd == 1, high, low).astype(BF16)
    side_gamma = jnp.where(odd == 1, low, high).astype(BF16)
    for row in range(rows):
        part = jnp.dot(main_gamma, blocks[XJ][row], preferred_element_type=F32)
        coulomb[0, row:row + 1, :] = part + jnp.dot(side_gamma, blocks[XS][row], preferred_element_type=F32)


def shared_products(me, tables, blocks, shares):
    rows, _, width = blocks[0].shape
    flat = jax.ShapeDtypeStruct
    return pl.pallas_call(
        shared_kernel,
        out_shape=[squares(n, width) for n in (3, 4, 4, 2, 2)]
        + [flat((1, rows, width), F32), flat(shares[0].shape, F32)],
        in_specs=smem(1 + len(tables)) + vmem(len(blocks) + len(shares)),
        out_specs=vmem(7),
        scratch_shapes=[pltpu.VMEM((len(PRODUCTS), width, width), F32)],
        compiler_params=pltpu.CompilerParams(vmem_limit_bytes=2 * LIMIT),
        cost_estimate=cost(*blocks),
    )(me, *tables, *blocks, *shares)


def band_kernel(aux, me, pairs, summed, own, kept, from_y, from_f, from_g, from_mate, passed, band):
    depth = pairs.shape[1]
    here = me[0]
    core, _, odd, _, _, _ = place_of(here)
    sign, cross = 1 - 2 * odd, 1 - 2 * core

    def put(ahead, value):
        far = jnp.abs(ahead)
        lower = summed[0, aux + jnp.maximum(here - far, 0) * depth + far - 1] > 0.5
        upper = pairs[0, far - 1] == 1
        there = jnp.logical_or(jnp.logical_and(ahead > 0, upper), jnp.logical_and(ahead < 0, lower))
        band[depth + ahead] = jnp.where(there, value, 0.0)

    band[depth] = own[0]
    put(cross, own[1])
    put(2 * sign, kept[0] + from_y[0])
    put(2 * sign + cross, from_mate[0] + from_y[1])
    put(-2 * sign, from_y[2] + from_f[2])
    put(-2 * sign + cross, passed[0] + from_f[3])
    put(4 * sign, kept[1] + from_g[0])
    put(-4 * sign, kept[2] + from_f[0])
    put(-3 * cross, from_mate[1] + from_f[1] + from_g[1])


def finish(aux, me, pairs, summed, own, *partials):
    depth, width = pairs.shape[1], own.shape[-1]
    return pl.pallas_call(
        functools.partial(band_kernel, aux),
        out_shape=squares(2 * depth + 1, width),
        in_specs=smem(3) + vmem(1 + len(partials)),
        out_specs=vmem(1)[0],
        compiler_params=pltpu.CompilerParams(vmem_limit_bytes=LIMIT),
        cost_estimate=cost(own, *partials),
    )(me, pairs, summed, own, *partials)


def add_kernel(*refs):
    refs[-1][...] = sum(share[...] for share in refs[:-1])


def added(shares):
    return pl.pallas_call(
        add_kernel,
        out_shape=jax.ShapeDtypeStruct(shares[0].shape, F32),
        in_specs=vmem(len(shares)),
        out_specs=vmem(1)[0],
        cost_estimate=cost(*shares),
    )(*shares)


def shares_of(values, count, step, ways):
    every = [values]
    for way in range(1, ways):
        every.append(lax.ppermute(values, "basis", [(i, i ^ (step * way)) for i in range(count)]))
    return every


def per_device(factors, coefs, domains, pairs):
    own = factors[0]
    _, aux, _ = own.shape
    count = lax.axis_size("basis")
    me = lax.axis_index("basis").astype(jnp.int32).reshape(1)

    swap = chip_route(count, lambda c: c, swap=True)
    across = chip_route(count, lambda c: c ^ 1)
    f_route = chip_route(count, lambda c: c - 2 if c % 2 == 0 else c + 2)
    g_route = chip_route(count, lambda c: c + 2 if c % 2 == 0 else c - 2)
    f_back, g_back = [(b, a) for a, b in f_route], [(b, a) for a, b in g_route]
    send = lambda value, route: lax.ppermute(value, "basis", route)

    side_part, main_part = cut(me, own)
    y = send(side_part, across)
    f = send(main_part, f_route)
    g = send(side_part, g_route)
    other = send(own, swap)
    own_pairs, share, *tables = own_products(me, domains, pairs, own, other, coefs[0])
    y_low, y_high, share = relay(y, shares_of(share, count, 1, 4))
    step = 4
    shares = [share]
    while step < count:
        if len(shares) > 1:
            shares = [added(shares)]
        ways = 4 if 4 * step <= count else 2
        shares = shares_of(shares[0], count, step, ways)
        step *= ways
    blocks = (main_part, other, y, send(y_low, swap), send(y_high, swap), f, g, side_part)
    kept, to_y, to_f, to_g, to_mate, coulomb_half, summed = shared_products(me, tables, blocks, shares)
    from_y = send(to_y, across)
    from_mate = send(to_mate, swap)
    from_f, from_g = send(to_f, f_back), send(to_g, g_back)
    passed = send(from_y[3:], swap)
    band = finish(aux, me, pairs, summed, own_pairs, kept, from_y, from_f, from_g, from_mate, passed)
    return (band[None], coulomb_half)


def solution(mesh):
    placed = (
        P(("groups", "basis"), None, None, None),
        P(("groups", "basis"), None, None),
        P("groups", None),
        P(("groups", "basis"), None),
    )
    return jax.shard_map(
        per_device,
        mesh=mesh,
        in_specs=placed,
        out_specs=(P(("groups", "basis"), None, None, None), P(("groups", "basis"), None, None)),
        check_vma=False,
    )
```

time: 277 us -> 78.5 us (0.28)
  blocking collectives: 99.9 us -> 0 us
  waiting for transfers between devices: 100 us -> 33.1 us
  matrix products: 37.1 us -> 0 us
  Pallas kernels: 0 us -> 18.8 us
  local copies, waits for them, and re-layouts: 18.6 us -> 4.13 us
  starting transfers between devices: 16.9 us -> 21.3 us
    psum x1 -> x0, blocking collectives: 99.9 us -> none  [per_device(): gamma = lax.psum(partial_sum, 'basis')]
    ppermute x8 -> x17, waiting for transfers between devices: 100 us -> 33.1 us  [the longest x11 28.6 us: per_device(): send = lambda value, route: lax.ppermute(value, 'basis', route)]
    dot_general x12 -> x0, matrix products: 37.1 us -> none  [the longest x5 21.7 us: contract(): jnp.einsum('kl,lpm->kpm', match, remote, preferred_element_type=jnp.float32)]
    pallas_call x0 -> x5, Pallas kernels: none -> 18.8 us  [the longest x1 11 us: own_products(): pl.pallas_call(own_kernel, out_shape=[squares(2, width), jax.ShapeDtypeSt...]
    convert_element_type x6 -> x0, local copies, waits for them, and re-layouts: 11.7 us -> none  [the longest x5 11.7 us: contract(): jnp.einsum('kl,lpm->kpm', match, remote, preferred_element_type=jnp.float32)]
    ppermute x8 -> x17, starting transfers between devices: 16.9 us -> 21.3 us  [the longest x11 15 us: per_device(): send = lambda value, route: lax.ppermute(value, 'basis', route)]
  transfers between devices with their start and end apart: 8 -> 17, of which waited for: 3 -> 6; matrix products, arithmetic and copies ran while one was open for 17% -> 1% of each run, Pallas kernels for 0% -> 15%
where the time goes in v2:
time: 78.5 us; the launch traced here: 78.2 us
  waiting for transfers between devices  33.1 us (42%)
  starting transfers between devices  21.3 us (27%)
  Pallas kernels  18.8 us (24%)
  local copies, waits for them, and re-layouts  4.13 us (5%)
    ppermute x11, waiting for transfers between devices, per_device(): send = lambda value, route: lax.ppermute(value, 'basis', route)  28.6 us
    ppermute x11, starting transfers between devices, per_device(): send = lambda value, route: lax.ppermute(value, 'basis', route)  15 us
    pallas_call x1, Pallas kernels, own_products(): pl.pallas_call(own_kernel, out_shape=[squares(2, width), jax.ShapeDtypeSt...  11 us
    ppermute x6, starting transfers between devices, shares_of(): lax.ppermute(values, 'basis', [(i, i ^ step * way) for i in range(count)])  6.32 us
    pallas_call x1, Pallas kernels, shared_products(): pl.pallas_call(shared_kernel, out_shape=[squares(n, width) for n in (3, 4...  5.78 us
    ppermute x6, waiting for transfers between devices, shares_of(): lax.ppermute(values, 'basis', [(i, i ^ step * way) for i in range(count)])  4.49 us
    unnamed x11, local copies, waits for them, and re-layouts  4.13 us
  transfers between devices with their start and end apart: 17, of which 6 were waited for; matrix products, arithmetic and copies ran while one was open for 1% of the time, Pallas kernels for 15%

profile of v2, /device:TPU:0, one launch (start us, length us, event | category | flops | bytes accessed | tf_op | source)
XLA Modules:
  0.0 78.2 jit_solution(487375132118152454)
XLA Ops:
  0.6 0.5 collective-permute-start
  1.1 2.1 %copy-done = bf16[1,30,512,128]{3,2,1,0:T(8,128)(2,1)S(1)} copy-done((bf16[1,30,512,128]{3,2,1,0:T(8,128)(2,1)S(1)}, bf16[1,30,512,128]{3,2,1,0:T(8,128)(2,1)}, u32[]{:S(2)}) %copy-start) | copy-done | bytes 3932184
  3.6 2.6 %collective-permute-start.1 = (bf16[30,256,128]{2,1,0:T(8,128)(2,1)S(1)}, bf16[30,256,128]{2,1,0:T(8,128)(2,1)S(1)}, u32[]{:S(2)}, u32[]{:S(2)}) collective-permute-start(bf16[30,256,128]{2,1,0:T(8,128)(2,1)S(1)} %get-tuple-element.23.refs_7_), channel_id=1, source_target_pairs={{0,2},{1,3},{2,0},{3,1},{4,6},{5,7},{6,4},{7,5},{8,10},{9,11},{10,... | collective-permute-start | bytes 5898248 | tf_op jit(solution)/shard_map/ppermute | solution.py:371
  6.2 1.3 %collective-permute-start.7 = (bf16[30,256,128]{2,1,0:T(8,128)(2,1)S(1)}, bf16[30,256,128]{2,1,0:T(8,128)(2,1)S(1)}, u32[]{:S(2)}, u32[]{:S(2)}) collective-permute-start(bf16[30,256,128]{2,1,0:T(8,128)(2,1)S(1)} %get-tuple-element.22.refs_0_), channel_id=1, source_target_pairs={{2,6},{3,7},{4,0},{5,1},{6,10},{7,11},{8,4},{9,5},{10,14},{11,15},... | collective-permute-start | bytes 5898248 | tf_op jit(solution)/shard_map/ppermute | solution.py:371
  7.5 4.7 %collective-permute-start.8 = (bf16[30,256,128]{2,1,0:T(8,128)(2,1)S(1)}, bf16[30,256,128]{2,1,0:T(8,128)(2,1)S(1)}, u32[]{:S(2)}, u32[]{:S(2)}) collective-permute-start(bf16[30,256,128]{2,1,0:T(8,128)(2,1)S(1)} %get-tuple-element.23.refs_7_), channel_id=1, source_target_pairs={{0,4},{1,5},{4,8},{5,9},{6,2},{7,3},{8,12},{9,13},{10,6},{11,7},{1... | collective-permute-start | bytes 5898248 | tf_op jit(solution)/shard_map/ppermute | solution.py:371
  12.2 0.7 copy-done.2
  12.9 0.7 copy-done.3
  13.6 11.0 %shard_map.59 = (f32[2,128,128]{2,1,0:T(8,128)S(1)}, f32[1,640]{1,0:T(1,128)S(1)}, s32[8]{0:T(128)S(1)}, s32[8,36]{1,0:T(8,128)S(1)}, s32[8,36]{1,0:T(8,128)S(1)}) custom-call(s32[1]{0:T(128)} %bitcast.me, s32[16,30]{1,0:T(8,128)S(1)} %copy-done.2, s32[1,4]{1,0:T(1,128)S(1)} %copy-done.4, bf16[30,512,128]{2,1,0:T(8,128)(2,1)S(1)} %bitcast.6, ...), custom_call_target="tpu_custom_call" | custom-call | flops 1 | bytes 7864320 | tf_op jit(solution)/shard_map/pallas_call | solution.py:175
  24.7 1.3 %collective-permute-start.3 = (f32[1,640]{1,0:T(1,128)S(1)}, f32[1,640]{1,0:T(1,128)S(1)}, u32[]{:S(2)}, u32[]{:S(2)}) collective-permute-start(f32[1,640]{1,0:T(1,128)S(1)} %get-tuple-element.24.refs_0_), channel_id=1, source_target_pairs={{0,2},{1,3},{2,0},{3,1},{4,6},{5,7},{6,4},{7,5},{8,10},{9,11},{10,... | collective-permute-start | bytes 7688 | tf_op jit(solution)/shard_map/ppermute | solution.py:356
  26.0 23.7 %collective-permute-done.1.value.refs_2_ = bf16[30,256,128]{2,1,0:T(8,128)(2,1)S(1)} collective-permute-done((bf16[30,256,128]{2,1,0:T(8,128)(2,1)S(1)}, bf16[30,256,128]{2,1,0:T(8,128)(2,1)S(1)}, u32[]{:S(2)}, u32[]{:S(2)}) %collective-permute-start.1) | collective-permute-done | bytes 1966112 | tf_op jit(solution)/shard_map/ppermute | solution.py:371
  49.8 1.1 %collective-permute-done.2.refs_1_ = f32[1,640]{1,0:T(1,128)S(1)} collective-permute-done((f32[1,640]{1,0:T(1,128)S(1)}, f32[1,640]{1,0:T(1,128)S(1)}, u32[]{:S(2)}, u32[]{:S(2)}) %collective-permute-start.2) | collective-permute-done | bytes 2592 | tf_op jit(solution)/shard_map/ppermute | solution.py:356
  51.3 0.3 collective-permute-start.6
  51.7 3.8 %collective-permute-start.11 = (f32[1,640]{1,0:T(1,128)S(1)}, f32[1,640]{1,0:T(1,128)S(1)}, u32[]{:S(2)}, u32[]{:S(2)}) collective-permute-start(f32[1,640]{1,0:T(1,128)S(1)} %get-tuple-element.27.refs_8_), channel_id=1, source_target_pairs={{0,12},{1,13},{2,14},{3,15},{4,8},{5,9},{6,10},{7,11},{8,4},{9,5},... | collective-permute-start | bytes 7688 | tf_op jit(solution)/shard_map/ppermute | solution.py:356
  55.6 1.1 %collective-permute-start.9 = (f32[1,640]{1,0:T(1,128)S(1)}, f32[1,640]{1,0:T(1,128)S(1)}, u32[]{:S(2)}, u32[]{:S(2)}) collective-permute-start(f32[1,640]{1,0:T(1,128)S(1)} %get-tuple-element.27.refs_8_), channel_id=1, source_target_pairs={{0,4},{1,5},{2,6},{3,7},{4,0},{5,1},{6,2},{7,3},{8,12},{9,13},{10,... | collective-permute-start | bytes 7688 | tf_op jit(solution)/shard_map/ppermute | solution.py:356
  56.7 0.4 collective-permute-done.11.refs_11_
  57.1 2.9 %collective-permute-done.10.refs_10_ = f32[1,640]{1,0:T(1,128)S(1)} collective-permute-done((f32[1,640]{1,0:T(1,128)S(1)}, f32[1,640]{1,0:T(1,128)S(1)}, u32[]{:S(2)}, u32[]{:S(2)}) %collective-permute-start.10) | collective-permute-done | bytes 2592 | tf_op jit(solution)/shard_map/ppermute | solution.py:356
  60.0 5.8 %shard_map.62 = (f32[3,128,128]{2,1,0:T(8,128)S(1)}, f32[4,128,128]{2,1,0:T(8,128)S(1)}, f32[4,128,128]{2,1,0:T(8,128)S(1)}, f32[2,128,128]{2,1,0:T(8,128)S(1)},...) custom-call(s32[1]{0:T(128)} %bitcast.me, s32[8]{0:T(128)S(1)} %get-tuple-element.19.number, ...), custom_call_target="tpu_custom_call" | custom-call | flops 1 | bytes 15728640 | tf_op jit(solution)/shard_map/pallas_call | solution.py:291
  65.8 1.6 %collective-permute-start.12 = (f32[4,128,128]{2,1,0:T(8,128)S(1)}, f32[4,128,128]{2,1,0:T(8,128)S(1)}, u32[]{:S(2)}, u32[]{:S(2)}) collective-permute-start(f32[4,128,128]{2,1,0:T(8,128)S(1)} %get-tuple-element.31), channel_id=1, source_target_pairs={{0,2},{1,3},{2,0},{3,1},{4,6},{5,7},{6,4},{7,5},{8,10},{9,11},{10,... | collective-permute-start | bytes 786440 | tf_op jit(solution)/shard_map/ppermute | solution.py:371
  67.3 2.4 %collective-permute-start.13 = (f32[4,128,128]{2,1,0:T(8,128)S(1)}, f32[4,128,128]{2,1,0:T(8,128)S(1)}, u32[]{:S(2)}, u32[]{:S(2)}) collective-permute-start(f32[4,128,128]{2,1,0:T(8,128)S(1)} %get-tuple-element.32), channel_id=1, source_target_pairs={{6,2},{7,3},{0,4},{1,5},{10,6},{11,7},{4,8},{5,9},{14,10},{15,11},... | collective-permute-start | bytes 786440 | tf_op jit(solution)/shard_map/ppermute | solution.py:371
  69.8 1.3 %collective-permute-start.14 = (f32[2,128,128]{2,1,0:T(8,128)S(1)}, f32[2,128,128]{2,1,0:T(8,128)S(1)}, u32[]{:S(2)}, u32[]{:S(2)}) collective-permute-start(f32[2,128,128]{2,1,0:T(8,128)S(1)} %get-tuple-element.33), channel_id=1, source_target_pairs={{4,0},{5,1},{8,4},{9,5},{2,6},{3,7},{12,8},{13,9},{6,10},{7,11},{1... | collective-permute-start | bytes 393224 | tf_op jit(solution)/shard_map/ppermute | solution.py:371
  71.2 1.6 %collective-permute-done.12.from_y = f32[4,128,128]{2,1,0:T(8,128)S(1)} collective-permute-done((f32[4,128,128]{2,1,0:T(8,128)S(1)}, f32[4,128,128]{2,1,0:T(8,128)S(1)}, u32[]{:S(2)}, u32[]{:S(2)}) %collective-permute-start.12) | collective-permute-done | bytes 262176 | tf_op jit(solution)/shard_map/ppermute | solution.py:371
  72.8 0.6 copy.6
  73.4 3.2 %collective-permute-done.14.from_g = f32[2,128,128]{2,1,0:T(8,128)S(1)} collective-permute-done((f32[2,128,128]{2,1,0:T(8,128)S(1)}, f32[2,128,128]{2,1,0:T(8,128)S(1)}, u32[]{:S(2)}, u32[]{:S(2)}) %collective-permute-start.14) | collective-permute-done | bytes 131104 | tf_op jit(solution)/shard_map/ppermute | solution.py:371
  76.7 1.5 %shard_map.63 = f32[9,128,128]{2,1,0:T(8,128)} custom-call(s32[1]{0:T(128)} %bitcast.me, s32[1,4]{1,0:T(1,128)S(1)} %copy-done.4, f32[1,640]{1,0:T(1,128)S(1)} %get-tuple-element.28.summed, f32[2,128,128]{2,1,0:T(8,128)S(1)} %get-tuple-element.29.own, f32[3,128,128]{2,1,0:T(8,128)S(1)} %get-tuple-element.30.kept, ...), custom_call_target="tpu_custom_call" | custom-call | flops 1 | bytes 1179648 | tf_op jit(solution)/shard_map/pallas_call | solution.py:329
  (27 shorter events, 1.1 us)
Async XLA Ops:
  0.6 11.5 %collective-permute-start = (bf16[30,512,128]{2,1,0:T(8,128)(2,1)}, bf16[30,512,128]{2,1,0:T(8,128)(2,1)}, u32[]{:S(2)}, u32[]{:S(2)}) collective-permute-start(bf16[30,512,128]{2,1,0:T(8,128)(2,1)} %bitcast.4), channel_id=1, source_target_pairs={{0,1},{1,0},{2,3},{3,2},{4,5},{5,4},{6,7},{7,6},{8,9},{9,8},{10,11... | collective-permute-start | bytes 11796488 | tf_op jit(solution)/shard_map/ppermute | solution.py:371
  1.1 2.1 %copy-start = (bf16[1,30,512,128]{3,2,1,0:T(8,128)(2,1)S(1)}, bf16[1,30,512,128]{3,2,1,0:T(8,128)(2,1)}, u32[]{:S(2)}) copy-start(bf16[1,30,512,128]{3,2,1,0:T(8,128)(2,1)} %param.4) | copy-start | bytes 11796484
  3.3 8.9 %copy-start.1 = (bf16[1,30,512,128]{3,2,1,0:T(8,128)(2,1)S(1)}, bf16[1,30,512,128]{3,2,1,0:T(8,128)(2,1)}, u32[]{:S(2)}) copy-start(bf16[1,30,512,128]{3,2,1,0:T(8,128)(2,1)} %param.4) | copy-start | bytes 11796484
  3.3 8.9 %copy-start.4 = (s32[1,4]{1,0:T(1,128)S(1)}, s32[1,4]{1,0:T(1,128)}, u32[]{:S(2)}) copy-start(s32[1,4]{1,0:T(1,128)} %pairs.3) | copy-start | bytes 52
  3.6 46.1 %collective-permute-start.1 = (bf16[30,256,128]{2,1,0:T(8,128)(2,1)S(1)}, bf16[30,256,128]{2,1,0:T(8,128)(2,1)S(1)}, u32[]{:S(2)}, u32[]{:S(2)}) collective-permute-start(bf16[30,256,128]{2,1,0:T(8,128)(2,1)S(1)} %get-tuple-element.23.refs_7_), channel_id=1, source_target_pairs={{0,2},{1,3},{2,0},{3,1},{4,6},{5,7},{6,4},{7,5},{8,10},{9,11},{10,... | collective-permute-start | bytes 5898248 | tf_op jit(solution)/shard_map/ppermute | solution.py:371
  6.2 49.3 %collective-permute-start.7 = (bf16[30,256,128]{2,1,0:T(8,128)(2,1)S(1)}, bf16[30,256,128]{2,1,0:T(8,128)(2,1)S(1)}, u32[]{:S(2)}, u32[]{:S(2)}) collective-permute-start(bf16[30,256,128]{2,1,0:T(8,128)(2,1)S(1)} %get-tuple-element.22.refs_0_), channel_id=1, source_target_pairs={{2,6},{3,7},{4,0},{5,1},{6,10},{7,11},{8,4},{9,5},{10,14},{11,15},... | collective-permute-start | bytes 5898248 | tf_op jit(solution)/shard_map/ppermute | solution.py:371
  7.5 48.1 %collective-permute-start.8 = (bf16[30,256,128]{2,1,0:T(8,128)(2,1)S(1)}, bf16[30,256,128]{2,1,0:T(8,128)(2,1)S(1)}, u32[]{:S(2)}, u32[]{:S(2)}) collective-permute-start(bf16[30,256,128]{2,1,0:T(8,128)(2,1)S(1)} %get-tuple-element.23.refs_7_), channel_id=1, source_target_pairs={{0,4},{1,5},{4,8},{5,9},{6,2},{7,3},{8,12},{9,13},{10,6},{11,7},{1... | collective-permute-start | bytes 5898248 | tf_op jit(solution)/shard_map/ppermute | solution.py:371
  12.2 0.7 copy-start.2
  12.9 0.7 copy-start.3
  24.6 25.1 %collective-permute-start.4 = (f32[1,640]{1,0:T(1,128)S(1)}, f32[1,640]{1,0:T(1,128)S(1)}, u32[]{:S(2)}, u32[]{:S(2)}) collective-permute-start(f32[1,640]{1,0:T(1,128)S(1)} %get-tuple-element.24.refs_0_), channel_id=1, source_target_pairs={{0,3},{1,2},{2,1},{3,0},{4,7},{5,6},{6,5},{7,4},{8,11},{9,10},{10,... | collective-permute-start | bytes 7688 | tf_op jit(solution)/shard_map/ppermute | solution.py:356
  24.7 25.1 %collective-permute-start.3 = (f32[1,640]{1,0:T(1,128)S(1)}, f32[1,640]{1,0:T(1,128)S(1)}, u32[]{:S(2)}, u32[]{:S(2)}) collective-permute-start(f32[1,640]{1,0:T(1,128)S(1)} %get-tuple-element.24.refs_0_), channel_id=1, source_target_pairs={{0,2},{1,3},{2,0},{3,1},{4,6},{5,7},{6,4},{7,5},{8,10},{9,11},{10,... | collective-permute-start | bytes 7688 | tf_op jit(solution)/shard_map/ppermute | solution.py:356
  49.7 1.2 %collective-permute-start.2 = (f32[1,640]{1,0:T(1,128)S(1)}, f32[1,640]{1,0:T(1,128)S(1)}, u32[]{:S(2)}, u32[]{:S(2)}) collective-permute-start(f32[1,640]{1,0:T(1,128)S(1)} %get-tuple-element.24.refs_0_), channel_id=1, source_target_pairs={{0,1},{1,0},{2,3},{3,2},{4,5},{5,4},{6,7},{7,6},{8,9},{9,8},{10,11... | collective-permute-start | bytes 7688 | tf_op jit(solution)/shard_map/ppermute | solution.py:356
  51.1 8.9 %collective-permute-start.5 = (bf16[30,128,128]{2,1,0:T(8,128)(2,1)S(1)}, bf16[30,128,128]{2,1,0:T(8,128)(2,1)S(1)}, u32[]{:S(2)}, u32[]{:S(2)}) collective-permute-start(bf16[30,128,128]{2,1,0:T(8,128)(2,1)S(1)} %get-tuple-element.25), channel_id=1, source_target_pairs={{0,1},{1,0},{2,3},{3,2},{4,5},{5,4},{6,7},{7,6},{8,9},{9,8},{10,11... | collective-permute-start | bytes 2949128 | tf_op jit(solution)/shard_map/ppermute | solution.py:371
  51.3 8.7 %collective-permute-start.6 = (bf16[30,128,128]{2,1,0:T(8,128)(2,1)S(1)}, bf16[30,128,128]{2,1,0:T(8,128)(2,1)S(1)}, u32[]{:S(2)}, u32[]{:S(2)}) collective-permute-start(bf16[30,128,128]{2,1,0:T(8,128)(2,1)S(1)} %get-tuple-element.26), channel_id=1, source_target_pairs={{0,1},{1,0},{2,3},{3,2},{4,5},{5,4},{6,7},{7,6},{8,9},{9,8},{10,11... | collective-permute-start | bytes 2949128 | tf_op jit(solution)/shard_map/ppermute | solution.py:371
  51.7 5.4 %collective-permute-start.11 = (f32[1,640]{1,0:T(1,128)S(1)}, f32[1,640]{1,0:T(1,128)S(1)}, u32[]{:S(2)}, u32[]{:S(2)}) collective-permute-start(f32[1,640]{1,0:T(1,128)S(1)} %get-tuple-element.27.refs_8_), channel_id=1, source_target_pairs={{0,12},{1,13},{2,14},{3,15},{4,8},{5,9},{6,10},{7,11},{8,4},{9,5},... | collective-permute-start | bytes 7688 | tf_op jit(solution)/shard_map/ppermute | solution.py:356
  55.5 4.5 %collective-permute-start.10 = (f32[1,640]{1,0:T(1,128)S(1)}, f32[1,640]{1,0:T(1,128)S(1)}, u32[]{:S(2)}, u32[]{:S(2)}) collective-permute-start(f32[1,640]{1,0:T(1,128)S(1)} %get-tuple-element.27.refs_8_), channel_id=1, source_target_pairs={{0,8},{1,9},{2,10},{3,11},{4,12},{5,13},{6,14},{7,15},{8,0},{9,1},... | collective-permute-start | bytes 7688 | tf_op jit(solution)/shard_map/ppermute | solution.py:356
  55.6 4.4 %collective-permute-start.9 = (f32[1,640]{1,0:T(1,128)S(1)}, f32[1,640]{1,0:T(1,128)S(1)}, u32[]{:S(2)}, u32[]{:S(2)}) collective-permute-start(f32[1,640]{1,0:T(1,128)S(1)} %get-tuple-element.27.refs_8_), channel_id=1, source_target_pairs={{0,4},{1,5},{2,6},{3,7},{4,0},{5,1},{6,2},{7,3},{8,12},{9,13},{10,... | collective-permute-start | bytes 7688 | tf_op jit(solution)/shard_map/ppermute | solution.py:356
  65.8 7.0 %collective-permute-start.12 = (f32[4,128,128]{2,1,0:T(8,128)S(1)}, f32[4,128,128]{2,1,0:T(8,128)S(1)}, u32[]{:S(2)}, u32[]{:S(2)}) collective-permute-start(f32[4,128,128]{2,1,0:T(8,128)S(1)} %get-tuple-element.31), channel_id=1, source_target_pairs={{0,2},{1,3},{2,0},{3,1},{4,6},{5,7},{6,4},{7,5},{8,10},{9,11},{10,... | collective-permute-start | bytes 786440 | tf_op jit(solution)/shard_map/ppermute | solution.py:371
  67.3 9.3 %collective-permute-start.13 = (f32[4,128,128]{2,1,0:T(8,128)S(1)}, f32[4,128,128]{2,1,0:T(8,128)S(1)}, u32[]{:S(2)}, u32[]{:S(2)}) collective-permute-start(f32[4,128,128]{2,1,0:T(8,128)S(1)} %get-tuple-element.32), channel_id=1, source_target_pairs={{6,2},{7,3},{0,4},{1,5},{10,6},{11,7},{4,8},{5,9},{14,10},{15,11},... | collective-permute-start | bytes 786440 | tf_op jit(solution)/shard_map/ppermute | solution.py:371
  69.8 6.9 %collective-permute-start.14 = (f32[2,128,128]{2,1,0:T(8,128)S(1)}, f32[2,128,128]{2,1,0:T(8,128)S(1)}, u32[]{:S(2)}, u32[]{:S(2)}) collective-permute-start(f32[2,128,128]{2,1,0:T(8,128)S(1)} %get-tuple-element.33), channel_id=1, source_target_pairs={{4,0},{5,1},{8,4},{9,5},{2,6},{3,7},{12,8},{13,9},{6,10},{7,11},{1... | collective-permute-start | bytes 393224 | tf_op jit(solution)/shard_map/ppermute | solution.py:371
  71.1 5.6 %collective-permute-start.15 = (f32[2,128,128]{2,1,0:T(8,128)S(1)}, f32[2,128,128]{2,1,0:T(8,128)S(1)}, u32[]{:S(2)}, u32[]{:S(2)}) collective-permute-start(f32[2,128,128]{2,1,0:T(8,128)S(1)} %get-tuple-element.34), channel_id=1, source_target_pairs={{0,1},{1,0},{2,3},{3,2},{4,5},{5,4},{6,7},{7,6},{8,9},{9,8},{10,11... | collective-permute-start | bytes 393224 | tf_op jit(solution)/shard_map/ppermute | solution.py:371
  72.8 3.9 %collective-permute-start.16 = (f32[1,128,128]{2,1,0:T(8,128)S(1)}, f32[1,128,128]{2,1,0:T(8,128)S(1)}, u32[]{:S(2)}, u32[]{:S(2)}) collective-permute-start(f32[1,128,128]{2,1,0:T(8,128)S(1)} %slice.4), channel_id=1, source_target_pairs={{0,1},{1,0},{2,3},{3,2},{4,5},{5,4},{6,7},{7,6},{8,9},{9,8},{10,11... | collective-permute-start | bytes 196616 | tf_op jit(solution)/shard_map/ppermute | solution.py:371

commit v3 on v2

v3 whole, which is shorter than its diff:
```python
import functools

import jax
import jax.numpy as jnp
from jax import lax
from jax.experimental import pallas as pl
from jax.experimental.pallas import tpu as pltpu
from jax.sharding import PartitionSpec as P

F32 = jnp.float32
BF16 = jnp.bfloat16

XJ, XO, XJ_SIDE, XO_SIDE, YJ, YO, YO_HIGH, FJ, GJ = range(9)
XY, XYO, XF, YF, YOF, CROSS_F, XG, CROSS_G, OWN = range(9)
PRODUCTS = (
    (XJ, YJ), (XO, YJ), (XJ, FJ), (YJ, FJ), (YO, FJ), (XO, FJ), (XJ_SIDE, GJ), (XO_SIDE, GJ), (XJ, XO)
)
SHARED = (XF, CROSS_F, YF, YOF, XG, CROSS_G, XY, XYO)
STACK, OWN_STACK = 9, 4
LIMIT = 12 * 2**20


def cost(*arrays):
    return pl.CostEstimate(flops=1, bytes_accessed=sum(a.size * a.dtype.itemsize for a in arrays), transcendentals=0)


def smem(n):
    return [pl.BlockSpec(memory_space=pltpu.SMEM)] * n


def vmem(n):
    return [pl.BlockSpec(memory_space=pltpu.VMEM)] * n


def squares(n, width):
    return jax.ShapeDtypeStruct((n, width, width), F32)


def multiply(left, right):
    return lax.dot_general(left, right, (((0,), (0,)), ((), ())), preferred_element_type=F32)


def chip_route(count, target, swap=False):
    chips = count // 2
    route = []
    for chip in range(chips):
        to = target(chip)
        if 0 <= to < chips:
            for core in range(2):
                route.append((2 * chip + core, 2 * to + (1 - core if swap else core)))
    return route


def place_of_device():
    me = lax.axis_index("basis")
    core, chip = me & 1, me >> 1
    odd = chip & 1
    return me, core, chip, odd, core == odd, chip + 2 - 4 * odd, chip - 2 + 4 * odd, odd == ((chip >> 1) & 1)


def cut_kernel(size, own, side, main, near, far, sems):
    _, _, _, odd, _, _, _, f_near = place_of_device()
    side_start, main_start = (1 - odd) * size, odd * size
    near_start, far_start = jnp.where(f_near, side_start, main_start), jnp.where(f_near, main_start, side_start)
    copies = []
    for i, (out, start) in enumerate(
        ((side, side_start), (near, near_start), (far, far_start), (main, main_start))
    ):
        rows = pl.ds(pl.multiple_of(start, 16), size)
        copies.append(pltpu.make_async_copy(own.at[:, rows, :], out, sems.at[i]))
    for copy in copies:
        copy.start()
    for copy in copies:
        copy.wait()


def cut(own):
    rows, aux, width = own.shape
    part = jax.ShapeDtypeStruct((rows, aux // 2, width), own.dtype)
    return pl.pallas_call(
        functools.partial(cut_kernel, aux // 2),
        out_shape=[part] * 4,
        in_specs=vmem(1),
        out_specs=vmem(4),
        scratch_shapes=[pltpu.SemaphoreType.DMA((4,))],
        compiler_params=pltpu.CompilerParams(vmem_limit_bytes=LIMIT),
        cost_estimate=cost(own, own),
    )(own)


def find_matches(domains, number, mine, theirs, spot):
    count, rows = domains.shape
    width = mine.shape[1]
    _, core, chip, _, flag, f_chip, g_chip, _ = place_of_device()
    mine_first, other_first = (chip, core), (chip, 1 - core)
    block = {XJ: mine_first, XJ_SIDE: mine_first, XO: other_first, XO_SIDE: other_first}
    block |= {YJ: (chip ^ 1, core), YO: (chip ^ 1, 1 - core), FJ: (f_chip, core), GJ: (g_chip, core)}

    for q, (left, right) in enumerate(PRODUCTS):
        there, ids = [], []
        for name in (left, right):
            at, one = block[name]
            there.append(jnp.logical_and(at >= 0, 2 * at < count))
            ids.append(2 * jnp.clip(at, 0, count // 2 - 1) + one)
        both = jnp.logical_and(*there)
        if q in (CROSS_F, CROSS_G):
            both = jnp.logical_and(both, flag if q == CROSS_F else jnp.logical_not(flag))
        base = 2 * ids[1]

        def clear(i, carry):
            spot[i] = -1
            return carry

        def fill(row, carry):
            spot[domains[ids[1], row] - base] = row
            return carry

        def clean(slot, carry):
            mine[q, slot] = 0
            theirs[q, slot] = 0
            return carry

        def scan(row, found):
            away = domains[ids[0], row] - base
            inside = jnp.logical_and(away >= 0, away < 2 * rows)
            other_row = spot[jnp.clip(away, 0, 2 * rows - 1)]
            hit = jnp.logical_and(jnp.logical_and(inside, both), other_row >= 0)
            mine[q, found] = row
            theirs[q, found] = jnp.maximum(other_row, 0)
            return found + hit.astype(jnp.int32)

        lax.fori_loop(0, 2 * rows, clear, 0, unroll=10)
        lax.fori_loop(0, rows, fill, 0, unroll=10)
        lax.fori_loop(0, width, clean, 0, unroll=9)
        number[q] = lax.fori_loop(0, rows, scan, 0, unroll=5)


def own_kernel(domains, pairs, own, other, own_side, other_side, coef, out, share, number, mine, theirs, spot):
    rows, half, width = own.shape
    me, _, _, odd, _, _, _, _ = place_of_device()
    find_matches(domains, number, mine, theirs, spot)
    out[...] = jnp.zeros_like(out)
    size = max(n for n in range(1, 11) if rows % n == 0)

    def square(step, carry):
        for part in (own, own_side):
            left = part[pl.ds(size * step, size)].reshape(size * half, width)
            out[0] += multiply(left, left)
        return carry

    lax.fori_loop(0, rows // size, square, 0)

    def beside(step, carry):
        lefts, rights = [], []
        for i in range(OWN_STACK):
            slot = OWN_STACK * step + i
            for part, other_part in ((own, other), (own_side, other_side)):
                left = part[mine[OWN, slot]]
                lefts.append(jnp.where(slot < number[OWN], left, jnp.zeros_like(left)))
                rights.append(other_part[theirs[OWN, slot]])
        out[1] += multiply(jnp.concatenate(lefts, axis=0), jnp.concatenate(rights, axis=0))
        return carry

    lax.fori_loop(0, (number[OWN] + OWN_STACK - 1) // OWN_STACK, beside, 0)

    tile = 128
    parts = []
    for part in (own, own_side):
        sums = []
        for start in range(0, half, tile):
            total = jnp.zeros((tile, width), F32)
            for row in range(rows):
                total += part[row, start:start + tile, :].astype(F32) * coef[row:row + 1, :].astype(F32)
            sums.append(jnp.sum(total.T, axis=0, keepdims=True))
        parts.append(jnp.concatenate(sums, axis=1))
    share[:, :half] = jnp.where(odd == 1, parts[1], parts[0])
    share[:, half:2 * half] = jnp.where(odd == 1, parts[0], parts[1])
    depth = pairs.shape[1]
    lane = lax.broadcasted_iota(jnp.int32, (1, share.shape[1] - 2 * half), 1)
    marks = jnp.zeros(lane.shape, F32)
    for r in range(depth):
        marks = jnp.where(lane == me * depth + r, pairs[0, r].astype(F32), marks)
    share[:, 2 * half:] = marks


def own_products(domains, pairs, own, other, own_side, other_side, coef):
    rows, half, width = own.shape
    count = domains.shape[0]
    marks = -(-count * pairs.shape[1] // 128) * 128
    most = max(-(-rows // n) * n for n in (STACK, OWN_STACK))
    table = jax.ShapeDtypeStruct((len(PRODUCTS), most), jnp.int32)
    return pl.pallas_call(
        own_kernel,
        out_shape=[
            squares(2, width),
            jax.ShapeDtypeStruct((1, 2 * half + marks), F32),
            jax.ShapeDtypeStruct((len(PRODUCTS),), jnp.int32),
            table,
            table,
        ],
        in_specs=smem(2) + vmem(5),
        out_specs=vmem(2) + smem(3),
        scratch_shapes=[pltpu.SMEM((2 * rows,), jnp.int32)],
        compiler_params=pltpu.CompilerParams(vmem_limit_bytes=LIMIT),
        cost_estimate=cost(own, other, own_side, other_side),
    )(domains, pairs, own, other, own_side, other_side, coef)


def relay_kernel(value, token, low, high, sems):
    size = low.shape[1]
    copies = [
        pltpu.make_async_copy(value.at[:, :size, :], low, sems.at[0]),
        pltpu.make_async_copy(value.at[:, size:, :], high, sems.at[1]),
    ]
    for copy in copies:
        copy.start()
    for copy in copies:
        copy.wait()


def relay(value, token):
    rows, size, width = value.shape
    part = jax.ShapeDtypeStruct((rows, size // 2, width), value.dtype)
    return pl.pallas_call(
        relay_kernel,
        out_shape=[part, part],
        in_specs=vmem(2),
        out_specs=vmem(2),
        scratch_shapes=[pltpu.SemaphoreType.DMA((2,))],
        compiler_params=pltpu.CompilerParams(vmem_limit_bytes=LIMIT),
        cost_estimate=cost(value, value),
    )(value, token)


def add_products(listed, tables, block, total):
    number, mine, theirs = tables

    def add(at, q, group):
        lefts, rights = [], []
        left_block, right_block = PRODUCTS[q]
        for i in range(STACK):
            slot = group * STACK + i
            row, other_row = mine[q, slot], theirs[q, slot]
            left = block[left_block][row]
            if left_block == YO:
                left = jnp.concatenate([left, block[YO_HIGH][row]], axis=0)
            lefts.append(jnp.where(slot < number[q], left, jnp.zeros_like(left)))
            rights.append(block[right_block][other_row])
        total[at] += multiply(jnp.concatenate(lefts, axis=0), jnp.concatenate(rights, axis=0))

    most = number[listed[0]]
    for q in listed:
        most = jnp.maximum(most, number[q])

    def step(group, carry):
        for at, q in enumerate(listed):
            add(at, q, group)
        return carry

    lax.fori_loop(0, (most + STACK - 1) // STACK, step, 0)


def shared_kernel(number, mine, theirs, xj, xo, xj_side, xo_side, yj, yo, yo_high, near, far, total):
    f_near = place_of_device()[-1]
    total[...] = jnp.zeros_like(total)

    def all_products(fj, gj):
        block = {XJ: xj, XO: xo, XJ_SIDE: xj_side, XO_SIDE: xo_side, YJ: yj, YO: yo, YO_HIGH: yo_high}
        block |= {FJ: fj, GJ: gj}
        add_products(SHARED, (number, mine, theirs), block, total)

    @pl.when(f_near)
    def _():
        all_products(near, far)

    @pl.when(jnp.logical_not(f_near))
    def _():
        all_products(far, near)


def shared_products(tables, *blocks):
    return pl.pallas_call(
        shared_kernel,
        out_shape=squares(len(SHARED), blocks[0].shape[-1]),
        in_specs=smem(len(tables)) + vmem(len(blocks)),
        out_specs=vmem(1)[0],
        compiler_params=pltpu.CompilerParams(vmem_limit_bytes=2 * LIMIT),
        cost_estimate=cost(*blocks),
    )(*tables, *blocks)


def message_kernel(total, *refs):
    shares, (to_near, to_far, to_mate, to_y, summed) = refs[:-5], refs[-5:]
    f_near = place_of_device()[-1]
    width = total.shape[1]

    def to_f_and_g(to_f, to_g):
        for i in range(4):
            to_f[i] = total[i].T
        for i in range(2):
            to_g[i] = total[4 + i].T
            to_g[2 + i] = jnp.zeros_like(total[i])

    @pl.when(f_near)
    def _():
        to_f_and_g(to_near, to_far)

    @pl.when(jnp.logical_not(f_near))
    def _():
        to_f_and_g(to_far, to_near)

    to_mate[0] = total[7]
    to_mate[1] = total[1] + total[5]
    for i, value in enumerate((total[6].T, total[7].T, total[2], total[3])):
        to_y[i * width:(i + 1) * width, :] = value
    gathered = sum(share[...] for share in shares)
    summed[...] = gathered
    to_y[4 * width:, :] = jnp.zeros((to_y.shape[0] - 4 * width, width), F32)
    for i in range(gathered.shape[1] // width):
        to_y[4 * width + i:4 * width + i + 1, :] = gathered[:, i * width:(i + 1) * width]


def messages(total, shares):
    width = total.shape[-1]
    lines = -(-shares[0].shape[1] // width // 8) * 8
    flat = jax.ShapeDtypeStruct
    return pl.pallas_call(
        message_kernel,
        out_shape=[squares(n, width) for n in (4, 4, 2)]
        + [flat((4 * width + lines, width), F32), flat(shares[0].shape, F32)],
        in_specs=vmem(1 + len(shares)),
        out_specs=vmem(5),
        compiler_params=pltpu.CompilerParams(vmem_limit_bytes=LIMIT),
        cost_estimate=cost(total, total),
    )(total, *shares)


def coulomb_kernel(own, own_side, share, from_y, out, summed, passed):
    rows, half, width = own.shape
    odd = place_of_device()[3]
    lines = [from_y[4 * width + i:4 * width + i + 1, :] for i in range(share.shape[1] // width)]
    gathered = share[...] + jnp.concatenate(lines, axis=1)
    summed[...] = gathered
    passed[0] = from_y[3 * width:4 * width, :]
    low, high = gathered[:, :half], gathered[:, half:2 * half]
    gamma = jnp.where(odd == 1, high, low).astype(BF16)
    side_gamma = jnp.where(odd == 1, low, high).astype(BF16)
    for row in range(rows):
        part = jnp.dot(gamma, own[row], preferred_element_type=F32)
        out[row] = part + jnp.dot(side_gamma, own_side[row], preferred_element_type=F32)


def coulomb(own, own_side, share, from_y):
    rows, _, width = own.shape
    flat = jax.ShapeDtypeStruct
    out, summed, passed = pl.pallas_call(
        coulomb_kernel,
        out_shape=[flat((rows, 1, width), F32), flat(share.shape, F32), squares(1, width)],
        in_specs=vmem(4),
        out_specs=vmem(3),
        compiler_params=pltpu.CompilerParams(vmem_limit_bytes=LIMIT),
        cost_estimate=cost(own, own_side),
    )(own, own_side, share, from_y)
    return jnp.swapaxes(out, 0, 1), summed, passed


def band_kernel(aux, pairs, summed, own, total, from_y, from_near, from_far, from_mate, passed, band):
    depth, width = pairs.shape[1], band.shape[1]
    me, core, _, odd, _, _, _, f_near = place_of_device()
    sign, cross = 1 - 2 * odd, 1 - 2 * core

    def put(ahead, value):
        far = jnp.abs(ahead)
        lower = summed[0, aux + jnp.maximum(me - far, 0) * depth + far - 1] > 0.5
        upper = pairs[0, far - 1] == 1
        there = jnp.logical_or(jnp.logical_and(ahead > 0, upper), jnp.logical_and(ahead < 0, lower))
        band[depth + ahead] = jnp.where(there, value, 0.0)

    from_f = lambda i: jnp.where(f_near, from_far[i], from_near[i])
    from_g = lambda i: jnp.where(f_near, from_near[i], from_far[i])
    band[depth] = own[0]
    put(cross, own[1])
    put(2 * sign, total[6] + from_y[0 * width:0 * width + width, :])
    put(2 * sign + cross, from_mate[0] + from_y[1 * width:1 * width + width, :])
    put(-2 * sign, from_y[2 * width:2 * width + width, :] + from_f(2))
    put(-2 * sign + cross, passed[0] + from_f(3))
    put(4 * sign, total[0] + from_g(0))
    put(-4 * sign, total[4] + from_f(0))
    put(-3 * cross, from_mate[1] + from_f(1) + from_g(1))


def finish(aux, pairs, summed, own, *partials):
    depth, width = pairs.shape[1], own.shape[-1]
    return pl.pallas_call(
        functools.partial(band_kernel, aux),
        out_shape=squares(2 * depth + 1, width),
        in_specs=smem(2) + vmem(1 + len(partials)),
        out_specs=vmem(1)[0],
        compiler_params=pltpu.CompilerParams(vmem_limit_bytes=LIMIT),
        cost_estimate=cost(own, *partials),
    )(pairs, summed, own, *partials)


def add_kernel(*refs):
    refs[-1][...] = sum(share[...] for share in refs[:-1])


def added(shares):
    return pl.pallas_call(
        add_kernel,
        out_shape=jax.ShapeDtypeStruct(shares[0].shape, F32),
        in_specs=vmem(len(shares)),
        out_specs=vmem(1)[0],
        compiler_params=pltpu.CompilerParams(vmem_limit_bytes=LIMIT),
        cost_estimate=cost(*shares),
    )(*shares)


def shares_of(values, count, step, ways=2):
    every = [values]
    for way in range(1, ways):
        every.append(lax.ppermute(values, "basis", [(i, i ^ (step * way)) for i in range(count)]))
    return every


def per_device(factors, coefs, domains, pairs):
    own = factors[0]
    _, aux, _ = own.shape
    count = lax.axis_size("basis")

    swap = chip_route(count, lambda c: c, swap=True)
    across = chip_route(count, lambda c: c ^ 1)
    to_near = chip_route(count, lambda c: c ^ 2)
    to_far = chip_route(count, lambda c: c - 2 if c & 2 == 0 else c + 2)
    send = lambda value, route: lax.ppermute(value, "basis", route)

    xj_side, xj, for_near, for_far = cut(own)
    yj = send(xj_side, across)
    near, far = send(for_near, to_near), send(for_far, to_far)
    xo, xo_side = send(xj, swap), send(xj_side, swap)
    own_pairs, share, *tables = own_products(domains, pairs, xj, xo, xj_side, xo_side, coefs[0])
    share = added(shares_of(share, count, 1))
    y_low, y_high = relay(yj, share)
    yo, yo_high = send(y_low, swap), send(y_high, swap)
    shares, step = [share], 4
    while step < count:
        if len(shares) > 1:
            shares = [added(shares)]
        ways = 4 if 4 * step <= count else 2
        shares = shares_of(shares[0], count, step, ways)
        step *= ways
    total = shared_products(tables, xj, xo, xj_side, xo_side, yj, yo, yo_high, near, far)
    for_near, for_far, for_mate, for_y, share = messages(total, shares)
    from_y, from_near, from_far = send(for_y, across), send(for_near, to_near), send(for_far, to_far)
    from_mate = send(for_mate, swap)
    coulomb_half, summed, passed = coulomb(xj, xj_side, share, from_y)
    passed = send(passed, swap)
    band = finish(aux, pairs, summed, own_pairs, total, from_y, from_near, from_far, from_mate, passed)
    return (band[None], coulomb_half)


def solution(mesh):
    placed = (
        P(("groups", "basis"), None, None, None),
        P(("groups", "basis"), None, None),
        P("groups", None),
        P(("groups", "basis"), None),
    )
    return jax.shard_map(
        per_device,
        mesh=mesh,
        in_specs=placed,
        out_specs=(P(("groups", "basis"), None, None, None), P(("groups", "basis"), None, None)),
        check_vma=False,
    )
```

time: 78.5 us -> 72.8 us (0.927); the launches traced: 78.2 us -> 71.4 us
  starting transfers between devices: 21.3 us -> 15.1 us
  local copies, waits for them, and re-layouts: 4.13 us -> 2.12 us
  waiting for transfers between devices: 33.1 us -> 35.1 us
    ppermute x11 -> x12, waiting for transfers between devices: 28.6 us -> 34.3 us  [per_device(): send = lambda value, route: lax.ppermute(value, 'basis', route)]
    ppermute x11 -> x12, starting transfers between devices: 15 us -> 9.39 us  [per_device(): send = lambda value, route: lax.ppermute(value, 'basis', route)]
    ppermute x6 -> x4, waiting for transfers between devices: 4.49 us -> 0.83 us  [shares_of(): lax.ppermute(values, 'basis', [(i, i ^ step * way) for i in range(count)])]
    unnamed x11 -> x8, local copies, waits for them, and re-layouts: 4.13 us -> 2.12 us
    ppermute x6 -> x4, starting transfers between devices: 6.32 us -> 5.75 us  [shares_of(): lax.ppermute(values, 'basis', [(i, i ^ step * way) for i in range(count)])]
    pallas_call x2 -> x5, Pallas kernels: 6 us -> 5.73 us  [the longest x1 3.98 us: shared_products(): pl.pallas_call(shared_kernel, out_shape=squares(len(SHARED), blocks[0].sh...]
  transfers between devices with their start and end apart: 17 -> 16, of which waited for: 6 -> 5; matrix products, arithmetic and copies ran while one was open for 1% -> 0% of each run, Pallas kernels for 15% -> 22%
where the time goes in v3:
time: 72.8 us; the launch traced here: 71.4 us
  waiting for transfers between devices  35.1 us (48%)
  Pallas kernels  18.3 us (25%)
  starting transfers between devices  15.1 us (21%)
  local copies, waits for them, and re-layouts  2.12 us (3%)
  between operations  0.77 us (1%)
    ppermute x12, waiting for transfers between devices, per_device(): send = lambda value, route: lax.ppermute(value, 'basis', route)  34.3 us
    pallas_call x1, Pallas kernels, own_products(): pl.pallas_call(own_kernel, out_shape=[squares(2, width), jax.ShapeDtypeSt...  10.4 us
    ppermute x12, starting transfers between devices, per_device(): send = lambda value, route: lax.ppermute(value, 'basis', route)  9.39 us
    ppermute x4, starting transfers between devices, shares_of(): lax.ppermute(values, 'basis', [(i, i ^ step * way) for i in range(count)])  5.75 us
    pallas_call x1, Pallas kernels, shared_products(): pl.pallas_call(shared_kernel, out_shape=squares(len(SHARED), blocks[0].sh...  3.98 us
    unnamed x8, local copies, waits for them, and re-layouts  2.12 us
    pallas_call x1, Pallas kernels, finish(): pl.pallas_call(functools.partial(band_kernel, aux), out_shape=squares(2 *...  1.49 us
  transfers between devices with their start and end apart: 16, of which 5 were waited for; matrix products, arithmetic and copies ran while one was open for 0% of the time, Pallas kernels for 22%

profile of v3, /device:TPU:0, one launch (start us, length us, event | category | flops | bytes accessed | tf_op | source)
XLA Modules:
  0.0 71.4 jit_solution(5688770165062490333)
XLA Ops:
  0.6 2.1 %copy-done = bf16[1,30,512,128]{3,2,1,0:T(8,128)(2,1)S(1)} copy-done((bf16[1,30,512,128]{3,2,1,0:T(8,128)(2,1)S(1)}, bf16[1,30,512,128]{3,2,1,0:T(8,128)(2,1)}, u32[]{:S(2)}) %copy-start) | copy-done | bytes 3932184
  2.8 0.7 shard_map.59
  3.4 0.5 collective-permute-start
  4.0 2.9 %collective-permute-start.2 = (bf16[30,256,128]{2,1,0:T(8,128)(2,1)S(1)}, bf16[30,256,128]{2,1,0:T(8,128)(2,1)S(1)}, u32[]{:S(2)}, u32[]{:S(2)}) collective-permute-start(bf16[30,256,128]{2,1,0:T(8,128)(2,1)S(1)} %get-tuple-element.22.own_side.xj_side), channel_id=1, source_target_pairs={{0,2},{1,3},{2,0},{3,1},{4,6},{5,7},{6,4},{7,5},{8,10},{9,11},{10,... | collective-permute-start | bytes 5898248 | tf_op jit(solution)/shard_map/ppermute | solution.py:435
  7.0 1.6 %collective-permute-start.6 = (bf16[30,256,128]{2,1,0:T(8,128)(2,1)S(1)}, bf16[30,256,128]{2,1,0:T(8,128)(2,1)S(1)}, u32[]{:S(2)}, u32[]{:S(2)}) collective-permute-start(bf16[30,256,128]{2,1,0:T(8,128)(2,1)S(1)} %get-tuple-element.29), channel_id=1, source_target_pairs={{0,4},{1,5},{2,6},{3,7},{4,0},{5,1},{6,2},{7,3},{8,12},{9,13},{10,... | collective-permute-start | bytes 5898248 | tf_op jit(solution)/shard_map/ppermute | solution.py:435
  8.6 0.8 %collective-permute-start.7 = (bf16[30,256,128]{2,1,0:T(8,128)(2,1)S(1)}, bf16[30,256,128]{2,1,0:T(8,128)(2,1)S(1)}, u32[]{:S(2)}, u32[]{:S(2)}) collective-permute-start(bf16[30,256,128]{2,1,0:T(8,128)(2,1)S(1)} %get-tuple-element.30), channel_id=1, source_target_pairs={{4,8},{5,9},{6,10},{7,11},{8,4},{9,5},{10,6},{11,7},{20,24},{21,25... | collective-permute-start | bytes 5898248 | tf_op jit(solution)/shard_map/ppermute | solution.py:435
  9.3 1.0 %collective-permute-done.1.other_side.xo_side = bf16[30,256,128]{2,1,0:T(8,128)(2,1)S(1)} collective-permute-done((bf16[30,256,128]{2,1,0:T(8,128)(2,1)S(1)}, bf16[30,256,128]{2,1,0:T(8,128)(2,1)S(1)}, u32[]{:S(2)}, u32[]{:S(2)}) %collective-permute-start.1) | collective-permute-done | bytes 1966112 | tf_op jit(solution)/shard_map/ppermute | solution.py:435
  10.4 10.4 %shard_map.60 = (f32[2,128,128]{2,1,0:T(8,128)S(1)}, f32[1,640]{1,0:T(1,128)S(1)}, s32[9]{0:T(128)S(1)}, s32[9,36]{1,0:T(8,128)S(1)}, s32[9,36]{1,0:T(8,128)S(1)}) custom-call(s32[16,30]{1,0:T(8,128)S(1)} %copy-done.1, s32[1,4]{1,0:T(1,128)S(1)} %copy-done.3, bf16[30,256,128]{2,1,0:T(8,128)(2,1)S(1)} %get-tuple-element.21.own.xj, ...), custom_call_target="tpu_custom_call" | custom-call | flops 1 | bytes 7864320 | tf_op jit(solution)/shard_map/pallas_call | solution.py:192
  20.8 0.4 collective-permute-start.3
  21.2 0.8 %collective-permute-done.3.refs_1_ = f32[1,640]{1,0:T(1,128)S(1)} collective-permute-done((f32[1,640]{1,0:T(1,128)S(1)}, f32[1,640]{1,0:T(1,128)S(1)}, u32[]{:S(2)}, u32[]{:S(2)}) %collective-permute-start.3) | collective-permute-done | bytes 2592 | tf_op jit(solution)/shard_map/ppermute | solution.py:422
  22.1 28.0 %collective-permute-done.2.value.yj = bf16[30,256,128]{2,1,0:T(8,128)(2,1)S(1)} collective-permute-done((bf16[30,256,128]{2,1,0:T(8,128)(2,1)S(1)}, bf16[30,256,128]{2,1,0:T(8,128)(2,1)S(1)}, u32[]{:S(2)}, u32[]{:S(2)}) %collective-permute-start.2) | collective-permute-done | bytes 1966112 | tf_op jit(solution)/shard_map/ppermute | solution.py:435
  50.0 0.2 shard_map.62
  50.3 0.5 collective-permute-start.5
  50.8 3.8 %collective-permute-start.10 = (f32[1,640]{1,0:T(1,128)S(1)}, f32[1,640]{1,0:T(1,128)S(1)}, u32[]{:S(2)}, u32[]{:S(2)}) collective-permute-start(f32[1,640]{1,0:T(1,128)S(1)} %shard_map.61.token.refs_0_), channel_id=1, source_target_pairs={{0,12},{1,13},{2,14},{3,15},{4,8},{5,9},{6,10},{7,11},{8,4},{9,5},... | collective-permute-start | bytes 7688 | tf_op jit(solution)/shard_map/ppermute | solution.py:422
  54.6 1.5 %collective-permute-start.8 = (f32[1,640]{1,0:T(1,128)S(1)}, f32[1,640]{1,0:T(1,128)S(1)}, u32[]{:S(2)}, u32[]{:S(2)}) collective-permute-start(f32[1,640]{1,0:T(1,128)S(1)} %shard_map.61.token.refs_0_), channel_id=1, source_target_pairs={{0,4},{1,5},{2,6},{3,7},{4,0},{5,1},{6,2},{7,3},{8,12},{9,13},{10,... | collective-permute-start | bytes 7688 | tf_op jit(solution)/shard_map/ppermute | solution.py:422
  56.1 4.0 %shard_map.63.total = f32[8,128,128]{2,1,0:T(8,128)S(1)} custom-call(s32[9]{0:T(128)S(1)} %get-tuple-element.23.number, s32[9,36]{1,0:T(8,128)S(1)} %get-tuple-element.24.mine, s32[9,36]{1,0:T(8,128)S(1)} %get-tuple-element.25.theirs, bf16[30,256,128]{2,1,0:T(8,128)(2,1)S(1)} %get-tuple-element.21.own.xj, ...), custom_call_target="tpu_custom_call" | custom-call | flops 1 | bytes 15728640 | tf_op jit(solution)/shard_map/pallas_call | solution.py:282
  60.1 0.3 shard_map.64
  60.4 0.9 %collective-permute-start.11 = (f32[520,128]{1,0:T(8,128)S(1)}, f32[520,128]{1,0:T(8,128)S(1)}, u32[]{:S(2)}, u32[]{:S(2)}) collective-permute-start(f32[520,128]{1,0:T(8,128)S(1)} %get-tuple-element.32), channel_id=1, source_target_pairs={{0,2},{1,3},{2,0},{3,1},{4,6},{5,7},{6,4},{7,5},{8,10},{9,11},{10,... | collective-permute-start | bytes 798728 | tf_op jit(solution)/shard_map/ppermute | solution.py:435
  61.3 1.3 %collective-permute-start.12 = (f32[4,128,128]{2,1,0:T(8,128)S(1)}, f32[4,128,128]{2,1,0:T(8,128)S(1)}, u32[]{:S(2)}, u32[]{:S(2)}) collective-permute-start(f32[4,128,128]{2,1,0:T(8,128)S(1)} %get-tuple-element.35), channel_id=1, source_target_pairs={{0,4},{1,5},{2,6},{3,7},{4,0},{5,1},{6,2},{7,3},{8,12},{9,13},{10,... | collective-permute-start | bytes 786440 | tf_op jit(solution)/shard_map/ppermute | solution.py:435
  62.6 0.7 collective-permute-start.13
  63.4 4.0 %collective-permute-done.11.from_y = f32[520,128]{1,0:T(8,128)S(1)} collective-permute-done((f32[520,128]{1,0:T(8,128)S(1)}, f32[520,128]{1,0:T(8,128)S(1)}, u32[]{:S(2)}, u32[]{:S(2)}) %collective-permute-start.11) | collective-permute-done | bytes 266272 | tf_op jit(solution)/shard_map/ppermute | solution.py:435
  67.4 1.3 %shard_map.65 = (f32[30,1,128]{2,1,0:T(1,128)}, f32[1,640]{1,0:T(1,128)S(1)}, f32[1,128,128]{2,1,0:T(8,128)S(1)}) custom-call(bf16[30,256,128]{2,1,0:T(8,128)(2,1)S(1)} %get-tuple-element.21.own.xj, bf16[30,256,128]{2,1,0:T(8,128)(2,1)S(1)} %get-tuple-element.22.own_side.xj_side, f32[1,640]{1,0:T(1,128)S(1)} %get-tuple-element.31.share, ...), custom_call_target="tpu_custom_call" | custom-call | flops 1 | bytes 3932160 | tf_op jit(solution)/shard_map/pallas_call | solution.py:356
  68.7 1.2 %collective-permute-done.15.passed = f32[1,128,128]{2,1,0:T(8,128)S(1)} collective-permute-done((f32[1,128,128]{2,1,0:T(8,128)S(1)}, f32[1,128,128]{2,1,0:T(8,128)S(1)}, u32[]{:S(2)}, u32[]{:S(2)}) %collective-permute-start.15) | collective-permute-done | bytes 65568 | tf_op jit(solution)/shard_map/ppermute | solution.py:435
  69.9 1.5 %shard_map.66 = f32[9,128,128]{2,1,0:T(8,128)} custom-call(s32[1,4]{1,0:T(1,128)S(1)} %copy-done.3, f32[1,640]{1,0:T(1,128)S(1)} %get-tuple-element.33.summed, f32[2,128,128]{2,1,0:T(8,128)S(1)} %get-tuple-element.34.own, f32[8,128,128]{2,1,0:T(8,128)S(1)} %shard_map.63.total, f32[520,128]{1,0:T(8,128)S(1)} %collective-permute-done.11.from_y, ...), custom_call_target="tpu_custom_call" | custom-call | flops 1 | bytes 1642496 | tf_op jit(solution)/shard_map/pallas_call | solution.py:394
  (24 shorter events, 0.3 us)
Async XLA Ops:
  0.6 2.1 %copy-start = (bf16[1,30,512,128]{3,2,1,0:T(8,128)(2,1)S(1)}, bf16[1,30,512,128]{3,2,1,0:T(8,128)(2,1)}, u32[]{:S(2)}) copy-start(bf16[1,30,512,128]{3,2,1,0:T(8,128)(2,1)} %param.4) | copy-start | bytes 11796484
  2.7 7.6 %copy-start.1 = (s32[16,30]{1,0:T(8,128)S(1)}, s32[16,30]{1,0:T(8,128)}, u32[]{:S(2)}) copy-start(s32[16,30]{1,0:T(8,128)} %domains.1) | copy-start | bytes 5764
  2.7 7.6 %copy-start.2 = (bf16[1,30,128]{2,1,0:T(8,128)(2,1)S(1)}, bf16[1,30,128]{2,1,0:T(8,128)(2,1)}, u32[]{:S(2)}) copy-start(bf16[1,30,128]{2,1,0:T(8,128)(2,1)} %param.5) | copy-start | bytes 23044
  2.7 7.6 %copy-start.3 = (s32[1,4]{1,0:T(1,128)S(1)}, s32[1,4]{1,0:T(1,128)}, u32[]{:S(2)}) copy-start(s32[1,4]{1,0:T(1,128)} %pairs.3) | copy-start | bytes 52
  3.4 5.9 %collective-permute-start = (bf16[30,256,128]{2,1,0:T(8,128)(2,1)S(1)}, bf16[30,256,128]{2,1,0:T(8,128)(2,1)S(1)}, u32[]{:S(2)}, u32[]{:S(2)}) collective-permute-start(bf16[30,256,128]{2,1,0:T(8,128)(2,1)S(1)} %get-tuple-element.21.own.xj), channel_id=1, source_target_pairs={{0,1},{1,0},{2,3},{3,2},{4,5},{5,4},{6,7},{7,6},{8,9},{9,8},{10,11... | collective-permute-start | bytes 5898248 | tf_op jit(solution)/shard_map/ppermute | solution.py:435
  3.9 6.4 %collective-permute-start.1 = (bf16[30,256,128]{2,1,0:T(8,128)(2,1)S(1)}, bf16[30,256,128]{2,1,0:T(8,128)(2,1)S(1)}, u32[]{:S(2)}, u32[]{:S(2)}) collective-permute-start(bf16[30,256,128]{2,1,0:T(8,128)(2,1)S(1)} %get-tuple-element.22.own_side.xj_side), channel_id=1, source_target_pairs={{0,1},{1,0},{2,3},{3,2},{4,5},{5,4},{6,7},{7,6},{8,9},{9,8},{10,11... | collective-permute-start | bytes 5898248 | tf_op jit(solution)/shard_map/ppermute | solution.py:435
  4.0 46.0 %collective-permute-start.2 = (bf16[30,256,128]{2,1,0:T(8,128)(2,1)S(1)}, bf16[30,256,128]{2,1,0:T(8,128)(2,1)S(1)}, u32[]{:S(2)}, u32[]{:S(2)}) collective-permute-start(bf16[30,256,128]{2,1,0:T(8,128)(2,1)S(1)} %get-tuple-element.22.own_side.xj_side), channel_id=1, source_target_pairs={{0,2},{1,3},{2,0},{3,1},{4,6},{5,7},{6,4},{7,5},{8,10},{9,11},{10,... | collective-permute-start | bytes 5898248 | tf_op jit(solution)/shard_map/ppermute | solution.py:435
  7.0 47.7 %collective-permute-start.6 = (bf16[30,256,128]{2,1,0:T(8,128)(2,1)S(1)}, bf16[30,256,128]{2,1,0:T(8,128)(2,1)S(1)}, u32[]{:S(2)}, u32[]{:S(2)}) collective-permute-start(bf16[30,256,128]{2,1,0:T(8,128)(2,1)S(1)} %get-tuple-element.29), channel_id=1, source_target_pairs={{0,4},{1,5},{2,6},{3,7},{4,0},{5,1},{6,2},{7,3},{8,12},{9,13},{10,... | collective-permute-start | bytes 5898248 | tf_op jit(solution)/shard_map/ppermute | solution.py:435
  8.6 46.1 %collective-permute-start.7 = (bf16[30,256,128]{2,1,0:T(8,128)(2,1)S(1)}, bf16[30,256,128]{2,1,0:T(8,128)(2,1)S(1)}, u32[]{:S(2)}, u32[]{:S(2)}) collective-permute-start(bf16[30,256,128]{2,1,0:T(8,128)(2,1)S(1)} %get-tuple-element.30), channel_id=1, source_target_pairs={{4,8},{5,9},{6,10},{7,11},{8,4},{9,5},{10,6},{11,7},{20,24},{21,25... | collective-permute-start | bytes 5898248 | tf_op jit(solution)/shard_map/ppermute | solution.py:435
  20.8 1.3 %collective-permute-start.3 = (f32[1,640]{1,0:T(1,128)S(1)}, f32[1,640]{1,0:T(1,128)S(1)}, u32[]{:S(2)}, u32[]{:S(2)}) collective-permute-start(f32[1,640]{1,0:T(1,128)S(1)} %get-tuple-element.26.refs_0_), channel_id=1, source_target_pairs={{0,1},{1,0},{2,3},{3,2},{4,5},{5,4},{6,7},{7,6},{8,9},{9,8},{10,11... | collective-permute-start | bytes 7688 | tf_op jit(solution)/shard_map/ppermute | solution.py:422
  50.2 5.9 %collective-permute-start.4 = (bf16[30,128,128]{2,1,0:T(8,128)(2,1)S(1)}, bf16[30,128,128]{2,1,0:T(8,128)(2,1)S(1)}, u32[]{:S(2)}, u32[]{:S(2)}) collective-permute-start(bf16[30,128,128]{2,1,0:T(8,128)(2,1)S(1)} %get-tuple-element.27), channel_id=1, source_target_pairs={{0,1},{1,0},{2,3},{3,2},{4,5},{5,4},{6,7},{7,6},{8,9},{9,8},{10,11... | collective-permute-start | bytes 2949128 | tf_op jit(solution)/shard_map/ppermute | solution.py:435
  50.3 5.8 %collective-permute-start.5 = (bf16[30,128,128]{2,1,0:T(8,128)(2,1)S(1)}, bf16[30,128,128]{2,1,0:T(8,128)(2,1)S(1)}, u32[]{:S(2)}, u32[]{:S(2)}) collective-permute-start(bf16[30,128,128]{2,1,0:T(8,128)(2,1)S(1)} %get-tuple-element.28), channel_id=1, source_target_pairs={{0,1},{1,0},{2,3},{3,2},{4,5},{5,4},{6,7},{7,6},{8,9},{9,8},{10,11... | collective-permute-start | bytes 2949128 | tf_op jit(solution)/shard_map/ppermute | solution.py:435
  50.8 9.3 %collective-permute-start.10 = (f32[1,640]{1,0:T(1,128)S(1)}, f32[1,640]{1,0:T(1,128)S(1)}, u32[]{:S(2)}, u32[]{:S(2)}) collective-permute-start(f32[1,640]{1,0:T(1,128)S(1)} %shard_map.61.token.refs_0_), channel_id=1, source_target_pairs={{0,12},{1,13},{2,14},{3,15},{4,8},{5,9},{6,10},{7,11},{8,4},{9,5},... | collective-permute-start | bytes 7688 | tf_op jit(solution)/shard_map/ppermute | solution.py:422
  54.6 5.5 %collective-permute-start.9 = (f32[1,640]{1,0:T(1,128)S(1)}, f32[1,640]{1,0:T(1,128)S(1)}, u32[]{:S(2)}, u32[]{:S(2)}) collective-permute-start(f32[1,640]{1,0:T(1,128)S(1)} %shard_map.61.token.refs_0_), channel_id=1, source_target_pairs={{0,8},{1,9},{2,10},{3,11},{4,12},{5,13},{6,14},{7,15},{8,0},{9,1},... | collective-permute-start | bytes 7688 | tf_op jit(solution)/shard_map/ppermute | solution.py:422
  54.6 5.5 %collective-permute-start.8 = (f32[1,640]{1,0:T(1,128)S(1)}, f32[1,640]{1,0:T(1,128)S(1)}, u32[]{:S(2)}, u32[]{:S(2)}) collective-permute-start(f32[1,640]{1,0:T(1,128)S(1)} %shard_map.61.token.refs_0_), channel_id=1, source_target_pairs={{0,4},{1,5},{2,6},{3,7},{4,0},{5,1},{6,2},{7,3},{8,12},{9,13},{10,... | collective-permute-start | bytes 7688 | tf_op jit(solution)/shard_map/ppermute | solution.py:422
  60.4 7.0 %collective-permute-start.11 = (f32[520,128]{1,0:T(8,128)S(1)}, f32[520,128]{1,0:T(8,128)S(1)}, u32[]{:S(2)}, u32[]{:S(2)}) collective-permute-start(f32[520,128]{1,0:T(8,128)S(1)} %get-tuple-element.32), channel_id=1, source_target_pairs={{0,2},{1,3},{2,0},{3,1},{4,6},{5,7},{6,4},{7,5},{8,10},{9,11},{10,... | collective-permute-start | bytes 798728 | tf_op jit(solution)/shard_map/ppermute | solution.py:435
  61.3 7.4 %collective-permute-start.12 = (f32[4,128,128]{2,1,0:T(8,128)S(1)}, f32[4,128,128]{2,1,0:T(8,128)S(1)}, u32[]{:S(2)}, u32[]{:S(2)}) collective-permute-start(f32[4,128,128]{2,1,0:T(8,128)S(1)} %get-tuple-element.35), channel_id=1, source_target_pairs={{0,4},{1,5},{2,6},{3,7},{4,0},{5,1},{6,2},{7,3},{8,12},{9,13},{10,... | collective-permute-start | bytes 786440 | tf_op jit(solution)/shard_map/ppermute | solution.py:435
  62.6 6.1 %collective-permute-start.13 = (f32[4,128,128]{2,1,0:T(8,128)S(1)}, f32[4,128,128]{2,1,0:T(8,128)S(1)}, u32[]{:S(2)}, u32[]{:S(2)}) collective-permute-start(f32[4,128,128]{2,1,0:T(8,128)S(1)} %get-tuple-element.36), channel_id=1, source_target_pairs={{4,8},{5,9},{6,10},{7,11},{8,4},{9,5},{10,6},{11,7},{20,24},{21,25... | collective-permute-start | bytes 786440 | tf_op jit(solution)/shard_map/ppermute | solution.py:435
  63.3 5.4 %collective-permute-start.14 = (f32[2,128,128]{2,1,0:T(8,128)S(1)}, f32[2,128,128]{2,1,0:T(8,128)S(1)}, u32[]{:S(2)}, u32[]{:S(2)}) collective-permute-start(f32[2,128,128]{2,1,0:T(8,128)S(1)} %get-tuple-element.37), channel_id=1, source_target_pairs={{0,1},{1,0},{2,3},{3,2},{4,5},{5,4},{6,7},{7,6},{8,9},{9,8},{10,11... | collective-permute-start | bytes 393224 | tf_op jit(solution)/shard_map/ppermute | solution.py:435
  68.7 1.3 %collective-permute-start.15 = (f32[1,128,128]{2,1,0:T(8,128)S(1)}, f32[1,128,128]{2,1,0:T(8,128)S(1)}, u32[]{:S(2)}, u32[]{:S(2)}) collective-permute-start(f32[1,128,128]{2,1,0:T(8,128)S(1)} %get-tuple-element.38), channel_id=1, source_target_pairs={{0,1},{1,0},{2,3},{3,2},{4,5},{5,4},{6,7},{7,6},{8,9},{9,8},{10,11... | collective-permute-start | bytes 196616 | tf_op jit(solution)/shard_map/ppermute | solution.py:435

commit v4 on v3

--- a/solution.py
+++ b/solution.py
@@ -16,7 +16,7 @@
     (XJ, YJ), (XO, YJ), (XJ, FJ), (YJ, FJ), (YO, FJ), (XO, FJ), (XJ_SIDE, GJ), (XO_SIDE, GJ), (XJ, XO)
 )
 SHARED = (XF, CROSS_F, YF, YOF, XG, CROSS_G, XY, XYO)
-STACK, OWN_STACK = 9, 4
+STACK, OWN_STACK = 20, 4
 LIMIT = 12 * 2**20
 
 
@@ -296,10 +296,10 @@
 
     def to_f_and_g(to_f, to_g):
         for i in range(4):
-            to_f[i] = total[i].T
+            to_f[i] = total[i].T.astype(BF16)
         for i in range(2):
-            to_g[i] = total[4 + i].T
-            to_g[2 + i] = jnp.zeros_like(total[i])
+            to_g[i] = total[4 + i].T.astype(BF16)
+            to_g[2 + i] = jnp.zeros(to_g.shape[1:], BF16)
 
     @pl.when(f_near)
     def _():
@@ -312,22 +312,27 @@
     to_mate[0] = total[7]
     to_mate[1] = total[1] + total[5]
     for i, value in enumerate((total[6].T, total[7].T, total[2], total[3])):
-        to_y[i * width:(i + 1) * width, :] = value
+        to_y[i * width:(i + 1) * width, :] = value.astype(BF16)
     gathered = sum(share[...] for share in shares)
     summed[...] = gathered
-    to_y[4 * width:, :] = jnp.zeros((to_y.shape[0] - 4 * width, width), F32)
-    for i in range(gathered.shape[1] // width):
-        to_y[4 * width + i:4 * width + i + 1, :] = gathered[:, i * width:(i + 1) * width]
+    lines = gathered.shape[1] // width
+    rest, rows = gathered, []
+    for _ in range(3):
+        part = rest.astype(BF16)
+        rest = rest - part.astype(F32)
+        rows += [part[:, i * width:(i + 1) * width].astype(F32) for i in range(lines)]
+    rows.append(jnp.zeros((to_y.shape[0] - 4 * width - 3 * lines, width), F32))
+    to_y[4 * width:, :] = jnp.concatenate(rows, axis=0).astype(BF16)
 
 
 def messages(total, shares):
     width = total.shape[-1]
-    lines = -(-shares[0].shape[1] // width // 8) * 8
+    lines = -(-3 * shares[0].shape[1] // width // 16) * 16
     flat = jax.ShapeDtypeStruct
     return pl.pallas_call(
         message_kernel,
-        out_shape=[squares(n, width) for n in (4, 4, 2)]
-        + [flat((4 * width + lines, width), F32), flat(shares[0].shape, F32)],
+        out_shape=[flat((4, width, width), BF16)] * 2
+        + [squares(2, width), flat((4 * width + lines, width), BF16), flat(shares[0].shape, F32)],
         in_specs=vmem(1 + len(shares)),
         out_specs=vmem(5),
         compiler_params=pltpu.CompilerParams(vmem_limit_bytes=LIMIT),
@@ -335,13 +340,14 @@
     )(total, *shares)
 
 
-def coulomb_kernel(own, own_side, share, from_y, out, summed, passed):
+def coulomb_kernel(own, own_side, share, from_y, out, summed):
     rows, half, width = own.shape
     odd = place_of_device()[3]
-    lines = [from_y[4 * width + i:4 * width + i + 1, :] for i in range(share.shape[1] // width)]
-    gathered = share[...] + jnp.concatenate(lines, axis=1)
+    lines = share.shape[1] // width
+    parts = from_y[4 * width:, :].astype(F32)
+    line = lambda i: jnp.concatenate([parts[i * lines + j:i * lines + j + 1] for j in range(lines)], axis=1)
+    gathered = share[...] + (line(0) + line(1) + line(2))
     summed[...] = gathered
-    passed[0] = from_y[3 * width:4 * width, :]
     low, high = gathered[:, :half], gathered[:, half:2 * half]
     gamma = jnp.where(odd == 1, high, low).astype(BF16)
     side_gamma = jnp.where(odd == 1, low, high).astype(BF16)
@@ -353,20 +359,21 @@
 def coulomb(own, own_side, share, from_y):
     rows, _, width = own.shape
     flat = jax.ShapeDtypeStruct
-    out, summed, passed = pl.pallas_call(
+    out, summed = pl.pallas_call(
         coulomb_kernel,
-        out_shape=[flat((rows, 1, width), F32), flat(share.shape, F32), squares(1, width)],
+        out_shape=[flat((rows, 1, width), F32), flat(share.shape, F32)],
         in_specs=vmem(4),
-        out_specs=vmem(3),
+        out_specs=vmem(2),
         compiler_params=pltpu.CompilerParams(vmem_limit_bytes=LIMIT),
         cost_estimate=cost(own, own_side),
     )(own, own_side, share, from_y)
-    return jnp.swapaxes(out, 0, 1), summed, passed
+    return jnp.swapaxes(out, 0, 1), summed
 
 
 def band_kernel(aux, pairs, summed, own, total, from_y, from_near, from_far, from_mate, passed, band):
     depth, width = pairs.shape[1], band.shape[1]
     me, core, _, odd, _, _, _, f_near = place_of_device()
+    count = lax.axis_size("basis")
     sign, cross = 1 - 2 * odd, 1 - 2 * core
 
     def put(ahead, value):
@@ -374,16 +381,18 @@
         lower = summed[0, aux + jnp.maximum(me - far, 0) * depth + far - 1] > 0.5
         upper = pairs[0, far - 1] == 1
         there = jnp.logical_or(jnp.logical_and(ahead > 0, upper), jnp.logical_and(ahead < 0, lower))
+        there = jnp.logical_and(there, jnp.logical_and(me + ahead >= 0, me + ahead < count))
         band[depth + ahead] = jnp.where(there, value, 0.0)
 
-    from_f = lambda i: jnp.where(f_near, from_far[i], from_near[i])
-    from_g = lambda i: jnp.where(f_near, from_near[i], from_far[i])
+    from_f = lambda i: jnp.where(f_near, from_far[i].astype(F32), from_near[i].astype(F32))
+    from_g = lambda i: jnp.where(f_near, from_near[i].astype(F32), from_far[i].astype(F32))
+    y_block = lambda i: from_y[i * width:(i + 1) * width, :].astype(F32)
     band[depth] = own[0]
     put(cross, own[1])
-    put(2 * sign, total[6] + from_y[0 * width:0 * width + width, :])
-    put(2 * sign + cross, from_mate[0] + from_y[1 * width:1 * width + width, :])
-    put(-2 * sign, from_y[2 * width:2 * width + width, :] + from_f(2))
-    put(-2 * sign + cross, passed[0] + from_f(3))
+    put(2 * sign, total[6] + y_block(0))
+    put(2 * sign + cross, from_mate[0] + y_block(1))
+    put(-2 * sign, y_block(2) + from_f(2))
+    put(-2 * sign + cross, passed[...].astype(F32) + from_f(3))
     put(4 * sign, total[0] + from_g(0))
     put(-4 * sign, total[4] + from_f(0))
     put(-3 * cross, from_mate[1] + from_f(1) + from_g(1))
@@ -432,6 +441,8 @@
     across = chip_route(count, lambda c: c ^ 1)
     to_near = chip_route(count, lambda c: c ^ 2)
     to_far = chip_route(count, lambda c: c - 2 if c & 2 == 0 else c + 2)
+    senders = {source for source, _ in to_far}
+    to_far += [(i, i ^ 1) for i in range(count) if i not in senders]
     send = lambda value, route: lax.ppermute(value, "basis", route)
 
     xj_side, xj, for_near, for_far = cut(own)
@@ -453,8 +464,9 @@
     for_near, for_far, for_mate, for_y, share = messages(total, shares)
     from_y, from_near, from_far = send(for_y, across), send(for_near, to_near), send(for_far, to_far)
     from_mate = send(for_mate, swap)
-    coulomb_half, summed, passed = coulomb(xj, xj_side, share, from_y)
-    passed = send(passed, swap)
+    width = own.shape[2]
+    passed = send(from_y[3 * width:4 * width], swap)
+    coulomb_half, summed = coulomb(xj, xj_side, share, from_y)
     band = finish(aux, pairs, summed, own_pairs, total, from_y, from_near, from_far, from_mate, passed)
     return (band[None], coulomb_half)
 

time: 72.8 us -> 68.2 us (0.937); the launches traced: 71.4 us -> 67.9 us
  waiting for transfers between devices: 35.1 us -> 32.3 us
  starting transfers between devices: 15.1 us -> 14.2 us
    ppermute x12, waiting for transfers between devices: 34.3 us -> 31.5 us  [per_device(): send = lambda value, route: lax.ppermute(value, 'basis', route)]
  transfers between devices with their start and end apart: 16 -> 16, of which waited for: 5 -> 4; matrix products, arithmetic and copies ran while one was open for 0% -> 0% of each run, Pallas kernels for 22% -> 24%
where the time goes in v4:
time: 68.2 us; the launch traced here: 67.9 us
  waiting for transfers between devices  32.3 us (47%)
  Pallas kernels  18.6 us (27%)
  starting transfers between devices  14.2 us (21%)
  local copies, waits for them, and re-layouts  2.12 us (3%)
  between operations  0.74 us (1%)
    ppermute x12, waiting for transfers between devices, per_device(): send = lambda value, route: lax.ppermute(value, 'basis', route)  31.5 us
    pallas_call x1, Pallas kernels, own_products(): pl.pallas_call(own_kernel, out_shape=[squares(2, width), jax.ShapeDtypeSt...  10.7 us
    ppermute x12, starting transfers between devices, per_device(): send = lambda value, route: lax.ppermute(value, 'basis', route)  8.86 us
    ppermute x4, starting transfers between devices, shares_of(): lax.ppermute(values, 'basis', [(i, i ^ step * way) for i in range(count)])  5.3 us
    pallas_call x1, Pallas kernels, shared_products(): pl.pallas_call(shared_kernel, out_shape=squares(len(SHARED), blocks[0].sh...  4.08 us
    unnamed x8, local copies, waits for them, and re-layouts  2.12 us
    pallas_call x1, Pallas kernels, finish(): pl.pallas_call(functools.partial(band_kernel, aux), out_shape=squares(2 *...  1.52 us
  transfers between devices with their start and end apart: 16, of which 4 were waited for; matrix products, arithmetic and copies ran while one was open for 0% of the time, Pallas kernels for 24%

profile of v4, /device:TPU:0, one launch (start us, length us, event | category | flops | bytes accessed | tf_op | source)
XLA Modules:
  0.0 67.9 jit_solution(11840952400517116037)
XLA Ops:
  0.6 2.1 %copy-done = bf16[1,30,512,128]{3,2,1,0:T(8,128)(2,1)S(1)} copy-done((bf16[1,30,512,128]{3,2,1,0:T(8,128)(2,1)S(1)}, bf16[1,30,512,128]{3,2,1,0:T(8,128)(2,1)}, u32[]{:S(2)}) %copy-start) | copy-done | bytes 3932184
  2.8 0.7 shard_map.59
  3.4 0.5 collective-permute-start
  3.9 0.1 collective-permute-start.1
  4.0 2.9 %collective-permute-start.2 = (bf16[30,256,128]{2,1,0:T(8,128)(2,1)S(1)}, bf16[30,256,128]{2,1,0:T(8,128)(2,1)S(1)}, u32[]{:S(2)}, u32[]{:S(2)}) collective-permute-start(bf16[30,256,128]{2,1,0:T(8,128)(2,1)S(1)} %get-tuple-element.21.own_side.xj_side), channel_id=1, source_target_pairs={{0,2},{1,3},{2,0},{3,1},{4,6},{5,7},{6,4},{7,5},{8,10},{9,11},{10,... | collective-permute-start | bytes 5898248 | tf_op jit(solution)/shard_map/ppermute | solution.py:446
  7.0 1.6 %collective-permute-start.6 = (bf16[30,256,128]{2,1,0:T(8,128)(2,1)S(1)}, bf16[30,256,128]{2,1,0:T(8,128)(2,1)S(1)}, u32[]{:S(2)}, u32[]{:S(2)}) collective-permute-start(bf16[30,256,128]{2,1,0:T(8,128)(2,1)S(1)} %get-tuple-element.28), channel_id=1, source_target_pairs={{0,4},{1,5},{2,6},{3,7},{4,0},{5,1},{6,2},{7,3},{8,12},{9,13},{10,... | collective-permute-start | bytes 5898248 | tf_op jit(solution)/shard_map/ppermute | solution.py:446
  8.6 1.8 %collective-permute-done.1.other_side.xo_side = bf16[30,256,128]{2,1,0:T(8,128)(2,1)S(1)} collective-permute-done((bf16[30,256,128]{2,1,0:T(8,128)(2,1)S(1)}, bf16[30,256,128]{2,1,0:T(8,128)(2,1)S(1)}, u32[]{:S(2)}, u32[]{:S(2)}) %collective-permute-start.1) | collective-permute-done | bytes 1966112 | tf_op jit(solution)/shard_map/ppermute | solution.py:446
  10.4 10.7 %shard_map.60 = (f32[2,128,128]{2,1,0:T(8,128)S(1)}, f32[1,640]{1,0:T(1,128)S(1)}, s32[9]{0:T(128)S(1)}, s32[9,40]{1,0:T(8,128)S(1)}, s32[9,40]{1,0:T(8,128)S(1)}) custom-call(s32[16,30]{1,0:T(8,128)S(1)} %copy-done.1, s32[1,4]{1,0:T(1,128)S(1)} %copy-done.3, bf16[30,256,128]{2,1,0:T(8,128)(2,1)S(1)} %get-tuple-element.20.own.xj, ...), custom_call_target="tpu_custom_call" | custom-call | flops 1 | bytes 7864320 | tf_op jit(solution)/shard_map/pallas_call | solution.py:192
  21.0 0.4 collective-permute-start.3
  21.5 0.8 %collective-permute-done.3.refs_1_ = f32[1,640]{1,0:T(1,128)S(1)} collective-permute-done((f32[1,640]{1,0:T(1,128)S(1)}, f32[1,640]{1,0:T(1,128)S(1)}, u32[]{:S(2)}, u32[]{:S(2)}) %collective-permute-start.3) | collective-permute-done | bytes 2592 | tf_op jit(solution)/shard_map/ppermute | solution.py:431
  22.3 27.7 %collective-permute-done.2.value.yj = bf16[30,256,128]{2,1,0:T(8,128)(2,1)S(1)} collective-permute-done((bf16[30,256,128]{2,1,0:T(8,128)(2,1)S(1)}, bf16[30,256,128]{2,1,0:T(8,128)(2,1)S(1)}, u32[]{:S(2)}, u32[]{:S(2)}) %collective-permute-start.2) | collective-permute-done | bytes 1966112 | tf_op jit(solution)/shard_map/ppermute | solution.py:446
  50.0 0.2 shard_map.62
  50.2 0.1 collective-permute-start.4
  50.3 0.5 collective-permute-start.5
  50.8 3.8 %collective-permute-start.10 = (f32[1,640]{1,0:T(1,128)S(1)}, f32[1,640]{1,0:T(1,128)S(1)}, u32[]{:S(2)}, u32[]{:S(2)}) collective-permute-start(f32[1,640]{1,0:T(1,128)S(1)} %shard_map.61.token.refs_0_), channel_id=1, source_target_pairs={{0,12},{1,13},{2,14},{3,15},{4,8},{5,9},{6,10},{7,11},{8,4},{9,5},... | collective-permute-start | bytes 7688 | tf_op jit(solution)/shard_map/ppermute | solution.py:431
  54.6 1.0 %collective-permute-start.8 = (f32[1,640]{1,0:T(1,128)S(1)}, f32[1,640]{1,0:T(1,128)S(1)}, u32[]{:S(2)}, u32[]{:S(2)}) collective-permute-start(f32[1,640]{1,0:T(1,128)S(1)} %shard_map.61.token.refs_0_), channel_id=1, source_target_pairs={{0,4},{1,5},{2,6},{3,7},{4,0},{5,1},{6,2},{7,3},{8,12},{9,13},{10,... | collective-permute-start | bytes 7688 | tf_op jit(solution)/shard_map/ppermute | solution.py:431
  55.7 4.1 %shard_map.63.total = f32[8,128,128]{2,1,0:T(8,128)S(1)} custom-call(s32[9]{0:T(128)S(1)} %get-tuple-element.22.number, s32[9,40]{1,0:T(8,128)S(1)} %get-tuple-element.23.mine, s32[9,40]{1,0:T(8,128)S(1)} %get-tuple-element.24.theirs, bf16[30,256,128]{2,1,0:T(8,128)(2,1)S(1)} %get-tuple-element.20.own.xj, ...), custom_call_target="tpu_custom_call" | custom-call | flops 1 | bytes 15728640 | tf_op jit(solution)/shard_map/pallas_call | solution.py:282
  59.8 0.2 shard_map.64
  60.0 1.3 %collective-permute-start.11 = (bf16[528,128]{1,0:T(8,128)(2,1)S(1)}, bf16[528,128]{1,0:T(8,128)(2,1)S(1)}, u32[]{:S(2)}, u32[]{:S(2)}) collective-permute-start(bf16[528,128]{1,0:T(8,128)(2,1)S(1)} %get-tuple-element.31), channel_id=1, source_target_pairs={{0,2},{1,3},{2,0},{3,1},{4,6},{5,7},{6,4},{7,5},{8,10},{9,11},{10,... | collective-permute-start | bytes 405512 | tf_op jit(solution)/shard_map/ppermute | solution.py:446
  61.4 1.3 %collective-permute-start.12 = (bf16[4,128,128]{2,1,0:T(8,128)(2,1)S(1)}, bf16[4,128,128]{2,1,0:T(8,128)(2,1)S(1)}, u32[]{:S(2)}, u32[]{:S(2)}) collective-permute-start(bf16[4,128,128]{2,1,0:T(8,128)(2,1)S(1)} %get-tuple-element.34), channel_id=1, source_target_pairs={{0,4},{1,5},{2,6},{3,7},{4,0},{5,1},{6,2},{7,3},{8,12},{9,13},{10,... | collective-permute-start | bytes 393224 | tf_op jit(solution)/shard_map/ppermute | solution.py:446
  62.7 0.5 collective-permute-start.14
  63.2 1.9 %collective-permute-done.11.from_y = bf16[528,128]{1,0:T(8,128)(2,1)S(1)} collective-permute-done((bf16[528,128]{1,0:T(8,128)(2,1)S(1)}, bf16[528,128]{1,0:T(8,128)(2,1)S(1)}, u32[]{:S(2)}, u32[]{:S(2)}) %collective-permute-start.11) | collective-permute-done | bytes 135200 | tf_op jit(solution)/shard_map/ppermute | solution.py:446
  65.1 1.3 %shard_map.65 = (f32[30,1,128]{2,1,0:T(1,128)}, f32[1,640]{1,0:T(1,128)S(1)}) custom-call(bf16[30,256,128]{2,1,0:T(8,128)(2,1)S(1)} %get-tuple-element.20.own.xj, bf16[30,256,128]{2,1,0:T(8,128)(2,1)S(1)} %get-tuple-element.21.own_side.xj_side, f32[1,640]{1,0:T(1,128)S(1)} %get-tuple-element.30.share, bf16[528,128]{1,0:T(8,128)(2,1)S(1)} %collective-permute-done.11.from_y), custom_call_target="tpu_custom_call" | custom-call | flops 1 | bytes 3932160 | tf_op jit(solution)/shard_map/pallas_call | solution.py:362
  66.4 1.5 %shard_map.66 = f32[9,128,128]{2,1,0:T(8,128)} custom-call(s32[1,4]{1,0:T(1,128)S(1)} %copy-done.3, f32[1,640]{1,0:T(1,128)S(1)} %get-tuple-element.32.summed, f32[2,128,128]{2,1,0:T(8,128)S(1)} %get-tuple-element.33.own, f32[8,128,128]{2,1,0:T(8,128)S(1)} %shard_map.63.total, bf16[528,128]{1,0:T(8,128)(2,1)S(1)} %collective-permute-done.11.from_y, ...), custom_call_target="tpu_custom_call" | custom-call | flops 1 | bytes 1216512 | tf_op jit(solution)/shard_map/pallas_call | solution.py:403
  (25 shorter events, 0.1 us)
Async XLA Ops:
  0.6 2.1 %copy-start = (bf16[1,30,512,128]{3,2,1,0:T(8,128)(2,1)S(1)}, bf16[1,30,512,128]{3,2,1,0:T(8,128)(2,1)}, u32[]{:S(2)}) copy-start(bf16[1,30,512,128]{3,2,1,0:T(8,128)(2,1)} %param.4) | copy-start | bytes 11796484
  2.7 7.6 %copy-start.1 = (s32[16,30]{1,0:T(8,128)S(1)}, s32[16,30]{1,0:T(8,128)}, u32[]{:S(2)}) copy-start(s32[16,30]{1,0:T(8,128)} %domains.1) | copy-start | bytes 5764
  2.7 7.6 %copy-start.2 = (bf16[1,30,128]{2,1,0:T(8,128)(2,1)S(1)}, bf16[1,30,128]{2,1,0:T(8,128)(2,1)}, u32[]{:S(2)}) copy-start(bf16[1,30,128]{2,1,0:T(8,128)(2,1)} %param.5) | copy-start | bytes 23044
  2.7 7.6 %copy-start.3 = (s32[1,4]{1,0:T(1,128)S(1)}, s32[1,4]{1,0:T(1,128)}, u32[]{:S(2)}) copy-start(s32[1,4]{1,0:T(1,128)} %pairs.3) | copy-start | bytes 52
  3.4 5.1 %collective-permute-start = (bf16[30,256,128]{2,1,0:T(8,128)(2,1)S(1)}, bf16[30,256,128]{2,1,0:T(8,128)(2,1)S(1)}, u32[]{:S(2)}, u32[]{:S(2)}) collective-permute-start(bf16[30,256,128]{2,1,0:T(8,128)(2,1)S(1)} %get-tuple-element.20.own.xj), channel_id=1, source_target_pairs={{0,1},{1,0},{2,3},{3,2},{4,5},{5,4},{6,7},{7,6},{8,9},{9,8},{10,11... | collective-permute-start | bytes 5898248 | tf_op jit(solution)/shard_map/ppermute | solution.py:446
  3.9 6.4 %collective-permute-start.1 = (bf16[30,256,128]{2,1,0:T(8,128)(2,1)S(1)}, bf16[30,256,128]{2,1,0:T(8,128)(2,1)S(1)}, u32[]{:S(2)}, u32[]{:S(2)}) collective-permute-start(bf16[30,256,128]{2,1,0:T(8,128)(2,1)S(1)} %get-tuple-element.21.own_side.xj_side), channel_id=1, source_target_pairs={{0,1},{1,0},{2,3},{3,2},{4,5},{5,4},{6,7},{7,6},{8,9},{9,8},{10,11... | collective-permute-start | bytes 5898248 | tf_op jit(solution)/shard_map/ppermute | solution.py:446
  4.0 46.0 %collective-permute-start.2 = (bf16[30,256,128]{2,1,0:T(8,128)(2,1)S(1)}, bf16[30,256,128]{2,1,0:T(8,128)(2,1)S(1)}, u32[]{:S(2)}, u32[]{:S(2)}) collective-permute-start(bf16[30,256,128]{2,1,0:T(8,128)(2,1)S(1)} %get-tuple-element.21.own_side.xj_side), channel_id=1, source_target_pairs={{0,2},{1,3},{2,0},{3,1},{4,6},{5,7},{6,4},{7,5},{8,10},{9,11},{10,... | collective-permute-start | bytes 5898248 | tf_op jit(solution)/shard_map/ppermute | solution.py:446
  7.0 47.7 %collective-permute-start.6 = (bf16[30,256,128]{2,1,0:T(8,128)(2,1)S(1)}, bf16[30,256,128]{2,1,0:T(8,128)(2,1)S(1)}, u32[]{:S(2)}, u32[]{:S(2)}) collective-permute-start(bf16[30,256,128]{2,1,0:T(8,128)(2,1)S(1)} %get-tuple-element.28), channel_id=1, source_target_pairs={{0,4},{1,5},{2,6},{3,7},{4,0},{5,1},{6,2},{7,3},{8,12},{9,13},{10,... | collective-permute-start | bytes 5898248 | tf_op jit(solution)/shard_map/ppermute | solution.py:446
  8.6 46.1 %collective-permute-start.7 = (bf16[30,256,128]{2,1,0:T(8,128)(2,1)S(1)}, bf16[30,256,128]{2,1,0:T(8,128)(2,1)S(1)}, u32[]{:S(2)}, u32[]{:S(2)}) collective-permute-start(bf16[30,256,128]{2,1,0:T(8,128)(2,1)S(1)} %get-tuple-element.29), channel_id=1, source_target_pairs={{4,8},{5,9},{6,10},{7,11},{8,4},{9,5},{10,6},{11,7},{0,1},{1,0},{2... | collective-permute-start | bytes 5898248 | tf_op jit(solution)/shard_map/ppermute | solution.py:446
  21.0 1.3 %collective-permute-start.3 = (f32[1,640]{1,0:T(1,128)S(1)}, f32[1,640]{1,0:T(1,128)S(1)}, u32[]{:S(2)}, u32[]{:S(2)}) collective-permute-start(f32[1,640]{1,0:T(1,128)S(1)} %get-tuple-element.25.refs_0_), channel_id=1, source_target_pairs={{0,1},{1,0},{2,3},{3,2},{4,5},{5,4},{6,7},{7,6},{8,9},{9,8},{10,11... | collective-permute-start | bytes 7688 | tf_op jit(solution)/shard_map/ppermute | solution.py:431
  50.2 5.4 %collective-permute-start.4 = (bf16[30,128,128]{2,1,0:T(8,128)(2,1)S(1)}, bf16[30,128,128]{2,1,0:T(8,128)(2,1)S(1)}, u32[]{:S(2)}, u32[]{:S(2)}) collective-permute-start(bf16[30,128,128]{2,1,0:T(8,128)(2,1)S(1)} %get-tuple-element.26), channel_id=1, source_target_pairs={{0,1},{1,0},{2,3},{3,2},{4,5},{5,4},{6,7},{7,6},{8,9},{9,8},{10,11... | collective-permute-start | bytes 2949128 | tf_op jit(solution)/shard_map/ppermute | solution.py:446
  50.3 5.4 %collective-permute-start.5 = (bf16[30,128,128]{2,1,0:T(8,128)(2,1)S(1)}, bf16[30,128,128]{2,1,0:T(8,128)(2,1)S(1)}, u32[]{:S(2)}, u32[]{:S(2)}) collective-permute-start(bf16[30,128,128]{2,1,0:T(8,128)(2,1)S(1)} %get-tuple-element.27), channel_id=1, source_target_pairs={{0,1},{1,0},{2,3},{3,2},{4,5},{5,4},{6,7},{7,6},{8,9},{9,8},{10,11... | collective-permute-start | bytes 2949128 | tf_op jit(solution)/shard_map/ppermute | solution.py:446
  50.8 9.0 %collective-permute-start.10 = (f32[1,640]{1,0:T(1,128)S(1)}, f32[1,640]{1,0:T(1,128)S(1)}, u32[]{:S(2)}, u32[]{:S(2)}) collective-permute-start(f32[1,640]{1,0:T(1,128)S(1)} %shard_map.61.token.refs_0_), channel_id=1, source_target_pairs={{0,12},{1,13},{2,14},{3,15},{4,8},{5,9},{6,10},{7,11},{8,4},{9,5},... | collective-permute-start | bytes 7688 | tf_op jit(solution)/shard_map/ppermute | solution.py:431
  54.6 5.1 %collective-permute-start.9 = (f32[1,640]{1,0:T(1,128)S(1)}, f32[1,640]{1,0:T(1,128)S(1)}, u32[]{:S(2)}, u32[]{:S(2)}) collective-permute-start(f32[1,640]{1,0:T(1,128)S(1)} %shard_map.61.token.refs_0_), channel_id=1, source_target_pairs={{0,8},{1,9},{2,10},{3,11},{4,12},{5,13},{6,14},{7,15},{8,0},{9,1},... | collective-permute-start | bytes 7688 | tf_op jit(solution)/shard_map/ppermute | solution.py:431
  54.6 5.1 %collective-permute-start.8 = (f32[1,640]{1,0:T(1,128)S(1)}, f32[1,640]{1,0:T(1,128)S(1)}, u32[]{:S(2)}, u32[]{:S(2)}) collective-permute-start(f32[1,640]{1,0:T(1,128)S(1)} %shard_map.61.token.refs_0_), channel_id=1, source_target_pairs={{0,4},{1,5},{2,6},{3,7},{4,0},{5,1},{6,2},{7,3},{8,12},{9,13},{10,... | collective-permute-start | bytes 7688 | tf_op jit(solution)/shard_map/ppermute | solution.py:431
  60.0 5.1 %collective-permute-start.11 = (bf16[528,128]{1,0:T(8,128)(2,1)S(1)}, bf16[528,128]{1,0:T(8,128)(2,1)S(1)}, u32[]{:S(2)}, u32[]{:S(2)}) collective-permute-start(bf16[528,128]{1,0:T(8,128)(2,1)S(1)} %get-tuple-element.31), channel_id=1, source_target_pairs={{0,2},{1,3},{2,0},{3,1},{4,6},{5,7},{6,4},{7,5},{8,10},{9,11},{10,... | collective-permute-start | bytes 405512 | tf_op jit(solution)/shard_map/ppermute | solution.py:446
  61.4 5.0 %collective-permute-start.12 = (bf16[4,128,128]{2,1,0:T(8,128)(2,1)S(1)}, bf16[4,128,128]{2,1,0:T(8,128)(2,1)S(1)}, u32[]{:S(2)}, u32[]{:S(2)}) collective-permute-start(bf16[4,128,128]{2,1,0:T(8,128)(2,1)S(1)} %get-tuple-element.34), channel_id=1, source_target_pairs={{0,4},{1,5},{2,6},{3,7},{4,0},{5,1},{6,2},{7,3},{8,12},{9,13},{10,... | collective-permute-start | bytes 393224 | tf_op jit(solution)/shard_map/ppermute | solution.py:446
  62.7 3.7 %collective-permute-start.13 = (bf16[4,128,128]{2,1,0:T(8,128)(2,1)S(1)}, bf16[4,128,128]{2,1,0:T(8,128)(2,1)S(1)}, u32[]{:S(2)}, u32[]{:S(2)}) collective-permute-start(bf16[4,128,128]{2,1,0:T(8,128)(2,1)S(1)} %get-tuple-element.35), channel_id=1, source_target_pairs={{4,8},{5,9},{6,10},{7,11},{8,4},{9,5},{10,6},{11,7},{0,1},{1,0},{2... | collective-permute-start | bytes 393224 | tf_op jit(solution)/shard_map/ppermute | solution.py:446
  62.7 3.7 %collective-permute-start.14 = (f32[2,128,128]{2,1,0:T(8,128)S(1)}, f32[2,128,128]{2,1,0:T(8,128)S(1)}, u32[]{:S(2)}, u32[]{:S(2)}) collective-permute-start(f32[2,128,128]{2,1,0:T(8,128)S(1)} %get-tuple-element.36), channel_id=1, source_target_pairs={{0,1},{1,0},{2,3},{3,2},{4,5},{5,4},{6,7},{7,6},{8,9},{9,8},{10,11... | collective-permute-start | bytes 393224 | tf_op jit(solution)/shard_map/ppermute | solution.py:446
  65.1 1.3 %collective-permute-start.15 = (bf16[128,128]{1,0:T(8,128)(2,1)S(1)}, bf16[128,128]{1,0:T(8,128)(2,1)S(1)}, u32[]{:S(2)}, u32[]{:S(2)}) collective-permute-start(bf16[128,128]{1,0:T(8,128)(2,1)S(1)} %slice.4), channel_id=1, source_target_pairs={{0,1},{1,0},{2,3},{3,2},{4,5},{5,4},{6,7},{7,6},{8,9},{9,8},{10,11... | collective-permute-start | bytes 98312 | tf_op jit(solution)/shard_map/ppermute | solution.py:446

commit v5 on v4

--- a/solution.py
+++ b/solution.py
@@ -10,13 +10,11 @@
 F32 = jnp.float32
 BF16 = jnp.bfloat16
 
-XJ, XO, XJ_SIDE, XO_SIDE, YJ, YO, YO_HIGH, FJ, GJ = range(9)
-XY, XYO, XF, YF, YOF, CROSS_F, XG, CROSS_G, OWN = range(9)
-PRODUCTS = (
-    (XJ, YJ), (XO, YJ), (XJ, FJ), (YJ, FJ), (YO, FJ), (XO, FJ), (XJ_SIDE, GJ), (XO_SIDE, GJ), (XJ, XO)
-)
-SHARED = (XF, CROSS_F, YF, YOF, XG, CROSS_G, XY, XYO)
-STACK, OWN_STACK = 20, 4
+XJ, XO, XJ_SIDE, YJ, YO, YO_HIGH, FJ, GJ = range(8)
+XF, YF, YOF, XG, XY, XYO, CROSS, OWN = range(8)
+PRODUCTS = ((XJ, FJ), (YJ, FJ), (YO, FJ), (XJ_SIDE, GJ), (XJ, YJ), (XO, YJ), (XO, None), (XJ, XO))
+SHARED = (XF, YF, YOF, XG, XY, XYO, CROSS)
+STACK, OWN_STACK = 10, 4
 LIMIT = 12 * 2**20
 
 
@@ -93,7 +91,7 @@
     width = mine.shape[1]
     _, core, chip, _, flag, f_chip, g_chip, _ = place_of_device()
     mine_first, other_first = (chip, core), (chip, 1 - core)
-    block = {XJ: mine_first, XJ_SIDE: mine_first, XO: other_first, XO_SIDE: other_first}
+    block = {XJ: mine_first, XJ_SIDE: mine_first, XO: other_first, None: (jnp.where(flag, f_chip, g_chip), core)}
     block |= {YJ: (chip ^ 1, core), YO: (chip ^ 1, 1 - core), FJ: (f_chip, core), GJ: (g_chip, core)}
 
     for q, (left, right) in enumerate(PRODUCTS):
@@ -103,8 +101,6 @@
             there.append(jnp.logical_and(at >= 0, 2 * at < count))
             ids.append(2 * jnp.clip(at, 0, count // 2 - 1) + one)
         both = jnp.logical_and(*there)
-        if q in (CROSS_F, CROSS_G):
-            both = jnp.logical_and(both, flag if q == CROSS_F else jnp.logical_not(flag))
         base = 2 * ids[1]
 
         def clear(i, carry):
@@ -135,7 +131,7 @@
         number[q] = lax.fori_loop(0, rows, scan, 0, unroll=5)
 
 
-def own_kernel(domains, pairs, own, other, own_side, other_side, coef, out, share, number, mine, theirs, spot):
+def own_kernel(domains, pairs, own, own_side, other, coef, out, share, number, mine, theirs, spot):
     rows, half, width = own.shape
     me, _, _, odd, _, _, _, _ = place_of_device()
     find_matches(domains, number, mine, theirs, spot)
@@ -154,10 +150,10 @@
         lefts, rights = [], []
         for i in range(OWN_STACK):
             slot = OWN_STACK * step + i
-            for part, other_part in ((own, other), (own_side, other_side)):
+            for part, start in ((own, odd * half), (own_side, (1 - odd) * half)):
                 left = part[mine[OWN, slot]]
                 lefts.append(jnp.where(slot < number[OWN], left, jnp.zeros_like(left)))
-                rights.append(other_part[theirs[OWN, slot]])
+                rights.append(other[theirs[OWN, slot], pl.ds(pl.multiple_of(start, 16), half), :])
         out[1] += multiply(jnp.concatenate(lefts, axis=0), jnp.concatenate(rights, axis=0))
         return carry
 
@@ -183,7 +179,7 @@
     share[:, 2 * half:] = marks
 
 
-def own_products(domains, pairs, own, other, own_side, other_side, coef):
+def own_products(domains, pairs, own, own_side, other, coef):
     rows, half, width = own.shape
     count = domains.shape[0]
     marks = -(-count * pairs.shape[1] // 128) * 128
@@ -198,12 +194,12 @@
             table,
             table,
         ],
-        in_specs=smem(2) + vmem(5),
+        in_specs=smem(2) + vmem(4),
         out_specs=vmem(2) + smem(3),
         scratch_shapes=[pltpu.SMEM((2 * rows,), jnp.int32)],
         compiler_params=pltpu.CompilerParams(vmem_limit_bytes=LIMIT),
-        cost_estimate=cost(own, other, own_side, other_side),
-    )(domains, pairs, own, other, own_side, other_side, coef)
+        cost_estimate=cost(own, own_side, other),
+    )(domains, pairs, own, own_side, other, coef)
 
 
 def relay_kernel(value, token, low, high, sems):
@@ -232,42 +228,44 @@
     )(value, token)
 
 
-def add_products(listed, tables, block, total):
-    number, mine, theirs = tables
-
-    def add(at, q, group):
+def shared_kernel(number, mine, theirs, xj, xj_side, xo, yj, yo, yo_high, near, far, total):
+    _, _, _, odd, flag, _, _, f_near = place_of_device()
+    half = xj.shape[1]
+    main = pl.ds(pl.multiple_of(odd * half, 16), half)
+    cross = pl.ds(pl.multiple_of(jnp.where(flag, odd, 1 - odd) * half, 16), half)
+
+    def product(q, group, block):
         lefts, rights = [], []
         left_block, right_block = PRODUCTS[q]
         for i in range(STACK):
             slot = group * STACK + i
             row, other_row = mine[q, slot], theirs[q, slot]
-            left = block[left_block][row]
-            if left_block == YO:
-                left = jnp.concatenate([left, block[YO_HIGH][row]], axis=0)
+            if left_block == XO:
+                left = xo[row, cross if q == CROSS else main, :]
+            elif left_block == YO:
+                left = jnp.concatenate([yo[row], yo_high[row]], axis=0)
+            else:
+                left = block[left_block][row]
             lefts.append(jnp.where(slot < number[q], left, jnp.zeros_like(left)))
-            rights.append(block[right_block][other_row])
-        total[at] += multiply(jnp.concatenate(lefts, axis=0), jnp.concatenate(rights, axis=0))
-
-    most = number[listed[0]]
-    for q in listed:
-        most = jnp.maximum(most, number[q])
-
-    def step(group, carry):
-        for at, q in enumerate(listed):
-            add(at, q, group)
-        return carry
-
-    lax.fori_loop(0, (most + STACK - 1) // STACK, step, 0)
-
-
-def shared_kernel(number, mine, theirs, xj, xo, xj_side, xo_side, yj, yo, yo_high, near, far, total):
-    f_near = place_of_device()[-1]
-    total[...] = jnp.zeros_like(total)
+            if q == CROSS:
+                rights.append(jnp.where(flag, block[FJ][other_row], block[GJ][other_row]))
+            else:
+                rights.append(block[right_block][other_row])
+        return multiply(jnp.concatenate(lefts, axis=0), jnp.concatenate(rights, axis=0))
 
     def all_products(fj, gj):
-        block = {XJ: xj, XO: xo, XJ_SIDE: xj_side, XO_SIDE: xo_side, YJ: yj, YO: yo, YO_HIGH: yo_high}
-        block |= {FJ: fj, GJ: gj}
-        add_products(SHARED, (number, mine, theirs), block, total)
+        block = {XJ: xj, XJ_SIDE: xj_side, YJ: yj, FJ: fj, GJ: gj}
+        most = number[SHARED[0]]
+        for at, q in enumerate(SHARED):
+            most = jnp.maximum(most, number[q])
+            total[at] = product(q, 0, block)
+
+        def step(group, carry):
+            for at, q in enumerate(SHARED):
+                total[at] += product(q, group, block)
+            return carry
+
+        lax.fori_loop(1, (most + STACK - 1) // STACK, step, 0)
 
     @pl.when(f_near)
     def _():
@@ -291,15 +289,17 @@
 
 def message_kernel(total, *refs):
     shares, (to_near, to_far, to_mate, to_y, summed) = refs[:-5], refs[-5:]
-    f_near = place_of_device()[-1]
+    _, _, _, _, flag, _, _, f_near = place_of_device()
     width = total.shape[1]
 
     def to_f_and_g(to_f, to_g):
-        for i in range(4):
-            to_f[i] = total[i].T.astype(BF16)
-        for i in range(2):
-            to_g[i] = total[4 + i].T.astype(BF16)
-            to_g[2 + i] = jnp.zeros(to_g.shape[1:], BF16)
+        cross = total[CROSS].T
+        nothing = jnp.zeros_like(cross)
+        from_total = (total[XF].T, jnp.where(flag, cross, nothing), total[YF].T, total[YOF].T)
+        for i, value in enumerate(from_total):
+            to_f[i] = value.astype(BF16)
+        for i, value in enumerate((total[XG].T, jnp.where(flag, nothing, cross), nothing, nothing)):
+            to_g[i] = value.astype(BF16)
 
     @pl.when(f_near)
     def _():
@@ -309,9 +309,9 @@
     def _():
         to_f_and_g(to_far, to_near)
 
-    to_mate[0] = total[7]
-    to_mate[1] = total[1] + total[5]
-    for i, value in enumerate((total[6].T, total[7].T, total[2], total[3])):
+    to_mate[0] = total[XYO]
+    to_mate[1] = total[CROSS]
+    for i, value in enumerate((total[XY].T, total[XYO].T, total[YF], total[YOF])):
         to_y[i * width:(i + 1) * width, :] = value.astype(BF16)
     gathered = sum(share[...] for share in shares)
     summed[...] = gathered
@@ -370,41 +370,52 @@
     return jnp.swapaxes(out, 0, 1), summed
 
 
-def band_kernel(aux, pairs, summed, own, total, from_y, from_near, from_far, from_mate, passed, band):
+def band_kernel(aux, pairs, summed, own, total, from_y, from_near, from_far, from_mate, passed, band, made, sems):
     depth, width = pairs.shape[1], band.shape[1]
     me, core, _, odd, _, _, _, f_near = place_of_device()
     count = lax.axis_size("basis")
     sign, cross = 1 - 2 * odd, 1 - 2 * core
+    copies = []
 
     def put(ahead, value):
         far = jnp.abs(ahead)
-        lower = summed[0, aux + jnp.maximum(me - far, 0) * depth + far - 1] > 0.5
-        upper = pairs[0, far - 1] == 1
-        there = jnp.logical_or(jnp.logical_and(ahead > 0, upper), jnp.logical_and(ahead < 0, lower))
-        there = jnp.logical_and(there, jnp.logical_and(me + ahead >= 0, me + ahead < count))
-        band[depth + ahead] = jnp.where(there, value, 0.0)
+        slot = len(copies)
+        if slot == 0:
+            made[slot] = value
+        else:
+            lower = summed[0, aux + jnp.maximum(me - far, 0) * depth + far - 1] > 0.5
+            upper = pairs[0, far - 1] == 1
+            there = jnp.logical_or(jnp.logical_and(ahead > 0, upper), jnp.logical_and(ahead < 0, lower))
+            there = jnp.logical_and(there, jnp.logical_and(me + ahead >= 0, me + ahead < count))
+            made[slot] = jnp.where(there, value, 0.0)
+        copies.append(pltpu.make_async_copy(made.at[slot], band.at[depth + ahead], sems.at[slot]))
+        copies[-1].start()
 
     from_f = lambda i: jnp.where(f_near, from_far[i].astype(F32), from_near[i].astype(F32))
     from_g = lambda i: jnp.where(f_near, from_near[i].astype(F32), from_far[i].astype(F32))
     y_block = lambda i: from_y[i * width:(i + 1) * width, :].astype(F32)
-    band[depth] = own[0]
+    put(0, own[0])
     put(cross, own[1])
-    put(2 * sign, total[6] + y_block(0))
+    put(2 * sign, total[XY] + y_block(0))
     put(2 * sign + cross, from_mate[0] + y_block(1))
     put(-2 * sign, y_block(2) + from_f(2))
     put(-2 * sign + cross, passed[...].astype(F32) + from_f(3))
-    put(4 * sign, total[0] + from_g(0))
-    put(-4 * sign, total[4] + from_f(0))
+    put(4 * sign, total[XF] + from_g(0))
+    put(-4 * sign, total[XG] + from_f(0))
     put(-3 * cross, from_mate[1] + from_f(1) + from_g(1))
+    for copy in copies:
+        copy.wait()
 
 
 def finish(aux, pairs, summed, own, *partials):
     depth, width = pairs.shape[1], own.shape[-1]
+    size = 2 * depth + 1
     return pl.pallas_call(
         functools.partial(band_kernel, aux),
-        out_shape=squares(2 * depth + 1, width),
+        out_shape=squares(size, width),
         in_specs=smem(2) + vmem(1 + len(partials)),
-        out_specs=vmem(1)[0],
+        out_specs=pl.BlockSpec(memory_space=pl.ANY),
+        scratch_shapes=[pltpu.VMEM((size, width, width), F32), pltpu.SemaphoreType.DMA((size,))],
         compiler_params=pltpu.CompilerParams(vmem_limit_bytes=LIMIT),
         cost_estimate=cost(own, *partials),
     )(pairs, summed, own, *partials)
@@ -445,11 +456,11 @@
     to_far += [(i, i ^ 1) for i in range(count) if i not in senders]
     send = lambda value, route: lax.ppermute(value, "basis", route)
 
+    xo = send(own, swap)
     xj_side, xj, for_near, for_far = cut(own)
     yj = send(xj_side, across)
     near, far = send(for_near, to_near), send(for_far, to_far)
-    xo, xo_side = send(xj, swap), send(xj_side, swap)
-    own_pairs, share, *tables = own_products(domains, pairs, xj, xo, xj_side, xo_side, coefs[0])
+    own_pairs, share, *tables = own_products(domains, pairs, xj, xj_side, xo, coefs[0])
     share = added(shares_of(share, count, 1))
     y_low, y_high = relay(yj, share)
     yo, yo_high = send(y_low, swap), send(y_high, swap)
@@ -460,7 +471,7 @@
         ways = 4 if 4 * step <= count else 2
         shares = shares_of(shares[0], count, step, ways)
         step *= ways
-    total = shared_products(tables, xj, xo, xj_side, xo_side, yj, yo, yo_high, near, far)
+    total = shared_products(tables, xj, xj_side, xo, yj, yo, yo_high, near, far)
     for_near, for_far, for_mate, for_y, share = messages(total, shares)
     from_y, from_near, from_far = send(for_y, across), send(for_near, to_near), send(for_far, to_far)
     from_mate = send(for_mate, swap)

time: 68.2 us -> 67.8 us (level)
  Pallas kernels: 18.6 us -> 16.6 us
  waiting for transfers between devices: 32.3 us -> 34.3 us
    ppermute x12 -> x11, waiting for transfers between devices: 31.5 us -> 33.4 us  [per_device(): send = lambda value, route: lax.ppermute(value, 'basis', route)]
    pallas_call x1, Pallas kernels: 10.7 us -> 8.95 us  [own_products(): pl.pallas_call(own_kernel, out_shape=[squares(2, width), jax.ShapeDtypeSt...]
    ppermute x12 -> x11, starting transfers between devices: 8.86 us -> 8.44 us  [per_device(): send = lambda value, route: lax.ppermute(value, 'basis', route)]
  transfers between devices with their start and end apart: 16 -> 15, of which waited for: 4 -> 3; matrix products, arithmetic and copies ran while one was open for 0% -> 0% of each run, Pallas kernels for 24% -> 22%
where the time goes in v5:
time: 67.8 us; the launch traced here: 67.6 us
  waiting for transfers between devices  34.3 us (51%)
  Pallas kernels  16.6 us (24%)
  starting transfers between devices  13.8 us (20%)
  local copies, waits for them, and re-layouts  2.13 us (3%)
  between operations  0.75 us (1%)
    ppermute x11, waiting for transfers between devices, per_device(): send = lambda value, route: lax.ppermute(value, 'basis', route)  33.4 us
    pallas_call x1, Pallas kernels, own_products(): pl.pallas_call(own_kernel, out_shape=[squares(2, width), jax.ShapeDtypeSt...  8.95 us
    ppermute x11, starting transfers between devices, per_device(): send = lambda value, route: lax.ppermute(value, 'basis', route)  8.44 us
    ppermute x4, starting transfers between devices, shares_of(): lax.ppermute(values, 'basis', [(i, i ^ step * way) for i in range(count)])  5.39 us
    pallas_call x1, Pallas kernels, shared_products(): pl.pallas_call(shared_kernel, out_shape=squares(len(SHARED), blocks[0].sh...  3.78 us
    unnamed x8, local copies, waits for them, and re-layouts  2.12 us
    pallas_call x1, Pallas kernels, finish(): pl.pallas_call(functools.partial(band_kernel, aux), out_shape=squares(siz...  1.47 us
  transfers between devices with their start and end apart: 15, of which 3 were waited for; matrix products, arithmetic and copies ran while one was open for 0% of the time, Pallas kernels for 22%

profile of v5, /device:TPU:0, one launch (start us, length us, event | category | flops | bytes accessed | tf_op | source)
XLA Modules:
  0.0 67.6 jit_solution(7222425490401214420)
XLA Ops:
  0.6 0.5 collective-permute-start
  1.2 2.1 %copy-done = bf16[1,30,512,128]{3,2,1,0:T(8,128)(2,1)S(1)} copy-done((bf16[1,30,512,128]{3,2,1,0:T(8,128)(2,1)S(1)}, bf16[1,30,512,128]{3,2,1,0:T(8,128)(2,1)}, u32[]{:S(2)}) %copy-start) | copy-done | bytes 3932184
  3.3 0.7 %shard_map.59 = (bf16[30,256,128]{2,1,0:T(8,128)(2,1)S(1)}, bf16[30,256,128]{2,1,0:T(8,128)(2,1)S(1)}, bf16[30,256,128]{2,1,0:T(8,128)(2,1)S(1)}, bf16[30,256,128]{2,1,0:T(8,128)(2,1)S(1)}) custom-call(bf16[30,512,128]{2,1,0:T(8,128)(2,1)S(1)} %bitcast.5), custom_call_target="tpu_custom_call" | custom-call | flops 1 | bytes 7864320 | tf_op jit(solution)/shard_map/pallas_call | solution.py:78
  4.0 2.6 %collective-permute-start.1 = (bf16[30,256,128]{2,1,0:T(8,128)(2,1)S(1)}, bf16[30,256,128]{2,1,0:T(8,128)(2,1)S(1)}, u32[]{:S(2)}, u32[]{:S(2)}) collective-permute-start(bf16[30,256,128]{2,1,0:T(8,128)(2,1)S(1)} %get-tuple-element.21.own_side.xj_side), channel_id=1, source_target_pairs={{0,2},{1,3},{2,0},{3,1},{4,6},{5,7},{6,4},{7,5},{8,10},{9,11},{10,... | collective-permute-start | bytes 5898248 | tf_op jit(solution)/shard_map/ppermute | solution.py:457
  6.5 1.6 %collective-permute-start.5 = (bf16[30,256,128]{2,1,0:T(8,128)(2,1)S(1)}, bf16[30,256,128]{2,1,0:T(8,128)(2,1)S(1)}, u32[]{:S(2)}, u32[]{:S(2)}) collective-permute-start(bf16[30,256,128]{2,1,0:T(8,128)(2,1)S(1)} %get-tuple-element.28), channel_id=1, source_target_pairs={{0,4},{1,5},{2,6},{3,7},{4,0},{5,1},{6,2},{7,3},{8,12},{9,13},{10,... | collective-permute-start | bytes 5898248 | tf_op jit(solution)/shard_map/ppermute | solution.py:457
  8.2 8.9 %shard_map.60 = (f32[2,128,128]{2,1,0:T(8,128)S(1)}, f32[1,640]{1,0:T(1,128)S(1)}, s32[8]{0:T(128)S(1)}, s32[8,32]{1,0:T(8,128)S(1)}, s32[8,32]{1,0:T(8,128)S(1)}) custom-call(s32[16,30]{1,0:T(8,128)S(1)} %copy-done.1, s32[1,4]{1,0:T(1,128)S(1)} %copy-done.3, bf16[30,256,128]{2,1,0:T(8,128)(2,1)S(1)} %get-tuple-element.20.own.xj, ...), custom_call_target="tpu_custom_call" | custom-call | flops 1 | bytes 7864320 | tf_op jit(solution)/shard_map/pallas_call | solution.py:188
  17.1 0.6 collective-permute-start.2
  17.7 0.8 %collective-permute-done.2.refs_1_ = f32[1,640]{1,0:T(1,128)S(1)} collective-permute-done((f32[1,640]{1,0:T(1,128)S(1)}, f32[1,640]{1,0:T(1,128)S(1)}, u32[]{:S(2)}, u32[]{:S(2)}) %collective-permute-start.2) | collective-permute-done | bytes 2592 | tf_op jit(solution)/shard_map/ppermute | solution.py:442
  18.5 31.5 %collective-permute-done.1.value.yj = bf16[30,256,128]{2,1,0:T(8,128)(2,1)S(1)} collective-permute-done((bf16[30,256,128]{2,1,0:T(8,128)(2,1)S(1)}, bf16[30,256,128]{2,1,0:T(8,128)(2,1)S(1)}, u32[]{:S(2)}, u32[]{:S(2)}) %collective-permute-start.1) | collective-permute-done | bytes 1966112 | tf_op jit(solution)/shard_map/ppermute | solution.py:457
  50.0 0.2 shard_map.62
  50.2 0.1 collective-permute-start.3
  50.3 0.5 collective-permute-start.4
  50.8 3.8 %collective-permute-start.9 = (f32[1,640]{1,0:T(1,128)S(1)}, f32[1,640]{1,0:T(1,128)S(1)}, u32[]{:S(2)}, u32[]{:S(2)}) collective-permute-start(f32[1,640]{1,0:T(1,128)S(1)} %shard_map.61.token.refs_0_), channel_id=1, source_target_pairs={{0,12},{1,13},{2,14},{3,15},{4,8},{5,9},{6,10},{7,11},{8,4},{9,5},... | collective-permute-start | bytes 7688 | tf_op jit(solution)/shard_map/ppermute | solution.py:442
  54.6 0.0 collective-permute-start.8
  54.7 0.0 collective-permute-done.6.far
  54.7 1.0 %collective-permute-start.7 = (f32[1,640]{1,0:T(1,128)S(1)}, f32[1,640]{1,0:T(1,128)S(1)}, u32[]{:S(2)}, u32[]{:S(2)}) collective-permute-start(f32[1,640]{1,0:T(1,128)S(1)} %shard_map.61.token.refs_0_), channel_id=1, source_target_pairs={{0,4},{1,5},{2,6},{3,7},{4,0},{5,1},{6,2},{7,3},{8,12},{9,13},{10,... | collective-permute-start | bytes 7688 | tf_op jit(solution)/shard_map/ppermute | solution.py:442
  55.7 3.8 %shard_map.63.total = f32[7,128,128]{2,1,0:T(8,128)S(1)} custom-call(s32[8]{0:T(128)S(1)} %get-tuple-element.22.number, s32[8,32]{1,0:T(8,128)S(1)} %get-tuple-element.23.mine, s32[8,32]{1,0:T(8,128)S(1)} %get-tuple-element.24.theirs, bf16[30,256,128]{2,1,0:T(8,128)(2,1)S(1)} %get-tuple-element.20.own.xj, ...), custom_call_target="tpu_custom_call" | custom-call | flops 1 | bytes 15728640 | tf_op jit(solution)/shard_map/pallas_call | solution.py:280
  59.5 0.2 shard_map.64
  59.7 1.4 %collective-permute-start.10 = (bf16[528,128]{1,0:T(8,128)(2,1)S(1)}, bf16[528,128]{1,0:T(8,128)(2,1)S(1)}, u32[]{:S(2)}, u32[]{:S(2)}) collective-permute-start(bf16[528,128]{1,0:T(8,128)(2,1)S(1)} %get-tuple-element.31), channel_id=1, source_target_pairs={{0,2},{1,3},{2,0},{3,1},{4,6},{5,7},{6,4},{7,5},{8,10},{9,11},{10,... | collective-permute-start | bytes 405512 | tf_op jit(solution)/shard_map/ppermute | solution.py:457
  61.1 1.3 %collective-permute-start.11 = (bf16[4,128,128]{2,1,0:T(8,128)(2,1)S(1)}, bf16[4,128,128]{2,1,0:T(8,128)(2,1)S(1)}, u32[]{:S(2)}, u32[]{:S(2)}) collective-permute-start(bf16[4,128,128]{2,1,0:T(8,128)(2,1)S(1)} %get-tuple-element.34), channel_id=1, source_target_pairs={{0,4},{1,5},{2,6},{3,7},{4,0},{5,1},{6,2},{7,3},{8,12},{9,13},{10,... | collective-permute-start | bytes 393224 | tf_op jit(solution)/shard_map/ppermute | solution.py:457
  62.4 0.5 collective-permute-start.13
  62.9 1.9 %collective-permute-done.10.from_y = bf16[528,128]{1,0:T(8,128)(2,1)S(1)} collective-permute-done((bf16[528,128]{1,0:T(8,128)(2,1)S(1)}, bf16[528,128]{1,0:T(8,128)(2,1)S(1)}, u32[]{:S(2)}, u32[]{:S(2)}) %collective-permute-start.10) | collective-permute-done | bytes 135200 | tf_op jit(solution)/shard_map/ppermute | solution.py:457
  64.8 1.3 %shard_map.65 = (f32[30,1,128]{2,1,0:T(1,128)}, f32[1,640]{1,0:T(1,128)S(1)}) custom-call(bf16[30,256,128]{2,1,0:T(8,128)(2,1)S(1)} %get-tuple-element.20.own.xj, bf16[30,256,128]{2,1,0:T(8,128)(2,1)S(1)} %get-tuple-element.21.own_side.xj_side, f32[1,640]{1,0:T(1,128)S(1)} %get-tuple-element.30.share, bf16[528,128]{1,0:T(8,128)(2,1)S(1)} %collective-permute-done.10.from_y), custom_call_target="tpu_custom_call" | custom-call | flops 1 | bytes 3932160 | tf_op jit(solution)/shard_map/pallas_call | solution.py:362
  66.1 1.5 %shard_map.66 = f32[9,128,128]{2,1,0:T(8,128)} custom-call(s32[1,4]{1,0:T(1,128)S(1)} %copy-done.3, f32[1,640]{1,0:T(1,128)S(1)} %get-tuple-element.32.summed, f32[2,128,128]{2,1,0:T(8,128)S(1)} %get-tuple-element.33.own, f32[7,128,128]{2,1,0:T(8,128)S(1)} %shard_map.63.total, bf16[528,128]{1,0:T(8,128)(2,1)S(1)} %collective-permute-done.10.from_y, ...), custom_call_target="tpu_custom_call" | custom-call | flops 1 | bytes 1150976 | tf_op jit(solution)/shard_map/pallas_call | solution.py:413
  (23 shorter events, 0.1 us)
Async XLA Ops:
  0.6 7.5 %collective-permute-start = (bf16[30,512,128]{2,1,0:T(8,128)(2,1)}, bf16[30,512,128]{2,1,0:T(8,128)(2,1)S(1)}, u32[]{:S(2)}, u32[]{:S(2)}) collective-permute-start(bf16[30,512,128]{2,1,0:T(8,128)(2,1)} %bitcast.4), channel_id=1, source_target_pairs={{0,1},{1,0},{2,3},{3,2},{4,5},{5,4},{6,7},{7,6},{8,9},{9,8},{10,11... | collective-permute-start | bytes 11796488 | tf_op jit(solution)/shard_map/ppermute | solution.py:457
  1.1 2.1 %copy-start = (bf16[1,30,512,128]{3,2,1,0:T(8,128)(2,1)S(1)}, bf16[1,30,512,128]{3,2,1,0:T(8,128)(2,1)}, u32[]{:S(2)}) copy-start(bf16[1,30,512,128]{3,2,1,0:T(8,128)(2,1)} %param.4) | copy-start | bytes 11796484
  3.3 4.9 %copy-start.1 = (s32[16,30]{1,0:T(8,128)S(1)}, s32[16,30]{1,0:T(8,128)}, u32[]{:S(2)}) copy-start(s32[16,30]{1,0:T(8,128)} %domains.1) | copy-start | bytes 5764
  3.3 4.9 %copy-start.2 = (bf16[1,30,128]{2,1,0:T(8,128)(2,1)S(1)}, bf16[1,30,128]{2,1,0:T(8,128)(2,1)}, u32[]{:S(2)}) copy-start(bf16[1,30,128]{2,1,0:T(8,128)(2,1)} %param.5) | copy-start | bytes 23044
  3.3 4.9 %copy-start.3 = (s32[1,4]{1,0:T(1,128)S(1)}, s32[1,4]{1,0:T(1,128)}, u32[]{:S(2)}) copy-start(s32[1,4]{1,0:T(1,128)} %pairs.3) | copy-start | bytes 52
  4.0 46.1 %collective-permute-start.1 = (bf16[30,256,128]{2,1,0:T(8,128)(2,1)S(1)}, bf16[30,256,128]{2,1,0:T(8,128)(2,1)S(1)}, u32[]{:S(2)}, u32[]{:S(2)}) collective-permute-start(bf16[30,256,128]{2,1,0:T(8,128)(2,1)S(1)} %get-tuple-element.21.own_side.xj_side), channel_id=1, source_target_pairs={{0,2},{1,3},{2,0},{3,1},{4,6},{5,7},{6,4},{7,5},{8,10},{9,11},{10,... | collective-permute-start | bytes 5898248 | tf_op jit(solution)/shard_map/ppermute | solution.py:457
  6.5 48.1 %collective-permute-start.5 = (bf16[30,256,128]{2,1,0:T(8,128)(2,1)S(1)}, bf16[30,256,128]{2,1,0:T(8,128)(2,1)S(1)}, u32[]{:S(2)}, u32[]{:S(2)}) collective-permute-start(bf16[30,256,128]{2,1,0:T(8,128)(2,1)S(1)} %get-tuple-element.28), channel_id=1, source_target_pairs={{0,4},{1,5},{2,6},{3,7},{4,0},{5,1},{6,2},{7,3},{8,12},{9,13},{10,... | collective-permute-start | bytes 5898248 | tf_op jit(solution)/shard_map/ppermute | solution.py:457
  8.1 46.5 %collective-permute-start.6 = (bf16[30,256,128]{2,1,0:T(8,128)(2,1)S(1)}, bf16[30,256,128]{2,1,0:T(8,128)(2,1)S(1)}, u32[]{:S(2)}, u32[]{:S(2)}) collective-permute-start(bf16[30,256,128]{2,1,0:T(8,128)(2,1)S(1)} %get-tuple-element.29), channel_id=1, source_target_pairs={{4,8},{5,9},{6,10},{7,11},{8,4},{9,5},{10,6},{11,7},{0,1},{1,0},{2... | collective-permute-start | bytes 5898248 | tf_op jit(solution)/shard_map/ppermute | solution.py:457
  17.1 1.4 %collective-permute-start.2 = (f32[1,640]{1,0:T(1,128)S(1)}, f32[1,640]{1,0:T(1,128)S(1)}, u32[]{:S(2)}, u32[]{:S(2)}) collective-permute-start(f32[1,640]{1,0:T(1,128)S(1)} %get-tuple-element.25.refs_0_), channel_id=1, source_target_pairs={{0,1},{1,0},{2,3},{3,2},{4,5},{5,4},{6,7},{7,6},{8,9},{9,8},{10,11... | collective-permute-start | bytes 7688 | tf_op jit(solution)/shard_map/ppermute | solution.py:442
  50.2 5.4 %collective-permute-start.3 = (bf16[30,128,128]{2,1,0:T(8,128)(2,1)S(1)}, bf16[30,128,128]{2,1,0:T(8,128)(2,1)S(1)}, u32[]{:S(2)}, u32[]{:S(2)}) collective-permute-start(bf16[30,128,128]{2,1,0:T(8,128)(2,1)S(1)} %get-tuple-element.26), channel_id=1, source_target_pairs={{0,1},{1,0},{2,3},{3,2},{4,5},{5,4},{6,7},{7,6},{8,9},{9,8},{10,11... | collective-permute-start | bytes 2949128 | tf_op jit(solution)/shard_map/ppermute | solution.py:457
  50.3 5.3 %collective-permute-start.4 = (bf16[30,128,128]{2,1,0:T(8,128)(2,1)S(1)}, bf16[30,128,128]{2,1,0:T(8,128)(2,1)S(1)}, u32[]{:S(2)}, u32[]{:S(2)}) collective-permute-start(bf16[30,128,128]{2,1,0:T(8,128)(2,1)S(1)} %get-tuple-element.27), channel_id=1, source_target_pairs={{0,1},{1,0},{2,3},{3,2},{4,5},{5,4},{6,7},{7,6},{8,9},{9,8},{10,11... | collective-permute-start | bytes 2949128 | tf_op jit(solution)/shard_map/ppermute | solution.py:457
  50.8 8.6 %collective-permute-start.9 = (f32[1,640]{1,0:T(1,128)S(1)}, f32[1,640]{1,0:T(1,128)S(1)}, u32[]{:S(2)}, u32[]{:S(2)}) collective-permute-start(f32[1,640]{1,0:T(1,128)S(1)} %shard_map.61.token.refs_0_), channel_id=1, source_target_pairs={{0,12},{1,13},{2,14},{3,15},{4,8},{5,9},{6,10},{7,11},{8,4},{9,5},... | collective-permute-start | bytes 7688 | tf_op jit(solution)/shard_map/ppermute | solution.py:442
  54.6 4.8 %collective-permute-start.8 = (f32[1,640]{1,0:T(1,128)S(1)}, f32[1,640]{1,0:T(1,128)S(1)}, u32[]{:S(2)}, u32[]{:S(2)}) collective-permute-start(f32[1,640]{1,0:T(1,128)S(1)} %shard_map.61.token.refs_0_), channel_id=1, source_target_pairs={{0,8},{1,9},{2,10},{3,11},{4,12},{5,13},{6,14},{7,15},{8,0},{9,1},... | collective-permute-start | bytes 7688 | tf_op jit(solution)/shard_map/ppermute | solution.py:442
  54.7 4.8 %collective-permute-start.7 = (f32[1,640]{1,0:T(1,128)S(1)}, f32[1,640]{1,0:T(1,128)S(1)}, u32[]{:S(2)}, u32[]{:S(2)}) collective-permute-start(f32[1,640]{1,0:T(1,128)S(1)} %shard_map.61.token.refs_0_), channel_id=1, source_target_pairs={{0,4},{1,5},{2,6},{3,7},{4,0},{5,1},{6,2},{7,3},{8,12},{9,13},{10,... | collective-permute-start | bytes 7688 | tf_op jit(solution)/shard_map/ppermute | solution.py:442
  59.7 5.1 %collective-permute-start.10 = (bf16[528,128]{1,0:T(8,128)(2,1)S(1)}, bf16[528,128]{1,0:T(8,128)(2,1)S(1)}, u32[]{:S(2)}, u32[]{:S(2)}) collective-permute-start(bf16[528,128]{1,0:T(8,128)(2,1)S(1)} %get-tuple-element.31), channel_id=1, source_target_pairs={{0,2},{1,3},{2,0},{3,1},{4,6},{5,7},{6,4},{7,5},{8,10},{9,11},{10,... | collective-permute-start | bytes 405512 | tf_op jit(solution)/shard_map/ppermute | solution.py:457
  61.1 5.0 %collective-permute-start.11 = (bf16[4,128,128]{2,1,0:T(8,128)(2,1)S(1)}, bf16[4,128,128]{2,1,0:T(8,128)(2,1)S(1)}, u32[]{:S(2)}, u32[]{:S(2)}) collective-permute-start(bf16[4,128,128]{2,1,0:T(8,128)(2,1)S(1)} %get-tuple-element.34), channel_id=1, source_target_pairs={{0,4},{1,5},{2,6},{3,7},{4,0},{5,1},{6,2},{7,3},{8,12},{9,13},{10,... | collective-permute-start | bytes 393224 | tf_op jit(solution)/shard_map/ppermute | solution.py:457
  62.4 3.7 %collective-permute-start.12 = (bf16[4,128,128]{2,1,0:T(8,128)(2,1)S(1)}, bf16[4,128,128]{2,1,0:T(8,128)(2,1)S(1)}, u32[]{:S(2)}, u32[]{:S(2)}) collective-permute-start(bf16[4,128,128]{2,1,0:T(8,128)(2,1)S(1)} %get-tuple-element.35), channel_id=1, source_target_pairs={{4,8},{5,9},{6,10},{7,11},{8,4},{9,5},{10,6},{11,7},{0,1},{1,0},{2... | collective-permute-start | bytes 393224 | tf_op jit(solution)/shard_map/ppermute | solution.py:457
  62.4 3.7 %collective-permute-start.13 = (f32[2,128,128]{2,1,0:T(8,128)S(1)}, f32[2,128,128]{2,1,0:T(8,128)S(1)}, u32[]{:S(2)}, u32[]{:S(2)}) collective-permute-start(f32[2,128,128]{2,1,0:T(8,128)S(1)} %get-tuple-element.36), channel_id=1, source_target_pairs={{0,1},{1,0},{2,3},{3,2},{4,5},{5,4},{6,7},{7,6},{8,9},{9,8},{10,11... | collective-permute-start | bytes 393224 | tf_op jit(solution)/shard_map/ppermute | solution.py:457
  64.8 1.3 %collective-permute-start.14 = (bf16[128,128]{1,0:T(8,128)(2,1)S(1)}, bf16[128,128]{1,0:T(8,128)(2,1)S(1)}, u32[]{:S(2)}, u32[]{:S(2)}) collective-permute-start(bf16[128,128]{1,0:T(8,128)(2,1)S(1)} %slice.4), channel_id=1, source_target_pairs={{0,1},{1,0},{2,3},{3,2},{4,5},{5,4},{6,7},{7,6},{8,9},{9,8},{10,11... | collective-permute-start | bytes 98312 | tf_op jit(solution)/shard_map/ppermute | solution.py:457

commit v6 on v5

--- a/solution.py
+++ b/solution.py
@@ -14,7 +14,7 @@
 XF, YF, YOF, XG, XY, XYO, CROSS, OWN = range(8)
 PRODUCTS = ((XJ, FJ), (YJ, FJ), (YO, FJ), (XJ_SIDE, GJ), (XJ, YJ), (XO, YJ), (XO, None), (XJ, XO))
 SHARED = (XF, YF, YOF, XG, XY, XYO, CROSS)
-STACK, OWN_STACK = 10, 4
+STACK, SHORT_STACK, OWN_STACK = 10, 8, 4
 LIMIT = 12 * 2**20
 
 
@@ -202,7 +202,8 @@
     )(domains, pairs, own, own_side, other, coef)
 
 
-def relay_kernel(value, token, low, high, sems):
+def relay_kernel(value, *refs):
+    shares, (low, high, total, sems) = refs[:-4], refs[-4:]
     size = low.shape[1]
     copies = [
         pltpu.make_async_copy(value.at[:, :size, :], low, sems.at[0]),
@@ -210,22 +211,23 @@
     ]
     for copy in copies:
         copy.start()
+    total[...] = sum(share[...] for share in shares)
     for copy in copies:
         copy.wait()
 
 
-def relay(value, token):
+def relay(value, shares):
     rows, size, width = value.shape
     part = jax.ShapeDtypeStruct((rows, size // 2, width), value.dtype)
     return pl.pallas_call(
         relay_kernel,
-        out_shape=[part, part],
-        in_specs=vmem(2),
-        out_specs=vmem(2),
+        out_shape=[part, part, jax.ShapeDtypeStruct(shares[0].shape, F32)],
+        in_specs=vmem(1 + len(shares)),
+        out_specs=vmem(3),
         scratch_shapes=[pltpu.SemaphoreType.DMA((2,))],
         compiler_params=pltpu.CompilerParams(vmem_limit_bytes=LIMIT),
         cost_estimate=cost(value, value),
-    )(value, token)
+    )(value, *shares)
 
 
 def shared_kernel(number, mine, theirs, xj, xj_side, xo, yj, yo, yo_high, near, far, total):
@@ -234,11 +236,11 @@
     main = pl.ds(pl.multiple_of(odd * half, 16), half)
     cross = pl.ds(pl.multiple_of(jnp.where(flag, odd, 1 - odd) * half, 16), half)
 
-    def product(q, group, block):
+    def product(q, first, size, block):
         lefts, rights = [], []
         left_block, right_block = PRODUCTS[q]
-        for i in range(STACK):
-            slot = group * STACK + i
+        for i in range(size):
+            slot = first + i
             row, other_row = mine[q, slot], theirs[q, slot]
             if left_block == XO:
                 left = xo[row, cross if q == CROSS else main, :]
@@ -258,14 +260,20 @@
         most = number[SHARED[0]]
         for at, q in enumerate(SHARED):
             most = jnp.maximum(most, number[q])
-            total[at] = product(q, 0, block)
-
-        def step(group, carry):
-            for at, q in enumerate(SHARED):
-                total[at] += product(q, group, block)
-            return carry
-
-        lax.fori_loop(1, (most + STACK - 1) // STACK, step, 0)
+            total[at] = product(q, 0, STACK, block)
+
+        def steps(size):
+            def step(i, carry):
+                for at, q in enumerate(SHARED):
+                    total[at] += product(q, STACK + i * size, size, block)
+                return carry
+
+            return step
+
+        short = most <= STACK + SHORT_STACK
+        more = jnp.maximum(most - STACK, 0)
+        lax.fori_loop(0, jnp.where(short, jnp.minimum(more, 1), 0), steps(SHORT_STACK), 0)
+        lax.fori_loop(0, jnp.where(short, 0, (more + STACK - 1) // STACK), steps(STACK), 0)
 
     @pl.when(f_near)
     def _():
@@ -288,18 +296,19 @@
 
 
 def message_kernel(total, *refs):
-    shares, (to_near, to_far, to_mate, to_y, summed) = refs[:-5], refs[-5:]
+    shares, (to_near, to_far, to_mate, to_y, to_y_other, summed) = refs[:-6], refs[-6:]
     _, _, _, _, flag, _, _, f_near = place_of_device()
     width = total.shape[1]
+
+    def put(out, values):
+        for i, value in enumerate(values):
+            out[i * width:(i + 1) * width, :] = value.astype(BF16)
 
     def to_f_and_g(to_f, to_g):
         cross = total[CROSS].T
         nothing = jnp.zeros_like(cross)
-        from_total = (total[XF].T, jnp.where(flag, cross, nothing), total[YF].T, total[YOF].T)
-        for i, value in enumerate(from_total):
-            to_f[i] = value.astype(BF16)
-        for i, value in enumerate((total[XG].T, jnp.where(flag, nothing, cross), nothing, nothing)):
-            to_g[i] = value.astype(BF16)
+        put(to_f, (total[XF].T, jnp.where(flag, cross, nothing), total[YF].T, total[YOF].T))
+        put(to_g, (total[XG].T, jnp.where(flag, nothing, cross), nothing, nothing))
 
     @pl.when(f_near)
     def _():
@@ -309,10 +318,11 @@
     def _():
         to_f_and_g(to_far, to_near)
 
+    put(to_y, (total[XY].T, total[XYO].T, total[YF]))
+    to_y[3 * width:, :] = jnp.zeros((to_y.shape[0] - 3 * width, width), BF16)
+    put(to_y_other, (total[YOF],))
     to_mate[0] = total[XYO]
     to_mate[1] = total[CROSS]
-    for i, value in enumerate((total[XY].T, total[XYO].T, total[YF], total[YOF])):
-        to_y[i * width:(i + 1) * width, :] = value.astype(BF16)
     gathered = sum(share[...] for share in shares)
     summed[...] = gathered
     lines = gathered.shape[1] // width
@@ -321,30 +331,33 @@
         part = rest.astype(BF16)
         rest = rest - part.astype(F32)
         rows += [part[:, i * width:(i + 1) * width].astype(F32) for i in range(lines)]
-    rows.append(jnp.zeros((to_y.shape[0] - 4 * width - 3 * lines, width), F32))
-    to_y[4 * width:, :] = jnp.concatenate(rows, axis=0).astype(BF16)
+    rows.append(jnp.zeros((to_near.shape[0] - 4 * width - 3 * lines, width), F32))
+    to_near[4 * width:, :] = jnp.concatenate(rows, axis=0).astype(BF16)
 
 
 def messages(total, shares):
     width = total.shape[-1]
     lines = -(-3 * shares[0].shape[1] // width // 16) * 16
     flat = jax.ShapeDtypeStruct
+    sent = lambda rows: flat((rows, width), BF16)
     return pl.pallas_call(
         message_kernel,
-        out_shape=[flat((4, width, width), BF16)] * 2
-        + [squares(2, width), flat((4 * width + lines, width), BF16), flat(shares[0].shape, F32)],
+        out_shape=[
+            sent(4 * width + lines + 16), sent(4 * width), squares(2, width), sent(4 * width + 16), sent(width),
+            flat(shares[0].shape, F32),
+        ],
         in_specs=vmem(1 + len(shares)),
-        out_specs=vmem(5),
+        out_specs=vmem(6),
         compiler_params=pltpu.CompilerParams(vmem_limit_bytes=LIMIT),
         cost_estimate=cost(total, total),
     )(total, *shares)
 
 
-def coulomb_kernel(own, own_side, share, from_y, out, summed):
+def coulomb_kernel(own, own_side, share, from_near, out, summed):
     rows, half, width = own.shape
     odd = place_of_device()[3]
     lines = share.shape[1] // width
-    parts = from_y[4 * width:, :].astype(F32)
+    parts = from_near[4 * width:, :].astype(F32)
     line = lambda i: jnp.concatenate([parts[i * lines + j:i * lines + j + 1] for j in range(lines)], axis=1)
     gathered = share[...] + (line(0) + line(1) + line(2))
     summed[...] = gathered
@@ -356,7 +369,7 @@
         out[row] = part + jnp.dot(side_gamma, own_side[row], preferred_element_type=F32)
 
 
-def coulomb(own, own_side, share, from_y):
+def coulomb(own, own_side, share, from_near):
     rows, _, width = own.shape
     flat = jax.ShapeDtypeStruct
     out, summed = pl.pallas_call(
@@ -366,11 +379,11 @@
         out_specs=vmem(2),
         compiler_params=pltpu.CompilerParams(vmem_limit_bytes=LIMIT),
         cost_estimate=cost(own, own_side),
-    )(own, own_side, share, from_y)
+    )(own, own_side, share, from_near)
     return jnp.swapaxes(out, 0, 1), summed
 
 
-def band_kernel(aux, pairs, summed, own, total, from_y, from_near, from_far, from_mate, passed, band, made, sems):
+def band_kernel(aux, pairs, summed, own, total, from_y, from_near, from_far, from_mate, from_y_other, band, made, sems):
     depth, width = pairs.shape[1], band.shape[1]
     me, core, _, odd, _, _, _, f_near = place_of_device()
     count = lax.axis_size("basis")
@@ -391,15 +404,15 @@
         copies.append(pltpu.make_async_copy(made.at[slot], band.at[depth + ahead], sems.at[slot]))
         copies[-1].start()
 
-    from_f = lambda i: jnp.where(f_near, from_far[i].astype(F32), from_near[i].astype(F32))
-    from_g = lambda i: jnp.where(f_near, from_near[i].astype(F32), from_far[i].astype(F32))
-    y_block = lambda i: from_y[i * width:(i + 1) * width, :].astype(F32)
+    block = lambda ref, i: ref[i * width:(i + 1) * width, :].astype(F32)
+    from_f = lambda i: jnp.where(f_near, block(from_far, i), block(from_near, i))
+    from_g = lambda i: jnp.where(f_near, block(from_near, i), block(from_far, i))
     put(0, own[0])
     put(cross, own[1])
-    put(2 * sign, total[XY] + y_block(0))
-    put(2 * sign + cross, from_mate[0] + y_block(1))
-    put(-2 * sign, y_block(2) + from_f(2))
-    put(-2 * sign + cross, passed[...].astype(F32) + from_f(3))
+    put(2 * sign, total[XY] + block(from_y, 0))
+    put(2 * sign + cross, from_mate[0] + block(from_y, 1))
+    put(-2 * sign, block(from_y, 2) + from_f(2))
+    put(-2 * sign + cross, block(from_y_other, 0) + from_f(3))
     put(4 * sign, total[XF] + from_g(0))
     put(-4 * sign, total[XG] + from_f(0))
     put(-3 * cross, from_mate[1] + from_f(1) + from_g(1))
@@ -436,11 +449,8 @@
     )(*shares)
 
 
-def shares_of(values, count, step, ways=2):
-    every = [values]
-    for way in range(1, ways):
-        every.append(lax.ppermute(values, "basis", [(i, i ^ (step * way)) for i in range(count)]))
-    return every
+def shares_of(values, count, step):
+    return [values, lax.ppermute(values, "basis", [(i, i ^ step) for i in range(count)])]
 
 
 def per_device(factors, coefs, domains, pairs):
@@ -462,23 +472,21 @@
     near, far = send(for_near, to_near), send(for_far, to_far)
     own_pairs, share, *tables = own_products(domains, pairs, xj, xj_side, xo, coefs[0])
     share = added(shares_of(share, count, 1))
-    y_low, y_high = relay(yj, share)
+    y_low, y_high, share = relay(yj, shares_of(share, count, 2))
     yo, yo_high = send(y_low, swap), send(y_high, swap)
-    shares, step = [share], 4
+    shares, step = [share], 8
     while step < count:
         if len(shares) > 1:
             shares = [added(shares)]
-        ways = 4 if 4 * step <= count else 2
-        shares = shares_of(shares[0], count, step, ways)
-        step *= ways
+        shares = shares_of(shares[0], count, step)
+        step *= 2
     total = shared_products(tables, xj, xj_side, xo, yj, yo, yo_high, near, far)
-    for_near, for_far, for_mate, for_y, share = messages(total, shares)
-    from_y, from_near, from_far = send(for_y, across), send(for_near, to_near), send(for_far, to_far)
+    for_near, for_far, for_mate, for_y, for_y_other, share = messages(total, shares)
+    from_near, from_far = send(for_near, to_near), send(for_far, to_far)
+    from_y, from_y_other = send(for_y, across), send(for_y_other, chip_route(count, lambda c: c ^ 1, swap=True))
     from_mate = send(for_mate, swap)
-    width = own.shape[2]
-    passed = send(from_y[3 * width:4 * width], swap)
-    coulomb_half, summed = coulomb(xj, xj_side, share, from_y)
-    band = finish(aux, pairs, summed, own_pairs, total, from_y, from_near, from_far, from_mate, passed)
+    coulomb_half, summed = coulomb(xj, xj_side, share, from_near)
+    band = finish(aux, pairs, summed, own_pairs, total, from_y, from_near, from_far, from_mate, from_y_other)
     return (band[None], coulomb_half)
 
 

time: 67.8 us -> 67.4 us (level)
  waiting for transfers between devices: 34.3 us -> 32.7 us
  starting transfers between devices: 13.8 us -> 15 us
    ppermute x11, waiting for transfers between devices: 33.4 us -> 31.9 us  [per_device(): send = lambda value, route: lax.ppermute(value, 'basis', route)]
    ppermute x11, starting transfers between devices: 8.44 us -> 9.26 us  [per_device(): send = lambda value, route: lax.ppermute(value, 'basis', route)]
    ppermute x4 -> x3, starting transfers between devices: 5.39 us -> 5.73 us  [shares_of(): lax.ppermute(values, 'basis', [(i, i ^ step) for i in range(count)])]
  transfers between devices with their start and end apart: 15 -> 14, of which waited for: 3 -> 5; matrix products, arithmetic and copies ran while one was open for 0% -> 0% of each run, Pallas kernels for 22% -> 22%
where the time goes in v6:
time: 67.4 us; the launch traced here: 67.3 us
  waiting for transfers between devices  32.7 us (49%)
  Pallas kernels  16.7 us (25%)
  starting transfers between devices  15 us (22%)
  local copies, waits for them, and re-layouts  2.12 us (3%)
  between operations  0.72 us (1%)
    ppermute x11, waiting for transfers between devices, per_device(): send = lambda value, route: lax.ppermute(value, 'basis', route)  31.9 us
    pallas_call x1, Pallas kernels, own_products(): pl.pallas_call(own_kernel, out_shape=[squares(2, width), jax.ShapeDtypeSt...  9.29 us
    ppermute x11, starting transfers between devices, per_device(): send = lambda value, route: lax.ppermute(value, 'basis', route)  9.26 us
    ppermute x3, starting transfers between devices, shares_of(): lax.ppermute(values, 'basis', [(i, i ^ step) for i in range(count)])  5.73 us
    pallas_call x1, Pallas kernels, shared_products(): pl.pallas_call(shared_kernel, out_shape=squares(len(SHARED), blocks[0].sh...  3.54 us
    unnamed x8, local copies, waits for them, and re-layouts  2.12 us
    pallas_call x1, Pallas kernels, finish(): pl.pallas_call(functools.partial(band_kernel, aux), out_shape=squares(siz...  1.47 us
  transfers between devices with their start and end apart: 14, of which 5 were waited for; matrix products, arithmetic and copies ran while one was open for 0% of the time, Pallas kernels for 22%

profile of v6, /device:TPU:0, one launch (start us, length us, event | category | flops | bytes accessed | tf_op | source)
XLA Modules:
  0.0 67.3 jit_solution(7997344957872142189)
XLA Ops:
  0.6 0.5 collective-permute-start
  1.2 2.1 %copy-done = bf16[1,30,512,128]{3,2,1,0:T(8,128)(2,1)S(1)} copy-done((bf16[1,30,512,128]{3,2,1,0:T(8,128)(2,1)S(1)}, bf16[1,30,512,128]{3,2,1,0:T(8,128)(2,1)}, u32[]{:S(2)}) %copy-start) | copy-done | bytes 3932184
  3.3 0.7 %shard_map.59 = (bf16[30,256,128]{2,1,0:T(8,128)(2,1)S(1)}, bf16[30,256,128]{2,1,0:T(8,128)(2,1)S(1)}, bf16[30,256,128]{2,1,0:T(8,128)(2,1)S(1)}, bf16[30,256,128]{2,1,0:T(8,128)(2,1)S(1)}) custom-call(bf16[30,512,128]{2,1,0:T(8,128)(2,1)S(1)} %bitcast.5), custom_call_target="tpu_custom_call" | custom-call | flops 1 | bytes 7864320 | tf_op jit(solution)/shard_map/pallas_call | solution.py:78
  4.0 2.6 %collective-permute-start.1 = (bf16[30,256,128]{2,1,0:T(8,128)(2,1)S(1)}, bf16[30,256,128]{2,1,0:T(8,128)(2,1)S(1)}, u32[]{:S(2)}, u32[]{:S(2)}) collective-permute-start(bf16[30,256,128]{2,1,0:T(8,128)(2,1)S(1)} %get-tuple-element.23.own_side.xj_side), channel_id=1, source_target_pairs={{0,2},{1,3},{2,0},{3,1},{4,6},{5,7},{6,4},{7,5},{8,10},{9,11},{10,... | collective-permute-start | bytes 5898248 | tf_op jit(solution)/shard_map/ppermute | solution.py:467
  6.5 1.6 %collective-permute-start.6 = (bf16[30,256,128]{2,1,0:T(8,128)(2,1)S(1)}, bf16[30,256,128]{2,1,0:T(8,128)(2,1)S(1)}, u32[]{:S(2)}, u32[]{:S(2)}) collective-permute-start(bf16[30,256,128]{2,1,0:T(8,128)(2,1)S(1)} %get-tuple-element.30), channel_id=1, source_target_pairs={{0,4},{1,5},{2,6},{3,7},{4,0},{5,1},{6,2},{7,3},{8,12},{9,13},{10,... | collective-permute-start | bytes 5898248 | tf_op jit(solution)/shard_map/ppermute | solution.py:467
  8.2 9.3 %shard_map.60 = (f32[2,128,128]{2,1,0:T(8,128)S(1)}, f32[1,640]{1,0:T(1,128)S(1)}, s32[8]{0:T(128)S(1)}, s32[8,32]{1,0:T(8,128)S(1)}, s32[8,32]{1,0:T(8,128)S(1)}) custom-call(s32[16,30]{1,0:T(8,128)S(1)} %copy-done.1, s32[1,4]{1,0:T(1,128)S(1)} %copy-done.3, bf16[30,256,128]{2,1,0:T(8,128)(2,1)S(1)} %get-tuple-element.22.own.xj, ...), custom_call_target="tpu_custom_call" | custom-call | flops 1 | bytes 7864320 | tf_op jit(solution)/shard_map/pallas_call | solution.py:188
  17.5 0.6 collective-permute-start.2
  18.0 0.8 %collective-permute-done.2.refs_1_ = f32[1,640]{1,0:T(1,128)S(1)} collective-permute-done((f32[1,640]{1,0:T(1,128)S(1)}, f32[1,640]{1,0:T(1,128)S(1)}, u32[]{:S(2)}, u32[]{:S(2)}) %collective-permute-start.2) | collective-permute-done | bytes 2592 | tf_op jit(solution)/shard_map/ppermute | solution.py:453
  18.9 2.3 %collective-permute-start.3 = (f32[1,640]{1,0:T(1,128)S(1)}, f32[1,640]{1,0:T(1,128)S(1)}, u32[]{:S(2)}, u32[]{:S(2)}) collective-permute-start(f32[1,640]{1,0:T(1,128)S(1)} %shard_map.61.refs_0_), channel_id=1, source_target_pairs={{0,2},{1,3},{2,0},{3,1},{4,6},{5,7},{6,4},{7,5},{8,10},{9,11},{10,... | collective-permute-start | bytes 7688 | tf_op jit(solution)/shard_map/ppermute | solution.py:453
  21.2 28.9 %collective-permute-done.1.value.yj = bf16[30,256,128]{2,1,0:T(8,128)(2,1)S(1)} collective-permute-done((bf16[30,256,128]{2,1,0:T(8,128)(2,1)S(1)}, bf16[30,256,128]{2,1,0:T(8,128)(2,1)S(1)}, u32[]{:S(2)}, u32[]{:S(2)}) %collective-permute-start.1) | collective-permute-done | bytes 1966112 | tf_op jit(solution)/shard_map/ppermute | solution.py:467
  50.1 0.2 shard_map.62
  50.4 0.5 collective-permute-start.5
  50.9 2.8 %collective-permute-start.8 = (f32[1,640]{1,0:T(1,128)S(1)}, f32[1,640]{1,0:T(1,128)S(1)}, u32[]{:S(2)}, u32[]{:S(2)}) collective-permute-start(f32[1,640]{1,0:T(1,128)S(1)} %get-tuple-element.32.refs_0_), channel_id=1, source_target_pairs={{0,8},{1,9},{2,10},{3,11},{4,12},{5,13},{6,14},{7,15},{8,0},{9,1},... | collective-permute-start | bytes 7688 | tf_op jit(solution)/shard_map/ppermute | solution.py:453
  53.7 0.6 collective-permute-done.5.yo_high
  54.3 3.5 %shard_map.63.total = f32[7,128,128]{2,1,0:T(8,128)S(1)} custom-call(s32[8]{0:T(128)S(1)} %get-tuple-element.24.number, s32[8,32]{1,0:T(8,128)S(1)} %get-tuple-element.25.mine, s32[8,32]{1,0:T(8,128)S(1)} %get-tuple-element.26.theirs, bf16[30,256,128]{2,1,0:T(8,128)(2,1)S(1)} %get-tuple-element.22.own.xj, ...), custom_call_target="tpu_custom_call" | custom-call | flops 1 | bytes 15728640 | tf_op jit(solution)/shard_map/pallas_call | solution.py:288
  57.9 0.2 shard_map.64
  58.2 1.9 %collective-permute-start.9 = (bf16[544,128]{1,0:T(8,128)(2,1)S(1)}, bf16[544,128]{1,0:T(8,128)(2,1)S(1)}, u32[]{:S(2)}, u32[]{:S(2)}) collective-permute-start(bf16[544,128]{1,0:T(8,128)(2,1)S(1)} %get-tuple-element.34), channel_id=1, source_target_pairs={{0,4},{1,5},{2,6},{3,7},{4,0},{5,1},{6,2},{7,3},{8,12},{9,13},{10,... | collective-permute-start | bytes 417800 | tf_op jit(solution)/shard_map/ppermute | solution.py:467
  60.0 1.5 %collective-permute-start.10 = (bf16[528,128]{1,0:T(8,128)(2,1)S(1)}, bf16[528,128]{1,0:T(8,128)(2,1)S(1)}, u32[]{:S(2)}, u32[]{:S(2)}) collective-permute-start(bf16[528,128]{1,0:T(8,128)(2,1)S(1)} %get-tuple-element.37), channel_id=1, source_target_pairs={{0,2},{1,3},{2,0},{3,1},{4,6},{5,7},{6,4},{7,5},{8,10},{9,11},{10,... | collective-permute-start | bytes 405512 | tf_op jit(solution)/shard_map/ppermute | solution.py:467
  61.5 0.5 collective-permute-start.12
  62.0 0.1 collective-permute-start.13
  62.2 1.8 %collective-permute-done.9.from_near = bf16[544,128]{1,0:T(8,128)(2,1)S(1)} collective-permute-done((bf16[544,128]{1,0:T(8,128)(2,1)S(1)}, bf16[544,128]{1,0:T(8,128)(2,1)S(1)}, u32[]{:S(2)}, u32[]{:S(2)}) %collective-permute-start.9) | collective-permute-done | bytes 139296 | tf_op jit(solution)/shard_map/ppermute | solution.py:467
  64.0 1.3 %shard_map.65 = (f32[30,1,128]{2,1,0:T(1,128)}, f32[1,640]{1,0:T(1,128)S(1)}) custom-call(bf16[30,256,128]{2,1,0:T(8,128)(2,1)S(1)} %get-tuple-element.22.own.xj, bf16[30,256,128]{2,1,0:T(8,128)(2,1)S(1)} %get-tuple-element.23.own_side.xj_side, f32[1,640]{1,0:T(1,128)S(1)} %get-tuple-element.33.share, bf16[544,128]{1,0:T(8,128)(2,1)S(1)} %collective-permute-done.9.from_near), custom_call_target="tpu_custom_call" | custom-call | flops 1 | bytes 3932160 | tf_op jit(solution)/shard_map/pallas_call | solution.py:375
  65.3 0.5 collective-permute-done.13.from_y_other
  65.8 1.5 %shard_map.66 = f32[9,128,128]{2,1,0:T(8,128)} custom-call(s32[1,4]{1,0:T(1,128)S(1)} %copy-done.3, f32[1,640]{1,0:T(1,128)S(1)} %get-tuple-element.35.summed, f32[2,128,128]{2,1,0:T(8,128)S(1)} %get-tuple-element.36.own, f32[7,128,128]{2,1,0:T(8,128)S(1)} %shard_map.63.total, bf16[528,128]{1,0:T(8,128)(2,1)S(1)} %collective-permute-done.10.from_y, ...), custom_call_target="tpu_custom_call" | custom-call | flops 1 | bytes 1159168 | tf_op jit(solution)/shard_map/pallas_call | solution.py:426
  (20 shorter events, 0.1 us)
Async XLA Ops:
  0.6 7.5 %collective-permute-start = (bf16[30,512,128]{2,1,0:T(8,128)(2,1)}, bf16[30,512,128]{2,1,0:T(8,128)(2,1)S(1)}, u32[]{:S(2)}, u32[]{:S(2)}) collective-permute-start(bf16[30,512,128]{2,1,0:T(8,128)(2,1)} %bitcast.4), channel_id=1, source_target_pairs={{0,1},{1,0},{2,3},{3,2},{4,5},{5,4},{6,7},{7,6},{8,9},{9,8},{10,11... | collective-permute-start | bytes 11796488 | tf_op jit(solution)/shard_map/ppermute | solution.py:467
  1.1 2.1 %copy-start = (bf16[1,30,512,128]{3,2,1,0:T(8,128)(2,1)S(1)}, bf16[1,30,512,128]{3,2,1,0:T(8,128)(2,1)}, u32[]{:S(2)}) copy-start(bf16[1,30,512,128]{3,2,1,0:T(8,128)(2,1)} %param.4) | copy-start | bytes 11796484
  3.3 4.9 %copy-start.1 = (s32[16,30]{1,0:T(8,128)S(1)}, s32[16,30]{1,0:T(8,128)}, u32[]{:S(2)}) copy-start(s32[16,30]{1,0:T(8,128)} %domains.1) | copy-start | bytes 5764
  3.3 4.9 %copy-start.2 = (bf16[1,30,128]{2,1,0:T(8,128)(2,1)S(1)}, bf16[1,30,128]{2,1,0:T(8,128)(2,1)}, u32[]{:S(2)}) copy-start(bf16[1,30,128]{2,1,0:T(8,128)(2,1)} %param.5) | copy-start | bytes 23044
  3.3 4.9 %copy-start.3 = (s32[1,4]{1,0:T(1,128)S(1)}, s32[1,4]{1,0:T(1,128)}, u32[]{:S(2)}) copy-start(s32[1,4]{1,0:T(1,128)} %pairs.3) | copy-start | bytes 52
  4.0 46.1 %collective-permute-start.1 = (bf16[30,256,128]{2,1,0:T(8,128)(2,1)S(1)}, bf16[30,256,128]{2,1,0:T(8,128)(2,1)S(1)}, u32[]{:S(2)}, u32[]{:S(2)}) collective-permute-start(bf16[30,256,128]{2,1,0:T(8,128)(2,1)S(1)} %get-tuple-element.23.own_side.xj_side), channel_id=1, source_target_pairs={{0,2},{1,3},{2,0},{3,1},{4,6},{5,7},{6,4},{7,5},{8,10},{9,11},{10,... | collective-permute-start | bytes 5898248 | tf_op jit(solution)/shard_map/ppermute | solution.py:467
  6.5 47.1 %collective-permute-start.6 = (bf16[30,256,128]{2,1,0:T(8,128)(2,1)S(1)}, bf16[30,256,128]{2,1,0:T(8,128)(2,1)S(1)}, u32[]{:S(2)}, u32[]{:S(2)}) collective-permute-start(bf16[30,256,128]{2,1,0:T(8,128)(2,1)S(1)} %get-tuple-element.30), channel_id=1, source_target_pairs={{0,4},{1,5},{2,6},{3,7},{4,0},{5,1},{6,2},{7,3},{8,12},{9,13},{10,... | collective-permute-start | bytes 5898248 | tf_op jit(solution)/shard_map/ppermute | solution.py:467
  8.1 45.6 %collective-permute-start.7 = (bf16[30,256,128]{2,1,0:T(8,128)(2,1)S(1)}, bf16[30,256,128]{2,1,0:T(8,128)(2,1)S(1)}, u32[]{:S(2)}, u32[]{:S(2)}) collective-permute-start(bf16[30,256,128]{2,1,0:T(8,128)(2,1)S(1)} %get-tuple-element.31), channel_id=1, source_target_pairs={{4,8},{5,9},{6,10},{7,11},{8,4},{9,5},{10,6},{11,7},{0,1},{1,0},{2... | collective-permute-start | bytes 5898248 | tf_op jit(solution)/shard_map/ppermute | solution.py:467
  17.5 1.4 %collective-permute-start.2 = (f32[1,640]{1,0:T(1,128)S(1)}, f32[1,640]{1,0:T(1,128)S(1)}, u32[]{:S(2)}, u32[]{:S(2)}) collective-permute-start(f32[1,640]{1,0:T(1,128)S(1)} %get-tuple-element.27.refs_0_), channel_id=1, source_target_pairs={{0,1},{1,0},{2,3},{3,2},{4,5},{5,4},{6,7},{7,6},{8,9},{9,8},{10,11... | collective-permute-start | bytes 7688 | tf_op jit(solution)/shard_map/ppermute | solution.py:453
  18.9 31.2 %collective-permute-start.3 = (f32[1,640]{1,0:T(1,128)S(1)}, f32[1,640]{1,0:T(1,128)S(1)}, u32[]{:S(2)}, u32[]{:S(2)}) collective-permute-start(f32[1,640]{1,0:T(1,128)S(1)} %shard_map.61.refs_0_), channel_id=1, source_target_pairs={{0,2},{1,3},{2,0},{3,1},{4,6},{5,7},{6,4},{7,5},{8,10},{9,11},{10,... | collective-permute-start | bytes 7688 | tf_op jit(solution)/shard_map/ppermute | solution.py:453
  50.3 3.4 %collective-permute-start.4 = (bf16[30,128,128]{2,1,0:T(8,128)(2,1)S(1)}, bf16[30,128,128]{2,1,0:T(8,128)(2,1)S(1)}, u32[]{:S(2)}, u32[]{:S(2)}) collective-permute-start(bf16[30,128,128]{2,1,0:T(8,128)(2,1)S(1)} %get-tuple-element.28), channel_id=1, source_target_pairs={{0,1},{1,0},{2,3},{3,2},{4,5},{5,4},{6,7},{7,6},{8,9},{9,8},{10,11... | collective-permute-start | bytes 2949128 | tf_op jit(solution)/shard_map/ppermute | solution.py:467
  50.4 4.0 %collective-permute-start.5 = (bf16[30,128,128]{2,1,0:T(8,128)(2,1)S(1)}, bf16[30,128,128]{2,1,0:T(8,128)(2,1)S(1)}, u32[]{:S(2)}, u32[]{:S(2)}) collective-permute-start(bf16[30,128,128]{2,1,0:T(8,128)(2,1)S(1)} %get-tuple-element.29), channel_id=1, source_target_pairs={{0,1},{1,0},{2,3},{3,2},{4,5},{5,4},{6,7},{7,6},{8,9},{9,8},{10,11... | collective-permute-start | bytes 2949128 | tf_op jit(solution)/shard_map/ppermute | solution.py:467
  50.9 7.0 %collective-permute-start.8 = (f32[1,640]{1,0:T(1,128)S(1)}, f32[1,640]{1,0:T(1,128)S(1)}, u32[]{:S(2)}, u32[]{:S(2)}) collective-permute-start(f32[1,640]{1,0:T(1,128)S(1)} %get-tuple-element.32.refs_0_), channel_id=1, source_target_pairs={{0,8},{1,9},{2,10},{3,11},{4,12},{5,13},{6,14},{7,15},{8,0},{9,1},... | collective-permute-start | bytes 7688 | tf_op jit(solution)/shard_map/ppermute | solution.py:453
  58.2 5.8 %collective-permute-start.9 = (bf16[544,128]{1,0:T(8,128)(2,1)S(1)}, bf16[544,128]{1,0:T(8,128)(2,1)S(1)}, u32[]{:S(2)}, u32[]{:S(2)}) collective-permute-start(bf16[544,128]{1,0:T(8,128)(2,1)S(1)} %get-tuple-element.34), channel_id=1, source_target_pairs={{0,4},{1,5},{2,6},{3,7},{4,0},{5,1},{6,2},{7,3},{8,12},{9,13},{10,... | collective-permute-start | bytes 417800 | tf_op jit(solution)/shard_map/ppermute | solution.py:467
  60.0 5.8 %collective-permute-start.10 = (bf16[528,128]{1,0:T(8,128)(2,1)S(1)}, bf16[528,128]{1,0:T(8,128)(2,1)S(1)}, u32[]{:S(2)}, u32[]{:S(2)}) collective-permute-start(bf16[528,128]{1,0:T(8,128)(2,1)S(1)} %get-tuple-element.37), channel_id=1, source_target_pairs={{0,2},{1,3},{2,0},{3,1},{4,6},{5,7},{6,4},{7,5},{8,10},{9,11},{10,... | collective-permute-start | bytes 405512 | tf_op jit(solution)/shard_map/ppermute | solution.py:467
  61.5 4.3 %collective-permute-start.11 = (bf16[512,128]{1,0:T(8,128)(2,1)S(1)}, bf16[512,128]{1,0:T(8,128)(2,1)S(1)}, u32[]{:S(2)}, u32[]{:S(2)}) collective-permute-start(bf16[512,128]{1,0:T(8,128)(2,1)S(1)} %get-tuple-element.38), channel_id=1, source_target_pairs={{4,8},{5,9},{6,10},{7,11},{8,4},{9,5},{10,6},{11,7},{0,1},{1,0},{2... | collective-permute-start | bytes 393224 | tf_op jit(solution)/shard_map/ppermute | solution.py:467
  61.5 4.3 %collective-permute-start.12 = (f32[2,128,128]{2,1,0:T(8,128)S(1)}, f32[2,128,128]{2,1,0:T(8,128)S(1)}, u32[]{:S(2)}, u32[]{:S(2)}) collective-permute-start(f32[2,128,128]{2,1,0:T(8,128)S(1)} %get-tuple-element.39), channel_id=1, source_target_pairs={{0,1},{1,0},{2,3},{3,2},{4,5},{5,4},{6,7},{7,6},{8,9},{9,8},{10,11... | collective-permute-start | bytes 393224 | tf_op jit(solution)/shard_map/ppermute | solution.py:467
  62.0 3.7 %collective-permute-start.13 = (bf16[128,128]{1,0:T(8,128)(2,1)S(1)}, bf16[128,128]{1,0:T(8,128)(2,1)S(1)}, u32[]{:S(2)}, u32[]{:S(2)}) collective-permute-start(bf16[128,128]{1,0:T(8,128)(2,1)S(1)} %get-tuple-element.40), channel_id=1, source_target_pairs={{0,3},{1,2},{2,1},{3,0},{4,7},{5,6},{6,5},{7,4},{8,11},{9,10},{10,... | collective-permute-start | bytes 98312 | tf_op jit(solution)/shard_map/ppermute | solution.py:467

commit v7 on v6

--- a/solution.py
+++ b/solution.py
@@ -13,7 +13,7 @@
 XJ, XO, XJ_SIDE, YJ, YO, YO_HIGH, FJ, GJ = range(8)
 XF, YF, YOF, XG, XY, XYO, CROSS, OWN = range(8)
 PRODUCTS = ((XJ, FJ), (YJ, FJ), (YO, FJ), (XJ_SIDE, GJ), (XJ, YJ), (XO, YJ), (XO, None), (XJ, XO))
-SHARED = (XF, YF, YOF, XG, XY, XYO, CROSS)
+SHARED, WITH_Y = (XF, YF, YOF, XG, CROSS), (XY, XYO)
 STACK, SHORT_STACK, OWN_STACK = 10, 8, 4
 LIMIT = 12 * 2**20
 
@@ -86,9 +86,14 @@
     )(own)
 
 
-def find_matches(domains, number, mine, theirs, spot):
+def lists_of(table):
+    width = table.shape[1] // 2 - 4
+    return lambda q: table[q, 2 * width], lambda q, slot: table[q, slot], lambda q, slot: table[q, width + slot]
+
+
+def find_matches(domains, table, spot):
     count, rows = domains.shape
-    width = mine.shape[1]
+    width = table.shape[1] // 2 - 4
     _, core, chip, _, flag, f_chip, g_chip, _ = place_of_device()
     mine_first, other_first = (chip, core), (chip, 1 - core)
     block = {XJ: mine_first, XJ_SIDE: mine_first, XO: other_first, None: (jnp.where(flag, f_chip, g_chip), core)}
@@ -112,8 +117,8 @@
             return carry
 
         def clean(slot, carry):
-            mine[q, slot] = 0
-            theirs[q, slot] = 0
+            table[q, slot] = 0
+            table[q, width + slot] = 0
             return carry
 
         def scan(row, found):
@@ -121,20 +126,21 @@
             inside = jnp.logical_and(away >= 0, away < 2 * rows)
             other_row = spot[jnp.clip(away, 0, 2 * rows - 1)]
             hit = jnp.logical_and(jnp.logical_and(inside, both), other_row >= 0)
-            mine[q, found] = row
-            theirs[q, found] = jnp.maximum(other_row, 0)
+            table[q, found] = row
+            table[q, width + found] = jnp.maximum(other_row, 0)
             return found + hit.astype(jnp.int32)
 
         lax.fori_loop(0, 2 * rows, clear, 0, unroll=10)
         lax.fori_loop(0, rows, fill, 0, unroll=10)
         lax.fori_loop(0, width, clean, 0, unroll=9)
-        number[q] = lax.fori_loop(0, rows, scan, 0, unroll=5)
-
-
-def own_kernel(domains, pairs, own, own_side, other, coef, out, share, number, mine, theirs, spot):
+        table[q, 2 * width] = lax.fori_loop(0, rows, scan, 0, unroll=5)
+
+
+def own_kernel(domains, pairs, own, own_side, other, coef, out, share, table, spot):
     rows, half, width = own.shape
     me, _, _, odd, _, _, _, _ = place_of_device()
-    find_matches(domains, number, mine, theirs, spot)
+    find_matches(domains, table, spot)
+    number, mine, theirs = lists_of(table)
     out[...] = jnp.zeros_like(out)
     size = max(n for n in range(1, 11) if rows % n == 0)
 
@@ -151,13 +157,13 @@
         for i in range(OWN_STACK):
             slot = OWN_STACK * step + i
             for part, start in ((own, odd * half), (own_side, (1 - odd) * half)):
-                left = part[mine[OWN, slot]]
-                lefts.append(jnp.where(slot < number[OWN], left, jnp.zeros_like(left)))
-                rights.append(other[theirs[OWN, slot], pl.ds(pl.multiple_of(start, 16), half), :])
+                left = part[mine(OWN, slot)]
+                lefts.append(jnp.where(slot < number(OWN), left, jnp.zeros_like(left)))
+                rights.append(other[theirs(OWN, slot), pl.ds(pl.multiple_of(start, 16), half), :])
         out[1] += multiply(jnp.concatenate(lefts, axis=0), jnp.concatenate(rights, axis=0))
         return carry
 
-    lax.fori_loop(0, (number[OWN] + OWN_STACK - 1) // OWN_STACK, beside, 0)
+    lax.fori_loop(0, (number(OWN) + OWN_STACK - 1) // OWN_STACK, beside, 0)
 
     tile = 128
     parts = []
@@ -184,18 +190,16 @@
     count = domains.shape[0]
     marks = -(-count * pairs.shape[1] // 128) * 128
     most = max(-(-rows // n) * n for n in (STACK, OWN_STACK))
-    table = jax.ShapeDtypeStruct((len(PRODUCTS), most), jnp.int32)
+    table = jax.ShapeDtypeStruct((len(PRODUCTS), 2 * most + 8), jnp.int32)
     return pl.pallas_call(
         own_kernel,
         out_shape=[
             squares(2, width),
             jax.ShapeDtypeStruct((1, 2 * half + marks), F32),
-            jax.ShapeDtypeStruct((len(PRODUCTS),), jnp.int32),
-            table,
             table,
         ],
         in_specs=smem(2) + vmem(4),
-        out_specs=vmem(2) + smem(3),
+        out_specs=vmem(2) + smem(1),
         scratch_shapes=[pltpu.SMEM((2 * rows,), jnp.int32)],
         compiler_params=pltpu.CompilerParams(vmem_limit_bytes=LIMIT),
         cost_estimate=cost(own, own_side, other),
@@ -230,50 +234,57 @@
     )(value, *shares)
 
 
-def shared_kernel(number, mine, theirs, xj, xj_side, xo, yj, yo, yo_high, near, far, total):
-    _, _, _, odd, flag, _, _, f_near = place_of_device()
-    half = xj.shape[1]
-    main = pl.ds(pl.multiple_of(odd * half, 16), half)
-    cross = pl.ds(pl.multiple_of(jnp.where(flag, odd, 1 - odd) * half, 16), half)
-
-    def product(q, first, size, block):
+def add_products(listed, table, rows_of, total):
+    number, mine, theirs = lists_of(table)
+
+    def product(q, first, size):
         lefts, rights = [], []
         left_block, right_block = PRODUCTS[q]
         for i in range(size):
             slot = first + i
-            row, other_row = mine[q, slot], theirs[q, slot]
-            if left_block == XO:
-                left = xo[row, cross if q == CROSS else main, :]
-            elif left_block == YO:
-                left = jnp.concatenate([yo[row], yo_high[row]], axis=0)
-            else:
-                left = block[left_block][row]
-            lefts.append(jnp.where(slot < number[q], left, jnp.zeros_like(left)))
-            if q == CROSS:
-                rights.append(jnp.where(flag, block[FJ][other_row], block[GJ][other_row]))
-            else:
-                rights.append(block[right_block][other_row])
+            left = rows_of(left_block, q, mine(q, slot))
+            lefts.append(jnp.where(slot < number(q), left, jnp.zeros_like(left)))
+            rights.append(rows_of(right_block, q, theirs(q, slot)))
         return multiply(jnp.concatenate(lefts, axis=0), jnp.concatenate(rights, axis=0))
 
+    most = number(listed[0])
+    for at, q in enumerate(listed):
+        most = jnp.maximum(most, number(q))
+        total[at] = product(q, 0, STACK)
+
+    def steps(size):
+        def step(i, carry):
+            for at, q in enumerate(listed):
+                total[at] += product(q, STACK + i * size, size)
+            return carry
+
+        return step
+
+    short = most <= STACK + SHORT_STACK
+    more = jnp.maximum(most - STACK, 0)
+    lax.fori_loop(0, jnp.where(short, jnp.minimum(more, 1), 0), steps(SHORT_STACK), 0)
+    lax.fori_loop(0, jnp.where(short, 0, (more + STACK - 1) // STACK), steps(STACK), 0)
+
+
+def y_kernel(table, xj, xo, yj, total):
+    odd, half = place_of_device()[3], xj.shape[1]
+    main = pl.ds(pl.multiple_of(odd * half, 16), half)
+    block = {XJ: lambda row: xj[row], YJ: lambda row: yj[row], XO: lambda row: xo[row, main, :]}
+    add_products(WITH_Y, table, lambda name, q, row: block[name](row), total)
+
+
+def shared_kernel(table, xj, xj_side, xo, yj, yo, yo_high, near, far, token, total):
+    _, _, _, odd, flag, _, _, f_near = place_of_device()
+    half = xj.shape[1]
+    cross = pl.ds(pl.multiple_of(jnp.where(flag, odd, 1 - odd) * half, 16), half)
+    block = {XJ: lambda row: xj[row], XJ_SIDE: lambda row: xj_side[row], YJ: lambda row: yj[row]}
+    block[XO] = lambda row: xo[row, cross, :]
+    block[YO] = lambda row: jnp.concatenate([yo[row], yo_high[row]], axis=0)
+
     def all_products(fj, gj):
-        block = {XJ: xj, XJ_SIDE: xj_side, YJ: yj, FJ: fj, GJ: gj}
-        most = number[SHARED[0]]
-        for at, q in enumerate(SHARED):
-            most = jnp.maximum(most, number[q])
-            total[at] = product(q, 0, STACK, block)
-
-        def steps(size):
-            def step(i, carry):
-                for at, q in enumerate(SHARED):
-                    total[at] += product(q, STACK + i * size, size, block)
-                return carry
-
-            return step
-
-        short = most <= STACK + SHORT_STACK
-        more = jnp.maximum(most - STACK, 0)
-        lax.fori_loop(0, jnp.where(short, jnp.minimum(more, 1), 0), steps(SHORT_STACK), 0)
-        lax.fori_loop(0, jnp.where(short, 0, (more + STACK - 1) // STACK), steps(STACK), 0)
+        block[FJ], block[GJ] = lambda row: fj[row], lambda row: gj[row]
+        block[None] = lambda row: jnp.where(flag, fj[row], gj[row])
+        add_products(SHARED, table, lambda name, q, row: block[name](row), total)
 
     @pl.when(f_near)
     def _():
@@ -284,18 +295,18 @@
         all_products(far, near)
 
 
-def shared_products(tables, *blocks):
-    return pl.pallas_call(
-        shared_kernel,
-        out_shape=squares(len(SHARED), blocks[0].shape[-1]),
-        in_specs=smem(len(tables)) + vmem(len(blocks)),
+def products(kernel, listed, table, *blocks):
+    return pl.pallas_call(
+        kernel,
+        out_shape=squares(len(listed), blocks[0].shape[-1]),
+        in_specs=smem(1) + vmem(len(blocks)),
         out_specs=vmem(1)[0],
         compiler_params=pltpu.CompilerParams(vmem_limit_bytes=2 * LIMIT),
         cost_estimate=cost(*blocks),
-    )(*tables, *blocks)
-
-
-def message_kernel(total, *refs):
+    )(table, *blocks)
+
+
+def message_kernel(total, with_y, *refs):
     shares, (to_near, to_far, to_mate, to_y, to_y_other, summed) = refs[:-6], refs[-6:]
     _, _, _, _, flag, _, _, f_near = place_of_device()
     width = total.shape[1]
@@ -305,10 +316,10 @@
             out[i * width:(i + 1) * width, :] = value.astype(BF16)
 
     def to_f_and_g(to_f, to_g):
-        cross = total[CROSS].T
+        cross = total[SHARED.index(CROSS)].T
         nothing = jnp.zeros_like(cross)
-        put(to_f, (total[XF].T, jnp.where(flag, cross, nothing), total[YF].T, total[YOF].T))
-        put(to_g, (total[XG].T, jnp.where(flag, nothing, cross), nothing, nothing))
+        put(to_f, (total[SHARED.index(XF)].T, jnp.where(flag, cross, nothing), total[SHARED.index(YF)].T, total[SHARED.index(YOF)].T))
+        put(to_g, (total[SHARED.index(XG)].T, jnp.where(flag, nothing, cross), nothing, nothing))
 
     @pl.when(f_near)
     def _():
@@ -318,11 +329,11 @@
     def _():
         to_f_and_g(to_far, to_near)
 
-    put(to_y, (total[XY].T, total[XYO].T, total[YF]))
+    put(to_y, (with_y[0].T, with_y[1].T, total[SHARED.index(YF)]))
     to_y[3 * width:, :] = jnp.zeros((to_y.shape[0] - 3 * width, width), BF16)
-    put(to_y_other, (total[YOF],))
-    to_mate[0] = total[XYO]
-    to_mate[1] = total[CROSS]
+    put(to_y_other, (total[SHARED.index(YOF)],))
+    to_mate[0] = with_y[1]
+    to_mate[1] = total[SHARED.index(CROSS)]
     gathered = sum(share[...] for share in shares)
     summed[...] = gathered
     lines = gathered.shape[1] // width
@@ -335,7 +346,7 @@
     to_near[4 * width:, :] = jnp.concatenate(rows, axis=0).astype(BF16)
 
 
-def messages(total, shares):
+def messages(total, with_y, shares):
     width = total.shape[-1]
     lines = -(-3 * shares[0].shape[1] // width // 16) * 16
     flat = jax.ShapeDtypeStruct
@@ -346,11 +357,11 @@
             sent(4 * width + lines + 16), sent(4 * width), squares(2, width), sent(4 * width + 16), sent(width),
             flat(shares[0].shape, F32),
         ],
-        in_specs=vmem(1 + len(shares)),
+        in_specs=vmem(2 + len(shares)),
         out_specs=vmem(6),
         compiler_params=pltpu.CompilerParams(vmem_limit_bytes=LIMIT),
         cost_estimate=cost(total, total),
-    )(total, *shares)
+    )(total, with_y, *shares)
 
 
 def coulomb_kernel(own, own_side, share, from_near, out, summed):
@@ -383,7 +394,7 @@
     return jnp.swapaxes(out, 0, 1), summed
 
 
-def band_kernel(aux, pairs, summed, own, total, from_y, from_near, from_far, from_mate, from_y_other, band, made, sems):
+def band_kernel(aux, pairs, summed, own, total, with_y, from_y, from_near, from_far, from_mate, from_y_other, band, made, sems):
     depth, width = pairs.shape[1], band.shape[1]
     me, core, _, odd, _, _, _, f_near = place_of_device()
     count = lax.axis_size("basis")
@@ -409,12 +420,12 @@
     from_g = lambda i: jnp.where(f_near, block(from_near, i), block(from_far, i))
     put(0, own[0])
     put(cross, own[1])
-    put(2 * sign, total[XY] + block(from_y, 0))
+    put(2 * sign, with_y[0] + block(from_y, 0))
     put(2 * sign + cross, from_mate[0] + block(from_y, 1))
     put(-2 * sign, block(from_y, 2) + from_f(2))
     put(-2 * sign + cross, block(from_y_other, 0) + from_f(3))
-    put(4 * sign, total[XF] + from_g(0))
-    put(-4 * sign, total[XG] + from_f(0))
+    put(4 * sign, total[SHARED.index(XF)] + from_g(0))
+    put(-4 * sign, total[SHARED.index(XG)] + from_f(0))
     put(-3 * cross, from_mate[1] + from_f(1) + from_g(1))
     for copy in copies:
         copy.wait()
@@ -470,7 +481,7 @@
     xj_side, xj, for_near, for_far = cut(own)
     yj = send(xj_side, across)
     near, far = send(for_near, to_near), send(for_far, to_far)
-    own_pairs, share, *tables = own_products(domains, pairs, xj, xj_side, xo, coefs[0])
+    own_pairs, share, table = own_products(domains, pairs, xj, xj_side, xo, coefs[0])
     share = added(shares_of(share, count, 1))
     y_low, y_high, share = relay(yj, shares_of(share, count, 2))
     yo, yo_high = send(y_low, swap), send(y_high, swap)
@@ -480,13 +491,14 @@
             shares = [added(shares)]
         shares = shares_of(shares[0], count, step)
         step *= 2
-    total = shared_products(tables, xj, xj_side, xo, yj, yo, yo_high, near, far)
-    for_near, for_far, for_mate, for_y, for_y_other, share = messages(total, shares)
+    with_y = products(y_kernel, WITH_Y, table, xj, xo, yj)
+    total = products(shared_kernel, SHARED, table, xj, xj_side, xo, yj, yo, yo_high, near, far, with_y)
+    for_near, for_far, for_mate, for_y, for_y_other, share = messages(total, with_y, shares)
     from_near, from_far = send(for_near, to_near), send(for_far, to_far)
     from_y, from_y_other = send(for_y, across), send(for_y_other, chip_route(count, lambda c: c ^ 1, swap=True))
     from_mate = send(for_mate, swap)
     coulomb_half, summed = coulomb(xj, xj_side, share, from_near)
-    band = finish(aux, pairs, summed, own_pairs, total, from_y, from_near, from_far, from_mate, from_y_other)
+    band = finish(aux, pairs, summed, own_pairs, total, with_y, from_y, from_near, from_far, from_mate, from_y_other)
     return (band[None], coulomb_half)
 
 

time: 67.4 us -> 67.3 us (level)
  waiting for transfers between devices: 32.7 us -> 31.3 us
  Pallas kernels: 16.7 us -> 17.8 us
    ppermute x11, waiting for transfers between devices: 31.9 us -> 30.5 us  [per_device(): send = lambda value, route: lax.ppermute(value, 'basis', route)]
    pallas_call x1 -> x2, Pallas kernels: 3.54 us -> 4.47 us  [products(): pl.pallas_call(kernel, out_shape=squares(len(listed), blocks[0].shape[-1]...]
  transfers between devices with their start and end apart: 14 -> 14, of which waited for: 5 -> 4; matrix products, arithmetic and copies ran while one was open for 0% -> 0% of each run, Pallas kernels for 22% -> 24%
where the time goes in v7:
time: 67.3 us; the launch traced here: 67.2 us
  waiting for transfers between devices  31.3 us (47%)
  Pallas kernels  17.8 us (26%)
  starting transfers between devices  15.1 us (22%)
  local copies, waits for them, and re-layouts  2.12 us (3%)
  between operations  0.76 us (1%)
    ppermute x11, waiting for transfers between devices, per_device(): send = lambda value, route: lax.ppermute(value, 'basis', route)  30.5 us
    pallas_call x1, Pallas kernels, own_products(): pl.pallas_call(own_kernel, out_shape=[squares(2, width), jax.ShapeDtypeSt...  9.53 us
    ppermute x11, starting transfers between devices, per_device(): send = lambda value, route: lax.ppermute(value, 'basis', route)  9.08 us
    ppermute x3, starting transfers between devices, shares_of(): lax.ppermute(values, 'basis', [(i, i ^ step) for i in range(count)])  6.07 us
    pallas_call x2, Pallas kernels, products(): pl.pallas_call(kernel, out_shape=squares(len(listed), blocks[0].shape[-1]...  4.47 us
    unnamed x8, local copies, waits for them, and re-layouts  2.12 us
    pallas_call x1, Pallas kernels, finish(): pl.pallas_call(functools.partial(band_kernel, aux), out_shape=squares(siz...  1.47 us
  transfers between devices with their start and end apart: 14, of which 4 were waited for; matrix products, arithmetic and copies ran while one was open for 0% of the time, Pallas kernels for 24%

profile of v7, /device:TPU:0, one launch (start us, length us, event | category | flops | bytes accessed | tf_op | source)
XLA Modules:
  0.0 67.2 jit_solution(10318436559552283377)
XLA Ops:
  0.6 0.5 collective-permute-start
  1.2 2.1 %copy-done = bf16[1,30,512,128]{3,2,1,0:T(8,128)(2,1)S(1)} copy-done((bf16[1,30,512,128]{3,2,1,0:T(8,128)(2,1)S(1)}, bf16[1,30,512,128]{3,2,1,0:T(8,128)(2,1)}, u32[]{:S(2)}) %copy-start) | copy-done | bytes 3932184
  3.3 0.7 %shard_map.59 = (bf16[30,256,128]{2,1,0:T(8,128)(2,1)S(1)}, bf16[30,256,128]{2,1,0:T(8,128)(2,1)S(1)}, bf16[30,256,128]{2,1,0:T(8,128)(2,1)S(1)}, bf16[30,256,128]{2,1,0:T(8,128)(2,1)S(1)}) custom-call(bf16[30,512,128]{2,1,0:T(8,128)(2,1)S(1)} %bitcast.5), custom_call_target="tpu_custom_call" | custom-call | flops 1 | bytes 7864320 | tf_op jit(solution)/shard_map/pallas_call | solution.py:78
  4.0 2.6 %collective-permute-start.1 = (bf16[30,256,128]{2,1,0:T(8,128)(2,1)S(1)}, bf16[30,256,128]{2,1,0:T(8,128)(2,1)S(1)}, u32[]{:S(2)}, u32[]{:S(2)}) collective-permute-start(bf16[30,256,128]{2,1,0:T(8,128)(2,1)S(1)} %get-tuple-element.21.own_side.xj_side), channel_id=1, source_target_pairs={{0,2},{1,3},{2,0},{3,1},{4,6},{5,7},{6,4},{7,5},{8,10},{9,11},{10,... | collective-permute-start | bytes 5898248 | tf_op jit(solution)/shard_map/ppermute | solution.py:478
  6.5 1.6 %collective-permute-start.6 = (bf16[30,256,128]{2,1,0:T(8,128)(2,1)S(1)}, bf16[30,256,128]{2,1,0:T(8,128)(2,1)S(1)}, u32[]{:S(2)}, u32[]{:S(2)}) collective-permute-start(bf16[30,256,128]{2,1,0:T(8,128)(2,1)S(1)} %get-tuple-element.26), channel_id=1, source_target_pairs={{0,4},{1,5},{2,6},{3,7},{4,0},{5,1},{6,2},{7,3},{8,12},{9,13},{10,... | collective-permute-start | bytes 5898248 | tf_op jit(solution)/shard_map/ppermute | solution.py:478
  8.2 9.5 %shard_map.60 = (f32[2,128,128]{2,1,0:T(8,128)S(1)}, f32[1,640]{1,0:T(1,128)S(1)}, s32[8,72]{1,0:T(8,128)S(1)}) custom-call(s32[16,30]{1,0:T(8,128)S(1)} %copy-done.1, s32[1,4]{1,0:T(1,128)S(1)} %copy-done.3, bf16[30,256,128]{2,1,0:T(8,128)(2,1)S(1)} %get-tuple-element.20.own.xj, bf16[30,256,128]{2,1,0:T(8,128)(2,1)S(1)} %get-tuple-element.21.own_side.xj_side, ...), custom_call_target="tpu_custom_call" | custom-call | flops 1 | bytes 7864320 | tf_op jit(solution)/shard_map/pallas_call | solution.py:194
  17.7 0.6 collective-permute-start.2
  18.3 0.8 %collective-permute-done.2.refs_1_ = f32[1,640]{1,0:T(1,128)S(1)} collective-permute-done((f32[1,640]{1,0:T(1,128)S(1)}, f32[1,640]{1,0:T(1,128)S(1)}, u32[]{:S(2)}, u32[]{:S(2)}) %collective-permute-start.2) | collective-permute-done | bytes 2592 | tf_op jit(solution)/shard_map/ppermute | solution.py:464
  19.1 2.7 %collective-permute-start.3 = (f32[1,640]{1,0:T(1,128)S(1)}, f32[1,640]{1,0:T(1,128)S(1)}, u32[]{:S(2)}, u32[]{:S(2)}) collective-permute-start(f32[1,640]{1,0:T(1,128)S(1)} %shard_map.61.refs_0_), channel_id=1, source_target_pairs={{0,2},{1,3},{2,0},{3,1},{4,6},{5,7},{6,4},{7,5},{8,10},{9,11},{10,... | collective-permute-start | bytes 7688 | tf_op jit(solution)/shard_map/ppermute | solution.py:464
  21.8 28.3 %collective-permute-done.1.value.yj = bf16[30,256,128]{2,1,0:T(8,128)(2,1)S(1)} collective-permute-done((bf16[30,256,128]{2,1,0:T(8,128)(2,1)S(1)}, bf16[30,256,128]{2,1,0:T(8,128)(2,1)S(1)}, u32[]{:S(2)}, u32[]{:S(2)}) %collective-permute-start.1) | collective-permute-done | bytes 1966112 | tf_op jit(solution)/shard_map/ppermute | solution.py:478
  50.1 0.2 shard_map.62
  50.4 0.5 collective-permute-start.5
  50.9 2.8 %collective-permute-start.8 = (f32[1,640]{1,0:T(1,128)S(1)}, f32[1,640]{1,0:T(1,128)S(1)}, u32[]{:S(2)}, u32[]{:S(2)}) collective-permute-start(f32[1,640]{1,0:T(1,128)S(1)} %get-tuple-element.28.refs_0_), channel_id=1, source_target_pairs={{0,8},{1,9},{2,10},{3,11},{4,12},{5,13},{6,14},{7,15},{8,0},{9,1},... | collective-permute-start | bytes 7688 | tf_op jit(solution)/shard_map/ppermute | solution.py:464
  53.7 1.7 %shard_map.63.token.with_y = f32[2,128,128]{2,1,0:T(8,128)S(1)} custom-call(s32[8,72]{1,0:T(8,128)S(1)} %get-tuple-element.22.table, bf16[30,256,128]{2,1,0:T(8,128)(2,1)S(1)} %get-tuple-element.20.own.xj, bf16[30,512,128]{2,1,0:T(8,128)(2,1)S(1)} %collective-permute-done.other.xo, bf16[30,256,128]{2,1,0:T(8,128)(2,1)S(1)} %collective-permute-done.1.value.yj), custom_call_target="tpu_custom_call" | custom-call | flops 1 | bytes 7864320 | tf_op jit(solution)/shard_map/pallas_call | solution.py:299
  55.4 2.8 %shard_map.64.total = f32[5,128,128]{2,1,0:T(8,128)S(1)} custom-call(s32[8,72]{1,0:T(8,128)S(1)} %get-tuple-element.22.table, bf16[30,256,128]{2,1,0:T(8,128)(2,1)S(1)} %get-tuple-element.20.own.xj, bf16[30,256,128]{2,1,0:T(8,128)(2,1)S(1)} %get-tuple-element.21.own_side.xj_side, bf16[30,512,128]{2,1,0:T(8,128)(2,1)S(1)} %collective-permute-done.other.xo, ...), custom_call_target="tpu_custom_call" | custom-call | flops 1 | bytes 15859712 | tf_op jit(solution)/shard_map/pallas_call | solution.py:299
  58.2 0.2 shard_map.65
  58.5 1.7 %collective-permute-start.9 = (bf16[544,128]{1,0:T(8,128)(2,1)S(1)}, bf16[544,128]{1,0:T(8,128)(2,1)S(1)}, u32[]{:S(2)}, u32[]{:S(2)}) collective-permute-start(bf16[544,128]{1,0:T(8,128)(2,1)S(1)} %get-tuple-element.30), channel_id=1, source_target_pairs={{0,4},{1,5},{2,6},{3,7},{4,0},{5,1},{6,2},{7,3},{8,12},{9,13},{10,... | collective-permute-start | bytes 417800 | tf_op jit(solution)/shard_map/ppermute | solution.py:478
  60.1 1.5 %collective-permute-start.10 = (bf16[528,128]{1,0:T(8,128)(2,1)S(1)}, bf16[528,128]{1,0:T(8,128)(2,1)S(1)}, u32[]{:S(2)}, u32[]{:S(2)}) collective-permute-start(bf16[528,128]{1,0:T(8,128)(2,1)S(1)} %get-tuple-element.33), channel_id=1, source_target_pairs={{0,2},{1,3},{2,0},{3,1},{4,6},{5,7},{6,4},{7,5},{8,10},{9,11},{10,... | collective-permute-start | bytes 405512 | tf_op jit(solution)/shard_map/ppermute | solution.py:478
  61.6 0.5 collective-permute-start.12
  62.1 0.2 collective-permute-start.13
  62.3 1.6 %collective-permute-done.9.from_near = bf16[544,128]{1,0:T(8,128)(2,1)S(1)} collective-permute-done((bf16[544,128]{1,0:T(8,128)(2,1)S(1)}, bf16[544,128]{1,0:T(8,128)(2,1)S(1)}, u32[]{:S(2)}, u32[]{:S(2)}) %collective-permute-start.9) | collective-permute-done | bytes 139296 | tf_op jit(solution)/shard_map/ppermute | solution.py:478
  63.9 1.3 %shard_map.66 = (f32[30,1,128]{2,1,0:T(1,128)}, f32[1,640]{1,0:T(1,128)S(1)}) custom-call(bf16[30,256,128]{2,1,0:T(8,128)(2,1)S(1)} %get-tuple-element.20.own.xj, bf16[30,256,128]{2,1,0:T(8,128)(2,1)S(1)} %get-tuple-element.21.own_side.xj_side, f32[1,640]{1,0:T(1,128)S(1)} %get-tuple-element.29.share, bf16[544,128]{1,0:T(8,128)(2,1)S(1)} %collective-permute-done.9.from_near), custom_call_target="tpu_custom_call" | custom-call | flops 1 | bytes 3932160 | tf_op jit(solution)/shard_map/pallas_call | solution.py:386
  65.1 0.6 collective-permute-done.13.from_y_other
  65.7 1.5 %shard_map.67 = f32[9,128,128]{2,1,0:T(8,128)} custom-call(s32[1,4]{1,0:T(1,128)S(1)} %copy-done.3, f32[1,640]{1,0:T(1,128)S(1)} %get-tuple-element.31.summed, f32[2,128,128]{2,1,0:T(8,128)S(1)} %get-tuple-element.32.own, f32[5,128,128]{2,1,0:T(8,128)S(1)} %shard_map.64.total, f32[2,128,128]{2,1,0:T(8,128)S(1)} %shard_map.63.token.with_y, ...), custom_call_target="tpu_custom_call" | custom-call | flops 1 | bytes 1159168 | tf_op jit(solution)/shard_map/pallas_call | solution.py:437
  (21 shorter events, 0.1 us)
Async XLA Ops:
  0.6 7.5 %collective-permute-start = (bf16[30,512,128]{2,1,0:T(8,128)(2,1)}, bf16[30,512,128]{2,1,0:T(8,128)(2,1)S(1)}, u32[]{:S(2)}, u32[]{:S(2)}) collective-permute-start(bf16[30,512,128]{2,1,0:T(8,128)(2,1)} %bitcast.4), channel_id=1, source_target_pairs={{0,1},{1,0},{2,3},{3,2},{4,5},{5,4},{6,7},{7,6},{8,9},{9,8},{10,11... | collective-permute-start | bytes 11796488 | tf_op jit(solution)/shard_map/ppermute | solution.py:478
  1.1 2.1 %copy-start = (bf16[1,30,512,128]{3,2,1,0:T(8,128)(2,1)S(1)}, bf16[1,30,512,128]{3,2,1,0:T(8,128)(2,1)}, u32[]{:S(2)}) copy-start(bf16[1,30,512,128]{3,2,1,0:T(8,128)(2,1)} %param.4) | copy-start | bytes 11796484
  3.3 4.9 %copy-start.1 = (s32[16,30]{1,0:T(8,128)S(1)}, s32[16,30]{1,0:T(8,128)}, u32[]{:S(2)}) copy-start(s32[16,30]{1,0:T(8,128)} %domains.1) | copy-start | bytes 5764
  3.3 4.9 %copy-start.2 = (bf16[1,30,128]{2,1,0:T(8,128)(2,1)S(1)}, bf16[1,30,128]{2,1,0:T(8,128)(2,1)}, u32[]{:S(2)}) copy-start(bf16[1,30,128]{2,1,0:T(8,128)(2,1)} %param.5) | copy-start | bytes 23044
  3.3 4.9 %copy-start.3 = (s32[1,4]{1,0:T(1,128)S(1)}, s32[1,4]{1,0:T(1,128)}, u32[]{:S(2)}) copy-start(s32[1,4]{1,0:T(1,128)} %pairs.3) | copy-start | bytes 52
  4.0 46.1 %collective-permute-start.1 = (bf16[30,256,128]{2,1,0:T(8,128)(2,1)S(1)}, bf16[30,256,128]{2,1,0:T(8,128)(2,1)S(1)}, u32[]{:S(2)}, u32[]{:S(2)}) collective-permute-start(bf16[30,256,128]{2,1,0:T(8,128)(2,1)S(1)} %get-tuple-element.21.own_side.xj_side), channel_id=1, source_target_pairs={{0,2},{1,3},{2,0},{3,1},{4,6},{5,7},{6,4},{7,5},{8,10},{9,11},{10,... | collective-permute-start | bytes 5898248 | tf_op jit(solution)/shard_map/ppermute | solution.py:478
  6.5 48.8 %collective-permute-start.6 = (bf16[30,256,128]{2,1,0:T(8,128)(2,1)S(1)}, bf16[30,256,128]{2,1,0:T(8,128)(2,1)S(1)}, u32[]{:S(2)}, u32[]{:S(2)}) collective-permute-start(bf16[30,256,128]{2,1,0:T(8,128)(2,1)S(1)} %get-tuple-element.26), channel_id=1, source_target_pairs={{0,4},{1,5},{2,6},{3,7},{4,0},{5,1},{6,2},{7,3},{8,12},{9,13},{10,... | collective-permute-start | bytes 5898248 | tf_op jit(solution)/shard_map/ppermute | solution.py:478
  8.1 47.3 %collective-permute-start.7 = (bf16[30,256,128]{2,1,0:T(8,128)(2,1)S(1)}, bf16[30,256,128]{2,1,0:T(8,128)(2,1)S(1)}, u32[]{:S(2)}, u32[]{:S(2)}) collective-permute-start(bf16[30,256,128]{2,1,0:T(8,128)(2,1)S(1)} %get-tuple-element.27), channel_id=1, source_target_pairs={{4,8},{5,9},{6,10},{7,11},{8,4},{9,5},{10,6},{11,7},{0,1},{1,0},{2... | collective-permute-start | bytes 5898248 | tf_op jit(solution)/shard_map/ppermute | solution.py:478
  17.7 1.4 %collective-permute-start.2 = (f32[1,640]{1,0:T(1,128)S(1)}, f32[1,640]{1,0:T(1,128)S(1)}, u32[]{:S(2)}, u32[]{:S(2)}) collective-permute-start(f32[1,640]{1,0:T(1,128)S(1)} %get-tuple-element.23.refs_0_), channel_id=1, source_target_pairs={{0,1},{1,0},{2,3},{3,2},{4,5},{5,4},{6,7},{7,6},{8,9},{9,8},{10,11... | collective-permute-start | bytes 7688 | tf_op jit(solution)/shard_map/ppermute | solution.py:464
  19.1 31.0 %collective-permute-start.3 = (f32[1,640]{1,0:T(1,128)S(1)}, f32[1,640]{1,0:T(1,128)S(1)}, u32[]{:S(2)}, u32[]{:S(2)}) collective-permute-start(f32[1,640]{1,0:T(1,128)S(1)} %shard_map.61.refs_0_), channel_id=1, source_target_pairs={{0,2},{1,3},{2,0},{3,1},{4,6},{5,7},{6,4},{7,5},{8,10},{9,11},{10,... | collective-permute-start | bytes 7688 | tf_op jit(solution)/shard_map/ppermute | solution.py:464
  50.3 5.1 %collective-permute-start.4 = (bf16[30,128,128]{2,1,0:T(8,128)(2,1)S(1)}, bf16[30,128,128]{2,1,0:T(8,128)(2,1)S(1)}, u32[]{:S(2)}, u32[]{:S(2)}) collective-permute-start(bf16[30,128,128]{2,1,0:T(8,128)(2,1)S(1)} %get-tuple-element.24), channel_id=1, source_target_pairs={{0,1},{1,0},{2,3},{3,2},{4,5},{5,4},{6,7},{7,6},{8,9},{9,8},{10,11... | collective-permute-start | bytes 2949128 | tf_op jit(solution)/shard_map/ppermute | solution.py:478
  50.4 5.0 %collective-permute-start.5 = (bf16[30,128,128]{2,1,0:T(8,128)(2,1)S(1)}, bf16[30,128,128]{2,1,0:T(8,128)(2,1)S(1)}, u32[]{:S(2)}, u32[]{:S(2)}) collective-permute-start(bf16[30,128,128]{2,1,0:T(8,128)(2,1)S(1)} %get-tuple-element.25), channel_id=1, source_target_pairs={{0,1},{1,0},{2,3},{3,2},{4,5},{5,4},{6,7},{7,6},{8,9},{9,8},{10,11... | collective-permute-start | bytes 2949128 | tf_op jit(solution)/shard_map/ppermute | solution.py:478
  50.9 7.3 %collective-permute-start.8 = (f32[1,640]{1,0:T(1,128)S(1)}, f32[1,640]{1,0:T(1,128)S(1)}, u32[]{:S(2)}, u32[]{:S(2)}) collective-permute-start(f32[1,640]{1,0:T(1,128)S(1)} %get-tuple-element.28.refs_0_), channel_id=1, source_target_pairs={{0,8},{1,9},{2,10},{3,11},{4,12},{5,13},{6,14},{7,15},{8,0},{9,1},... | collective-permute-start | bytes 7688 | tf_op jit(solution)/shard_map/ppermute | solution.py:464
  58.5 5.4 %collective-permute-start.9 = (bf16[544,128]{1,0:T(8,128)(2,1)S(1)}, bf16[544,128]{1,0:T(8,128)(2,1)S(1)}, u32[]{:S(2)}, u32[]{:S(2)}) collective-permute-start(bf16[544,128]{1,0:T(8,128)(2,1)S(1)} %get-tuple-element.30), channel_id=1, source_target_pairs={{0,4},{1,5},{2,6},{3,7},{4,0},{5,1},{6,2},{7,3},{8,12},{9,13},{10,... | collective-permute-start | bytes 417800 | tf_op jit(solution)/shard_map/ppermute | solution.py:478
  60.1 5.6 %collective-permute-start.10 = (bf16[528,128]{1,0:T(8,128)(2,1)S(1)}, bf16[528,128]{1,0:T(8,128)(2,1)S(1)}, u32[]{:S(2)}, u32[]{:S(2)}) collective-permute-start(bf16[528,128]{1,0:T(8,128)(2,1)S(1)} %get-tuple-element.33), channel_id=1, source_target_pairs={{0,2},{1,3},{2,0},{3,1},{4,6},{5,7},{6,4},{7,5},{8,10},{9,11},{10,... | collective-permute-start | bytes 405512 | tf_op jit(solution)/shard_map/ppermute | solution.py:478
  61.6 4.1 %collective-permute-start.11 = (bf16[512,128]{1,0:T(8,128)(2,1)S(1)}, bf16[512,128]{1,0:T(8,128)(2,1)S(1)}, u32[]{:S(2)}, u32[]{:S(2)}) collective-permute-start(bf16[512,128]{1,0:T(8,128)(2,1)S(1)} %get-tuple-element.34), channel_id=1, source_target_pairs={{4,8},{5,9},{6,10},{7,11},{8,4},{9,5},{10,6},{11,7},{0,1},{1,0},{2... | collective-permute-start | bytes 393224 | tf_op jit(solution)/shard_map/ppermute | solution.py:478
  61.6 4.1 %collective-permute-start.12 = (f32[2,128,128]{2,1,0:T(8,128)S(1)}, f32[2,128,128]{2,1,0:T(8,128)S(1)}, u32[]{:S(2)}, u32[]{:S(2)}) collective-permute-start(f32[2,128,128]{2,1,0:T(8,128)S(1)} %get-tuple-element.35), channel_id=1, source_target_pairs={{0,1},{1,0},{2,3},{3,2},{4,5},{5,4},{6,7},{7,6},{8,9},{9,8},{10,11... | collective-permute-start | bytes 393224 | tf_op jit(solution)/shard_map/ppermute | solution.py:478
  62.1 3.6 %collective-permute-start.13 = (bf16[128,128]{1,0:T(8,128)(2,1)S(1)}, bf16[128,128]{1,0:T(8,128)(2,1)S(1)}, u32[]{:S(2)}, u32[]{:S(2)}) collective-permute-start(bf16[128,128]{1,0:T(8,128)(2,1)S(1)} %get-tuple-element.36), channel_id=1, source_target_pairs={{0,3},{1,2},{2,1},{3,0},{4,7},{5,6},{6,5},{7,4},{8,11},{9,10},{10,... | collective-permute-start | bytes 98312 | tf_op jit(solution)/shard_map/ppermute | solution.py:478

commit v8 on v6

--- a/solution.py
+++ b/solution.py
@@ -10,12 +10,13 @@
 F32 = jnp.float32
 BF16 = jnp.bfloat16
 
-XJ, XO, XJ_SIDE, YJ, YO, YO_HIGH, FJ, GJ = range(8)
+XJ, XO, XJ_SIDE, YJ, YO, FJ, GJ = range(7)
 XF, YF, YOF, XG, XY, XYO, CROSS, OWN = range(8)
 PRODUCTS = ((XJ, FJ), (YJ, FJ), (YO, FJ), (XJ_SIDE, GJ), (XJ, YJ), (XO, YJ), (XO, None), (XJ, XO))
 SHARED = (XF, YF, YOF, XG, XY, XYO, CROSS)
 STACK, SHORT_STACK, OWN_STACK = 10, 8, 4
 LIMIT = 12 * 2**20
+LATE = 144
 
 
 def cost(*arrays):
@@ -56,15 +57,15 @@
     return me, core, chip, odd, core == odd, chip + 2 - 4 * odd, chip - 2 + 4 * odd, odd == ((chip >> 1) & 1)
 
 
-def cut_kernel(size, own, side, main, near, far, sems):
+def cut_kernel(size, own, early, late, near, far, main, side, sems):
     _, _, _, odd, _, _, _, f_near = place_of_device()
     side_start, main_start = (1 - odd) * size, odd * size
     near_start, far_start = jnp.where(f_near, side_start, main_start), jnp.where(f_near, main_start, side_start)
+    outs = (early, late, near, far, main, side)
+    starts = (side_start, side_start + size - LATE, near_start, far_start, main_start, side_start)
     copies = []
-    for i, (out, start) in enumerate(
-        ((side, side_start), (near, near_start), (far, far_start), (main, main_start))
-    ):
-        rows = pl.ds(pl.multiple_of(start, 16), size)
+    for i, (out, start) in enumerate(zip(outs, starts)):
+        rows = pl.ds(pl.multiple_of(start, 16), out.shape[1])
         copies.append(pltpu.make_async_copy(own.at[:, rows, :], out, sems.at[i]))
     for copy in copies:
         copy.start()
@@ -74,21 +75,27 @@
 
 def cut(own):
     rows, aux, width = own.shape
-    part = jax.ShapeDtypeStruct((rows, aux // 2, width), own.dtype)
-    return pl.pallas_call(
-        functools.partial(cut_kernel, aux // 2),
-        out_shape=[part] * 4,
+    half = aux // 2
+    sizes = (half - LATE, LATE, half, half, half, half)
+    return pl.pallas_call(
+        functools.partial(cut_kernel, half),
+        out_shape=[jax.ShapeDtypeStruct((rows, size, width), own.dtype) for size in sizes],
         in_specs=vmem(1),
-        out_specs=vmem(4),
-        scratch_shapes=[pltpu.SemaphoreType.DMA((4,))],
+        out_specs=vmem(6),
+        scratch_shapes=[pltpu.SemaphoreType.DMA((6,))],
         compiler_params=pltpu.CompilerParams(vmem_limit_bytes=LIMIT),
         cost_estimate=cost(own, own),
     )(own)
 
 
-def find_matches(domains, number, mine, theirs, spot):
+def lists_of(table):
+    width = table.shape[1] // 2 - 4
+    return lambda q: table[q, 2 * width], lambda q, slot: table[q, slot], lambda q, slot: table[q, width + slot]
+
+
+def find_matches(domains, table, spot):
     count, rows = domains.shape
-    width = mine.shape[1]
+    width = table.shape[1] // 2 - 4
     _, core, chip, _, flag, f_chip, g_chip, _ = place_of_device()
     mine_first, other_first = (chip, core), (chip, 1 - core)
     block = {XJ: mine_first, XJ_SIDE: mine_first, XO: other_first, None: (jnp.where(flag, f_chip, g_chip), core)}
@@ -112,8 +119,8 @@
             return carry
 
         def clean(slot, carry):
-            mine[q, slot] = 0
-            theirs[q, slot] = 0
+            table[q, slot] = 0
+            table[q, width + slot] = 0
             return carry
 
         def scan(row, found):
@@ -121,20 +128,21 @@
             inside = jnp.logical_and(away >= 0, away < 2 * rows)
             other_row = spot[jnp.clip(away, 0, 2 * rows - 1)]
             hit = jnp.logical_and(jnp.logical_and(inside, both), other_row >= 0)
-            mine[q, found] = row
-            theirs[q, found] = jnp.maximum(other_row, 0)
+            table[q, found] = row
+            table[q, width + found] = jnp.maximum(other_row, 0)
             return found + hit.astype(jnp.int32)
 
         lax.fori_loop(0, 2 * rows, clear, 0, unroll=10)
         lax.fori_loop(0, rows, fill, 0, unroll=10)
         lax.fori_loop(0, width, clean, 0, unroll=9)
-        number[q] = lax.fori_loop(0, rows, scan, 0, unroll=5)
-
-
-def own_kernel(domains, pairs, own, own_side, other, coef, out, share, number, mine, theirs, spot):
+        table[q, 2 * width] = lax.fori_loop(0, rows, scan, 0, unroll=5)
+
+
+def own_kernel(domains, pairs, own, own_side, other, coef, out, share, table, spot):
     rows, half, width = own.shape
     me, _, _, odd, _, _, _, _ = place_of_device()
-    find_matches(domains, number, mine, theirs, spot)
+    find_matches(domains, table, spot)
+    number, mine, theirs = lists_of(table)
     out[...] = jnp.zeros_like(out)
     size = max(n for n in range(1, 11) if rows % n == 0)
 
@@ -151,13 +159,13 @@
         for i in range(OWN_STACK):
             slot = OWN_STACK * step + i
             for part, start in ((own, odd * half), (own_side, (1 - odd) * half)):
-                left = part[mine[OWN, slot]]
-                lefts.append(jnp.where(slot < number[OWN], left, jnp.zeros_like(left)))
-                rights.append(other[theirs[OWN, slot], pl.ds(pl.multiple_of(start, 16), half), :])
+                left = part[mine(OWN, slot)]
+                lefts.append(jnp.where(slot < number(OWN), left, jnp.zeros_like(left)))
+                rights.append(other[theirs(OWN, slot), pl.ds(pl.multiple_of(start, 16), half), :])
         out[1] += multiply(jnp.concatenate(lefts, axis=0), jnp.concatenate(rights, axis=0))
         return carry
 
-    lax.fori_loop(0, (number[OWN] + OWN_STACK - 1) // OWN_STACK, beside, 0)
+    lax.fori_loop(0, (number(OWN) + OWN_STACK - 1) // OWN_STACK, beside, 0)
 
     tile = 128
     parts = []
@@ -184,31 +192,29 @@
     count = domains.shape[0]
     marks = -(-count * pairs.shape[1] // 128) * 128
     most = max(-(-rows // n) * n for n in (STACK, OWN_STACK))
-    table = jax.ShapeDtypeStruct((len(PRODUCTS), most), jnp.int32)
+    table = jax.ShapeDtypeStruct((len(PRODUCTS), 2 * most + 8), jnp.int32)
     return pl.pallas_call(
         own_kernel,
         out_shape=[
             squares(2, width),
             jax.ShapeDtypeStruct((1, 2 * half + marks), F32),
-            jax.ShapeDtypeStruct((len(PRODUCTS),), jnp.int32),
-            table,
             table,
         ],
         in_specs=smem(2) + vmem(4),
-        out_specs=vmem(2) + smem(3),
+        out_specs=vmem(2) + smem(1),
         scratch_shapes=[pltpu.SMEM((2 * rows,), jnp.int32)],
         compiler_params=pltpu.CompilerParams(vmem_limit_bytes=LIMIT),
         cost_estimate=cost(own, own_side, other),
     )(domains, pairs, own, own_side, other, coef)
 
 
-def relay_kernel(value, *refs):
-    shares, (low, high, total, sems) = refs[:-4], refs[-4:]
-    size = low.shape[1]
-    copies = [
-        pltpu.make_async_copy(value.at[:, :size, :], low, sems.at[0]),
-        pltpu.make_async_copy(value.at[:, size:, :], high, sems.at[1]),
-    ]
+def relay_kernel(count, parts, value, *refs):
+    shares, (*outs, total, sems) = refs[:count], refs[-parts - 2:]
+    copies, start = [], 0
+    for i, out in enumerate(outs):
+        size = out.shape[1]
+        copies.append(pltpu.make_async_copy(value.at[:, start:start + size, :], out, sems.at[i]))
+        start += size
     for copy in copies:
         copy.start()
     total[...] = sum(share[...] for share in shares)
@@ -216,23 +222,25 @@
         copy.wait()
 
 
-def relay(value, shares):
-    rows, size, width = value.shape
-    part = jax.ShapeDtypeStruct((rows, size // 2, width), value.dtype)
-    return pl.pallas_call(
-        relay_kernel,
-        out_shape=[part, part, jax.ShapeDtypeStruct(shares[0].shape, F32)],
-        in_specs=vmem(1 + len(shares)),
-        out_specs=vmem(3),
-        scratch_shapes=[pltpu.SemaphoreType.DMA((2,))],
+def relay(value, sizes, shares, *earlier):
+    rows, _, width = value.shape
+    parts = len(sizes)
+    return pl.pallas_call(
+        functools.partial(relay_kernel, len(shares), parts),
+        out_shape=[jax.ShapeDtypeStruct((rows, size, width), value.dtype) for size in sizes] + [jax.ShapeDtypeStruct(shares[0].shape, F32)],
+        in_specs=vmem(1 + len(shares) + len(earlier)),
+        out_specs=vmem(parts + 1),
+        scratch_shapes=[pltpu.SemaphoreType.DMA((parts,))],
         compiler_params=pltpu.CompilerParams(vmem_limit_bytes=LIMIT),
         cost_estimate=cost(value, value),
-    )(value, *shares)
-
-
-def shared_kernel(number, mine, theirs, xj, xj_side, xo, yj, yo, yo_high, near, far, total):
+    )(value, *shares, *earlier)
+
+
+def shared_kernel(table, xj, xj_side, xo, near, far, *refs):
+    yj, yo, total = refs[:2], refs[2:-1], refs[-1]
     _, _, _, odd, flag, _, _, f_near = place_of_device()
     half = xj.shape[1]
+    number, mine, theirs = lists_of(table)
     main = pl.ds(pl.multiple_of(odd * half, 16), half)
     cross = pl.ds(pl.multiple_of(jnp.where(flag, odd, 1 - odd) * half, 16), half)
 
@@ -241,25 +249,29 @@
         left_block, right_block = PRODUCTS[q]
         for i in range(size):
             slot = first + i
-            row, other_row = mine[q, slot], theirs[q, slot]
+            row, other_row = mine(q, slot), theirs(q, slot)
             if left_block == XO:
                 left = xo[row, cross if q == CROSS else main, :]
             elif left_block == YO:
-                left = jnp.concatenate([yo[row], yo_high[row]], axis=0)
+                left = jnp.concatenate([part[row] for part in yo], axis=0)
+            elif left_block == YJ:
+                left = jnp.concatenate([part[row] for part in yj], axis=0)
             else:
                 left = block[left_block][row]
-            lefts.append(jnp.where(slot < number[q], left, jnp.zeros_like(left)))
+            lefts.append(jnp.where(slot < number(q), left, jnp.zeros_like(left)))
             if q == CROSS:
                 rights.append(jnp.where(flag, block[FJ][other_row], block[GJ][other_row]))
+            elif right_block == YJ:
+                rights.append(jnp.concatenate([part[other_row] for part in yj], axis=0))
             else:
                 rights.append(block[right_block][other_row])
         return multiply(jnp.concatenate(lefts, axis=0), jnp.concatenate(rights, axis=0))
 
     def all_products(fj, gj):
-        block = {XJ: xj, XJ_SIDE: xj_side, YJ: yj, FJ: fj, GJ: gj}
-        most = number[SHARED[0]]
+        block = {XJ: xj, XJ_SIDE: xj_side, FJ: fj, GJ: gj}
+        most = number(SHARED[0])
         for at, q in enumerate(SHARED):
-            most = jnp.maximum(most, number[q])
+            most = jnp.maximum(most, number(q))
             total[at] = product(q, 0, STACK, block)
 
         def steps(size):
@@ -284,15 +296,15 @@
         all_products(far, near)
 
 
-def shared_products(tables, *blocks):
+def shared_products(table, *blocks):
     return pl.pallas_call(
         shared_kernel,
         out_shape=squares(len(SHARED), blocks[0].shape[-1]),
-        in_specs=smem(len(tables)) + vmem(len(blocks)),
+        in_specs=smem(1) + vmem(len(blocks)),
         out_specs=vmem(1)[0],
         compiler_params=pltpu.CompilerParams(vmem_limit_bytes=2 * LIMIT),
         cost_estimate=cost(*blocks),
-    )(*tables, *blocks)
+    )(table, *blocks)
 
 
 def message_kernel(total, *refs):
@@ -467,20 +479,23 @@
     send = lambda value, route: lax.ppermute(value, "basis", route)
 
     xo = send(own, swap)
-    xj_side, xj, for_near, for_far = cut(own)
-    yj = send(xj_side, across)
+    early, late, for_near, for_far, xj, xj_side = cut(own)
+    yj = send(early, across), send(late, across)
     near, far = send(for_near, to_near), send(for_far, to_far)
-    own_pairs, share, *tables = own_products(domains, pairs, xj, xj_side, xo, coefs[0])
+    own_pairs, share, table = own_products(domains, pairs, xj, xj_side, xo, coefs[0])
     share = added(shares_of(share, count, 1))
-    y_low, y_high, share = relay(yj, shares_of(share, count, 2))
-    yo, yo_high = send(y_low, swap), send(y_high, swap)
+    part, _ = relay(yj[0], (yj[0].shape[1],), [share])
+    yo = [send(part, swap)]
+    first = LATE // 32 * 16 + LATE % 32
+    *parts, share = relay(yj[1], (first, LATE - first), shares_of(share, count, 2), *yo)
+    yo += [send(part, swap) for part in parts]
     shares, step = [share], 8
     while step < count:
         if len(shares) > 1:
             shares = [added(shares)]
         shares = shares_of(shares[0], count, step)
         step *= 2
-    total = shared_products(tables, xj, xj_side, xo, yj, yo, yo_high, near, far)
+    total = shared_products(table, xj, xj_side, xo, near, far, *yj, *yo)
     for_near, for_far, for_mate, for_y, for_y_other, share = messages(total, shares)
     from_near, from_far = send(for_near, to_near), send(for_far, to_far)
     from_y, from_y_other = send(for_y, across), send(for_y_other, chip_route(count, lambda c: c ^ 1, swap=True))

time: 67.4 us -> 66.5 us (0.987)
  waiting for transfers between devices: 32.7 us -> 30.5 us
  Pallas kernels: 16.7 us -> 18.2 us
    ppermute x11 -> x13, waiting for transfers between devices: 31.9 us -> 29.6 us  [per_device(): send = lambda value, route: lax.ppermute(value, 'basis', route)]
    pallas_call x2 -> x3, Pallas kernels: 0.89 us -> 1.7 us  [the longest x1 0.86 us: cut(): pl.pallas_call(functools.partial(cut_kernel, half), out_shape=[jax.ShapeD...]
    ppermute x11 -> x13, starting transfers between devices: 9.26 us -> 9.63 us  [per_device(): send = lambda value, route: lax.ppermute(value, 'basis', route)]
  transfers between devices with their start and end apart: 14 -> 16, of which waited for: 5 -> 5; matrix products, arithmetic and copies ran while one was open for 0% -> 0% of each run, Pallas kernels for 22% -> 25%
where the time goes in v8:
time: 66.5 us; the launch traced here: 66.3 us
  waiting for transfers between devices  30.5 us (46%)
  Pallas kernels  18.2 us (27%)
  starting transfers between devices  14.7 us (22%)
  local copies, waits for them, and re-layouts  2.12 us (3%)
  between operations  0.74 us (1%)
    ppermute x13, waiting for transfers between devices, per_device(): send = lambda value, route: lax.ppermute(value, 'basis', route)  29.6 us
    pallas_call x1, Pallas kernels, own_products(): pl.pallas_call(own_kernel, out_shape=[squares(2, width), jax.ShapeDtypeSt...  9.91 us
    ppermute x13, starting transfers between devices, per_device(): send = lambda value, route: lax.ppermute(value, 'basis', route)  9.63 us
    ppermute x3, starting transfers between devices, shares_of(): lax.ppermute(values, 'basis', [(i, i ^ step) for i in range(count)])  5.1 us
    pallas_call x1, Pallas kernels, shared_products(): pl.pallas_call(shared_kernel, out_shape=squares(len(SHARED), blocks[0].sh...  3.58 us
    unnamed x8, local copies, waits for them, and re-layouts  2.12 us
    pallas_call x1, Pallas kernels, finish(): pl.pallas_call(functools.partial(band_kernel, aux), out_shape=squares(siz...  1.47 us
  transfers between devices with their start and end apart: 16, of which 5 were waited for; matrix products, arithmetic and copies ran while one was open for 0% of the time, Pallas kernels for 25%

profile of v8, /device:TPU:0, one launch (start us, length us, event | category | flops | bytes accessed | tf_op | source)
XLA Modules:
  0.0 66.3 jit_solution(562049891898401775)
XLA Ops:
  0.6 0.5 collective-permute-start
  1.2 2.1 %copy-done = bf16[1,30,512,128]{3,2,1,0:T(8,128)(2,1)S(1)} copy-done((bf16[1,30,512,128]{3,2,1,0:T(8,128)(2,1)S(1)}, bf16[1,30,512,128]{3,2,1,0:T(8,128)(2,1)}, u32[]{:S(2)}) %copy-start) | copy-done | bytes 3932184
  3.3 0.9 %shard_map.59 = (bf16[30,112,128]{2,1,0:T(8,128)(2,1)S(1)}, bf16[30,144,128]{2,1,0:T(8,128)(2,1)S(1)}, bf16[30,256,128]{2,1,0:T(8,128)(2,1)S(1)}, bf16[30,256,12...) custom-call(bf16[30,512,128]{2,1,0:T(8,128)(2,1)S(1)} %bitcast.5), custom_call_target="tpu_custom_call" | custom-call | flops 1 | bytes 7864320 | tf_op jit(solution)/shard_map/pallas_call | solution.py:80
  4.1 2.6 %collective-permute-start.3 = (bf16[30,112,128]{2,1,0:T(8,128)(2,1)S(1)}, bf16[30,112,128]{2,1,0:T(8,128)(2,1)S(1)}, u32[]{:S(2)}, u32[]{:S(2)}) collective-permute-start(bf16[30,112,128]{2,1,0:T(8,128)(2,1)S(1)} %get-tuple-element.28), channel_id=1, source_target_pairs={{0,2},{1,3},{2,0},{3,1},{4,6},{5,7},{6,4},{7,5},{8,10},{9,11},{10,... | collective-permute-start | bytes 2580488 | tf_op jit(solution)/shard_map/ppermute | solution.py:479
  6.7 1.6 %collective-permute-start.1 = (bf16[30,256,128]{2,1,0:T(8,128)(2,1)S(1)}, bf16[30,256,128]{2,1,0:T(8,128)(2,1)S(1)}, u32[]{:S(2)}, u32[]{:S(2)}) collective-permute-start(bf16[30,256,128]{2,1,0:T(8,128)(2,1)S(1)} %get-tuple-element.26), channel_id=1, source_target_pairs={{0,4},{1,5},{2,6},{3,7},{4,0},{5,1},{6,2},{7,3},{8,12},{9,13},{10,... | collective-permute-start | bytes 5898248 | tf_op jit(solution)/shard_map/ppermute | solution.py:479
  8.3 0.5 collective-permute-start.4
  8.8 9.9 %shard_map.60 = (f32[2,128,128]{2,1,0:T(8,128)S(1)}, f32[1,640]{1,0:T(1,128)S(1)}, s32[8,72]{1,0:T(8,128)S(1)}) custom-call(s32[16,30]{1,0:T(8,128)S(1)} %copy-done.1, s32[1,4]{1,0:T(1,128)S(1)} %copy-done.3, bf16[30,256,128]{2,1,0:T(8,128)(2,1)S(1)} %get-tuple-element.23.own.xj, bf16[30,256,128]{2,1,0:T(8,128)(2,1)S(1)} %get-tuple-element.24.own_side.xj_side, ...), custom_call_target="tpu_custom_call" | custom-call | flops 1 | bytes 7864320 | tf_op jit(solution)/shard_map/pallas_call | solution.py:196
  18.8 0.3 collective-permute-start.5
  19.0 0.9 %collective-permute-done.5.refs_1_ = f32[1,640]{1,0:T(1,128)S(1)} collective-permute-done((f32[1,640]{1,0:T(1,128)S(1)}, f32[1,640]{1,0:T(1,128)S(1)}, u32[]{:S(2)}, u32[]{:S(2)}) %collective-permute-start.5) | collective-permute-done | bytes 2592 | tf_op jit(solution)/shard_map/ppermute | solution.py:465
  20.0 6.7 %collective-permute-done.3.value.refs_0_ = bf16[30,112,128]{2,1,0:T(8,128)(2,1)S(1)} collective-permute-done((bf16[30,112,128]{2,1,0:T(8,128)(2,1)S(1)}, bf16[30,112,128]{2,1,0:T(8,128)(2,1)S(1)}, u32[]{:S(2)}, u32[]{:S(2)}) %collective-permute-start.3) | collective-permute-done | bytes 860192 | tf_op jit(solution)/shard_map/ppermute | solution.py:479
  26.7 0.7 %shard_map.62 = (bf16[30,112,128]{2,1,0:T(8,128)(2,1)S(1)}, f32[1,640]{1,0:T(1,128)}) custom-call(bf16[30,112,128]{2,1,0:T(8,128)(2,1)S(1)} %collective-permute-done.3.value.refs_0_, f32[1,640]{1,0:T(1,128)S(1)} %shard_map.61.refs_0_), custom_call_target="tpu_custom_call" | custom-call | flops 1 | bytes 1720320 | tf_op jit(solution)/shard_map/pallas_call | solution.py:228
  27.5 2.0 %collective-permute-start.7 = (f32[1,640]{1,0:T(1,128)S(1)}, f32[1,640]{1,0:T(1,128)S(1)}, u32[]{:S(2)}, u32[]{:S(2)}) collective-permute-start(f32[1,640]{1,0:T(1,128)S(1)} %shard_map.61.refs_0_), channel_id=1, source_target_pairs={{0,2},{1,3},{2,0},{3,1},{4,6},{5,7},{6,4},{7,5},{8,10},{9,11},{10,... | collective-permute-start | bytes 7688 | tf_op jit(solution)/shard_map/ppermute | solution.py:465
  29.5 20.7 %collective-permute-done.4.value.refs_1_ = bf16[30,144,128]{2,1,0:T(8,128)(2,1)S(1)} collective-permute-done((bf16[30,144,128]{2,1,0:T(8,128)(2,1)S(1)}, bf16[30,144,128]{2,1,0:T(8,128)(2,1)S(1)}, u32[]{:S(2)}, u32[]{:S(2)}) %collective-permute-start.4) | collective-permute-done | bytes 1105952 | tf_op jit(solution)/shard_map/ppermute | solution.py:479
  50.5 0.5 collective-permute-start.9
  51.0 2.8 %collective-permute-start.10 = (f32[1,640]{1,0:T(1,128)S(1)}, f32[1,640]{1,0:T(1,128)S(1)}, u32[]{:S(2)}, u32[]{:S(2)}) collective-permute-start(f32[1,640]{1,0:T(1,128)S(1)} %get-tuple-element.34.refs_0_), channel_id=1, source_target_pairs={{0,8},{1,9},{2,10},{3,11},{4,12},{5,13},{6,14},{7,15},{8,0},{9,1},... | collective-permute-start | bytes 7688 | tf_op jit(solution)/shard_map/ppermute | solution.py:465
  53.8 3.6 %shard_map.64.total = f32[7,128,128]{2,1,0:T(8,128)S(1)} custom-call(s32[8,72]{1,0:T(8,128)S(1)} %get-tuple-element.25.table, bf16[30,256,128]{2,1,0:T(8,128)(2,1)S(1)} %get-tuple-element.23.own.xj, bf16[30,256,128]{2,1,0:T(8,128)(2,1)S(1)} %get-tuple-element.24.own_side.xj_side, bf16[30,512,128]{2,1,0:T(8,128)(2,1)S(1)} %collective-permute-done.other.xo, ...), custom_call_target="tpu_custom_call" | custom-call | flops 1 | bytes 15728640 | tf_op jit(solution)/shard_map/pallas_call | solution.py:300
  57.4 0.2 shard_map.65
  57.6 1.7 %collective-permute-start.11 = (bf16[544,128]{1,0:T(8,128)(2,1)S(1)}, bf16[544,128]{1,0:T(8,128)(2,1)S(1)}, u32[]{:S(2)}, u32[]{:S(2)}) collective-permute-start(bf16[544,128]{1,0:T(8,128)(2,1)S(1)} %get-tuple-element.36), channel_id=1, source_target_pairs={{0,4},{1,5},{2,6},{3,7},{4,0},{5,1},{6,2},{7,3},{8,12},{9,13},{10,... | collective-permute-start | bytes 417800 | tf_op jit(solution)/shard_map/ppermute | solution.py:479
  59.3 1.5 %collective-permute-start.12 = (bf16[528,128]{1,0:T(8,128)(2,1)S(1)}, bf16[528,128]{1,0:T(8,128)(2,1)S(1)}, u32[]{:S(2)}, u32[]{:S(2)}) collective-permute-start(bf16[528,128]{1,0:T(8,128)(2,1)S(1)} %get-tuple-element.39), channel_id=1, source_target_pairs={{0,2},{1,3},{2,0},{3,1},{4,6},{5,7},{6,4},{7,5},{8,10},{9,11},{10,... | collective-permute-start | bytes 405512 | tf_op jit(solution)/shard_map/ppermute | solution.py:479
  60.8 0.5 collective-permute-start.14
  61.4 1.6 %collective-permute-done.11.from_near = bf16[544,128]{1,0:T(8,128)(2,1)S(1)} collective-permute-done((bf16[544,128]{1,0:T(8,128)(2,1)S(1)}, bf16[544,128]{1,0:T(8,128)(2,1)S(1)}, u32[]{:S(2)}, u32[]{:S(2)}) %collective-permute-start.11) | collective-permute-done | bytes 139296 | tf_op jit(solution)/shard_map/ppermute | solution.py:479
  63.1 1.3 %shard_map.66 = (f32[30,1,128]{2,1,0:T(1,128)}, f32[1,640]{1,0:T(1,128)S(1)}) custom-call(bf16[30,256,128]{2,1,0:T(8,128)(2,1)S(1)} %get-tuple-element.23.own.xj, bf16[30,256,128]{2,1,0:T(8,128)(2,1)S(1)} %get-tuple-element.24.own_side.xj_side, f32[1,640]{1,0:T(1,128)S(1)} %get-tuple-element.35.share, bf16[544,128]{1,0:T(8,128)(2,1)S(1)} %collective-permute-done.11.from_near), custom_call_target="tpu_custom_call" | custom-call | flops 1 | bytes 3932160 | tf_op jit(solution)/shard_map/pallas_call | solution.py:387
  64.4 0.5 collective-permute-done.15.from_y_other
  64.8 1.5 %shard_map.67 = f32[9,128,128]{2,1,0:T(8,128)} custom-call(s32[1,4]{1,0:T(1,128)S(1)} %copy-done.3, f32[1,640]{1,0:T(1,128)S(1)} %get-tuple-element.37.summed, f32[2,128,128]{2,1,0:T(8,128)S(1)} %get-tuple-element.38.own, f32[7,128,128]{2,1,0:T(8,128)S(1)} %shard_map.64.total, bf16[528,128]{1,0:T(8,128)(2,1)S(1)} %collective-permute-done.12.from_y, ...), custom_call_target="tpu_custom_call" | custom-call | flops 1 | bytes 1159168 | tf_op jit(solution)/shard_map/pallas_call | solution.py:438
  (25 shorter events, 0.5 us)
Async XLA Ops:
  0.6 8.2 %collective-permute-start = (bf16[30,512,128]{2,1,0:T(8,128)(2,1)}, bf16[30,512,128]{2,1,0:T(8,128)(2,1)S(1)}, u32[]{:S(2)}, u32[]{:S(2)}) collective-permute-start(bf16[30,512,128]{2,1,0:T(8,128)(2,1)} %bitcast.4), channel_id=1, source_target_pairs={{0,1},{1,0},{2,3},{3,2},{4,5},{5,4},{6,7},{7,6},{8,9},{9,8},{10,11... | collective-permute-start | bytes 11796488 | tf_op jit(solution)/shard_map/ppermute | solution.py:479
  1.1 2.1 %copy-start = (bf16[1,30,512,128]{3,2,1,0:T(8,128)(2,1)S(1)}, bf16[1,30,512,128]{3,2,1,0:T(8,128)(2,1)}, u32[]{:S(2)}) copy-start(bf16[1,30,512,128]{3,2,1,0:T(8,128)(2,1)} %param.4) | copy-start | bytes 11796484
  3.3 5.6 %copy-start.1 = (s32[16,30]{1,0:T(8,128)S(1)}, s32[16,30]{1,0:T(8,128)}, u32[]{:S(2)}) copy-start(s32[16,30]{1,0:T(8,128)} %domains.1) | copy-start | bytes 5764
  3.3 5.6 %copy-start.2 = (bf16[1,30,128]{2,1,0:T(8,128)(2,1)S(1)}, bf16[1,30,128]{2,1,0:T(8,128)(2,1)}, u32[]{:S(2)}) copy-start(bf16[1,30,128]{2,1,0:T(8,128)(2,1)} %param.5) | copy-start | bytes 23044
  3.3 5.6 %copy-start.3 = (s32[1,4]{1,0:T(1,128)S(1)}, s32[1,4]{1,0:T(1,128)}, u32[]{:S(2)}) copy-start(s32[1,4]{1,0:T(1,128)} %pairs.3) | copy-start | bytes 52
  4.1 22.6 %collective-permute-start.3 = (bf16[30,112,128]{2,1,0:T(8,128)(2,1)S(1)}, bf16[30,112,128]{2,1,0:T(8,128)(2,1)S(1)}, u32[]{:S(2)}, u32[]{:S(2)}) collective-permute-start(bf16[30,112,128]{2,1,0:T(8,128)(2,1)S(1)} %get-tuple-element.28), channel_id=1, source_target_pairs={{0,2},{1,3},{2,0},{3,1},{4,6},{5,7},{6,4},{7,5},{8,10},{9,11},{10,... | collective-permute-start | bytes 2580488 | tf_op jit(solution)/shard_map/ppermute | solution.py:479
  6.7 47.0 %collective-permute-start.1 = (bf16[30,256,128]{2,1,0:T(8,128)(2,1)S(1)}, bf16[30,256,128]{2,1,0:T(8,128)(2,1)S(1)}, u32[]{:S(2)}, u32[]{:S(2)}) collective-permute-start(bf16[30,256,128]{2,1,0:T(8,128)(2,1)S(1)} %get-tuple-element.26), channel_id=1, source_target_pairs={{0,4},{1,5},{2,6},{3,7},{4,0},{5,1},{6,2},{7,3},{8,12},{9,13},{10,... | collective-permute-start | bytes 5898248 | tf_op jit(solution)/shard_map/ppermute | solution.py:479
  8.3 45.5 %collective-permute-start.2 = (bf16[30,256,128]{2,1,0:T(8,128)(2,1)S(1)}, bf16[30,256,128]{2,1,0:T(8,128)(2,1)S(1)}, u32[]{:S(2)}, u32[]{:S(2)}) collective-permute-start(bf16[30,256,128]{2,1,0:T(8,128)(2,1)S(1)} %get-tuple-element.27), channel_id=1, source_target_pairs={{4,8},{5,9},{6,10},{7,11},{8,4},{9,5},{10,6},{11,7},{0,1},{1,0},{2... | collective-permute-start | bytes 5898248 | tf_op jit(solution)/shard_map/ppermute | solution.py:479
  8.3 41.9 %collective-permute-start.4 = (bf16[30,144,128]{2,1,0:T(8,128)(2,1)S(1)}, bf16[30,144,128]{2,1,0:T(8,128)(2,1)S(1)}, u32[]{:S(2)}, u32[]{:S(2)}) collective-permute-start(bf16[30,144,128]{2,1,0:T(8,128)(2,1)S(1)} %get-tuple-element.29), channel_id=1, source_target_pairs={{0,2},{1,3},{2,0},{3,1},{4,6},{5,7},{6,4},{7,5},{8,10},{9,11},{10,... | collective-permute-start | bytes 3317768 | tf_op jit(solution)/shard_map/ppermute | solution.py:479
  18.8 1.2 %collective-permute-start.5 = (f32[1,640]{1,0:T(1,128)S(1)}, f32[1,640]{1,0:T(1,128)S(1)}, u32[]{:S(2)}, u32[]{:S(2)}) collective-permute-start(f32[1,640]{1,0:T(1,128)S(1)} %get-tuple-element.30.refs_0_), channel_id=1, source_target_pairs={{0,1},{1,0},{2,3},{3,2},{4,5},{5,4},{6,7},{7,6},{8,9},{9,8},{10,11... | collective-permute-start | bytes 7688 | tf_op jit(solution)/shard_map/ppermute | solution.py:465
  27.4 22.8 %collective-permute-start.6 = (bf16[30,112,128]{2,1,0:T(8,128)(2,1)S(1)}, bf16[30,112,128]{2,1,0:T(8,128)(2,1)S(1)}, u32[]{:S(2)}, u32[]{:S(2)}) collective-permute-start(bf16[30,112,128]{2,1,0:T(8,128)(2,1)S(1)} %get-tuple-element.31), channel_id=1, source_target_pairs={{0,1},{1,0},{2,3},{3,2},{4,5},{5,4},{6,7},{7,6},{8,9},{9,8},{10,11... | collective-permute-start | bytes 2580488 | tf_op jit(solution)/shard_map/ppermute | solution.py:479
  27.5 22.7 %collective-permute-start.7 = (f32[1,640]{1,0:T(1,128)S(1)}, f32[1,640]{1,0:T(1,128)S(1)}, u32[]{:S(2)}, u32[]{:S(2)}) collective-permute-start(f32[1,640]{1,0:T(1,128)S(1)} %shard_map.61.refs_0_), channel_id=1, source_target_pairs={{0,2},{1,3},{2,0},{3,1},{4,6},{5,7},{6,4},{7,5},{8,10},{9,11},{10,... | collective-permute-start | bytes 7688 | tf_op jit(solution)/shard_map/ppermute | solution.py:465
  50.4 3.4 %collective-permute-start.8 = (bf16[30,80,128]{2,1,0:T(8,128)(2,1)S(1)}, bf16[30,80,128]{2,1,0:T(8,128)(2,1)S(1)}, u32[]{:S(2)}, u32[]{:S(2)}) collective-permute-start(bf16[30,80,128]{2,1,0:T(8,128)(2,1)S(1)} %get-tuple-element.32), channel_id=1, source_target_pairs={{0,1},{1,0},{2,3},{3,2},{4,5},{5,4},{6,7},{7,6},{8,9},{9,8},{10,11... | collective-permute-start | bytes 1843208 | tf_op jit(solution)/shard_map/ppermute | solution.py:479
  50.5 3.3 %collective-permute-start.9 = (bf16[30,64,128]{2,1,0:T(8,128)(2,1)S(1)}, bf16[30,64,128]{2,1,0:T(8,128)(2,1)S(1)}, u32[]{:S(2)}, u32[]{:S(2)}) collective-permute-start(bf16[30,64,128]{2,1,0:T(8,128)(2,1)S(1)} %get-tuple-element.33), channel_id=1, source_target_pairs={{0,1},{1,0},{2,3},{3,2},{4,5},{5,4},{6,7},{7,6},{8,9},{9,8},{10,11... | collective-permute-start | bytes 1474568 | tf_op jit(solution)/shard_map/ppermute | solution.py:479
  51.0 6.4 %collective-permute-start.10 = (f32[1,640]{1,0:T(1,128)S(1)}, f32[1,640]{1,0:T(1,128)S(1)}, u32[]{:S(2)}, u32[]{:S(2)}) collective-permute-start(f32[1,640]{1,0:T(1,128)S(1)} %get-tuple-element.34.refs_0_), channel_id=1, source_target_pairs={{0,8},{1,9},{2,10},{3,11},{4,12},{5,13},{6,14},{7,15},{8,0},{9,1},... | collective-permute-start | bytes 7688 | tf_op jit(solution)/shard_map/ppermute | solution.py:465
  57.6 5.4 %collective-permute-start.11 = (bf16[544,128]{1,0:T(8,128)(2,1)S(1)}, bf16[544,128]{1,0:T(8,128)(2,1)S(1)}, u32[]{:S(2)}, u32[]{:S(2)}) collective-permute-start(bf16[544,128]{1,0:T(8,128)(2,1)S(1)} %get-tuple-element.36), channel_id=1, source_target_pairs={{0,4},{1,5},{2,6},{3,7},{4,0},{5,1},{6,2},{7,3},{8,12},{9,13},{10,... | collective-permute-start | bytes 417800 | tf_op jit(solution)/shard_map/ppermute | solution.py:479
  59.3 5.5 %collective-permute-start.12 = (bf16[528,128]{1,0:T(8,128)(2,1)S(1)}, bf16[528,128]{1,0:T(8,128)(2,1)S(1)}, u32[]{:S(2)}, u32[]{:S(2)}) collective-permute-start(bf16[528,128]{1,0:T(8,128)(2,1)S(1)} %get-tuple-element.39), channel_id=1, source_target_pairs={{0,2},{1,3},{2,0},{3,1},{4,6},{5,7},{6,4},{7,5},{8,10},{9,11},{10,... | collective-permute-start | bytes 405512 | tf_op jit(solution)/shard_map/ppermute | solution.py:479
  60.8 4.0 %collective-permute-start.13 = (bf16[512,128]{1,0:T(8,128)(2,1)S(1)}, bf16[512,128]{1,0:T(8,128)(2,1)S(1)}, u32[]{:S(2)}, u32[]{:S(2)}) collective-permute-start(bf16[512,128]{1,0:T(8,128)(2,1)S(1)} %get-tuple-element.40), channel_id=1, source_target_pairs={{4,8},{5,9},{6,10},{7,11},{8,4},{9,5},{10,6},{11,7},{0,1},{1,0},{2... | collective-permute-start | bytes 393224 | tf_op jit(solution)/shard_map/ppermute | solution.py:479
  60.8 4.0 %collective-permute-start.14 = (f32[2,128,128]{2,1,0:T(8,128)S(1)}, f32[2,128,128]{2,1,0:T(8,128)S(1)}, u32[]{:S(2)}, u32[]{:S(2)}) collective-permute-start(f32[2,128,128]{2,1,0:T(8,128)S(1)} %get-tuple-element.41), channel_id=1, source_target_pairs={{0,1},{1,0},{2,3},{3,2},{4,5},{5,4},{6,7},{7,6},{8,9},{9,8},{10,11... | collective-permute-start | bytes 393224 | tf_op jit(solution)/shard_map/ppermute | solution.py:479
  61.3 3.5 %collective-permute-start.15 = (bf16[128,128]{1,0:T(8,128)(2,1)S(1)}, bf16[128,128]{1,0:T(8,128)(2,1)S(1)}, u32[]{:S(2)}, u32[]{:S(2)}) collective-permute-start(bf16[128,128]{1,0:T(8,128)(2,1)S(1)} %get-tuple-element.42), channel_id=1, source_target_pairs={{0,3},{1,2},{2,1},{3,0},{4,7},{5,6},{6,5},{7,4},{8,11},{9,10},{10,... | collective-permute-start | bytes 98312 | tf_op jit(solution)/shard_map/ppermute | solution.py:479

commit v9 on v8

--- a/solution.py
+++ b/solution.py
@@ -236,43 +236,72 @@
     )(value, *shares, *earlier)
 
 
-def shared_kernel(table, xj, xj_side, xo, near, far, *refs):
+def rows_product(table, q, first, size, left_of, right_of):
+    number, mine, theirs = lists_of(table)
+    lefts, rights = [], []
+    for i in range(size):
+        slot = first + i
+        left = left_of(mine(q, slot))
+        lefts.append(jnp.where(slot < number(q), left, jnp.zeros_like(left)))
+        rights.append(right_of(theirs(q, slot)))
+    return multiply(jnp.concatenate(lefts, axis=0), jnp.concatenate(rights, axis=0))
+
+
+def early_kernel(table, xj, xo, yj, total):
+    odd, (half, size) = place_of_device()[3], (xj.shape[1], yj.shape[1])
+    main = pl.ds(pl.multiple_of(odd * half, 16), size)
+    lefts = lambda row: xj[row, :size, :], lambda row: xo[row, main, :]
+    number, _, _ = lists_of(table)
+    for at, q in enumerate((XY, XYO)):
+        total[at] = jnp.zeros(total.shape[1:], F32)
+
+        def step(group, carry, at=at, q=q):
+            total[at] += rows_product(table, q, group * STACK, STACK, lefts[at], lambda row: yj[row])
+            return carry
+
+        lax.fori_loop(0, (number(q) + STACK - 1) // STACK, step, 0)
+
+
+def early_products(table, xj, xo, yj):
+    return pl.pallas_call(
+        early_kernel,
+        out_shape=squares(2, xj.shape[-1]),
+        in_specs=smem(1) + vmem(3),
+        out_specs=vmem(1)[0],
+        compiler_params=pltpu.CompilerParams(vmem_limit_bytes=2 * LIMIT),
+        cost_estimate=cost(xj, xo, yj),
+    )(table, xj, xo, yj)
+
+
+def shared_kernel(table, xj, xj_side, xo, near, far, early, *refs):
     yj, yo, total = refs[:2], refs[2:-1], refs[-1]
     _, _, _, odd, flag, _, _, f_near = place_of_device()
-    half = xj.shape[1]
-    number, mine, theirs = lists_of(table)
-    main = pl.ds(pl.multiple_of(odd * half, 16), half)
+    half, done = xj.shape[1], yj[0].shape[1]
+    number, _, _ = lists_of(table)
+    late = pl.ds(pl.multiple_of(odd * half + done, 16), half - done)
     cross = pl.ds(pl.multiple_of(jnp.where(flag, odd, 1 - odd) * half, 16), half)
+    joined = lambda parts: lambda row: jnp.concatenate([part[row] for part in parts], axis=0)
 
     def product(q, first, size, block):
-        lefts, rights = [], []
-        left_block, right_block = PRODUCTS[q]
-        for i in range(size):
-            slot = first + i
-            row, other_row = mine(q, slot), theirs(q, slot)
-            if left_block == XO:
-                left = xo[row, cross if q == CROSS else main, :]
-            elif left_block == YO:
-                left = jnp.concatenate([part[row] for part in yo], axis=0)
-            elif left_block == YJ:
-                left = jnp.concatenate([part[row] for part in yj], axis=0)
-            else:
-                left = block[left_block][row]
-            lefts.append(jnp.where(slot < number(q), left, jnp.zeros_like(left)))
-            if q == CROSS:
-                rights.append(jnp.where(flag, block[FJ][other_row], block[GJ][other_row]))
-            elif right_block == YJ:
-                rights.append(jnp.concatenate([part[other_row] for part in yj], axis=0))
-            else:
-                rights.append(block[right_block][other_row])
-        return multiply(jnp.concatenate(lefts, axis=0), jnp.concatenate(rights, axis=0))
+        left_of, right_of = {
+            XF: (lambda row: xj[row], lambda row: block[FJ][row]),
+            YF: (joined(yj), lambda row: block[FJ][row]),
+            YOF: (joined(yo), lambda row: block[FJ][row]),
+            XG: (lambda row: xj_side[row], lambda row: block[GJ][row]),
+            XY: (lambda row: xj[row, done:, :], lambda row: yj[1][row]),
+            XYO: (lambda row: xo[row, late, :], lambda row: yj[1][row]),
+            CROSS: (lambda row: xo[row, cross, :], lambda row: jnp.where(flag, block[FJ][row], block[GJ][row])),
+        }[q]
+        return rows_product(table, q, first, size, left_of, right_of)
 
     def all_products(fj, gj):
-        block = {XJ: xj, XJ_SIDE: xj_side, FJ: fj, GJ: gj}
+        block = {FJ: fj, GJ: gj}
         most = number(SHARED[0])
         for at, q in enumerate(SHARED):
             most = jnp.maximum(most, number(q))
             total[at] = product(q, 0, STACK, block)
+            if q in (XY, XYO):
+                total[at] += early[(XY, XYO).index(q)]
 
         def steps(size):
             def step(i, carry):
@@ -484,10 +513,11 @@
     near, far = send(for_near, to_near), send(for_far, to_far)
     own_pairs, share, table = own_products(domains, pairs, xj, xj_side, xo, coefs[0])
     share = added(shares_of(share, count, 1))
+    with_y = early_products(table, xj, xo, yj[0])
     part, _ = relay(yj[0], (yj[0].shape[1],), [share])
     yo = [send(part, swap)]
     first = LATE // 32 * 16 + LATE % 32
-    *parts, share = relay(yj[1], (first, LATE - first), shares_of(share, count, 2), *yo)
+    *parts, share = relay(yj[1], (first, LATE - first), shares_of(share, count, 2), with_y, *yo)
     yo += [send(part, swap) for part in parts]
     shares, step = [share], 8
     while step < count:
@@ -495,7 +525,7 @@
             shares = [added(shares)]
         shares = shares_of(shares[0], count, step)
         step *= 2
-    total = shared_products(table, xj, xj_side, xo, near, far, *yj, *yo)
+    total = shared_products(table, xj, xj_side, xo, near, far, with_y, *yj, *yo)
     for_near, for_far, for_mate, for_y, for_y_other, share = messages(total, shares)
     from_near, from_far = send(for_near, to_near), send(for_far, to_far)
     from_y, from_y_other = send(for_y, across), send(for_y_other, chip_route(count, lambda c: c ^ 1, swap=True))

time: 66.5 us -> 66.2 us (level)
  waiting for transfers between devices: 30.5 us -> 29.1 us
  Pallas kernels: 18.2 us -> 19.3 us
    pallas_call x0 -> x1, Pallas kernels: none -> 1.83 us  [early_products(): pl.pallas_call(early_kernel, out_shape=squares(2, xj.shape[-1]), in_specs...]
    ppermute x13, waiting for transfers between devices: 29.6 us -> 28.1 us  [per_device(): send = lambda value, route: lax.ppermute(value, 'basis', route)]
  transfers between devices with their start and end apart: 16 -> 16, of which waited for: 5 -> 5; matrix products, arithmetic and copies ran while one was open for 0% -> 0% of each run, Pallas kernels for 25% -> 27%
where the time goes in v9:
time: 66.2 us; the launch traced here: 66 us
  waiting for transfers between devices  29.1 us (44%)
  Pallas kernels  19.3 us (29%)
  starting transfers between devices  14.7 us (22%)
  local copies, waits for them, and re-layouts  2.12 us (3%)
  between operations  0.75 us (1%)
    ppermute x13, waiting for transfers between devices, per_device(): send = lambda value, route: lax.ppermute(value, 'basis', route)  28.1 us
    ppermute x13, starting transfers between devices, per_device(): send = lambda value, route: lax.ppermute(value, 'basis', route)  9.63 us
    pallas_call x1, Pallas kernels, own_products(): pl.pallas_call(own_kernel, out_shape=[squares(2, width), jax.ShapeDtypeSt...  9.53 us
    ppermute x3, starting transfers between devices, shares_of(): lax.ppermute(values, 'basis', [(i, i ^ step) for i in range(count)])  5.11 us
    pallas_call x1, Pallas kernels, shared_products(): pl.pallas_call(shared_kernel, out_shape=squares(len(SHARED), blocks[0].sh...  3.33 us
    unnamed x8, local copies, waits for them, and re-layouts  2.12 us
    pallas_call x1, Pallas kernels, early_products(): pl.pallas_call(early_kernel, out_shape=squares(2, xj.shape[-1]), in_specs...  1.83 us
    pallas_call x1, Pallas kernels, finish(): pl.pallas_call(functools.partial(band_kernel, aux), out_shape=squares(siz...  1.47 us
  transfers between devices with their start and end apart: 16, of which 5 were waited for; matrix products, arithmetic and copies ran while one was open for 0% of the time, Pallas kernels for 27%

profile of v9, /device:TPU:0, one launch (start us, length us, event | category | flops | bytes accessed | tf_op | source)
XLA Modules:
  0.0 66.0 jit_solution(12775362938900015183)
XLA Ops:
  0.6 0.5 collective-permute-start
  1.2 2.1 %copy-done = bf16[1,30,512,128]{3,2,1,0:T(8,128)(2,1)S(1)} copy-done((bf16[1,30,512,128]{3,2,1,0:T(8,128)(2,1)S(1)}, bf16[1,30,512,128]{3,2,1,0:T(8,128)(2,1)}, u32[]{:S(2)}) %copy-start) | copy-done | bytes 3932184
  3.3 0.8 %shard_map.59 = (bf16[30,112,128]{2,1,0:T(8,128)(2,1)S(1)}, bf16[30,144,128]{2,1,0:T(8,128)(2,1)S(1)}, bf16[30,256,128]{2,1,0:T(8,128)(2,1)S(1)}, bf16[30,256,12...) custom-call(bf16[30,512,128]{2,1,0:T(8,128)(2,1)S(1)} %bitcast.5), custom_call_target="tpu_custom_call" | custom-call | flops 1 | bytes 7864320 | tf_op jit(solution)/shard_map/pallas_call | solution.py:80
  4.1 2.6 %collective-permute-start.3 = (bf16[30,112,128]{2,1,0:T(8,128)(2,1)S(1)}, bf16[30,112,128]{2,1,0:T(8,128)(2,1)S(1)}, u32[]{:S(2)}, u32[]{:S(2)}) collective-permute-start(bf16[30,112,128]{2,1,0:T(8,128)(2,1)S(1)} %get-tuple-element.28), channel_id=1, source_target_pairs={{0,2},{1,3},{2,0},{3,1},{4,6},{5,7},{6,4},{7,5},{8,10},{9,11},{10,... | collective-permute-start | bytes 2580488 | tf_op jit(solution)/shard_map/ppermute | solution.py:508
  6.7 1.6 %collective-permute-start.1 = (bf16[30,256,128]{2,1,0:T(8,128)(2,1)S(1)}, bf16[30,256,128]{2,1,0:T(8,128)(2,1)S(1)}, u32[]{:S(2)}, u32[]{:S(2)}) collective-permute-start(bf16[30,256,128]{2,1,0:T(8,128)(2,1)S(1)} %get-tuple-element.26), channel_id=1, source_target_pairs={{0,4},{1,5},{2,6},{3,7},{4,0},{5,1},{6,2},{7,3},{8,12},{9,13},{10,... | collective-permute-start | bytes 5898248 | tf_op jit(solution)/shard_map/ppermute | solution.py:508
  8.3 0.5 collective-permute-start.4
  8.8 9.5 %shard_map.60 = (f32[2,128,128]{2,1,0:T(8,128)S(1)}, f32[1,640]{1,0:T(1,128)S(1)}, s32[8,72]{1,0:T(8,128)S(1)}) custom-call(s32[16,30]{1,0:T(8,128)S(1)} %copy-done.1, s32[1,4]{1,0:T(1,128)S(1)} %copy-done.3, bf16[30,256,128]{2,1,0:T(8,128)(2,1)S(1)} %get-tuple-element.23.own.xj, bf16[30,256,128]{2,1,0:T(8,128)(2,1)S(1)} %get-tuple-element.24.own_side.xj_side, ...), custom_call_target="tpu_custom_call" | custom-call | flops 1 | bytes 7864320 | tf_op jit(solution)/shard_map/pallas_call | solution.py:196
  18.3 0.3 collective-permute-start.5
  18.6 0.9 %collective-permute-done.5.refs_1_ = f32[1,640]{1,0:T(1,128)S(1)} collective-permute-done((f32[1,640]{1,0:T(1,128)S(1)}, f32[1,640]{1,0:T(1,128)S(1)}, u32[]{:S(2)}, u32[]{:S(2)}) %collective-permute-start.5) | collective-permute-done | bytes 2592 | tf_op jit(solution)/shard_map/ppermute | solution.py:494
  19.6 7.1 %collective-permute-done.3.yj.value.refs_0_ = bf16[30,112,128]{2,1,0:T(8,128)(2,1)S(1)} collective-permute-done((bf16[30,112,128]{2,1,0:T(8,128)(2,1)S(1)}, bf16[30,112,128]{2,1,0:T(8,128)(2,1)S(1)}, u32[]{:S(2)}, u32[]{:S(2)}) %collective-permute-start.3) | collective-permute-done | bytes 860192 | tf_op jit(solution)/shard_map/ppermute | solution.py:508
  26.7 0.7 %shard_map.63 = (bf16[30,112,128]{2,1,0:T(8,128)(2,1)S(1)}, f32[1,640]{1,0:T(1,128)}) custom-call(bf16[30,112,128]{2,1,0:T(8,128)(2,1)S(1)} %collective-permute-done.3.yj.value.refs_0_, f32[1,640]{1,0:T(1,128)S(1)} %shard_map.62.refs_0_), custom_call_target="tpu_custom_call" | custom-call | flops 1 | bytes 1720320 | tf_op jit(solution)/shard_map/pallas_call | solution.py:228
  27.5 2.0 %collective-permute-start.7 = (f32[1,640]{1,0:T(1,128)S(1)}, f32[1,640]{1,0:T(1,128)S(1)}, u32[]{:S(2)}, u32[]{:S(2)}) collective-permute-start(f32[1,640]{1,0:T(1,128)S(1)} %shard_map.62.refs_0_), channel_id=1, source_target_pairs={{0,2},{1,3},{2,0},{3,1},{4,6},{5,7},{6,4},{7,5},{8,10},{9,11},{10,... | collective-permute-start | bytes 7688 | tf_op jit(solution)/shard_map/ppermute | solution.py:494
  29.5 1.8 %shard_map.61.refs_2_.early = f32[2,128,128]{2,1,0:T(8,128)S(1)} custom-call(s32[8,72]{1,0:T(8,128)S(1)} %get-tuple-element.25.table, bf16[30,256,128]{2,1,0:T(8,128)(2,1)S(1)} %get-tuple-element.23.own.xj, bf16[30,512,128]{2,1,0:T(8,128)(2,1)S(1)} %collective-permute-done.other.xo, bf16[30,112,128]{2,1,0:T(8,128)(2,1)S(1)} %collective-permute-done.3.yj.value.refs_0_), custom_call_target="tpu_custom_call" | custom-call | flops 1 | bytes 6758400 | tf_op jit(solution)/shard_map/pallas_call | solution.py:266
  31.3 18.9 %collective-permute-done.4.value.refs_1_ = bf16[30,144,128]{2,1,0:T(8,128)(2,1)S(1)} collective-permute-done((bf16[30,144,128]{2,1,0:T(8,128)(2,1)S(1)}, bf16[30,144,128]{2,1,0:T(8,128)(2,1)S(1)}, u32[]{:S(2)}, u32[]{:S(2)}) %collective-permute-start.4) | collective-permute-done | bytes 1105952 | tf_op jit(solution)/shard_map/ppermute | solution.py:508
  50.4 0.5 collective-permute-start.9
  50.9 2.8 %collective-permute-start.10 = (f32[1,640]{1,0:T(1,128)S(1)}, f32[1,640]{1,0:T(1,128)S(1)}, u32[]{:S(2)}, u32[]{:S(2)}) collective-permute-start(f32[1,640]{1,0:T(1,128)S(1)} %get-tuple-element.34.refs_0_), channel_id=1, source_target_pairs={{0,8},{1,9},{2,10},{3,11},{4,12},{5,13},{6,14},{7,15},{8,0},{9,1},... | collective-permute-start | bytes 7688 | tf_op jit(solution)/shard_map/ppermute | solution.py:494
  53.8 3.3 %shard_map.65.total = f32[7,128,128]{2,1,0:T(8,128)S(1)} custom-call(s32[8,72]{1,0:T(8,128)S(1)} %get-tuple-element.25.table, bf16[30,256,128]{2,1,0:T(8,128)(2,1)S(1)} %get-tuple-element.23.own.xj, bf16[30,256,128]{2,1,0:T(8,128)(2,1)S(1)} %get-tuple-element.24.own_side.xj_side, bf16[30,512,128]{2,1,0:T(8,128)(2,1)S(1)} %collective-permute-done.other.xo, ...), custom_call_target="tpu_custom_call" | custom-call | flops 1 | bytes 15859712 | tf_op jit(solution)/shard_map/pallas_call | solution.py:329
  57.4 1.6 %collective-permute-start.11 = (bf16[544,128]{1,0:T(8,128)(2,1)S(1)}, bf16[544,128]{1,0:T(8,128)(2,1)S(1)}, u32[]{:S(2)}, u32[]{:S(2)}) collective-permute-start(bf16[544,128]{1,0:T(8,128)(2,1)S(1)} %get-tuple-element.36), channel_id=1, source_target_pairs={{0,4},{1,5},{2,6},{3,7},{4,0},{5,1},{6,2},{7,3},{8,12},{9,13},{10,... | collective-permute-start | bytes 417800 | tf_op jit(solution)/shard_map/ppermute | solution.py:508
  59.0 1.5 %collective-permute-start.12 = (bf16[528,128]{1,0:T(8,128)(2,1)S(1)}, bf16[528,128]{1,0:T(8,128)(2,1)S(1)}, u32[]{:S(2)}, u32[]{:S(2)}) collective-permute-start(bf16[528,128]{1,0:T(8,128)(2,1)S(1)} %get-tuple-element.39), channel_id=1, source_target_pairs={{0,2},{1,3},{2,0},{3,1},{4,6},{5,7},{6,4},{7,5},{8,10},{9,11},{10,... | collective-permute-start | bytes 405512 | tf_op jit(solution)/shard_map/ppermute | solution.py:508
  60.5 0.5 collective-permute-start.14
  61.2 1.7 %collective-permute-done.11.from_near = bf16[544,128]{1,0:T(8,128)(2,1)S(1)} collective-permute-done((bf16[544,128]{1,0:T(8,128)(2,1)S(1)}, bf16[544,128]{1,0:T(8,128)(2,1)S(1)}, u32[]{:S(2)}, u32[]{:S(2)}) %collective-permute-start.11) | collective-permute-done | bytes 139296 | tf_op jit(solution)/shard_map/ppermute | solution.py:508
  62.8 1.2 %shard_map.67 = (f32[30,1,128]{2,1,0:T(1,128)}, f32[1,640]{1,0:T(1,128)S(1)}) custom-call(bf16[30,256,128]{2,1,0:T(8,128)(2,1)S(1)} %get-tuple-element.23.own.xj, bf16[30,256,128]{2,1,0:T(8,128)(2,1)S(1)} %get-tuple-element.24.own_side.xj_side, f32[1,640]{1,0:T(1,128)S(1)} %get-tuple-element.35.share, bf16[544,128]{1,0:T(8,128)(2,1)S(1)} %collective-permute-done.11.from_near), custom_call_target="tpu_custom_call" | custom-call | flops 1 | bytes 3932160 | tf_op jit(solution)/shard_map/pallas_call | solution.py:416
  64.1 0.5 collective-permute-done.15.from_y_other
  64.6 1.5 %shard_map.68 = f32[9,128,128]{2,1,0:T(8,128)} custom-call(s32[1,4]{1,0:T(1,128)S(1)} %copy-done.3, f32[1,640]{1,0:T(1,128)S(1)} %get-tuple-element.37.summed, f32[2,128,128]{2,1,0:T(8,128)S(1)} %get-tuple-element.38.own, f32[7,128,128]{2,1,0:T(8,128)S(1)} %shard_map.65.total, bf16[528,128]{1,0:T(8,128)(2,1)S(1)} %collective-permute-done.12.from_y, ...), custom_call_target="tpu_custom_call" | custom-call | flops 1 | bytes 1159168 | tf_op jit(solution)/shard_map/pallas_call | solution.py:467
  (26 shorter events, 0.7 us)
Async XLA Ops:
  0.6 8.2 %collective-permute-start = (bf16[30,512,128]{2,1,0:T(8,128)(2,1)}, bf16[30,512,128]{2,1,0:T(8,128)(2,1)S(1)}, u32[]{:S(2)}, u32[]{:S(2)}) collective-permute-start(bf16[30,512,128]{2,1,0:T(8,128)(2,1)} %bitcast.4), channel_id=1, source_target_pairs={{0,1},{1,0},{2,3},{3,2},{4,5},{5,4},{6,7},{7,6},{8,9},{9,8},{10,11... | collective-permute-start | bytes 11796488 | tf_op jit(solution)/shard_map/ppermute | solution.py:508
  1.1 2.1 %copy-start = (bf16[1,30,512,128]{3,2,1,0:T(8,128)(2,1)S(1)}, bf16[1,30,512,128]{3,2,1,0:T(8,128)(2,1)}, u32[]{:S(2)}) copy-start(bf16[1,30,512,128]{3,2,1,0:T(8,128)(2,1)} %param.4) | copy-start | bytes 11796484
  3.3 5.5 %copy-start.1 = (s32[16,30]{1,0:T(8,128)S(1)}, s32[16,30]{1,0:T(8,128)}, u32[]{:S(2)}) copy-start(s32[16,30]{1,0:T(8,128)} %domains.1) | copy-start | bytes 5764
  3.3 5.5 %copy-start.2 = (bf16[1,30,128]{2,1,0:T(8,128)(2,1)S(1)}, bf16[1,30,128]{2,1,0:T(8,128)(2,1)}, u32[]{:S(2)}) copy-start(bf16[1,30,128]{2,1,0:T(8,128)(2,1)} %param.5) | copy-start | bytes 23044
  3.3 5.5 %copy-start.3 = (s32[1,4]{1,0:T(1,128)S(1)}, s32[1,4]{1,0:T(1,128)}, u32[]{:S(2)}) copy-start(s32[1,4]{1,0:T(1,128)} %pairs.3) | copy-start | bytes 52
  4.1 22.6 %collective-permute-start.3 = (bf16[30,112,128]{2,1,0:T(8,128)(2,1)S(1)}, bf16[30,112,128]{2,1,0:T(8,128)(2,1)S(1)}, u32[]{:S(2)}, u32[]{:S(2)}) collective-permute-start(bf16[30,112,128]{2,1,0:T(8,128)(2,1)S(1)} %get-tuple-element.28), channel_id=1, source_target_pairs={{0,2},{1,3},{2,0},{3,1},{4,6},{5,7},{6,4},{7,5},{8,10},{9,11},{10,... | collective-permute-start | bytes 2580488 | tf_op jit(solution)/shard_map/ppermute | solution.py:508
  6.7 47.0 %collective-permute-start.1 = (bf16[30,256,128]{2,1,0:T(8,128)(2,1)S(1)}, bf16[30,256,128]{2,1,0:T(8,128)(2,1)S(1)}, u32[]{:S(2)}, u32[]{:S(2)}) collective-permute-start(bf16[30,256,128]{2,1,0:T(8,128)(2,1)S(1)} %get-tuple-element.26), channel_id=1, source_target_pairs={{0,4},{1,5},{2,6},{3,7},{4,0},{5,1},{6,2},{7,3},{8,12},{9,13},{10,... | collective-permute-start | bytes 5898248 | tf_op jit(solution)/shard_map/ppermute | solution.py:508
  8.3 45.5 %collective-permute-start.2 = (bf16[30,256,128]{2,1,0:T(8,128)(2,1)S(1)}, bf16[30,256,128]{2,1,0:T(8,128)(2,1)S(1)}, u32[]{:S(2)}, u32[]{:S(2)}) collective-permute-start(bf16[30,256,128]{2,1,0:T(8,128)(2,1)S(1)} %get-tuple-element.27), channel_id=1, source_target_pairs={{4,8},{5,9},{6,10},{7,11},{8,4},{9,5},{10,6},{11,7},{0,1},{1,0},{2... | collective-permute-start | bytes 5898248 | tf_op jit(solution)/shard_map/ppermute | solution.py:508
  8.3 41.9 %collective-permute-start.4 = (bf16[30,144,128]{2,1,0:T(8,128)(2,1)S(1)}, bf16[30,144,128]{2,1,0:T(8,128)(2,1)S(1)}, u32[]{:S(2)}, u32[]{:S(2)}) collective-permute-start(bf16[30,144,128]{2,1,0:T(8,128)(2,1)S(1)} %get-tuple-element.29), channel_id=1, source_target_pairs={{0,2},{1,3},{2,0},{3,1},{4,6},{5,7},{6,4},{7,5},{8,10},{9,11},{10,... | collective-permute-start | bytes 3317768 | tf_op jit(solution)/shard_map/ppermute | solution.py:508
  18.3 1.2 %collective-permute-start.5 = (f32[1,640]{1,0:T(1,128)S(1)}, f32[1,640]{1,0:T(1,128)S(1)}, u32[]{:S(2)}, u32[]{:S(2)}) collective-permute-start(f32[1,640]{1,0:T(1,128)S(1)} %get-tuple-element.30.refs_0_), channel_id=1, source_target_pairs={{0,1},{1,0},{2,3},{3,2},{4,5},{5,4},{6,7},{7,6},{8,9},{9,8},{10,11... | collective-permute-start | bytes 7688 | tf_op jit(solution)/shard_map/ppermute | solution.py:494
  27.4 22.8 %collective-permute-start.6 = (bf16[30,112,128]{2,1,0:T(8,128)(2,1)S(1)}, bf16[30,112,128]{2,1,0:T(8,128)(2,1)S(1)}, u32[]{:S(2)}, u32[]{:S(2)}) collective-permute-start(bf16[30,112,128]{2,1,0:T(8,128)(2,1)S(1)} %get-tuple-element.31), channel_id=1, source_target_pairs={{0,1},{1,0},{2,3},{3,2},{4,5},{5,4},{6,7},{7,6},{8,9},{9,8},{10,11... | collective-permute-start | bytes 2580488 | tf_op jit(solution)/shard_map/ppermute | solution.py:508
  27.5 22.7 %collective-permute-start.7 = (f32[1,640]{1,0:T(1,128)S(1)}, f32[1,640]{1,0:T(1,128)S(1)}, u32[]{:S(2)}, u32[]{:S(2)}) collective-permute-start(f32[1,640]{1,0:T(1,128)S(1)} %shard_map.62.refs_0_), channel_id=1, source_target_pairs={{0,2},{1,3},{2,0},{3,1},{4,6},{5,7},{6,4},{7,5},{8,10},{9,11},{10,... | collective-permute-start | bytes 7688 | tf_op jit(solution)/shard_map/ppermute | solution.py:494
  50.4 3.4 %collective-permute-start.8 = (bf16[30,80,128]{2,1,0:T(8,128)(2,1)S(1)}, bf16[30,80,128]{2,1,0:T(8,128)(2,1)S(1)}, u32[]{:S(2)}, u32[]{:S(2)}) collective-permute-start(bf16[30,80,128]{2,1,0:T(8,128)(2,1)S(1)} %get-tuple-element.32), channel_id=1, source_target_pairs={{0,1},{1,0},{2,3},{3,2},{4,5},{5,4},{6,7},{7,6},{8,9},{9,8},{10,11... | collective-permute-start | bytes 1843208 | tf_op jit(solution)/shard_map/ppermute | solution.py:508
  50.4 3.3 %collective-permute-start.9 = (bf16[30,64,128]{2,1,0:T(8,128)(2,1)S(1)}, bf16[30,64,128]{2,1,0:T(8,128)(2,1)S(1)}, u32[]{:S(2)}, u32[]{:S(2)}) collective-permute-start(bf16[30,64,128]{2,1,0:T(8,128)(2,1)S(1)} %get-tuple-element.33), channel_id=1, source_target_pairs={{0,1},{1,0},{2,3},{3,2},{4,5},{5,4},{6,7},{7,6},{8,9},{9,8},{10,11... | collective-permute-start | bytes 1474568 | tf_op jit(solution)/shard_map/ppermute | solution.py:508
  50.9 6.2 %collective-permute-start.10 = (f32[1,640]{1,0:T(1,128)S(1)}, f32[1,640]{1,0:T(1,128)S(1)}, u32[]{:S(2)}, u32[]{:S(2)}) collective-permute-start(f32[1,640]{1,0:T(1,128)S(1)} %get-tuple-element.34.refs_0_), channel_id=1, source_target_pairs={{0,8},{1,9},{2,10},{3,11},{4,12},{5,13},{6,14},{7,15},{8,0},{9,1},... | collective-permute-start | bytes 7688 | tf_op jit(solution)/shard_map/ppermute | solution.py:494
  57.4 5.5 %collective-permute-start.11 = (bf16[544,128]{1,0:T(8,128)(2,1)S(1)}, bf16[544,128]{1,0:T(8,128)(2,1)S(1)}, u32[]{:S(2)}, u32[]{:S(2)}) collective-permute-start(bf16[544,128]{1,0:T(8,128)(2,1)S(1)} %get-tuple-element.36), channel_id=1, source_target_pairs={{0,4},{1,5},{2,6},{3,7},{4,0},{5,1},{6,2},{7,3},{8,12},{9,13},{10,... | collective-permute-start | bytes 417800 | tf_op jit(solution)/shard_map/ppermute | solution.py:508
  59.0 5.5 %collective-permute-start.12 = (bf16[528,128]{1,0:T(8,128)(2,1)S(1)}, bf16[528,128]{1,0:T(8,128)(2,1)S(1)}, u32[]{:S(2)}, u32[]{:S(2)}) collective-permute-start(bf16[528,128]{1,0:T(8,128)(2,1)S(1)} %get-tuple-element.39), channel_id=1, source_target_pairs={{0,2},{1,3},{2,0},{3,1},{4,6},{5,7},{6,4},{7,5},{8,10},{9,11},{10,... | collective-permute-start | bytes 405512 | tf_op jit(solution)/shard_map/ppermute | solution.py:508
  60.5 4.0 %collective-permute-start.13 = (bf16[512,128]{1,0:T(8,128)(2,1)S(1)}, bf16[512,128]{1,0:T(8,128)(2,1)S(1)}, u32[]{:S(2)}, u32[]{:S(2)}) collective-permute-start(bf16[512,128]{1,0:T(8,128)(2,1)S(1)} %get-tuple-element.40), channel_id=1, source_target_pairs={{4,8},{5,9},{6,10},{7,11},{8,4},{9,5},{10,6},{11,7},{0,1},{1,0},{2... | collective-permute-start | bytes 393224 | tf_op jit(solution)/shard_map/ppermute | solution.py:508
  60.5 4.0 %collective-permute-start.14 = (f32[2,128,128]{2,1,0:T(8,128)S(1)}, f32[2,128,128]{2,1,0:T(8,128)S(1)}, u32[]{:S(2)}, u32[]{:S(2)}) collective-permute-start(f32[2,128,128]{2,1,0:T(8,128)S(1)} %get-tuple-element.41), channel_id=1, source_target_pairs={{0,1},{1,0},{2,3},{3,2},{4,5},{5,4},{6,7},{7,6},{8,9},{9,8},{10,11... | collective-permute-start | bytes 393224 | tf_op jit(solution)/shard_map/ppermute | solution.py:508
  61.0 3.5 %collective-permute-start.15 = (bf16[128,128]{1,0:T(8,128)(2,1)S(1)}, bf16[128,128]{1,0:T(8,128)(2,1)S(1)}, u32[]{:S(2)}, u32[]{:S(2)}) collective-permute-start(bf16[128,128]{1,0:T(8,128)(2,1)S(1)} %get-tuple-element.42), channel_id=1, source_target_pairs={{0,3},{1,2},{2,1},{3,0},{4,7},{5,6},{6,5},{7,4},{8,11},{9,10},{10,... | collective-permute-start | bytes 98312 | tf_op jit(solution)/shard_map/ppermute | solution.py:508

commit v10 on v9

--- a/solution.py
+++ b/solution.py
@@ -57,15 +57,15 @@
     return me, core, chip, odd, core == odd, chip + 2 - 4 * odd, chip - 2 + 4 * odd, odd == ((chip >> 1) & 1)
 
 
-def cut_kernel(size, own, early, late, near, far, main, side, sems):
+def cut_kernel(size, wanted, own, *refs):
+    outs, sems = refs[:-1], refs[-1]
     _, _, _, odd, _, _, _, f_near = place_of_device()
-    side_start, main_start = (1 - odd) * size, odd * size
-    near_start, far_start = jnp.where(f_near, side_start, main_start), jnp.where(f_near, main_start, side_start)
-    outs = (early, late, near, far, main, side)
-    starts = (side_start, side_start + size - LATE, near_start, far_start, main_start, side_start)
+    side, main = (1 - odd) * size, odd * size
+    near, far = jnp.where(f_near, side, main), jnp.where(f_near, main, side)
+    starts = (side, side + size - LATE, near, far, main, side)
     copies = []
-    for i, (out, start) in enumerate(zip(outs, starts)):
-        rows = pl.ds(pl.multiple_of(start, 16), out.shape[1])
+    for i, (out, at) in enumerate(zip(outs, wanted)):
+        rows = pl.ds(pl.multiple_of(starts[at], 16), out.shape[1])
         copies.append(pltpu.make_async_copy(own.at[:, rows, :], out, sems.at[i]))
     for copy in copies:
         copy.start()
@@ -73,16 +73,16 @@
         copy.wait()
 
 
-def cut(own):
+def cut(own, wanted):
     rows, aux, width = own.shape
     half = aux // 2
     sizes = (half - LATE, LATE, half, half, half, half)
     return pl.pallas_call(
-        functools.partial(cut_kernel, half),
-        out_shape=[jax.ShapeDtypeStruct((rows, size, width), own.dtype) for size in sizes],
+        functools.partial(cut_kernel, half, wanted),
+        out_shape=[jax.ShapeDtypeStruct((rows, sizes[at], width), own.dtype) for at in wanted],
         in_specs=vmem(1),
-        out_specs=vmem(6),
-        scratch_shapes=[pltpu.SemaphoreType.DMA((6,))],
+        out_specs=vmem(len(wanted)),
+        scratch_shapes=[pltpu.SemaphoreType.DMA((len(wanted),))],
         compiler_params=pltpu.CompilerParams(vmem_limit_bytes=LIMIT),
         cost_estimate=cost(own, own),
     )(own)
@@ -508,7 +508,8 @@
     send = lambda value, route: lax.ppermute(value, "basis", route)
 
     xo = send(own, swap)
-    early, late, for_near, for_far, xj, xj_side = cut(own)
+    (early,) = cut(own, (0,))
+    late, for_near, for_far, xj, xj_side = cut(own, (1, 2, 3, 4, 5))
     yj = send(early, across), send(late, across)
     near, far = send(for_near, to_near), send(for_far, to_far)
     own_pairs, share, table = own_products(domains, pairs, xj, xj_side, xo, coefs[0])

time: 66.2 us -> 66.2 us (level); the launches traced: 66 us -> 65.3 us
  waiting for transfers between devices: 29.1 us -> 27.9 us
    ppermute x13, waiting for transfers between devices: 28.1 us -> 27 us  [per_device(): send = lambda value, route: lax.ppermute(value, 'basis', route)]
  transfers between devices with their start and end apart: 16 -> 16, of which waited for: 5 -> 5; matrix products, arithmetic and copies ran while one was open for 0% -> 0% of each run, Pallas kernels for 27% -> 28%
where the time goes in v10:
time: 66.2 us; the launch traced here: 65.3 us
  waiting for transfers between devices  27.9 us (42%)
  Pallas kernels  19.7 us (30%)
  starting transfers between devices  14.8 us (22%)
  local copies, waits for them, and re-layouts  2.13 us (3%)
  between operations  0.78 us (1%)
    ppermute x13, waiting for transfers between devices, per_device(): send = lambda value, route: lax.ppermute(value, 'basis', route)  27 us
    pallas_call x1, Pallas kernels, own_products(): pl.pallas_call(own_kernel, out_shape=[squares(2, width), jax.ShapeDtypeSt...  9.88 us
    ppermute x13, starting transfers between devices, per_device(): send = lambda value, route: lax.ppermute(value, 'basis', route)  9.67 us
    ppermute x3, starting transfers between devices, shares_of(): lax.ppermute(values, 'basis', [(i, i ^ step) for i in range(count)])  5.11 us
    pallas_call x1, Pallas kernels, shared_products(): pl.pallas_call(shared_kernel, out_shape=squares(len(SHARED), blocks[0].sh...  3.35 us
    unnamed x8, local copies, waits for them, and re-layouts  2.13 us
    pallas_call x1, Pallas kernels, early_products(): pl.pallas_call(early_kernel, out_shape=squares(2, xj.shape[-1]), in_specs...  1.83 us
    pallas_call x1, Pallas kernels, finish(): pl.pallas_call(functools.partial(band_kernel, aux), out_shape=squares(siz...  1.47 us
  transfers between devices with their start and end apart: 16, of which 5 were waited for; matrix products, arithmetic and copies ran while one was open for 0% of the time, Pallas kernels for 28%

profile of v10, /device:TPU:0, one launch (start us, length us, event | category | flops | bytes accessed | tf_op | source)
XLA Modules:
  0.0 65.3 jit_solution(11872530740273102808)
XLA Ops:
  0.6 0.5 collective-permute-start
  1.1 2.1 %copy-done = bf16[1,30,512,128]{3,2,1,0:T(8,128)(2,1)S(1)} copy-done((bf16[1,30,512,128]{3,2,1,0:T(8,128)(2,1)S(1)}, bf16[1,30,512,128]{3,2,1,0:T(8,128)(2,1)}, u32[]{:S(2)}) %copy-start) | copy-done | bytes 3932184
  3.4 2.6 %collective-permute-start.3 = (bf16[30,112,128]{2,1,0:T(8,128)(2,1)S(1)}, bf16[30,112,128]{2,1,0:T(8,128)(2,1)S(1)}, u32[]{:S(2)}, u32[]{:S(2)}) collective-permute-start(bf16[30,112,128]{2,1,0:T(8,128)(2,1)S(1)} %shard_map.61), channel_id=1, source_target_pairs={{0,2},{1,3},{2,0},{3,1},{4,6},{5,7},{6,4},{7,5},{8,10},{9,11},{10,... | collective-permute-start | bytes 2580488 | tf_op jit(solution)/shard_map/ppermute | solution.py:508
  6.0 0.8 %shard_map.59 = (bf16[30,144,128]{2,1,0:T(8,128)(2,1)S(1)}, bf16[30,256,128]{2,1,0:T(8,128)(2,1)S(1)}, bf16[30,256,128]{2,1,0:T(8,128)(2,1)S(1)}, bf16[30,256,12...) custom-call(bf16[30,512,128]{2,1,0:T(8,128)(2,1)S(1)} %bitcast.6), custom_call_target="tpu_custom_call" | custom-call | flops 1 | bytes 7864320 | tf_op jit(solution)/shard_map/pallas_call | solution.py:80
  6.7 1.6 %collective-permute-start.1 = (bf16[30,256,128]{2,1,0:T(8,128)(2,1)S(1)}, bf16[30,256,128]{2,1,0:T(8,128)(2,1)S(1)}, u32[]{:S(2)}, u32[]{:S(2)}) collective-permute-start(bf16[30,256,128]{2,1,0:T(8,128)(2,1)S(1)} %get-tuple-element.25), channel_id=1, source_target_pairs={{0,4},{1,5},{2,6},{3,7},{4,0},{5,1},{6,2},{7,3},{8,12},{9,13},{10,... | collective-permute-start | bytes 5898248 | tf_op jit(solution)/shard_map/ppermute | solution.py:508
  8.4 0.5 collective-permute-start.4
  8.9 9.9 %shard_map.60 = (f32[2,128,128]{2,1,0:T(8,128)S(1)}, f32[1,640]{1,0:T(1,128)S(1)}, s32[8,72]{1,0:T(8,128)S(1)}) custom-call(s32[16,30]{1,0:T(8,128)S(1)} %copy-done.1, s32[1,4]{1,0:T(1,128)S(1)} %copy-done.3, bf16[30,256,128]{2,1,0:T(8,128)(2,1)S(1)} %get-tuple-element.22.own.xj, bf16[30,256,128]{2,1,0:T(8,128)(2,1)S(1)} %get-tuple-element.23.own_side.xj_side, ...), custom_call_target="tpu_custom_call" | custom-call | flops 1 | bytes 7864320 | tf_op jit(solution)/shard_map/pallas_call | solution.py:196
  18.8 0.3 collective-permute-start.5
  19.1 0.9 %collective-permute-done.5.refs_1_ = f32[1,640]{1,0:T(1,128)S(1)} collective-permute-done((f32[1,640]{1,0:T(1,128)S(1)}, f32[1,640]{1,0:T(1,128)S(1)}, u32[]{:S(2)}, u32[]{:S(2)}) %collective-permute-start.5) | collective-permute-done | bytes 2592 | tf_op jit(solution)/shard_map/ppermute | solution.py:494
  20.0 5.9 %collective-permute-done.3.yj.value.refs_0_ = bf16[30,112,128]{2,1,0:T(8,128)(2,1)S(1)} collective-permute-done((bf16[30,112,128]{2,1,0:T(8,128)(2,1)S(1)}, bf16[30,112,128]{2,1,0:T(8,128)(2,1)S(1)}, u32[]{:S(2)}, u32[]{:S(2)}) %collective-permute-start.3) | collective-permute-done | bytes 860192 | tf_op jit(solution)/shard_map/ppermute | solution.py:508
  25.9 0.7 %shard_map.64 = (bf16[30,112,128]{2,1,0:T(8,128)(2,1)S(1)}, f32[1,640]{1,0:T(1,128)}) custom-call(bf16[30,112,128]{2,1,0:T(8,128)(2,1)S(1)} %collective-permute-done.3.yj.value.refs_0_, f32[1,640]{1,0:T(1,128)S(1)} %shard_map.63.refs_0_), custom_call_target="tpu_custom_call" | custom-call | flops 1 | bytes 1720320 | tf_op jit(solution)/shard_map/pallas_call | solution.py:228
  26.8 2.0 %collective-permute-start.7 = (f32[1,640]{1,0:T(1,128)S(1)}, f32[1,640]{1,0:T(1,128)S(1)}, u32[]{:S(2)}, u32[]{:S(2)}) collective-permute-start(f32[1,640]{1,0:T(1,128)S(1)} %shard_map.63.refs_0_), channel_id=1, source_target_pairs={{0,2},{1,3},{2,0},{3,1},{4,6},{5,7},{6,4},{7,5},{8,10},{9,11},{10,... | collective-permute-start | bytes 7688 | tf_op jit(solution)/shard_map/ppermute | solution.py:494
  28.8 1.8 %shard_map.62.refs_2_.early = f32[2,128,128]{2,1,0:T(8,128)S(1)} custom-call(s32[8,72]{1,0:T(8,128)S(1)} %get-tuple-element.24.table, bf16[30,256,128]{2,1,0:T(8,128)(2,1)S(1)} %get-tuple-element.22.own.xj, bf16[30,512,128]{2,1,0:T(8,128)(2,1)S(1)} %collective-permute-done.other.xo, bf16[30,112,128]{2,1,0:T(8,128)(2,1)S(1)} %collective-permute-done.3.yj.value.refs_0_), custom_call_target="tpu_custom_call" | custom-call | flops 1 | bytes 6758400 | tf_op jit(solution)/shard_map/pallas_call | solution.py:266
  30.6 18.9 %collective-permute-done.4.value.refs_1_ = bf16[30,144,128]{2,1,0:T(8,128)(2,1)S(1)} collective-permute-done((bf16[30,144,128]{2,1,0:T(8,128)(2,1)S(1)}, bf16[30,144,128]{2,1,0:T(8,128)(2,1)S(1)}, u32[]{:S(2)}, u32[]{:S(2)}) %collective-permute-start.4) | collective-permute-done | bytes 1105952 | tf_op jit(solution)/shard_map/ppermute | solution.py:508
  49.7 0.5 collective-permute-start.9
  50.2 2.8 %collective-permute-start.10 = (f32[1,640]{1,0:T(1,128)S(1)}, f32[1,640]{1,0:T(1,128)S(1)}, u32[]{:S(2)}, u32[]{:S(2)}) collective-permute-start(f32[1,640]{1,0:T(1,128)S(1)} %get-tuple-element.32.refs_0_), channel_id=1, source_target_pairs={{0,8},{1,9},{2,10},{3,11},{4,12},{5,13},{6,14},{7,15},{8,0},{9,1},... | collective-permute-start | bytes 7688 | tf_op jit(solution)/shard_map/ppermute | solution.py:494
  53.0 3.3 %shard_map.66.total = f32[7,128,128]{2,1,0:T(8,128)S(1)} custom-call(s32[8,72]{1,0:T(8,128)S(1)} %get-tuple-element.24.table, bf16[30,256,128]{2,1,0:T(8,128)(2,1)S(1)} %get-tuple-element.22.own.xj, bf16[30,256,128]{2,1,0:T(8,128)(2,1)S(1)} %get-tuple-element.23.own_side.xj_side, bf16[30,512,128]{2,1,0:T(8,128)(2,1)S(1)} %collective-permute-done.other.xo, ...), custom_call_target="tpu_custom_call" | custom-call | flops 1 | bytes 15859712 | tf_op jit(solution)/shard_map/pallas_call | solution.py:329
  56.7 1.6 %collective-permute-start.11 = (bf16[544,128]{1,0:T(8,128)(2,1)S(1)}, bf16[544,128]{1,0:T(8,128)(2,1)S(1)}, u32[]{:S(2)}, u32[]{:S(2)}) collective-permute-start(bf16[544,128]{1,0:T(8,128)(2,1)S(1)} %get-tuple-element.34), channel_id=1, source_target_pairs={{0,4},{1,5},{2,6},{3,7},{4,0},{5,1},{6,2},{7,3},{8,12},{9,13},{10,... | collective-permute-start | bytes 417800 | tf_op jit(solution)/shard_map/ppermute | solution.py:508
  58.3 1.5 %collective-permute-start.12 = (bf16[528,128]{1,0:T(8,128)(2,1)S(1)}, bf16[528,128]{1,0:T(8,128)(2,1)S(1)}, u32[]{:S(2)}, u32[]{:S(2)}) collective-permute-start(bf16[528,128]{1,0:T(8,128)(2,1)S(1)} %get-tuple-element.37), channel_id=1, source_target_pairs={{0,2},{1,3},{2,0},{3,1},{4,6},{5,7},{6,4},{7,5},{8,10},{9,11},{10,... | collective-permute-start | bytes 405512 | tf_op jit(solution)/shard_map/ppermute | solution.py:508
  59.8 0.5 collective-permute-start.14
  60.4 1.7 %collective-permute-done.11.from_near = bf16[544,128]{1,0:T(8,128)(2,1)S(1)} collective-permute-done((bf16[544,128]{1,0:T(8,128)(2,1)S(1)}, bf16[544,128]{1,0:T(8,128)(2,1)S(1)}, u32[]{:S(2)}, u32[]{:S(2)}) %collective-permute-start.11) | collective-permute-done | bytes 139296 | tf_op jit(solution)/shard_map/ppermute | solution.py:508
  62.1 1.2 %shard_map.68 = (f32[30,1,128]{2,1,0:T(1,128)}, f32[1,640]{1,0:T(1,128)S(1)}) custom-call(bf16[30,256,128]{2,1,0:T(8,128)(2,1)S(1)} %get-tuple-element.22.own.xj, bf16[30,256,128]{2,1,0:T(8,128)(2,1)S(1)} %get-tuple-element.23.own_side.xj_side, f32[1,640]{1,0:T(1,128)S(1)} %get-tuple-element.33.share, bf16[544,128]{1,0:T(8,128)(2,1)S(1)} %collective-permute-done.11.from_near), custom_call_target="tpu_custom_call" | custom-call | flops 1 | bytes 3932160 | tf_op jit(solution)/shard_map/pallas_call | solution.py:416
  63.3 0.5 collective-permute-done.15.from_y_other
  63.8 1.5 %shard_map.69 = f32[9,128,128]{2,1,0:T(8,128)} custom-call(s32[1,4]{1,0:T(1,128)S(1)} %copy-done.3, f32[1,640]{1,0:T(1,128)S(1)} %get-tuple-element.35.summed, f32[2,128,128]{2,1,0:T(8,128)S(1)} %get-tuple-element.36.own, f32[7,128,128]{2,1,0:T(8,128)S(1)} %shard_map.66.total, bf16[528,128]{1,0:T(8,128)(2,1)S(1)} %collective-permute-done.12.from_y, ...), custom_call_target="tpu_custom_call" | custom-call | flops 1 | bytes 1159168 | tf_op jit(solution)/shard_map/pallas_call | solution.py:467
  (27 shorter events, 0.8 us)
Async XLA Ops:
  0.6 8.3 %collective-permute-start = (bf16[30,512,128]{2,1,0:T(8,128)(2,1)}, bf16[30,512,128]{2,1,0:T(8,128)(2,1)S(1)}, u32[]{:S(2)}, u32[]{:S(2)}) collective-permute-start(bf16[30,512,128]{2,1,0:T(8,128)(2,1)} %bitcast.4), channel_id=1, source_target_pairs={{0,1},{1,0},{2,3},{3,2},{4,5},{5,4},{6,7},{7,6},{8,9},{9,8},{10,11... | collective-permute-start | bytes 11796488 | tf_op jit(solution)/shard_map/ppermute | solution.py:508
  1.1 2.1 %copy-start = (bf16[1,30,512,128]{3,2,1,0:T(8,128)(2,1)S(1)}, bf16[1,30,512,128]{3,2,1,0:T(8,128)(2,1)}, u32[]{:S(2)}) copy-start(bf16[1,30,512,128]{3,2,1,0:T(8,128)(2,1)} %param.4) | copy-start | bytes 11796484
  3.3 5.5 %copy-start.1 = (s32[16,30]{1,0:T(8,128)S(1)}, s32[16,30]{1,0:T(8,128)}, u32[]{:S(2)}) copy-start(s32[16,30]{1,0:T(8,128)} %domains.1) | copy-start | bytes 5764
  3.4 5.5 %copy-start.2 = (bf16[1,30,128]{2,1,0:T(8,128)(2,1)S(1)}, bf16[1,30,128]{2,1,0:T(8,128)(2,1)}, u32[]{:S(2)}) copy-start(bf16[1,30,128]{2,1,0:T(8,128)(2,1)} %param.5) | copy-start | bytes 23044
  3.4 5.5 %copy-start.3 = (s32[1,4]{1,0:T(1,128)S(1)}, s32[1,4]{1,0:T(1,128)}, u32[]{:S(2)}) copy-start(s32[1,4]{1,0:T(1,128)} %pairs.3) | copy-start | bytes 52
  3.4 22.6 %collective-permute-start.3 = (bf16[30,112,128]{2,1,0:T(8,128)(2,1)S(1)}, bf16[30,112,128]{2,1,0:T(8,128)(2,1)S(1)}, u32[]{:S(2)}, u32[]{:S(2)}) collective-permute-start(bf16[30,112,128]{2,1,0:T(8,128)(2,1)S(1)} %shard_map.61), channel_id=1, source_target_pairs={{0,2},{1,3},{2,0},{3,1},{4,6},{5,7},{6,4},{7,5},{8,10},{9,11},{10,... | collective-permute-start | bytes 2580488 | tf_op jit(solution)/shard_map/ppermute | solution.py:508
  6.7 46.3 %collective-permute-start.1 = (bf16[30,256,128]{2,1,0:T(8,128)(2,1)S(1)}, bf16[30,256,128]{2,1,0:T(8,128)(2,1)S(1)}, u32[]{:S(2)}, u32[]{:S(2)}) collective-permute-start(bf16[30,256,128]{2,1,0:T(8,128)(2,1)S(1)} %get-tuple-element.25), channel_id=1, source_target_pairs={{0,4},{1,5},{2,6},{3,7},{4,0},{5,1},{6,2},{7,3},{8,12},{9,13},{10,... | collective-permute-start | bytes 5898248 | tf_op jit(solution)/shard_map/ppermute | solution.py:508
  8.4 44.6 %collective-permute-start.2 = (bf16[30,256,128]{2,1,0:T(8,128)(2,1)S(1)}, bf16[30,256,128]{2,1,0:T(8,128)(2,1)S(1)}, u32[]{:S(2)}, u32[]{:S(2)}) collective-permute-start(bf16[30,256,128]{2,1,0:T(8,128)(2,1)S(1)} %get-tuple-element.26), channel_id=1, source_target_pairs={{4,8},{5,9},{6,10},{7,11},{8,4},{9,5},{10,6},{11,7},{0,1},{1,0},{2... | collective-permute-start | bytes 5898248 | tf_op jit(solution)/shard_map/ppermute | solution.py:508
  8.4 41.1 %collective-permute-start.4 = (bf16[30,144,128]{2,1,0:T(8,128)(2,1)S(1)}, bf16[30,144,128]{2,1,0:T(8,128)(2,1)S(1)}, u32[]{:S(2)}, u32[]{:S(2)}) collective-permute-start(bf16[30,144,128]{2,1,0:T(8,128)(2,1)S(1)} %get-tuple-element.27), channel_id=1, source_target_pairs={{0,2},{1,3},{2,0},{3,1},{4,6},{5,7},{6,4},{7,5},{8,10},{9,11},{10,... | collective-permute-start | bytes 3317768 | tf_op jit(solution)/shard_map/ppermute | solution.py:508
  18.8 1.2 %collective-permute-start.5 = (f32[1,640]{1,0:T(1,128)S(1)}, f32[1,640]{1,0:T(1,128)S(1)}, u32[]{:S(2)}, u32[]{:S(2)}) collective-permute-start(f32[1,640]{1,0:T(1,128)S(1)} %get-tuple-element.28.refs_0_), channel_id=1, source_target_pairs={{0,1},{1,0},{2,3},{3,2},{4,5},{5,4},{6,7},{7,6},{8,9},{9,8},{10,11... | collective-permute-start | bytes 7688 | tf_op jit(solution)/shard_map/ppermute | solution.py:494
  26.7 22.8 %collective-permute-start.6 = (bf16[30,112,128]{2,1,0:T(8,128)(2,1)S(1)}, bf16[30,112,128]{2,1,0:T(8,128)(2,1)S(1)}, u32[]{:S(2)}, u32[]{:S(2)}) collective-permute-start(bf16[30,112,128]{2,1,0:T(8,128)(2,1)S(1)} %get-tuple-element.29), channel_id=1, source_target_pairs={{0,1},{1,0},{2,3},{3,2},{4,5},{5,4},{6,7},{7,6},{8,9},{9,8},{10,11... | collective-permute-start | bytes 2580488 | tf_op jit(solution)/shard_map/ppermute | solution.py:508
  26.8 22.7 %collective-permute-start.7 = (f32[1,640]{1,0:T(1,128)S(1)}, f32[1,640]{1,0:T(1,128)S(1)}, u32[]{:S(2)}, u32[]{:S(2)}) collective-permute-start(f32[1,640]{1,0:T(1,128)S(1)} %shard_map.63.refs_0_), channel_id=1, source_target_pairs={{0,2},{1,3},{2,0},{3,1},{4,6},{5,7},{6,4},{7,5},{8,10},{9,11},{10,... | collective-permute-start | bytes 7688 | tf_op jit(solution)/shard_map/ppermute | solution.py:494
  49.6 3.4 %collective-permute-start.8 = (bf16[30,80,128]{2,1,0:T(8,128)(2,1)S(1)}, bf16[30,80,128]{2,1,0:T(8,128)(2,1)S(1)}, u32[]{:S(2)}, u32[]{:S(2)}) collective-permute-start(bf16[30,80,128]{2,1,0:T(8,128)(2,1)S(1)} %get-tuple-element.30), channel_id=1, source_target_pairs={{0,1},{1,0},{2,3},{3,2},{4,5},{5,4},{6,7},{7,6},{8,9},{9,8},{10,11... | collective-permute-start | bytes 1843208 | tf_op jit(solution)/shard_map/ppermute | solution.py:508
  49.7 3.3 %collective-permute-start.9 = (bf16[30,64,128]{2,1,0:T(8,128)(2,1)S(1)}, bf16[30,64,128]{2,1,0:T(8,128)(2,1)S(1)}, u32[]{:S(2)}, u32[]{:S(2)}) collective-permute-start(bf16[30,64,128]{2,1,0:T(8,128)(2,1)S(1)} %get-tuple-element.31), channel_id=1, source_target_pairs={{0,1},{1,0},{2,3},{3,2},{4,5},{5,4},{6,7},{7,6},{8,9},{9,8},{10,11... | collective-permute-start | bytes 1474568 | tf_op jit(solution)/shard_map/ppermute | solution.py:508
  50.2 6.2 %collective-permute-start.10 = (f32[1,640]{1,0:T(1,128)S(1)}, f32[1,640]{1,0:T(1,128)S(1)}, u32[]{:S(2)}, u32[]{:S(2)}) collective-permute-start(f32[1,640]{1,0:T(1,128)S(1)} %get-tuple-element.32.refs_0_), channel_id=1, source_target_pairs={{0,8},{1,9},{2,10},{3,11},{4,12},{5,13},{6,14},{7,15},{8,0},{9,1},... | collective-permute-start | bytes 7688 | tf_op jit(solution)/shard_map/ppermute | solution.py:494
  56.7 5.4 %collective-permute-start.11 = (bf16[544,128]{1,0:T(8,128)(2,1)S(1)}, bf16[544,128]{1,0:T(8,128)(2,1)S(1)}, u32[]{:S(2)}, u32[]{:S(2)}) collective-permute-start(bf16[544,128]{1,0:T(8,128)(2,1)S(1)} %get-tuple-element.34), channel_id=1, source_target_pairs={{0,4},{1,5},{2,6},{3,7},{4,0},{5,1},{6,2},{7,3},{8,12},{9,13},{10,... | collective-permute-start | bytes 417800 | tf_op jit(solution)/shard_map/ppermute | solution.py:508
  58.3 5.5 %collective-permute-start.12 = (bf16[528,128]{1,0:T(8,128)(2,1)S(1)}, bf16[528,128]{1,0:T(8,128)(2,1)S(1)}, u32[]{:S(2)}, u32[]{:S(2)}) collective-permute-start(bf16[528,128]{1,0:T(8,128)(2,1)S(1)} %get-tuple-element.37), channel_id=1, source_target_pairs={{0,2},{1,3},{2,0},{3,1},{4,6},{5,7},{6,4},{7,5},{8,10},{9,11},{10,... | collective-permute-start | bytes 405512 | tf_op jit(solution)/shard_map/ppermute | solution.py:508
  59.8 4.0 %collective-permute-start.13 = (bf16[512,128]{1,0:T(8,128)(2,1)S(1)}, bf16[512,128]{1,0:T(8,128)(2,1)S(1)}, u32[]{:S(2)}, u32[]{:S(2)}) collective-permute-start(bf16[512,128]{1,0:T(8,128)(2,1)S(1)} %get-tuple-element.38), channel_id=1, source_target_pairs={{4,8},{5,9},{6,10},{7,11},{8,4},{9,5},{10,6},{11,7},{0,1},{1,0},{2... | collective-permute-start | bytes 393224 | tf_op jit(solution)/shard_map/ppermute | solution.py:508
  59.8 4.0 %collective-permute-start.14 = (f32[2,128,128]{2,1,0:T(8,128)S(1)}, f32[2,128,128]{2,1,0:T(8,128)S(1)}, u32[]{:S(2)}, u32[]{:S(2)}) collective-permute-start(f32[2,128,128]{2,1,0:T(8,128)S(1)} %get-tuple-element.39), channel_id=1, source_target_pairs={{0,1},{1,0},{2,3},{3,2},{4,5},{5,4},{6,7},{7,6},{8,9},{9,8},{10,11... | collective-permute-start | bytes 393224 | tf_op jit(solution)/shard_map/ppermute | solution.py:508
  60.3 3.5 %collective-permute-start.15 = (bf16[128,128]{1,0:T(8,128)(2,1)S(1)}, bf16[128,128]{1,0:T(8,128)(2,1)S(1)}, u32[]{:S(2)}, u32[]{:S(2)}) collective-permute-start(bf16[128,128]{1,0:T(8,128)(2,1)S(1)} %get-tuple-element.40), channel_id=1, source_target_pairs={{0,3},{1,2},{2,1},{3,0},{4,7},{5,6},{6,5},{7,4},{8,11},{9,10},{10,... | collective-permute-start | bytes 98312 | tf_op jit(solution)/shard_map/ppermute | solution.py:508

commit v11 on v10

--- a/solution.py
+++ b/solution.py
@@ -509,7 +509,8 @@
 
     xo = send(own, swap)
     (early,) = cut(own, (0,))
-    late, for_near, for_far, xj, xj_side = cut(own, (1, 2, 3, 4, 5))
+    late, for_near, for_far = cut(own, (1, 2, 3))
+    xj, xj_side = cut(own, (4, 5))
     yj = send(early, across), send(late, across)
     near, far = send(for_near, to_near), send(for_far, to_far)
     own_pairs, share, table = own_products(domains, pairs, xj, xj_side, xo, coefs[0])

time: 66.2 us -> 65.4 us (0.988); the launches traced: 65.3 us -> 65.3 us
  transfers between devices with their start and end apart: 16 -> 16, of which waited for: 5 -> 5; matrix products, arithmetic and copies ran while one was open for 0% -> 0% of each run, Pallas kernels for 28% -> 27%
where the time goes in v11:
time: 65.4 us; the launch traced here: 65.3 us
  waiting for transfers between devices  28.2 us (43%)
  Pallas kernels  19.3 us (30%)
  starting transfers between devices  14.9 us (23%)
  local copies, waits for them, and re-layouts  2.12 us (3%)
  between operations  0.79 us (1%)
    ppermute x13, waiting for transfers between devices, per_device(): send = lambda value, route: lax.ppermute(value, 'basis', route)  27.2 us
    ppermute x13, starting transfers between devices, per_device(): send = lambda value, route: lax.ppermute(value, 'basis', route)  9.75 us
    pallas_call x1, Pallas kernels, own_products(): pl.pallas_call(own_kernel, out_shape=[squares(2, width), jax.ShapeDtypeSt...  9.54 us
    ppermute x3, starting transfers between devices, shares_of(): lax.ppermute(values, 'basis', [(i, i ^ step) for i in range(count)])  5.11 us
    pallas_call x1, Pallas kernels, shared_products(): pl.pallas_call(shared_kernel, out_shape=squares(len(SHARED), blocks[0].sh...  3.34 us
    unnamed x8, local copies, waits for them, and re-layouts  2.12 us
    pallas_call x1, Pallas kernels, early_products(): pl.pallas_call(early_kernel, out_shape=squares(2, xj.shape[-1]), in_specs...  1.83 us
    pallas_call x1, Pallas kernels, finish(): pl.pallas_call(functools.partial(band_kernel, aux), out_shape=squares(siz...  1.47 us
  transfers between devices with their start and end apart: 16, of which 5 were waited for; matrix products, arithmetic and copies ran while one was open for 0% of the time, Pallas kernels for 27%

profile of v11, /device:TPU:0, one launch (start us, length us, event | category | flops | bytes accessed | tf_op | source)
XLA Modules:
  0.0 65.3 jit_solution(6242671568922325091)
XLA Ops:
  0.6 0.5 collective-permute-start
  1.1 2.1 %copy-done = bf16[1,30,512,128]{3,2,1,0:T(8,128)(2,1)S(1)} copy-done((bf16[1,30,512,128]{3,2,1,0:T(8,128)(2,1)S(1)}, bf16[1,30,512,128]{3,2,1,0:T(8,128)(2,1)}, u32[]{:S(2)}) %copy-start) | copy-done | bytes 3932184
  3.3 2.6 %collective-permute-start.3 = (bf16[30,112,128]{2,1,0:T(8,128)(2,1)S(1)}, bf16[30,112,128]{2,1,0:T(8,128)(2,1)S(1)}, u32[]{:S(2)}, u32[]{:S(2)}) collective-permute-start(bf16[30,112,128]{2,1,0:T(8,128)(2,1)S(1)} %shard_map.62), channel_id=1, source_target_pairs={{0,2},{1,3},{2,0},{3,1},{4,6},{5,7},{6,4},{7,5},{8,10},{9,11},{10,... | collective-permute-start | bytes 2580488 | tf_op jit(solution)/shard_map/ppermute | solution.py:508
  5.9 0.4 shard_map.61
  6.3 1.6 %collective-permute-start.1 = (bf16[30,256,128]{2,1,0:T(8,128)(2,1)S(1)}, bf16[30,256,128]{2,1,0:T(8,128)(2,1)S(1)}, u32[]{:S(2)}, u32[]{:S(2)}) collective-permute-start(bf16[30,256,128]{2,1,0:T(8,128)(2,1)S(1)} %get-tuple-element.25), channel_id=1, source_target_pairs={{0,4},{1,5},{2,6},{3,7},{4,0},{5,1},{6,2},{7,3},{8,12},{9,13},{10,... | collective-permute-start | bytes 5898248 | tf_op jit(solution)/shard_map/ppermute | solution.py:508
  8.0 0.6 collective-permute-start.4
  8.6 0.4 shard_map.59
  9.0 9.5 %shard_map.60 = (f32[2,128,128]{2,1,0:T(8,128)S(1)}, f32[1,640]{1,0:T(1,128)S(1)}, s32[8,72]{1,0:T(8,128)S(1)}) custom-call(s32[16,30]{1,0:T(8,128)S(1)} %copy-done.1, s32[1,4]{1,0:T(1,128)S(1)} %copy-done.3, bf16[30,256,128]{2,1,0:T(8,128)(2,1)S(1)} %get-tuple-element.22.own.xj, bf16[30,256,128]{2,1,0:T(8,128)(2,1)S(1)} %get-tuple-element.23.own_side.xj_side, ...), custom_call_target="tpu_custom_call" | custom-call | flops 1 | bytes 7864320 | tf_op jit(solution)/shard_map/pallas_call | solution.py:196
  18.8 0.9 %collective-permute-done.5.refs_1_ = f32[1,640]{1,0:T(1,128)S(1)} collective-permute-done((f32[1,640]{1,0:T(1,128)S(1)}, f32[1,640]{1,0:T(1,128)S(1)}, u32[]{:S(2)}, u32[]{:S(2)}) %collective-permute-start.5) | collective-permute-done | bytes 2592 | tf_op jit(solution)/shard_map/ppermute | solution.py:494
  19.8 6.2 %collective-permute-done.3.yj.value.refs_0_ = bf16[30,112,128]{2,1,0:T(8,128)(2,1)S(1)} collective-permute-done((bf16[30,112,128]{2,1,0:T(8,128)(2,1)S(1)}, bf16[30,112,128]{2,1,0:T(8,128)(2,1)S(1)}, u32[]{:S(2)}, u32[]{:S(2)}) %collective-permute-start.3) | collective-permute-done | bytes 860192 | tf_op jit(solution)/shard_map/ppermute | solution.py:508
  25.9 0.7 %shard_map.65 = (bf16[30,112,128]{2,1,0:T(8,128)(2,1)S(1)}, f32[1,640]{1,0:T(1,128)}) custom-call(bf16[30,112,128]{2,1,0:T(8,128)(2,1)S(1)} %collective-permute-done.3.yj.value.refs_0_, f32[1,640]{1,0:T(1,128)S(1)} %shard_map.64.refs_0_), custom_call_target="tpu_custom_call" | custom-call | flops 1 | bytes 1720320 | tf_op jit(solution)/shard_map/pallas_call | solution.py:228
  26.7 2.0 %collective-permute-start.7 = (f32[1,640]{1,0:T(1,128)S(1)}, f32[1,640]{1,0:T(1,128)S(1)}, u32[]{:S(2)}, u32[]{:S(2)}) collective-permute-start(f32[1,640]{1,0:T(1,128)S(1)} %shard_map.64.refs_0_), channel_id=1, source_target_pairs={{0,2},{1,3},{2,0},{3,1},{4,6},{5,7},{6,4},{7,5},{8,10},{9,11},{10,... | collective-permute-start | bytes 7688 | tf_op jit(solution)/shard_map/ppermute | solution.py:494
  28.7 1.8 %shard_map.63.refs_2_.early = f32[2,128,128]{2,1,0:T(8,128)S(1)} custom-call(s32[8,72]{1,0:T(8,128)S(1)} %get-tuple-element.24.table, bf16[30,256,128]{2,1,0:T(8,128)(2,1)S(1)} %get-tuple-element.22.own.xj, bf16[30,512,128]{2,1,0:T(8,128)(2,1)S(1)} %collective-permute-done.other.xo, bf16[30,112,128]{2,1,0:T(8,128)(2,1)S(1)} %collective-permute-done.3.yj.value.refs_0_), custom_call_target="tpu_custom_call" | custom-call | flops 1 | bytes 6758400 | tf_op jit(solution)/shard_map/pallas_call | solution.py:266
  30.6 18.9 %collective-permute-done.4.value.refs_1_ = bf16[30,144,128]{2,1,0:T(8,128)(2,1)S(1)} collective-permute-done((bf16[30,144,128]{2,1,0:T(8,128)(2,1)S(1)}, bf16[30,144,128]{2,1,0:T(8,128)(2,1)S(1)}, u32[]{:S(2)}, u32[]{:S(2)}) %collective-permute-start.4) | collective-permute-done | bytes 1105952 | tf_op jit(solution)/shard_map/ppermute | solution.py:508
  49.7 0.5 collective-permute-start.9
  50.2 2.8 %collective-permute-start.10 = (f32[1,640]{1,0:T(1,128)S(1)}, f32[1,640]{1,0:T(1,128)S(1)}, u32[]{:S(2)}, u32[]{:S(2)}) collective-permute-start(f32[1,640]{1,0:T(1,128)S(1)} %get-tuple-element.32.refs_0_), channel_id=1, source_target_pairs={{0,8},{1,9},{2,10},{3,11},{4,12},{5,13},{6,14},{7,15},{8,0},{9,1},... | collective-permute-start | bytes 7688 | tf_op jit(solution)/shard_map/ppermute | solution.py:494
  53.0 3.3 %shard_map.67.total = f32[7,128,128]{2,1,0:T(8,128)S(1)} custom-call(s32[8,72]{1,0:T(8,128)S(1)} %get-tuple-element.24.table, bf16[30,256,128]{2,1,0:T(8,128)(2,1)S(1)} %get-tuple-element.22.own.xj, bf16[30,256,128]{2,1,0:T(8,128)(2,1)S(1)} %get-tuple-element.23.own_side.xj_side, bf16[30,512,128]{2,1,0:T(8,128)(2,1)S(1)} %collective-permute-done.other.xo, ...), custom_call_target="tpu_custom_call" | custom-call | flops 1 | bytes 15859712 | tf_op jit(solution)/shard_map/pallas_call | solution.py:329
  56.6 1.6 %collective-permute-start.11 = (bf16[544,128]{1,0:T(8,128)(2,1)S(1)}, bf16[544,128]{1,0:T(8,128)(2,1)S(1)}, u32[]{:S(2)}, u32[]{:S(2)}) collective-permute-start(bf16[544,128]{1,0:T(8,128)(2,1)S(1)} %get-tuple-element.34), channel_id=1, source_target_pairs={{0,4},{1,5},{2,6},{3,7},{4,0},{5,1},{6,2},{7,3},{8,12},{9,13},{10,... | collective-permute-start | bytes 417800 | tf_op jit(solution)/shard_map/ppermute | solution.py:508
  58.3 1.5 %collective-permute-start.12 = (bf16[528,128]{1,0:T(8,128)(2,1)S(1)}, bf16[528,128]{1,0:T(8,128)(2,1)S(1)}, u32[]{:S(2)}, u32[]{:S(2)}) collective-permute-start(bf16[528,128]{1,0:T(8,128)(2,1)S(1)} %get-tuple-element.37), channel_id=1, source_target_pairs={{0,2},{1,3},{2,0},{3,1},{4,6},{5,7},{6,4},{7,5},{8,10},{9,11},{10,... | collective-permute-start | bytes 405512 | tf_op jit(solution)/shard_map/ppermute | solution.py:508
  59.8 0.5 collective-permute-start.14
  60.4 1.6 %collective-permute-done.11.from_near = bf16[544,128]{1,0:T(8,128)(2,1)S(1)} collective-permute-done((bf16[544,128]{1,0:T(8,128)(2,1)S(1)}, bf16[544,128]{1,0:T(8,128)(2,1)S(1)}, u32[]{:S(2)}, u32[]{:S(2)}) %collective-permute-start.11) | collective-permute-done | bytes 139296 | tf_op jit(solution)/shard_map/ppermute | solution.py:508
  62.0 1.2 %shard_map.69 = (f32[30,1,128]{2,1,0:T(1,128)}, f32[1,640]{1,0:T(1,128)S(1)}) custom-call(bf16[30,256,128]{2,1,0:T(8,128)(2,1)S(1)} %get-tuple-element.22.own.xj, bf16[30,256,128]{2,1,0:T(8,128)(2,1)S(1)} %get-tuple-element.23.own_side.xj_side, f32[1,640]{1,0:T(1,128)S(1)} %get-tuple-element.33.share, bf16[544,128]{1,0:T(8,128)(2,1)S(1)} %collective-permute-done.11.from_near), custom_call_target="tpu_custom_call" | custom-call | flops 1 | bytes 3932160 | tf_op jit(solution)/shard_map/pallas_call | solution.py:416
  63.3 0.5 collective-permute-done.15.from_y_other
  63.8 1.5 %shard_map.70 = f32[9,128,128]{2,1,0:T(8,128)} custom-call(s32[1,4]{1,0:T(1,128)S(1)} %copy-done.3, f32[1,640]{1,0:T(1,128)S(1)} %get-tuple-element.35.summed, f32[2,128,128]{2,1,0:T(8,128)S(1)} %get-tuple-element.36.own, f32[7,128,128]{2,1,0:T(8,128)S(1)} %shard_map.67.total, bf16[528,128]{1,0:T(8,128)(2,1)S(1)} %collective-permute-done.12.from_y, ...), custom_call_target="tpu_custom_call" | custom-call | flops 1 | bytes 1159168 | tf_op jit(solution)/shard_map/pallas_call | solution.py:467
  (28 shorter events, 1.1 us)
Async XLA Ops:
  0.6 8.3 %collective-permute-start = (bf16[30,512,128]{2,1,0:T(8,128)(2,1)}, bf16[30,512,128]{2,1,0:T(8,128)(2,1)S(1)}, u32[]{:S(2)}, u32[]{:S(2)}) collective-permute-start(bf16[30,512,128]{2,1,0:T(8,128)(2,1)} %bitcast.4), channel_id=1, source_target_pairs={{0,1},{1,0},{2,3},{3,2},{4,5},{5,4},{6,7},{7,6},{8,9},{9,8},{10,11... | collective-permute-start | bytes 11796488 | tf_op jit(solution)/shard_map/ppermute | solution.py:508
  1.1 2.1 %copy-start = (bf16[1,30,512,128]{3,2,1,0:T(8,128)(2,1)S(1)}, bf16[1,30,512,128]{3,2,1,0:T(8,128)(2,1)}, u32[]{:S(2)}) copy-start(bf16[1,30,512,128]{3,2,1,0:T(8,128)(2,1)} %param.4) | copy-start | bytes 11796484
  3.3 22.6 %collective-permute-start.3 = (bf16[30,112,128]{2,1,0:T(8,128)(2,1)S(1)}, bf16[30,112,128]{2,1,0:T(8,128)(2,1)S(1)}, u32[]{:S(2)}, u32[]{:S(2)}) collective-permute-start(bf16[30,112,128]{2,1,0:T(8,128)(2,1)S(1)} %shard_map.62), channel_id=1, source_target_pairs={{0,2},{1,3},{2,0},{3,1},{4,6},{5,7},{6,4},{7,5},{8,10},{9,11},{10,... | collective-permute-start | bytes 2580488 | tf_op jit(solution)/shard_map/ppermute | solution.py:508
  6.3 46.6 %collective-permute-start.1 = (bf16[30,256,128]{2,1,0:T(8,128)(2,1)S(1)}, bf16[30,256,128]{2,1,0:T(8,128)(2,1)S(1)}, u32[]{:S(2)}, u32[]{:S(2)}) collective-permute-start(bf16[30,256,128]{2,1,0:T(8,128)(2,1)S(1)} %get-tuple-element.25), channel_id=1, source_target_pairs={{0,4},{1,5},{2,6},{3,7},{4,0},{5,1},{6,2},{7,3},{8,12},{9,13},{10,... | collective-permute-start | bytes 5898248 | tf_op jit(solution)/shard_map/ppermute | solution.py:508
  8.0 45.0 %collective-permute-start.2 = (bf16[30,256,128]{2,1,0:T(8,128)(2,1)S(1)}, bf16[30,256,128]{2,1,0:T(8,128)(2,1)S(1)}, u32[]{:S(2)}, u32[]{:S(2)}) collective-permute-start(bf16[30,256,128]{2,1,0:T(8,128)(2,1)S(1)} %get-tuple-element.26), channel_id=1, source_target_pairs={{4,8},{5,9},{6,10},{7,11},{8,4},{9,5},{10,6},{11,7},{0,1},{1,0},{2... | collective-permute-start | bytes 5898248 | tf_op jit(solution)/shard_map/ppermute | solution.py:508
  8.0 1.0 %copy-start.1 = (s32[16,30]{1,0:T(8,128)S(1)}, s32[16,30]{1,0:T(8,128)}, u32[]{:S(2)}) copy-start(s32[16,30]{1,0:T(8,128)} %domains.1) | copy-start | bytes 5764
  8.0 1.0 %copy-start.2 = (bf16[1,30,128]{2,1,0:T(8,128)(2,1)S(1)}, bf16[1,30,128]{2,1,0:T(8,128)(2,1)}, u32[]{:S(2)}) copy-start(bf16[1,30,128]{2,1,0:T(8,128)(2,1)} %param.5) | copy-start | bytes 23044
  8.0 1.0 %copy-start.3 = (s32[1,4]{1,0:T(1,128)S(1)}, s32[1,4]{1,0:T(1,128)}, u32[]{:S(2)}) copy-start(s32[1,4]{1,0:T(1,128)} %pairs.3) | copy-start | bytes 52
  8.0 41.4 %collective-permute-start.4 = (bf16[30,144,128]{2,1,0:T(8,128)(2,1)S(1)}, bf16[30,144,128]{2,1,0:T(8,128)(2,1)S(1)}, u32[]{:S(2)}, u32[]{:S(2)}) collective-permute-start(bf16[30,144,128]{2,1,0:T(8,128)(2,1)S(1)} %get-tuple-element.27), channel_id=1, source_target_pairs={{0,2},{1,3},{2,0},{3,1},{4,6},{5,7},{6,4},{7,5},{8,10},{9,11},{10,... | collective-permute-start | bytes 3317768 | tf_op jit(solution)/shard_map/ppermute | solution.py:508
  18.5 1.2 %collective-permute-start.5 = (f32[1,640]{1,0:T(1,128)S(1)}, f32[1,640]{1,0:T(1,128)S(1)}, u32[]{:S(2)}, u32[]{:S(2)}) collective-permute-start(f32[1,640]{1,0:T(1,128)S(1)} %get-tuple-element.28.refs_0_), channel_id=1, source_target_pairs={{0,1},{1,0},{2,3},{3,2},{4,5},{5,4},{6,7},{7,6},{8,9},{9,8},{10,11... | collective-permute-start | bytes 7688 | tf_op jit(solution)/shard_map/ppermute | solution.py:494
  26.7 22.8 %collective-permute-start.6 = (bf16[30,112,128]{2,1,0:T(8,128)(2,1)S(1)}, bf16[30,112,128]{2,1,0:T(8,128)(2,1)S(1)}, u32[]{:S(2)}, u32[]{:S(2)}) collective-permute-start(bf16[30,112,128]{2,1,0:T(8,128)(2,1)S(1)} %get-tuple-element.29), channel_id=1, source_target_pairs={{0,1},{1,0},{2,3},{3,2},{4,5},{5,4},{6,7},{7,6},{8,9},{9,8},{10,11... | collective-permute-start | bytes 2580488 | tf_op jit(solution)/shard_map/ppermute | solution.py:508
  26.7 22.7 %collective-permute-start.7 = (f32[1,640]{1,0:T(1,128)S(1)}, f32[1,640]{1,0:T(1,128)S(1)}, u32[]{:S(2)}, u32[]{:S(2)}) collective-permute-start(f32[1,640]{1,0:T(1,128)S(1)} %shard_map.64.refs_0_), channel_id=1, source_target_pairs={{0,2},{1,3},{2,0},{3,1},{4,6},{5,7},{6,4},{7,5},{8,10},{9,11},{10,... | collective-permute-start | bytes 7688 | tf_op jit(solution)/shard_map/ppermute | solution.py:494
  49.6 3.4 %collective-permute-start.8 = (bf16[30,80,128]{2,1,0:T(8,128)(2,1)S(1)}, bf16[30,80,128]{2,1,0:T(8,128)(2,1)S(1)}, u32[]{:S(2)}, u32[]{:S(2)}) collective-permute-start(bf16[30,80,128]{2,1,0:T(8,128)(2,1)S(1)} %get-tuple-element.30), channel_id=1, source_target_pairs={{0,1},{1,0},{2,3},{3,2},{4,5},{5,4},{6,7},{7,6},{8,9},{9,8},{10,11... | collective-permute-start | bytes 1843208 | tf_op jit(solution)/shard_map/ppermute | solution.py:508
  49.7 3.3 %collective-permute-start.9 = (bf16[30,64,128]{2,1,0:T(8,128)(2,1)S(1)}, bf16[30,64,128]{2,1,0:T(8,128)(2,1)S(1)}, u32[]{:S(2)}, u32[]{:S(2)}) collective-permute-start(bf16[30,64,128]{2,1,0:T(8,128)(2,1)S(1)} %get-tuple-element.31), channel_id=1, source_target_pairs={{0,1},{1,0},{2,3},{3,2},{4,5},{5,4},{6,7},{7,6},{8,9},{9,8},{10,11... | collective-permute-start | bytes 1474568 | tf_op jit(solution)/shard_map/ppermute | solution.py:508
  50.2 6.2 %collective-permute-start.10 = (f32[1,640]{1,0:T(1,128)S(1)}, f32[1,640]{1,0:T(1,128)S(1)}, u32[]{:S(2)}, u32[]{:S(2)}) collective-permute-start(f32[1,640]{1,0:T(1,128)S(1)} %get-tuple-element.32.refs_0_), channel_id=1, source_target_pairs={{0,8},{1,9},{2,10},{3,11},{4,12},{5,13},{6,14},{7,15},{8,0},{9,1},... | collective-permute-start | bytes 7688 | tf_op jit(solution)/shard_map/ppermute | solution.py:494
  56.6 5.4 %collective-permute-start.11 = (bf16[544,128]{1,0:T(8,128)(2,1)S(1)}, bf16[544,128]{1,0:T(8,128)(2,1)S(1)}, u32[]{:S(2)}, u32[]{:S(2)}) collective-permute-start(bf16[544,128]{1,0:T(8,128)(2,1)S(1)} %get-tuple-element.34), channel_id=1, source_target_pairs={{0,4},{1,5},{2,6},{3,7},{4,0},{5,1},{6,2},{7,3},{8,12},{9,13},{10,... | collective-permute-start | bytes 417800 | tf_op jit(solution)/shard_map/ppermute | solution.py:508
  58.3 5.5 %collective-permute-start.12 = (bf16[528,128]{1,0:T(8,128)(2,1)S(1)}, bf16[528,128]{1,0:T(8,128)(2,1)S(1)}, u32[]{:S(2)}, u32[]{:S(2)}) collective-permute-start(bf16[528,128]{1,0:T(8,128)(2,1)S(1)} %get-tuple-element.37), channel_id=1, source_target_pairs={{0,2},{1,3},{2,0},{3,1},{4,6},{5,7},{6,4},{7,5},{8,10},{9,11},{10,... | collective-permute-start | bytes 405512 | tf_op jit(solution)/shard_map/ppermute | solution.py:508
  59.8 4.0 %collective-permute-start.13 = (bf16[512,128]{1,0:T(8,128)(2,1)S(1)}, bf16[512,128]{1,0:T(8,128)(2,1)S(1)}, u32[]{:S(2)}, u32[]{:S(2)}) collective-permute-start(bf16[512,128]{1,0:T(8,128)(2,1)S(1)} %get-tuple-element.38), channel_id=1, source_target_pairs={{4,8},{5,9},{6,10},{7,11},{8,4},{9,5},{10,6},{11,7},{0,1},{1,0},{2... | collective-permute-start | bytes 393224 | tf_op jit(solution)/shard_map/ppermute | solution.py:508
  59.8 4.0 %collective-permute-start.14 = (f32[2,128,128]{2,1,0:T(8,128)S(1)}, f32[2,128,128]{2,1,0:T(8,128)S(1)}, u32[]{:S(2)}, u32[]{:S(2)}) collective-permute-start(f32[2,128,128]{2,1,0:T(8,128)S(1)} %get-tuple-element.39), channel_id=1, source_target_pairs={{0,1},{1,0},{2,3},{3,2},{4,5},{5,4},{6,7},{7,6},{8,9},{9,8},{10,11... | collective-permute-start | bytes 393224 | tf_op jit(solution)/shard_map/ppermute | solution.py:508
  60.3 3.5 %collective-permute-start.15 = (bf16[128,128]{1,0:T(8,128)(2,1)S(1)}, bf16[128,128]{1,0:T(8,128)(2,1)S(1)}, u32[]{:S(2)}, u32[]{:S(2)}) collective-permute-start(bf16[128,128]{1,0:T(8,128)(2,1)S(1)} %get-tuple-element.40), channel_id=1, source_target_pairs={{0,3},{1,2},{2,1},{3,0},{4,7},{5,6},{6,5},{7,4},{8,11},{9,10},{10,... | collective-permute-start | bytes 98312 | tf_op jit(solution)/shard_map/ppermute | solution.py:508
